TPU v7x, 32 devices: a whole 2x2x4 slice. The times are simulated.
32 devices in a mesh: dp: 8 (over y, x, core), patch: 4 (over z).
Axes of the slice: x: 2, y: 2, z: 4, core: 2. Of those that a mesh axis runs over, the one named last changes fastest.
Arguments:
- pixels: bfloat16 [256, 196, 768], P(('dp', 'patch')), may hold values from -6 to 6
- shuffle: int32 [256, 196], P(('dp', 'patch')), may hold values from 0 to 195, each once within a row
- vis_len: int32 [256], P(('dp', 'patch')), may hold values from 20 to 80, as said below
- block_owner: int32 [192], replicated, may hold values from 0 to 191, each once
- weights: float32 [192, 256, 256], P('dp'), may hold values from -0.21875 to 0.21875
- vectors: float32 [20480], P('dp')
- vec_moment: float32 [20480], P('dp'), may hold values from -1.9073486e-05 to 1.9073486e-05
- vec_second: float32 [20480], P('dp'), may hold values from 1.3768946e-13 to 5.5075784e-13
- left_stat: float32 [192, 256, 256], P('dp')
- right_stat: float32 [192, 256, 256], P('dp')
- left_root: float32 [192, 256, 256], P('dp')
- right_root: float32 [192, 256, 256], P('dp')
Outputs:
- loss_sum: float32 [], replicated
- masked_count: float32 [], replicated
- grad_norm: float32 [], replicated
- grads_clipped: float32 [192, 256, 256], P('dp')
- left_new: float32 [192, 256, 256], P('dp')
- right_new: float32 [192, 256, 256], P('dp')
- weights_new: float32 [192, 256, 256], P('dp')
- moment_new: float32 [20480], P('dp')
- second_new: float32 [20480], P('dp')
- vectors_new: float32 [20480], P('dp')
Inputs may be any that keep to these rules, and one draw needn't show every extreme that they name: `shuffle`: each row is an order of the 196 patches; its first vis_len entries are the visible ones. `vis_len`: at least one image has exactly 80 visible patches. `block_owner`: A permutation of the slots; a slot whose entry is 177 or more holds no tile.
All inputs are finite; a program needn't handle non-finite values.
Results may differ from a plain program's by a relative error of at most 0.0096.
Values may be sent and summed in bfloat16 or wider, within the bound.
No kernel may reach another device: no remote copies, remote signals or barrier semaphores. Data moves between devices by JAX's collectives and lax.ppermute only.
A program may use at most 384 MiB of HBM per device.

v0:
```python
import jax
import jax.numpy as jnp
from jax import lax
from jax.sharding import PartitionSpec as P

D = 768
HE = 12
FE = 3072
E = 512
HD = 16
FD = 2048
PIX = 768
POS = 196
VMAX = 80
BS = 256
STEP = 10
NBLK = 177


EXACT_DOT = lax.Precision.HIGHEST
EPS_NORM = 1e-06
EPS_ROOT = 1e-06
EPS_ADAM = 1e-08
CLIP_NORM = 0.01
RATE_MATRIX = 0.03
DECAY_MATRIX = 0.05
BETA_STAT = 0.5
BETA_FIRST = 0.9
BETA_SECOND = 0.999
RATE_VECTOR = 0.1
NEG_LARGE = -1e30


def cut_up(vector, lengths):
    pieces = []
    offset = 0
    for length in lengths:
        pieces.append(vector[offset : offset + length])
        offset += length
    return pieces


def matrix_shapes():
    return [
        (PIX, D),
        (D, 3 * D),
        (D, D),
        (D, FE),
        (FE, D),
        (D, E),
        (E, 3 * E),
        (E, E),
        (E, FD),
        (FD, E),
        (E, PIX),
    ]


def assemble(blocks):
    matrices = []
    offset = 0
    for row_count, col_count in matrix_shapes():
        row_tiles, col_tiles = (row_count // BS, col_count // BS)
        tile_grid = blocks[offset : offset + row_tiles * col_tiles].reshape(
            row_tiles, col_tiles, BS, BS
        )
        matrices.append(tile_grid.transpose(0, 2, 1, 3).reshape(row_count, col_count))
        offset += row_tiles * col_tiles
    return matrices


def disassemble(matrices):
    pieces = []
    for matrix in matrices:
        row_count, col_count = matrix.shape
        tile_grid = matrix.reshape(row_count // BS, BS, col_count // BS, BS).transpose(0, 2, 1, 3)
        pieces.append(tile_grid.reshape(-1, BS, BS))
    return jnp.concatenate(pieces, axis=0)


def sinusoid(count, model_width):
    half_width = model_width // 2
    frequency = jnp.exp(
        jnp.arange(half_width, dtype=jnp.float32) * (-jnp.log(10000.0) / half_width)
    )
    angles = jnp.arange(count, dtype=jnp.float32)[:, None] * frequency[None, :]
    return jnp.concatenate([jnp.sin(angles), jnp.cos(angles)], axis=1)


def layer_norm(inputs, gain_vec, shift_vec):
    centred = inputs - jnp.mean(inputs, axis=-1, keepdims=True)
    spread = jnp.mean(centred * centred, axis=-1, keepdims=True)
    return centred * lax.rsqrt(spread + EPS_NORM) * gain_vec + shift_vec


def target_norm(pixel_rows):
    centred = pixel_rows - jnp.mean(pixel_rows, axis=-1, keepdims=True)
    return centred * lax.rsqrt(jnp.mean(centred * centred, axis=-1, keepdims=True) + EPS_NORM)


def gelu_exact(inputs):
    return jax.nn.gelu(inputs, approximate=False)


def position_rank(shuffle):
    indices = jnp.arange(POS, dtype=jnp.int32)
    matches = shuffle[:, :, None] == indices[None, None, :]
    return jnp.sum(jnp.where(matches, indices[None, :, None], 0), axis=1)


def take_rows(source, indices):
    return jax.vmap(lambda one_image, one_index: one_image[one_index])(source, indices)


def matmul(inputs_low, matrix):
    return jnp.dot(inputs_low, matrix, preferred_element_type=jnp.float32)


def matmul_back(grads_low, matrix):
    return lax.dot_general(
        grads_low, matrix, (((2,), (1,)), ((), ())), preferred_element_type=jnp.float32
    )


def row_product(inputs_low, grads_low):
    return lax.dot_general(
        inputs_low, grads_low, (((0, 1), (0, 1)), ((), ())), preferred_element_type=jnp.float32
    )


def bias_grad(grads_low):
    return jnp.sum(grads_low, axis=(0, 1), dtype=jnp.float32)


def head_split(projected, head_count):
    batch_size, seq_length, triple = projected.shape
    head_size = triple // (3 * head_count)
    shaped = projected.reshape(batch_size, seq_length, 3, head_count, head_size)
    return (shaped[:, :, 0], shaped[:, :, 1], shaped[:, :, 2], head_size)


def attention_scores(queries, keys_in, key_valid, head_size):
    scores = jnp.einsum(
        "bqhd,bkhd->bhqk", queries, keys_in, preferred_element_type=jnp.float32
    ) * head_size ** (-0.5)
    return jnp.where(key_valid[:, None, None, :], scores, NEG_LARGE)


def layer_forward(residual_in, vector, matrices, head_count, key_valid):
    w_qkv, w_out, w_up, w_down = matrices
    batch_size, seq_length, model_width = residual_in.shape
    hidden = w_up.shape[1]
    (
        gain_one,
        shift_one,
        bias_query,
        bias_value,
        bias_out,
        gain_two,
        shift_two,
        bias_up,
        bias_down,
    ) = cut_up(vector, [model_width] * 7 + [hidden, model_width])
    normed, norm_one_back = jax.vjp(layer_norm, residual_in, gain_one, shift_one)
    normed_low = normed.astype(jnp.bfloat16)
    qkv_bias = jnp.concatenate([bias_query, jnp.zeros_like(bias_query), bias_value])
    projected = (matmul(normed_low, w_qkv) + qkv_bias).astype(jnp.bfloat16)
    queries, keys_in, values, head_size = head_split(projected, head_count)
    scores = attention_scores(queries, keys_in, key_valid, head_size)
    log_total = jax.nn.logsumexp(scores, axis=-1, keepdims=True)
    probs_low = jnp.exp(scores - log_total).astype(jnp.bfloat16)
    attended = jnp.einsum("bhqk,bkhd->bqhd", probs_low, values, preferred_element_type=jnp.float32)
    attended = attended.astype(jnp.bfloat16).reshape(batch_size, seq_length, model_width)
    residual_mid = residual_in + matmul(attended, w_out) + bias_out
    normed_two, norm_two_back = jax.vjp(layer_norm, residual_mid, gain_two, shift_two)
    normed_two_low = normed_two.astype(jnp.bfloat16)
    activation, gelu_back = jax.vjp(gelu_exact, matmul(normed_two_low, w_up) + bias_up)
    activation_low = activation.astype(jnp.bfloat16)
    residual_out = residual_mid + matmul(activation_low, w_down) + bias_down
    cached = (
        norm_one_back,
        normed_low,
        projected,
        log_total,
        attended,
        norm_two_back,
        normed_two_low,
        gelu_back,
        activation_low,
    )
    return (residual_out, cached)


def layer_backward(grad_out, cached, matrices, head_count, key_valid):
    (
        norm_one_back,
        normed_low,
        projected,
        log_total,
        attended,
        norm_two_back,
        normed_two_low,
        gelu_back,
        activation_low,
    ) = cached
    w_qkv, w_out, w_up, w_down = matrices
    batch_size, seq_length, model_width = grad_out.shape
    grad_down = grad_out.astype(jnp.bfloat16)
    d_down = row_product(activation_low, grad_down)
    grad_up = gelu_back(matmul_back(grad_down, w_down))[0].astype(jnp.bfloat16)
    d_up = row_product(normed_two_low, grad_up)
    grad_mid, d_gain_two, d_shift_two = norm_two_back(matmul_back(grad_up, w_up))
    grad_mid = grad_out + grad_mid
    grad_proj = grad_mid.astype(jnp.bfloat16)
    d_out = row_product(attended, grad_proj)
    queries, keys_in, values, head_size = head_split(projected, head_count)
    grad_att = (
        matmul_back(grad_proj, w_out)
        .astype(jnp.bfloat16)
        .reshape(batch_size, seq_length, head_count, head_size)
    )
    probs = jnp.exp(attention_scores(queries, keys_in, key_valid, head_size) - log_total)
    grad_probs = jnp.einsum("bqhd,bkhd->bhqk", grad_att, values, preferred_element_type=jnp.float32)
    grad_values = jnp.einsum(
        "bhqk,bqhd->bkhd", probs.astype(jnp.bfloat16), grad_att, preferred_element_type=jnp.float32
    )
    grad_scores = (
        probs * (grad_probs - jnp.sum(grad_probs * probs, axis=-1, keepdims=True))
    ).astype(jnp.bfloat16)
    scale_factor = head_size ** (-0.5)
    grad_queries = (
        jnp.einsum("bhqk,bkhd->bqhd", grad_scores, keys_in, preferred_element_type=jnp.float32)
        * scale_factor
    )
    grad_keys = (
        jnp.einsum("bhqk,bqhd->bkhd", grad_scores, queries, preferred_element_type=jnp.float32)
        * scale_factor
    )
    grad_qkv = (
        jnp.stack([grad_queries, grad_keys, grad_values], axis=2)
        .astype(jnp.bfloat16)
        .reshape(batch_size, seq_length, 3 * model_width)
    )
    d_qkv = row_product(normed_low, grad_qkv)
    qkv_sums = bias_grad(grad_qkv)
    grad_in, d_gain_one, d_shift_one = norm_one_back(matmul_back(grad_qkv, w_qkv))
    grad_in = grad_mid + grad_in
    vector_grad = jnp.concatenate(
        [
            d_gain_one,
            d_shift_one,
            qkv_sums[:model_width],
            qkv_sums[2 * model_width :],
            bias_grad(grad_proj),
            d_gain_two,
            d_shift_two,
            bias_grad(grad_up),
            bias_grad(grad_down),
        ]
    )
    return (grad_in, [d_qkv, d_out, d_up, d_down], vector_grad)


def optimizer_update(clipped, clipped_vec, states):
    weights, left_stat, right_stat, left_root, right_root, vectors, vec_moment, vec_second = states
    left_new = BETA_STAT * left_stat + (1.0 - BETA_STAT) * jnp.einsum(
        "sik,sjk->sij", clipped, clipped, precision=EXACT_DOT
    )
    right_new = BETA_STAT * right_stat + (1.0 - BETA_STAT) * jnp.einsum(
        "ski,skj->sij", clipped, clipped, precision=EXACT_DOT
    )
    direction = jnp.einsum(
        "sij,sjk->sik",
        jnp.einsum("sij,sjk->sik", left_root, clipped, precision=EXACT_DOT),
        right_root,
        precision=EXACT_DOT,
    )
    direction = direction * lax.rsqrt(
        jnp.mean(direction * direction, axis=(1, 2), keepdims=True) + EPS_ROOT
    )
    weights_new = weights - RATE_MATRIX * (direction + DECAY_MATRIX * weights)
    moment_new = BETA_FIRST * vec_moment + (1.0 - BETA_FIRST) * clipped_vec
    second_new = BETA_SECOND * vec_second + (1.0 - BETA_SECOND) * clipped_vec * clipped_vec
    corrected = moment_new / (1.0 - BETA_FIRST**STEP)
    second_scaled = second_new / (1.0 - BETA_SECOND**STEP)
    vectors_new = vectors - RATE_VECTOR * corrected / (jnp.sqrt(second_scaled) + EPS_ADAM)
    return (clipped, left_new, right_new, weights_new, moment_new, second_new, vectors_new)


def shards(
    pixels,
    shuffle,
    vis_len,
    block_owner,
    weights,
    vectors,
    vec_moment,
    vec_second,
    left_stat,
    right_stat,
    left_root,
    right_root,
):
    slots_low, vector_low = (
        lax.all_gather(weights.astype(jnp.bfloat16), "dp", axis=0, tiled=True),
        lax.all_gather(vectors.astype(jnp.bfloat16), "dp", axis=0, tiled=True),
    )
    slot_total = slots_low.shape[0]
    masked_local = jnp.sum(POS - vis_len).astype(jnp.float32)
    masked_count = lax.psum(masked_local, ("dp", "patch"))
    slot_index = jnp.arange(slot_total, dtype=jnp.int32)
    slot_of_block = jnp.sum(
        jnp.where(block_owner[None, :] == slot_index[:NBLK, None], slot_index[None, :], 0), axis=1
    )
    matrices = assemble(slots_low[slot_of_block])
    (
        w_embed,
        enc_qkv,
        enc_out,
        enc_up,
        enc_down,
        w_proj,
        dec_qkv,
        dec_out,
        dec_up,
        dec_down,
        w_head,
    ) = matrices
    vector = vector_low.astype(jnp.float32)
    (
        bias_embed,
        enc_vector,
        enc_gain,
        enc_shift,
        bias_proj,
        mask_token,
        dec_vector,
        dec_gain,
        dec_shift,
        bias_head,
    ) = cut_up(vector, [D, 8 * D + FE, D, D, E, E, 8 * E + FD, E, E, PIX])
    enc_mats = (enc_qkv, enc_out, enc_up, enc_down)
    dec_mats = (dec_qkv, dec_out, dec_up, dec_down)
    images = pixels.shape[0]
    visible_ids = shuffle[:, :VMAX]
    pixel_visible = take_rows(pixels, visible_ids)
    embedded = matmul(pixel_visible, w_embed) + bias_embed + sinusoid(POS, D)[visible_ids]
    slot_valid = jnp.arange(VMAX, dtype=jnp.int32)[None, :] < vis_len[:, None]
    encoded, enc_cached = layer_forward(embedded, enc_vector, enc_mats, HE, slot_valid)
    enc_normed, enc_norm_back = jax.vjp(layer_norm, encoded, enc_gain, enc_shift)
    enc_normed_low = enc_normed.astype(jnp.bfloat16)
    latent = matmul(enc_normed_low, w_proj) + bias_proj
    ranked = position_rank(shuffle)
    visible = ranked < vis_len[:, None]
    placed = take_rows(latent, jnp.minimum(ranked, VMAX - 1))
    decoded_in = jnp.where(visible[:, :, None], placed, mask_token) + sinusoid(POS, E)
    all_valid = jnp.ones((images, POS), jnp.bool_)
    decoded, dec_cached = layer_forward(decoded_in, dec_vector, dec_mats, HD, all_valid)
    dec_normed, dec_norm_back = jax.vjp(layer_norm, decoded, dec_gain, dec_shift)
    dec_normed_low = dec_normed.astype(jnp.bfloat16)
    predicted = matmul(dec_normed_low, w_head) + bias_head
    residual_pix = predicted - target_norm(pixels.astype(jnp.float32))
    patch_error = jnp.mean(residual_pix * residual_pix, axis=-1)
    loss_local = jnp.sum(jnp.where(visible, 0.0, patch_error))
    grad_pred = (
        jnp.where(visible[:, :, None], 0.0, residual_pix) * (2.0 / PIX) / masked_count
    ).astype(jnp.bfloat16)
    d_head = row_product(dec_normed_low, grad_pred)
    grad_dec, d_dec_gain, d_dec_shift = dec_norm_back(matmul_back(grad_pred, w_head))
    grad_dec_in, dec_grads, dec_vec_grad = layer_backward(
        grad_dec, dec_cached, dec_mats, HD, all_valid
    )
    d_mask = jnp.sum(jnp.where(visible[:, :, None], 0.0, grad_dec_in), axis=(0, 1))
    grad_latent = jnp.where(
        slot_valid[:, :, None], take_rows(grad_dec_in, visible_ids), 0.0
    ).astype(jnp.bfloat16)
    d_proj = row_product(enc_normed_low, grad_latent)
    grad_enc, d_enc_gain, d_enc_shift = enc_norm_back(matmul_back(grad_latent, w_proj))
    grad_embedded, enc_grads, enc_vec_grad = layer_backward(
        grad_enc, enc_cached, enc_mats, HE, slot_valid
    )
    grad_embed_low = grad_embedded.astype(jnp.bfloat16)
    d_embed = row_product(pixel_visible, grad_embed_low)
    grad_mats = [d_embed] + enc_grads + [d_proj] + dec_grads + [d_head]
    grad_vector = jnp.concatenate(
        [
            bias_grad(grad_embed_low),
            enc_vec_grad,
            d_enc_gain,
            d_enc_shift,
            bias_grad(grad_latent),
            d_mask,
            dec_vec_grad,
            d_dec_gain,
            d_dec_shift,
            bias_grad(grad_pred),
        ]
    )
    grad_blocks = jnp.concatenate(
        [disassemble(grad_mats), jnp.zeros((slot_total - NBLK, BS, BS), jnp.float32)], axis=0
    )
    grad_slots = grad_blocks[block_owner]
    full_states = (
        weights,
        left_stat,
        right_stat,
        left_root,
        right_root,
        vectors,
        vec_moment,
        vec_second,
    )
    grad_shard, vec_shard = (
        lax.psum_scatter(
            grad_slots.astype(jnp.bfloat16), "dp", scatter_dimension=0, tiled=True
        ).astype(jnp.float32),
        lax.psum_scatter(
            grad_vector.astype(jnp.bfloat16), "dp", scatter_dimension=0, tiled=True
        ).astype(jnp.float32),
    )
    grad_shard, vec_shard = lax.psum((grad_shard, vec_shard), "patch")
    own_square = jnp.sum(grad_shard * grad_shard) + jnp.sum(vec_shard * vec_shard)
    square_part = jnp.where(lax.axis_index("patch") == 0, own_square, 0.0)
    loss_sum, square_sum = lax.psum((loss_local, square_part), ("dp", "patch"))
    grad_norm = jnp.sqrt(square_sum)
    factor = jnp.minimum(1.0, CLIP_NORM / grad_norm)
    outputs = optimizer_update(grad_shard * factor, vec_shard * factor, full_states)
    clipped, left_new, right_new, weights_new, moment_new, second_new, vectors_new = outputs
    return (
        loss_sum,
        masked_count,
        grad_norm,
        clipped,
        left_new,
        right_new,
        weights_new,
        moment_new,
        second_new,
        vectors_new,
    )


def solution(mesh):
    return jax.shard_map(
        shards,
        mesh=mesh,
        in_specs=(
            P(("dp", "patch"), None, None),
            P(("dp", "patch"), None),
            P(("dp", "patch")),
            P(),
            P("dp", None, None),
            P("dp"),
            P("dp"),
            P("dp"),
            P("dp", None, None),
            P("dp", None, None),
            P("dp", None, None),
            P("dp", None, None),
        ),
        out_specs=(
            P(),
            P(),
            P(),
            P("dp", None, None),
            P("dp", None, None),
            P("dp", None, None),
            P("dp", None, None),
            P("dp"),
            P("dp"),
            P("dp"),
        ),
        check_vma=False,
    )
```

profile of v0, /device:TPU:0, one launch (start us, length us, event | category | flops | bytes accessed | tf_op | source)
XLA Modules:
  0.0 1321.5 jit_solution(2393194073233258916)
XLA Ops:
  13.5 42.4 %psum.36 = f32[]{:T(128)} all-reduce(f32[]{:T(128)S(6)} %convert_element_type.211), channel_id=1, replica_groups=mesh['dp'=8,'patch'=4] {'dp','patch'}, use_global_device_ids=true, to_apply=%region_24.25 | all-reduce | flops 1 | bytes 8 | tf_op jit(solution)/shard_map/psum | solution.py:310
  56.0 10.2 all-gather
  68.2 8.8 gather_fusion.3
  89.6 51.8 %all-gather.3.cloned.1.call-done = bf16[192,256,256]{2,1,0:T(8,128)(2,1)} async-done(((bf16[24,256,256]{2,1,0:T(8,128)(2,1)}), bf16[192,256,256]{2,1,0:T(8,128)(2,1)}) %all-gather.3.cloned.1.call-update) | async-done | bytes 25165840 | tf_op jit(solution)/shard_map/all_gather | solution.py:305
  141.4 19.0 %gather_fusion = bf16[177,256,256]{2,1,0:T(8,128)(2,1)} fusion(bf16[192,256,256]{2,1,0:T(8,128)(2,1)} %all-gather.3.cloned.1.call-done, s32[1024]{0:T(1024)S(1)} %pad_clamp_fusion.2), kind=kCustom, calls=%fused_computation | custom fusion | bytes 46400196 | tf_op jit(solution)/shard_map/gather | solution.py:315
  170.5 8.8 fusion.129
  253.9 8.0 copy.373
  261.9 9.2 reshape.657
  271.1 8.6 copy.214
  279.7 6.1 copy.341
  291.3 19.1 %multiply_convert_fusion.2 = (bf16[8,80,3072]{2,1,0:T(8,128)(2,1)S(1)}, f32[8,80,3072]{2,1,0:T(8,128)}) fusion(f32[8,80,3072]{2,1,0:T(8,128)S(1)} %get-tuple-element.126, f32[3072]{0:T(1024)S(1)} %copy-done.103, u8[80,3072]{1,0:T(8,128)(4,1)S(1)} %get-tuple-element.13, u8[80,3072]{1,0:T(8,128)(4,1)S(1)} %get-tuple-element.12), kind=kLoop, calls=%fused_computation.44 | loop fusion | flops 139591680 | bytes 20164608 | tf_op jit(solution)/shard_map/convert_element_type | solution.py:178
  316.1 24.7 %gather_fusion.4 = f32[1568,512]{1,0:T(8,128)} fusion(f32[8,80,512]{2,1,0:T(8,128)S(1)} %convolution_add_fusion, s32[1568]{0:T(1024)S(1)} %reshape.631), kind=kCustom, calls=%fused_computation.4 | custom fusion | bytes 6435072 | tf_op jit(solution)/shard_map/vmap()/gather | solution.py:112
  351.3 8.1 copy.219
  359.4 14.6 %multiply_reduce_fusion.1 = (f32[8,16,196]{2,1,0:T(8,128)S(1)}, f32[8,16,196,196]{2,3,1,0:T(8,128)}) fusion(bf16[8,196,3,16,32]{1,4,3,2,0:T(8,128)(2,1)} %bitcast.394), kind=kOutput, calls=%fused_computation.10 | convolution fusion | flops 324513280 | bytes 23963648 | tf_op jit(solution)/shard_map/bqhd,bkhd->bhqk/dot_general | solution.py:143
  374.0 9.4 exponential_reduce_fusion
  383.4 15.3 %convolution_convert_fusion = bf16[8,16,32,196]{3,2,1,0:T(8,128)(2,1)} fusion(bf16[8,196,3,16,32]{1,4,3,2,0:T(8,128)(2,1)} %bitcast.395, f32[8,16,196,196]{2,3,1,0:T(8,128)} %get-tuple-element.130, f32[8,16,196]{2,1,0:T(8,128)S(1)} %log_add_fusion), kind=kOutput, calls=%fused_computation.173 | convolution fusion | flops 330258432 | bytes 30017536 | tf_op jit(solution)/shard_map/bhqk,bkhd->bqhd/dot_general | solution.py:172
  410.1 7.3 fusion.35
  417.4 31.0 %multiply_convert_fusion.1 = (bf16[8,196,2048]{2,1,0:T(8,128)(2,1)S(1)}, f32[8,196,2048]{2,1,0:T(8,128)}) fusion(f32[8,196,2048]{2,1,0:T(8,128)S(1)} %get-tuple-element.132, f32[2048]{0:T(1024)S(1)} %copy-done.131, u8[196,2048]{1,0:T(8,128)(4,1)S(1)} %get-tuple-element.11, u8[196,2048]{1,0:T(8,128)(4,1)S(1)} %get-tuple-element.10), kind=kLoop, calls=%fused_computation.20 | loop fusion | flops 227999744 | bytes 32923648 | tf_op jit(solution)/shard_map/convert_element_type | solution.py:178
  448.5 5.7 fusion.124
  480.1 15.9 %fusion.140 = (bf16[2048]{0:T(1024)(128)(2,1)}, bf16[8,196,2048]{2,1,0:T(8,128)(2,1)}) fusion(f32[8,196,2048]{2,1,0:T(8,128)} %get-tuple-element.72, bf16[8,196,512]{2,1,0:T(8,128)(2,1)} %copy-done.59, bf16[2048,512,1]{1,0,2:T(8,128)(2,1)S(1)} %copy-done.58, f32[8,196,2048]{2,1,0:T(8,128)} %copy-done.28, f32[2048]{0:T(1024)S(1)} %copy-done.131), kind=kOutput, calls=%fused_computation.343 | convolution fusion | flops 3339712512 | bytes 35827712 | tf_op jit(solution)/shard_map/dot_general | solution.py:120
  496.0 7.8 multiply_reduce_fusion.7
  503.8 5.7 fusion.83
  517.6 14.8 %convolution_bitcast_fusion.3 = bf16[8,196,1,16,32]{1,4,3,0,2:T(8,128)(2,1)} fusion(bf16[8,196,16,32]{1,3,2,0:T(8,128)(2,1)S(1)} %bitcast.399, f32[8,16,196,196]{2,3,1,0:T(8,128)} %get-tuple-element.130, f32[8,16,196]{2,1,0:T(8,128)S(1)} %log_add_fusion), kind=kOutput, calls=%fused_computation.141 | convolution fusion | flops 329455616 | bytes 22980608 | tf_op jit(solution)/shard_map/bhqk,bqhd->bkhd/dot_general | solution.py:224
  532.4 18.6 %multiply_reduce_fusion = (f32[8,16,196]{2,1,0:T(8,128)S(1)}, f32[8,16,196,196]{2,3,1,0:T(8,128)}) fusion(f32[8,16,196,196]{2,3,1,0:T(8,128)} %get-tuple-element.130, f32[8,16,196]{2,1,0:T(8,128)S(1)} %log_add_fusion, bf16[8,196,16,32]{1,3,2,0:T(8,128)(2,1)S(1)} %bitcast.400, bf16[8,196,3,16,32]{1,4,3,2,0:T(8,128)(2,1)} %bitcast.396), kind=kOutput, calls=%fused_computation.7 | convolution fusion | flops 334347776 | bytes 49786880 | tf_op jit(solution)/shard_map/bqhd,bkhd->bhqk/dot_general | solution.py:223
  551.0 21.9 %multiply_convert_fusion = bf16[8,16,196,196]{2,3,1,0:T(8,128)(2,1)} fusion(f32[8,16,196,196]{2,3,1,0:T(8,128)} %get-tuple-element.139, f32[8,16,196,196]{2,3,1,0:T(8,128)} %get-tuple-element.130, f32[8,16,196]{2,1,0:T(8,128)S(1)} %get-tuple-element.138, f32[8,16,196]{2,1,0:T(8,128)S(1)} %log_add_fusion), kind=kLoop, calls=%fused_computation.6 | loop fusion | flops 24586240 | bytes 49373184 | tf_op jit(solution)/shard_map/convert_element_type | solution.py:229
  572.9 9.5 multiply_bitcast_fusion
  582.4 8.0 multiply_bitcast_fusion.1
  608.1 10.3 gather_fusion.5
  628.3 5.6 convolution_bitcast_fusion
  634.0 10.2 fusion.139
  644.2 6.5 multiply_reduce_fusion.16
  650.7 6.5 convolution_bitcast_fusion.1
  713.9 6.1 fusion.28
  724.8 9.2 reshape.589
  734.0 9.1 copy.257
  743.0 9.1 reshape.587
  752.2 6.9 copy.255
  777.0 6.2 copy.251
  783.2 8.1 copy.262
  821.3 19.6 %gather_fusion.2 = bf16[192,256,256]{2,1,0:T(8,128)(2,1)} fusion(bf16[192,256,256]{2,1,0:T(8,128)(2,1)} %broadcast_dynamic-update-slice_fusion, s32[1024]{0:T(1024)} %get-tuple-element.152), kind=kCustom, calls=%fused_computation.2 | custom fusion | bytes 50332416 | tf_op jit(solution)/shard_map/gather | solution.py:402
  848.7 23.9 %all-reduce = bf16[20480]{0:T(1024)(128)(2,1)S(1)} all-reduce(bf16[20480]{0:T(1024)(128)(2,1)S(1)} %dynamic-update-slice.25), channel_id=3, replica_groups=mesh['dp'=8,'patch'=4] {'dp'}, use_global_device_ids=true, to_apply=%region_66.67.clone | all-reduce | flops 20480 | bytes 81920
  873.3 125.0 %reduce-scatter.2.cloned.1.call-done = bf16[24,256,256]{2,1,0:T(8,128)(2,1)} async-done(((bf16[192,256,256]{2,1,0:T(8,128)(2,1)}), bf16[24,256,256]{2,1,0:T(8,128)(2,1)}) %reduce-scatter.2.cloned.1.call-update) | async-done | bytes 3145744 | tf_op jit(solution)/shard_map/reduce_scatter | solution.py:414
  998.4 216.6 %all-reduce.4 = (f32[24,256,256]{2,1,0:T(8,128)}, f32[2560]{0:T(1024)S(1)}) all-reduce(bf16[24,256,256]{2,1,0:T(8,128)(2,1)} %reduce-scatter.2.cloned.1.call-done, f32[2560]{0:T(1024)S(1)} %dynamic-slice_convert_fusion), channel_id=1, replica_groups=mesh['dp'=8,'patch'=4] {'patch'}, use_global_device_ids=true, to_apply=%region_40.41 | all-reduce | flops 1575424 | bytes 9457664 | tf_op jit(solution)/shard_map/psum | solution.py:421
  1221.9 38.2 %all-reduce.1 = (f32[]{:T(128)}, f32[]{:T(128)}) all-reduce(f32[]{:T(128)} %select_reduce_fusion.3, f32[]{:T(128)S(6)} %select_n.110), channel_id=1, replica_groups=mesh['dp'=8,'patch'=4] {'dp','patch'}, use_global_device_ids=true, to_apply=%region_22.23 | all-reduce | flops 2 | bytes 16 | tf_op jit(solution)/shard_map/psum | solution.py:424
  1265.5 8.3 fusion.141
  1273.9 9.4 multiply_reduce_fusion.2
  1283.3 14.8 %add_multiply_fusion = f32[24,256,256]{2,1,0:T(8,128)} fusion(f32[24,256,256]{2,1,0:T(8,128)} %param.21, f32[24,256,256]{2,1,0:T(8,128)S(1)} %broadcast_multiply_fusion), kind=kOutput, calls=%fused_computation.60 | convolution fusion | flops 4834983936 | bytes 18874368 | tf_op jit(solution)/shard_map/ski,skj->sij/dot_general | solution.py:269
  1298.2 10.4 add_multiply_fusion.1
  (649 shorter events, 329.9 us)
Async XLA Ops:
  7.2 48.8 %copy-start.105 = (f32[2560]{0:T(1024)S(1)}, f32[2560]{0:T(1024)}, u32[]{:S(2)}) copy-start(f32[2560]{0:T(1024)} %param.17) | copy-start | bytes 30724
  7.2 134.2 %all-gather.3.cloned.1.call-start = ((), (), s32[]{:S(2)}) async-start(), calls=%async_computation.1 | async-start | bytes 28311552 | tf_op jit(solution)/shard_map/all_gather | solution.py:305
  12.1 55.4 %copy-start.129 = (s32[8,196]{1,0:T(8,128)S(1)}, s32[8,196]{1,0:T(8,128)}, u32[]{:S(2)}) copy-start(s32[8,196]{1,0:T(8,128)} %param.13) | copy-start | bytes 18820
  12.1 56.1 %copy-start.5 = (bf16[8,196,768]{2,0,1:T(8,128)(2,1)S(1)}, bf16[8,196,768]{2,0,1:T(8,128)(2,1)}, u32[]{:S(2)}) copy-start(bf16[8,196,768]{2,0,1:T(8,128)(2,1)} %param.12) | copy-start | bytes 7225348
  12.2 986.2 %reduce-scatter.2.cloned.1.call-start = ((), (), s32[]{:S(2)}) async-start(), calls=%async_computation.2 | async-start | bytes 28311552 | tf_op jit(solution)/shard_map/reduce_scatter | solution.py:414
  67.7 9.3 copy-start.3
  68.1 19.1 %copy-start.76 = (s32[8,196]{1,0:T(8,128)}, s32[8,196]{1,0:T(8,128)S(1)}, u32[]{:S(2)}) copy-start(s32[8,196]{1,0:T(8,128)S(1)} %select_reduce_fusion.1) | copy-start | bytes 18820
  68.2 8.8 copy-start.169
  83.0 320.5 %copy-start.82 = (f32[512]{0:T(512)}, f32[512]{0:T(512)S(1)}, u32[]{:S(2)}) copy-start(f32[512]{0:T(512)S(1)} %get-tuple-element.110) | copy-start | bytes 6148
  88.0 72.4 %copy-start.94 = (f32[8,196]{1,0:T(8,128)}, f32[8,196]{1,0:T(8,128)S(1)}, u32[]{:S(2)}) copy-start(f32[8,196]{1,0:T(8,128)S(1)} %broadcast_multiply_fusion.1) | copy-start | bytes 18820
  170.5 8.8 slice-start
  170.5 12.3 slice-start.1
  237.3 73.2 %copy-start.11 = (f32[8,80,768]{2,1,0:T(8,128)}, f32[8,80,768]{2,1,0:T(8,128)S(1)}, u32[]{:S(2)}) copy-start(f32[8,80,768]{2,1,0:T(8,128)S(1)} %get-tuple-element.125) | copy-start | bytes 5898244
  237.3 48.5 %copy-start.96 = (f32[8,80]{1,0:T(8,128)}, f32[8,80]{1,0:T(8,128)S(1)}, u32[]{:S(2)}) copy-start(f32[8,80]{1,0:T(8,128)S(1)} %broadcast_multiply_fusion.6) | copy-start | bytes 7684
  237.7 48.2 %copy-start.111 = (f32[8,80]{1,0:T(8,128)}, f32[8,80]{1,0:T(8,128)S(1)}, u32[]{:S(2)}) copy-start(f32[8,80]{1,0:T(8,128)S(1)} %fusion.97) | copy-start | bytes 7684
  285.8 24.6 %copy-start.45 = (bf16[96,8,12,256]{3,1,2,0:T(8,128)(2,1)}, bf16[96,8,12,256]{3,1,2,0:T(8,128)(2,1)S(1)}, u32[]{:S(2)}) copy-start(bf16[96,8,12,256]{3,1,2,0:T(8,128)(2,1)S(1)} %copy.341) | copy-start | bytes 14155780
  291.3 19.1 %copy-start.38 = (f32[8,80,3072]{2,1,0:T(8,128)}, f32[8,80,3072]{2,1,0:T(8,128)S(1)}, u32[]{:S(2)}) copy-start(f32[8,80,3072]{2,1,0:T(8,128)S(1)} %get-tuple-element.126) | copy-start | bytes 23592964
  291.3 19.1 %copy-start.168 = (f32[768]{0:T(1024)S(1)}, f32[768]{0:T(1024)}, u32[]{:S(2)}) copy-start(f32[768]{0:T(1024)} %get-tuple-element.91) | copy-start | bytes 9220
  342.9 60.5 %copy-start.1 = (f32[8,196,512]{2,1,0:T(8,128)}, f32[8,196,512]{2,1,0:T(8,128)S(1)}, u32[]{:S(2)}) copy-start(f32[8,196,512]{2,1,0:T(8,128)S(1)} %reshape.634) | copy-start | bytes 9633796
  408.5 101.0 %copy-start.78 = (f32[8,196]{1,0:T(8,128)}, f32[8,196]{1,0:T(8,128)S(1)}, u32[]{:S(2)}) copy-start(f32[8,196]{1,0:T(8,128)S(1)} %broadcast_multiply_fusion.3) | copy-start | bytes 18820
  409.3 100.3 %copy-start.90 = (f32[8,196]{1,0:T(8,128)}, f32[8,196]{1,0:T(8,128)S(1)}, u32[]{:S(2)}) copy-start(f32[8,196]{1,0:T(8,128)S(1)} %fusion.94) | copy-start | bytes 18820
  417.4 31.1 %copy-start.28 = (f32[8,196,2048]{2,1,0:T(8,128)}, f32[8,196,2048]{2,1,0:T(8,128)S(1)}, u32[]{:S(2)}) copy-start(f32[8,196,2048]{2,1,0:T(8,128)S(1)} %get-tuple-element.132) | copy-start | bytes 38535172
  417.4 31.1 %copy-start.57 = (bf16[2048,512,1]{1,0,2:T(8,128)(2,1)S(1)}, bf16[2048,512,1]{1,0,2:T(8,128)(2,1)}, u32[]{:S(2)}) copy-start(bf16[2048,512,1]{1,0,2:T(8,128)(2,1)} %reshape.663) | copy-start | bytes 6291460
  417.4 31.1 %copy-start.156 = (f32[512]{0:T(512)S(1)}, f32[512]{0:T(512)}, u32[]{:S(2)}) copy-start(f32[512]{0:T(512)} %get-tuple-element.102) | copy-start | bytes 6148
  454.3 14.5 %copy-start.80 = (f32[8,196]{1,0:T(8,128)}, f32[8,196]{1,0:T(8,128)S(1)}, u32[]{:S(2)}) copy-start(f32[8,196]{1,0:T(8,128)S(1)} %broadcast_multiply_fusion.2) | copy-start | bytes 18820
  455.0 13.8 %copy-start.92 = (f32[8,196]{1,0:T(8,128)}, f32[8,196]{1,0:T(8,128)S(1)}, u32[]{:S(2)}) copy-start(f32[8,196]{1,0:T(8,128)S(1)} %fusion.95) | copy-start | bytes 18820
  470.4 40.6 %copy-start.9 = (f32[8,196,512]{2,1,0:T(8,128)}, f32[8,196,512]{2,1,0:T(8,128)S(1)}, u32[]{:S(2)}) copy-start(f32[8,196,512]{2,1,0:T(8,128)S(1)} %get-tuple-element.68) | copy-start | bytes 9633796
  471.4 8.7 copy-start.59
  608.1 10.3 copy-start.134
  608.1 12.2 copy-start.99
  608.1 12.2 copy-start.108
  608.1 12.2 copy-start.114
  608.1 12.2 copy-start.167
  626.2 33.9 %copy-start.16 = (f32[8,80,768]{2,1,0:T(8,128)}, f32[8,80,768]{2,1,0:T(8,128)S(1)}, u32[]{:S(2)}) copy-start(f32[8,80,768]{2,1,0:T(8,128)S(1)} %get-tuple-element.64) | copy-start | bytes 5898244
  633.9 10.3 copy-start.12
  633.9 10.3 copy-start.97
  633.9 10.2 copy-start.110
  634.0 10.2 copy-start.112
  665.7 10.4 slice-start.9
  841.2 31.5 %copy-start.77 = (s32[8,196]{1,0:T(8,128)S(1)}, s32[8,196]{1,0:T(8,128)}, u32[]{:S(2)}) copy-start(s32[8,196]{1,0:T(8,128)} %copy-done.76) | copy-start | bytes 18820
  841.2 31.5 %copy-start.153 = (f32[8,196]{1,0:T(8,128)S(1)}, f32[8,196]{1,0:T(8,128)}, u32[]{:S(2)}) copy-start(f32[8,196]{1,0:T(8,128)} %get-tuple-element.134) | copy-start | bytes 18820
  841.2 31.4 %copy-start.180 = (s32[8]{0:T(128)S(1)}, s32[8]{0:T(128)}, u32[]{:S(2)}) copy-start(s32[8]{0:T(128)} %param.14) | copy-start | bytes 100
  1265.5 32.6 %copy-start = (f32[24,256,256]{2,1,0:T(8,128)}, f32[24,256,256]{2,1,0:T(8,128)S(1)}, u32[]{:S(2)}) copy-start(f32[24,256,256]{2,1,0:T(8,128)S(1)} %broadcast_multiply_fusion) | copy-start | bytes 18874372
  1283.3 25.9 %slice-start.3 = ((s8[6291456]{0:T(1024)(128)(4,1)}), s8[4194304]{0:T(1024)(128)(4,1)S(1)}, s32[]{:S(2)}) async-start(s8[6291456]{0:T(1024)(128)(4,1)} %bitcast.401), calls=%async_computation.6 | async-start | bytes 8388608
  1298.1 10.5 copy-start.106
  1298.1 10.5 copy-start.145
  1298.1 10.5 copy-start.146
  1298.1 11.1 slice-start.4
  (161 other events, 633.5 us)
Sparse Core Ops, SparseCore 0:
  12.3 129.0 all-gather.2
  841.4 156.9 reduce-scatter.1
where the time goes:
time: 1330 us; the launch traced here: 1320 us
  local copies, waits for them, and re-layouts  348 us (26%)
  blocking collectives  331 us (25%)
  matrix products  286 us (22%)
  waiting for transfers between devices  177 us (13%)
  other arithmetic  159 us (12%)
  between operations  21.2 us (2%)
    psum x1, blocking collectives, shards(): grad_shard, vec_shard = lax.psum((grad_shard, vec_shard), 'patch')  217 us
    reduce_scatter x1, waiting for transfers between devices, shards(): lax.psum_scatter(grad_slots.astype(jnp.bfloat16), 'dp', scatter_dimension...  125 us
    dot_general x10, matrix products, matmul_back(): lax.dot_general(grads_low, matrix, (((2,), (1,)), ((), ())), preferred_el...  56.8 us
    unnamed x452, local copies, waits for them, and re-layouts  56.5 us
    all_gather x1, waiting for transfers between devices, shards(): lax.all_gather(weights.astype(jnp.bfloat16), 'dp', axis=0, tiled=True)  51.8 us
    convert_element_type x2, other arithmetic, layer_forward(): activation_low = activation.astype(jnp.bfloat16)  50.1 us
    gather x6, local copies, waits for them, and re-layouts, take_rows(): one_image[one_index]  46 us
    dot_general x11, matrix products, matmul(): return jnp.dot(inputs_low, matrix, preferred_element_type=jnp.float32)  44.8 us
  transfers between devices with their start and end apart: 2, of which 2 were waited for; matrix products, arithmetic and copies ran while one was open for 2% of the time, Pallas kernels for 0%

commit v1 on v0

v1 whole, which is shorter than its diff:
```python
import functools
import math

import jax
import jax.numpy as jnp
import numpy as np
from jax import lax
from jax.experimental import pallas as pl
from jax.experimental.pallas import tpu as pltpu
from jax.sharding import PartitionSpec as P

D = 768
HE = 12
FE = 3072
E = 512
HD = 16
FD = 2048
PIX = 768
POS = 196
VMAX = 80
BS = 256
STEP = 10
NBLK = 177

SD = 208

EPS_NORM = 1e-06
EPS_ROOT = 1e-06
EPS_ADAM = 1e-08
CLIP_NORM = 0.01
RATE_MATRIX = 0.03
DECAY_MATRIX = 0.05
BETA_STAT = 0.5
BETA_FIRST = 0.9
BETA_SECOND = 0.999
RATE_VECTOR = 0.1
NEG_LARGE = -1e30
LOG2E = math.log2(math.e)

BF = jnp.bfloat16
F32 = jnp.float32
VMEM_LIMIT = 60 * 1024 * 1024

T_EMBED, T_EQKV, T_EOUT, T_EUP, T_EDOWN, T_PROJ = 0, 9, 36, 45, 81, 117
T_DQKV, T_DOUT, T_DUP, T_DDOWN, T_HEAD = 123, 135, 139, 155, 171

V_EMBED = 0
V_ENC = D
V_ENORM = V_ENC + 9 * D + FE
V_PROJ = V_ENORM + 2 * D
V_MASK = V_PROJ + E
V_DEC = V_MASK + E
V_DNORM = V_DEC + 9 * E + FD
V_HEAD = V_DNORM + 2 * E
V_ALL = V_HEAD + PIX


def layer_offsets(start, width, hidden):
    names = ["g1", "s1", "bqkv", "bo", "g2", "s2", "bu", "bd"]
    sizes = [width, width, 3 * width, width, width, width, hidden, width]
    offsets = {}
    for name, size in zip(names, sizes):
        offsets[name] = start
        start += size
    return offsets


def mm(a, b):
    return jnp.dot(a, b, preferred_element_type=F32)


def mm_nt(a, b):
    return lax.dot_general(a, b, (((1,), (1,)), ((), ())), preferred_element_type=F32)


def mm_tn(a, b):
    return lax.dot_general(a, b, (((0,), (0,)), ((), ())), preferred_element_type=F32)


def fold8(x):
    rows, cols = x.shape
    return jnp.sum(x.reshape(rows // 8, 8, cols), axis=0)


def gelu_pair(u):
    t = 1.0 / (1.0 + (0.3275911 * math.sqrt(0.5)) * jnp.abs(u))
    e = jnp.exp2((-0.5 * LOG2E) * (u * u))
    poly = t * (
        0.5 * 0.254829592
        + t * (-0.5 * 0.284496736 + t * (0.5 * 1.421413741 + t * (-0.5 * 1.453152027 + t * (0.5 * 1.061405429))))
    )
    tail = poly * e
    phi = jnp.where(u >= 0, 1.0 - tail, tail)
    return u * phi, phi + u * (e * (1.0 / math.sqrt(2.0 * math.pi)))


def norm_parts(x):
    centred = x - jnp.mean(x, axis=-1, keepdims=True)
    inverse = lax.rsqrt(jnp.mean(centred * centred, axis=-1, keepdims=True) + EPS_NORM)
    return centred * inverse, inverse


def row_loop(rows, step, body, carry=0, unroll=2):
    count = rows // step

    def one(i, c):
        return body(pl.ds(pl.multiple_of(i * step, step), step), c)

    return lax.fori_loop(0, count, one, carry, unroll=unroll if count % unroll == 0 else 1)


def norm_forward(x_ref, gain, shift, out_ref):
    def body(sl, c):
        normed, _ = norm_parts(x_ref[sl, :])
        out_ref[sl, :] = (normed * gain + shift).astype(BF)
        return c

    row_loop(x_ref.shape[0], 16, body)


def norm_backward(x_ref, dy_ref, gain, out_ref, add):
    width = x_ref.shape[1]

    def body(sl, c):
        d_gain, d_shift = c
        normed, inverse = norm_parts(x_ref[sl, :])
        dy = dy_ref[sl, :]
        dn = dy * gain
        mean_one = jnp.mean(dn, axis=-1, keepdims=True)
        mean_two = jnp.mean(dn * normed, axis=-1, keepdims=True)
        dx = inverse * (dn - mean_one - normed * mean_two)
        out_ref[sl, :] = out_ref[sl, :] + dx if add else dx
        return (d_gain + fold8(dy * normed), d_shift + fold8(dy))

    zero = jnp.zeros((8, width), F32)
    return row_loop(x_ref.shape[0], 16, body, (zero, zero))


def col_loop(count, body):
    def one(j, c):
        body(j, pl.ds(pl.multiple_of(j * BS, BS), BS))
        return c

    lax.fori_loop(0, count, one, 0)


def vec_at(vec_ref, start, j):
    return vec_ref[:, pl.ds(pl.multiple_of(start + j * BS, BS), BS)]


def head_mask(head, head_size):
    lane = lax.broadcasted_iota(jnp.int32, (1, BS), 1)
    inside = (lane >= head * head_size) & (lane < (head + 1) * head_size)
    return jnp.where(inside, 1.0, 0.0).astype(BF)


def scores_of(k_masked, q, head_size, valid):
    scores = mm_nt(k_masked, q) * (head_size**-0.5 * LOG2E)
    return jnp.where(valid, scores, NEG_LARGE)


def attention_forward(qkv_ref, att_ref, lse_ref, image, seq, width, head_size, valid):
    rows = pl.ds(pl.multiple_of(image * seq, 16), seq)
    per = BS // head_size

    def group(g, c):
        def part(which):
            return qkv_ref[rows, pl.ds(pl.multiple_of(which * width + g * BS, BS), BS)]

        q, k, v = part(0), part(1), part(2)
        v_t = v.T
        outs, logs = [], []
        for h in range(per):
            scores = scores_of(k * head_mask(h, head_size), q, head_size, valid)
            top = jnp.max(scores, axis=0, keepdims=True)
            e = jnp.exp2(scores - top)
            total = jnp.sum(e, axis=0, keepdims=True)
            out = mm(v_t[h * head_size : (h + 1) * head_size, :], e.astype(BF))
            outs.append(out * (1.0 / total))
            logs.append(top + jnp.log2(total))
        att_ref[rows, pl.ds(pl.multiple_of(g * BS, BS), BS)] = jnp.concatenate(outs, axis=0).T.astype(BF)
        lse_ref[image, g] = jnp.concatenate(logs, axis=0)
        return c

    lax.fori_loop(0, width // BS, group, 0)


def attention_backward(qkv_ref, datt_ref, lse_ref, dqkv_ref, image, seq, width, head_size, valid):
    rows = pl.ds(pl.multiple_of(image * seq, 16), seq)
    per = BS // head_size
    scale = head_size**-0.5

    def group(g, c):
        def cols(which):
            return pl.ds(pl.multiple_of(which * width + g * BS, BS), BS)

        q, k, v = qkv_ref[rows, cols(0)], qkv_ref[rows, cols(1)], qkv_ref[rows, cols(2)]
        d_out = datt_ref[rows, cols(0)]
        lse = lse_ref[image, g]
        q_t, k_t, d_out_t = q.T, k.T, d_out.T
        d_q, d_k, d_v = [], [], []
        for h in range(per):
            mask = head_mask(h, head_size)
            part = slice(h * head_size, (h + 1) * head_size)
            probs = jnp.exp2(scores_of(k * mask, q, head_size, valid) - lse[h : h + 1, :])
            d_probs = mm_nt(v * mask, d_out)
            delta = jnp.sum(probs * d_probs, axis=0, keepdims=True)
            d_scores = (probs * (d_probs - delta)).astype(BF)
            d_v.append(mm_nt(d_out_t[part, :], probs.astype(BF)))
            d_k.append(mm_nt(q_t[part, :], d_scores))
            d_q.append(mm(k_t[part, :], d_scores))
        dqkv_ref[rows, cols(0)] = (jnp.concatenate(d_q, axis=0).T * scale).astype(BF)
        dqkv_ref[rows, cols(1)] = (jnp.concatenate(d_k, axis=0).T * scale).astype(BF)
        dqkv_ref[rows, cols(2)] = jnp.concatenate(d_v, axis=0).T.astype(BF)
        return c

    lax.fori_loop(0, width // BS, group, 0)


def fetch_tiles(row_ref, wg_ref, first, dst, sem):
    row_tiles, col_tiles = dst.shape[0] // BS, dst.shape[1] // BS
    for i in range(row_tiles):
        for j in range(col_tiles):
            start = pl.multiple_of(row_ref[first + i * col_tiles + j], 16)
            pltpu.make_async_copy(
                wg_ref.at[pl.ds(start, BS), :],
                dst.at[i * BS : (i + 1) * BS, j * BS : (j + 1) * BS],
                sem,
            ).start()


def await_tiles(dst, sem):
    pltpu.make_async_copy(dst, dst, sem).wait()


def fetch_all(first_step, row_ref, wg_ref, sems, matrices):
    @pl.when(first_step)
    def _():
        for i, (first, dst) in enumerate(matrices):
            fetch_tiles(row_ref, wg_ref, first, dst, sems.at[i])

    def ready(i):
        @pl.when(first_step)
        def _():
            await_tiles(matrices[i][1], sems.at[i])

    return ready


def qkv_forward(h_ref, w_ref, vec_ref, start, out_ref):
    def body(j, cols):
        out_ref[:, cols] = (mm(h_ref[...], w_ref[:, cols]) + vec_at(vec_ref, start, j)).astype(BF)

    col_loop(w_ref.shape[1] // BS, body)


def add_linear(x_ref, h_ref, w_ref, vec_ref, start, out_ref):
    def body(j, cols):
        out_ref[:, cols] = x_ref[:, cols] + (mm(h_ref[...], w_ref[:, cols]) + vec_at(vec_ref, start, j))

    col_loop(w_ref.shape[1] // BS, body)


def up_forward(h_ref, w_ref, vec_ref, start, act_ref, slope_ref):
    def body(j, cols):
        act, slope = gelu_pair(mm(h_ref[...], w_ref[:, cols]) + vec_at(vec_ref, start, j))
        act_ref[:, cols] = act.astype(BF)
        slope_ref[:, cols] = slope.astype(BF)

    col_loop(w_ref.shape[1] // BS, body)


def back_linear(g_ref, w_ref, out_ref):
    def body(j, cols):
        out_ref[:, cols] = mm_nt(g_ref[...], w_ref[cols, :])

    col_loop(w_ref.shape[0] // BS, body)


def back_up(g_ref, w_ref, slope_ref, du_ref, sum_ref, start):
    def body(j, cols):
        du = (mm_nt(g_ref[...], w_ref[cols, :]) * slope_ref[:, cols].astype(F32)).astype(BF)
        du_ref[:, cols] = du
        at = pl.ds(pl.multiple_of(start + j * BS, BS), BS)
        sum_ref[:, at] = sum_ref[:, at] + fold8(du.astype(F32))

    col_loop(w_ref.shape[0] // BS, body)


def round_and_sum(x_ref, out_ref, sum_ref, start):
    width = x_ref.shape[1]

    def body(sl, c):
        low = x_ref[sl, :].astype(BF)
        out_ref[sl, :] = low
        return c + fold8(low.astype(F32))

    total = row_loop(x_ref.shape[0], 16, body, jnp.zeros((8, width), F32))
    sum_ref[:, start : start + width] = sum_ref[:, start : start + width] + total


def sum_rows(x_ref, sum_ref, start):
    width = x_ref.shape[1]

    def body(sl, c):
        return c + fold8(x_ref[sl, :].astype(F32))

    total = row_loop(x_ref.shape[0], 16, body, jnp.zeros((8, width), F32))
    sum_ref[:, start : start + width] = sum_ref[:, start : start + width] + total


def add_sum(sum_ref, start, value):
    stop = start + value.shape[1]
    sum_ref[:, start:stop] = sum_ref[:, start:stop] + value


def order_kernel(shuffle_ref, pixels_ref, sin_d_ref, sin_e_ref, all_ref, visible_ref, pos_d_ref, pos_e_ref):
    ids = shuffle_ref[0]
    pick = jnp.where(ids == lax.broadcasted_iota(jnp.int32, (SD, POS), 1), 1.0, 0.0).astype(BF)
    ordered = mm(pick, pixels_ref[0]).astype(BF)
    all_ref[0] = ordered
    visible_ref[0] = ordered[:VMAX, :]
    few = pick[:VMAX, :]
    pos_d_ref[0] = mm(few, sin_d_ref[0]) + mm(few, sin_d_ref[1])
    pos_e_ref[0] = mm(pick, sin_e_ref[0]) + mm(pick, sin_e_ref[1])


def sinusoid_parts(count, width):
    half = width // 2
    frequency = np.exp(np.arange(half) * (-np.log(10000.0) / half))
    angles = np.arange(count)[:, None] * frequency[None, :]
    table = np.concatenate([np.sin(angles), np.cos(angles)], axis=1).astype(np.float32)
    high = table.astype(jnp.bfloat16)
    low = (table - high.astype(np.float32)).astype(jnp.bfloat16)
    return np.stack([high, low])


def order_patches(pixels, shuffle):
    images = pixels.shape[0]
    ids = jnp.pad(shuffle, ((0, 0), (0, SD - POS)), constant_values=-1)[:, :, None]

    def image(*dims):
        return pl.BlockSpec((1,) + dims, lambda b: (b,) + (0,) * len(dims))

    def whole(*dims):
        return pl.BlockSpec(dims, lambda b: (0,) * len(dims))

    return pl.pallas_call(
        order_kernel,
        grid=(images,),
        in_specs=[image(SD, 1), image(POS, PIX), whole(2, POS, D), whole(2, POS, E)],
        out_specs=[image(SD, PIX), image(VMAX, PIX), image(VMAX, D), image(SD, E)],
        out_shape=[
            jax.ShapeDtypeStruct((images, SD, PIX), BF),
            jax.ShapeDtypeStruct((images, VMAX, PIX), BF),
            jax.ShapeDtypeStruct((images, VMAX, D), F32),
            jax.ShapeDtypeStruct((images, SD, E), F32),
        ],
        compiler_params=pltpu.CompilerParams(vmem_limit_bytes=VMEM_LIMIT),
        name="order_patches",
    )(ids, pixels, jnp.asarray(sinusoid_parts(POS, D)), jnp.asarray(sinusoid_parts(POS, E)))


def group_call(kernel, steps, prefetch, in_arrays, out_list, scratch, name, flops):
    def spec(shape, kind):
        if kind == "any":
            return pl.BlockSpec(memory_space=pl.ANY)
        if kind == "rows":
            block = (shape[0] // steps,) + tuple(shape[1:])
            return pl.BlockSpec(block, lambda i, *_: (i,) + (0,) * (len(shape) - 1))
        return pl.BlockSpec(tuple(shape), lambda i, *_: (0,) * len(shape))

    return pl.pallas_call(
        kernel,
        grid_spec=pltpu.PrefetchScalarGridSpec(
            num_scalar_prefetch=len(prefetch),
            grid=(steps,),
            in_specs=[spec(a.shape, kind) for a, kind in in_arrays],
            out_specs=[spec(shape, kind) for shape, _, kind in out_list],
            scratch_shapes=scratch,
        ),
        out_shape=[jax.ShapeDtypeStruct(shape, dtype) for shape, dtype, _ in out_list],
        compiler_params=pltpu.CompilerParams(
            vmem_limit_bytes=VMEM_LIMIT, dimension_semantics=("arbitrary",)
        ),
        cost_estimate=pl.CostEstimate(
            flops=flops,
            bytes_accessed=sum(math.prod(s) * jnp.dtype(t).itemsize for s, t, _ in out_list) * 2,
            transcendentals=0,
        ),
        name=name,
    )(*prefetch, *[a for a, _ in in_arrays])


ENC = layer_offsets(V_ENC, D, FE)
DEC = layer_offsets(V_DEC, E, FD)


def encoder_forward_kernel(
    row_ref, len_ref, wg_ref, vec_ref, pix_ref, pos_ref,
    x0_ref, h1_ref, qkv_ref, lse_ref, att_ref, mid_ref, h2_ref, act_ref, slope_ref, x1_ref, hn_ref, latent_ref,
    w_embed, w_qkv, w_out, w_up, w_down, w_proj, sems,
):
    step = pl.program_id(0)
    images = lse_ref.shape[0]
    ready = fetch_all(
        step == 0,
        row_ref,
        wg_ref,
        sems,
        [
            (T_EMBED, w_embed),
            (T_EQKV, w_qkv),
            (T_EOUT, w_out),
            (T_EUP, w_up),
            (T_EDOWN, w_down),
            (T_PROJ, w_proj),
        ],
    )

    def vec(start, size=D):
        return vec_ref[:, start : start + size]

    ready(0)
    add_linear(pos_ref, pix_ref, w_embed, vec_ref, V_EMBED, x0_ref)
    norm_forward(x0_ref, vec(ENC["g1"]), vec(ENC["s1"]), h1_ref)
    ready(1)
    qkv_forward(h1_ref, w_qkv, vec_ref, ENC["bqkv"], qkv_ref)

    def one(image, c):
        valid = lax.broadcasted_iota(jnp.int32, (VMAX, 1), 0) < len_ref[step * images + image]
        attention_forward(qkv_ref, att_ref, lse_ref, image, VMAX, D, D // HE, valid)
        return c

    lax.fori_loop(0, images, one, 0)
    ready(2)
    add_linear(x0_ref, att_ref, w_out, vec_ref, ENC["bo"], mid_ref)
    norm_forward(mid_ref, vec(ENC["g2"]), vec(ENC["s2"]), h2_ref)
    ready(3)
    up_forward(h2_ref, w_up, vec_ref, ENC["bu"], act_ref, slope_ref)
    ready(4)
    add_linear(mid_ref, act_ref, w_down, vec_ref, ENC["bd"], x1_ref)
    norm_forward(x1_ref, vec(V_ENORM), vec(V_ENORM + D), hn_ref)
    ready(5)

    def project(j, cols):
        latent_ref[:, cols] = mm(hn_ref[...], w_proj[:, cols]) + vec_at(vec_ref, V_PROJ, j)

    col_loop(E // BS, project)


def encoder_forward(tile_rows, vis_len, gathered, vector, visible_pix, pos_d, steps):
    images = vis_len.shape[0]
    rows = images * VMAX
    outs = [
        ((rows, D), F32, "rows"),
        ((rows, D), BF, "rows"),
        ((rows, 3 * D), BF, "rows"),
        ((images, D // BS, BS * HE // D, VMAX), F32, "rows"),
        ((rows, D), BF, "rows"),
        ((rows, D), F32, "rows"),
        ((rows, D), BF, "rows"),
        ((rows, FE), BF, "rows"),
        ((rows, FE), BF, "rows"),
        ((rows, D), F32, "rows"),
        ((rows, D), BF, "rows"),
        ((rows, E), F32, "rows"),
    ]
    scratch = [pltpu.VMEM(s, BF) for s in [(PIX, D), (D, 3 * D), (D, D), (D, FE), (FE, D), (D, E)]]
    return group_call(
        encoder_forward_kernel,
        steps,
        (tile_rows, vis_len),
        [
            (gathered, "any"),
            (vector, "whole"),
            (visible_pix.reshape(rows, PIX), "rows"),
            (pos_d.reshape(rows, D), "rows"),
        ],
        outs,
        scratch + [pltpu.SemaphoreType.DMA((6,))],
        "encoder_forward",
        2 * rows * (PIX * D + 4 * D * D + 2 * D * FE + D * E),
    )


DS = layer_offsets(0, E, FD)
DS_NORM = 9 * E + FD
DS_HEAD = DS_NORM + 2 * E
DS_MASK = DS_HEAD + PIX
DS_LOSS = DS_MASK + E
DS_ALL = DS_LOSS + PIX


def decoder_kernel(
    row_ref, len_ref, wg_ref, vec_ref, latent_ref, pos_ref, pix_ref,
    h1_ref, dqkv_ref, att_ref, gproj_ref, h2_ref, du_ref, act_ref, gdown_ref, hn_ref, gpred_ref, glat_ref, sum_ref,
    w_qkv, w_out, w_up, w_down, w_head, x0, qkv, lse, mid, slope, x1, pred, dy, grad, datt, sems,
):
    step = pl.program_id(0)
    images = lse.shape[0]
    ready = fetch_all(
        step == 0,
        row_ref,
        wg_ref,
        sems,
        [(T_DQKV, w_qkv), (T_DOUT, w_out), (T_DUP, w_up), (T_DDOWN, w_down), (T_HEAD, w_head)],
    )

    @pl.when(step == 0)
    def _():
        sum_ref[...] = jnp.zeros_like(sum_ref)

    def vec(start, size=E):
        return vec_ref[:, start : start + size]

    def length(image):
        return len_ref[step * images + image]

    chunk = 16
    order = lax.broadcasted_iota(jnp.int32, (chunk, 1), 0)
    token = vec(V_MASK)

    def place(image, c):
        def head_rows(i, c):
            at = pl.ds(pl.multiple_of(image * SD + i * chunk, chunk), chunk)
            got = latent_ref[pl.ds(pl.multiple_of(image * VMAX + i * chunk, chunk), chunk), :]
            x0[at, :] = jnp.where(i * chunk + order < length(image), got, token) + pos_ref[at, :]
            return c

        def tail_rows(i, c):
            at = pl.ds(pl.multiple_of(image * SD + i * chunk, chunk), chunk)
            x0[at, :] = token + pos_ref[at, :]
            return c

        lax.fori_loop(0, VMAX // chunk, head_rows, 0)
        lax.fori_loop(VMAX // chunk, SD // chunk, tail_rows, 0)
        return c

    lax.fori_loop(0, images, place, 0)
    norm_forward(x0, vec(DEC["g1"]), vec(DEC["s1"]), h1_ref)
    ready(0)
    qkv_forward(h1_ref, w_qkv, vec_ref, DEC["bqkv"], qkv)
    valid = lax.broadcasted_iota(jnp.int32, (SD, 1), 0) < POS

    def attend(image, c):
        attention_forward(qkv, att_ref, lse, image, SD, E, E // HD, valid)
        return c

    lax.fori_loop(0, images, attend, 0)
    ready(1)
    add_linear(x0, att_ref, w_out, vec_ref, DEC["bo"], mid)
    norm_forward(mid, vec(DEC["g2"]), vec(DEC["s2"]), h2_ref)
    ready(2)
    up_forward(h2_ref, w_up, vec_ref, DEC["bu"], act_ref, slope)
    ready(3)
    add_linear(mid, act_ref, w_down, vec_ref, DEC["bd"], x1)
    norm_forward(x1, vec(V_DNORM), vec(V_DNORM + E), hn_ref)
    ready(4)

    def predict(j, cols):
        pred[:, cols] = mm(hn_ref[...], w_head[:, cols]) + vec_at(vec_ref, V_HEAD, j)

    col_loop(PIX // BS, predict)

    def errors(image, c):
        def one(i, c):
            loss, bias = c
            at = pl.ds(pl.multiple_of(image * SD + i * chunk, chunk), chunk)
            target, _ = norm_parts(pix_ref[at, :].astype(F32))
            place_in = i * chunk + order
            masked = (place_in >= length(image)) & (place_in < POS)
            residual = jnp.where(masked, pred[at, :] - target, 0.0)
            low = (residual * (2.0 / PIX)).astype(BF)
            gpred_ref[at, :] = low
            return (loss + fold8(residual * residual), bias + fold8(low.astype(F32)))

        return lax.fori_loop(0, SD // chunk, one, c)

    zero = jnp.zeros((8, PIX), F32)
    loss, bias = lax.fori_loop(0, images, errors, (zero, zero))
    add_sum(sum_ref, DS_LOSS, loss)
    add_sum(sum_ref, DS_HEAD, bias)

    back_linear(gpred_ref, w_head, dy)
    d_gain, d_shift = norm_backward(x1, dy, vec(V_DNORM), grad, False)
    add_sum(sum_ref, DS_NORM, d_gain)
    add_sum(sum_ref, DS_NORM + E, d_shift)
    round_and_sum(grad, gdown_ref, sum_ref, DS["bd"])
    back_up(gdown_ref, w_down, slope, du_ref, sum_ref, DS["bu"])
    back_linear(du_ref, w_up, dy)
    d_gain, d_shift = norm_backward(mid, dy, vec(DEC["g2"]), grad, True)
    add_sum(sum_ref, DS["g2"], d_gain)
    add_sum(sum_ref, DS["s2"], d_shift)
    round_and_sum(grad, gproj_ref, sum_ref, DS["bo"])

    def back_out(j, cols):
        datt[:, cols] = mm_nt(gproj_ref[...], w_out[cols, :]).astype(BF)

    col_loop(E // BS, back_out)

    def attend_back(image, c):
        attention_backward(qkv, datt, lse, dqkv_ref, image, SD, E, E // HD, valid)
        return c

    lax.fori_loop(0, images, attend_back, 0)
    sum_rows(dqkv_ref, sum_ref, DS["bqkv"])
    back_linear(dqkv_ref, w_qkv, dy)
    d_gain, d_shift = norm_backward(x0, dy, vec(DEC["g1"]), grad, True)
    add_sum(sum_ref, DS["g1"], d_gain)
    add_sum(sum_ref, DS["s1"], d_shift)

    def unplace(image, c):
        def head_rows(i, c):
            got = grad[pl.ds(pl.multiple_of(image * SD + i * chunk, chunk), chunk), :]
            seen = i * chunk + order < length(image)
            at = pl.ds(pl.multiple_of(image * VMAX + i * chunk, chunk), chunk)
            glat_ref[at, :] = jnp.where(seen, got, 0.0).astype(BF)
            return c + fold8(jnp.where(seen, 0.0, got))

        def tail_rows(i, c):
            got = grad[pl.ds(pl.multiple_of(image * SD + i * chunk, chunk), chunk), :]
            return c + fold8(jnp.where(i * chunk + order < POS, got, 0.0))

        c = lax.fori_loop(0, VMAX // chunk, head_rows, c)
        return lax.fori_loop(VMAX // chunk, SD // chunk, tail_rows, c)

    add_sum(sum_ref, DS_MASK, lax.fori_loop(0, images, unplace, jnp.zeros((8, E), F32)))


def decoder(tile_rows, vis_len, gathered, vector, latent, pos_e, ordered, steps):
    images = vis_len.shape[0]
    rows = images * SD
    part = rows // steps
    outs = [
        ((rows, E), BF, "rows"),
        ((rows, 3 * E), BF, "rows"),
        ((rows, E), BF, "rows"),
        ((rows, E), BF, "rows"),
        ((rows, E), BF, "rows"),
        ((rows, FD), BF, "rows"),
        ((rows, FD), BF, "rows"),
        ((rows, E), BF, "rows"),
        ((rows, E), BF, "rows"),
        ((rows, PIX), BF, "rows"),
        ((images * VMAX, E), BF, "rows"),
        ((8, DS_ALL), F32, "whole"),
    ]
    scratch = [pltpu.VMEM(s, BF) for s in [(E, 3 * E), (E, E), (E, FD), (FD, E), (E, PIX)]]
    scratch += [
        pltpu.VMEM((part, E), F32),
        pltpu.VMEM((part, 3 * E), BF),
        pltpu.VMEM((images // steps, E // BS, BS * HD // E, SD), F32),
        pltpu.VMEM((part, E), F32),
        pltpu.VMEM((part, FD), BF),
        pltpu.VMEM((part, E), F32),
        pltpu.VMEM((part, PIX), F32),
        pltpu.VMEM((part, E), F32),
        pltpu.VMEM((part, E), F32),
        pltpu.VMEM((part, E), BF),
        pltpu.SemaphoreType.DMA((5,)),
    ]
    return group_call(
        decoder_kernel,
        steps,
        (tile_rows, vis_len),
        [
            (gathered, "any"),
            (vector, "whole"),
            (latent, "rows"),
            (pos_e.reshape(rows, E), "rows"),
            (ordered.reshape(rows, PIX), "rows"),
        ],
        outs,
        scratch,
        "decoder",
        4 * rows * (4 * E * E + 2 * E * FD + E * PIX),
    )


EM_BD, EM_BU = 0, D
EM_G2, EM_S2 = D + FE, 2 * D + FE
EM_BO, EM_NORM = 3 * D + FE, 4 * D + FE
EM_PROJ = 6 * D + FE
EM_ALL = EM_PROJ + E
EA_QKV, EA_G1, EA_S1, EA_EMBED, EA_ALL = 0, 3 * D, 4 * D, 5 * D, 6 * D


def encoder_mlp_back_kernel(
    row_ref, wg_ref, vec_ref, glat_ref, x1_ref, mid_ref, slope_ref,
    gdown_ref, du_ref, grad_ref, gproj_ref, sum_ref,
    w_proj, w_down, w_up, dy, sems,
):
    step = pl.program_id(0)
    ready = fetch_all(
        step == 0, row_ref, wg_ref, sems, [(T_PROJ, w_proj), (T_EDOWN, w_down), (T_EUP, w_up)]
    )

    @pl.when(step == 0)
    def _():
        sum_ref[...] = jnp.zeros_like(sum_ref)

    def vec(start):
        return vec_ref[:, start : start + D]

    sum_rows(glat_ref, sum_ref, EM_PROJ)
    ready(0)
    back_linear(glat_ref, w_proj, dy)
    d_gain, d_shift = norm_backward(x1_ref, dy, vec(V_ENORM), grad_ref, False)
    add_sum(sum_ref, EM_NORM, d_gain)
    add_sum(sum_ref, EM_NORM + D, d_shift)
    round_and_sum(grad_ref, gdown_ref, sum_ref, EM_BD)
    ready(1)
    back_up(gdown_ref, w_down, slope_ref, du_ref, sum_ref, EM_BU)
    ready(2)
    back_linear(du_ref, w_up, dy)
    d_gain, d_shift = norm_backward(mid_ref, dy, vec(ENC["g2"]), grad_ref, True)
    add_sum(sum_ref, EM_G2, d_gain)
    add_sum(sum_ref, EM_S2, d_shift)
    round_and_sum(grad_ref, gproj_ref, sum_ref, EM_BO)


def encoder_mlp_back(tile_rows, gathered, vector, glat, x1, mid, slope, steps):
    rows = x1.shape[0]
    part = rows // steps
    outs = [
        ((rows, D), BF, "rows"),
        ((rows, FE), BF, "rows"),
        ((rows, D), F32, "rows"),
        ((rows, D), BF, "rows"),
        ((8, EM_ALL), F32, "whole"),
    ]
    scratch = [pltpu.VMEM(s, BF) for s in [(D, E), (FE, D), (D, FE)]]
    scratch += [pltpu.VMEM((part, D), F32), pltpu.SemaphoreType.DMA((3,))]
    return group_call(
        encoder_mlp_back_kernel,
        steps,
        (tile_rows,),
        [
            (gathered, "any"),
            (vector, "whole"),
            (glat, "rows"),
            (x1, "rows"),
            (mid, "rows"),
            (slope, "rows"),
        ],
        outs,
        scratch,
        "encoder_mlp_back",
        2 * rows * (D * E + 2 * D * FE),
    )


def encoder_attention_back_kernel(
    row_ref, len_ref, wg_ref, vec_ref, gproj_ref, grad_in_ref, qkv_ref, lse_ref, x0_ref,
    dqkv_ref, gembed_ref, sum_ref,
    w_out, w_qkv, dy, grad, datt, sems,
):
    step = pl.program_id(0)
    images = lse_ref.shape[0]
    ready = fetch_all(step == 0, row_ref, wg_ref, sems, [(T_EOUT, w_out), (T_EQKV, w_qkv)])

    @pl.when(step == 0)
    def _():
        sum_ref[...] = jnp.zeros_like(sum_ref)

    ready(0)

    def back_out(j, cols):
        datt[:, cols] = mm_nt(gproj_ref[...], w_out[cols, :]).astype(BF)

    col_loop(D // BS, back_out)

    def attend_back(image, c):
        valid = lax.broadcasted_iota(jnp.int32, (VMAX, 1), 0) < len_ref[step * images + image]
        attention_backward(qkv_ref, datt, lse_ref, dqkv_ref, image, VMAX, D, D // HE, valid)
        return c

    lax.fori_loop(0, images, attend_back, 0)
    sum_rows(dqkv_ref, sum_ref, EA_QKV)
    ready(1)
    back_linear(dqkv_ref, w_qkv, dy)
    grad[...] = grad_in_ref[...]
    gain = vec_ref[:, ENC["g1"] : ENC["g1"] + D]
    d_gain, d_shift = norm_backward(x0_ref, dy, gain, grad, True)
    add_sum(sum_ref, EA_G1, d_gain)
    add_sum(sum_ref, EA_S1, d_shift)
    round_and_sum(grad, gembed_ref, sum_ref, EA_EMBED)


def encoder_attention_back(tile_rows, vis_len, gathered, vector, gproj, grad, qkv, lse, x0, steps):
    rows = x0.shape[0]
    part = rows // steps
    outs = [((rows, 3 * D), BF, "rows"), ((rows, D), BF, "rows"), ((8, EA_ALL), F32, "whole")]
    scratch = [pltpu.VMEM(s, BF) for s in [(D, D), (D, 3 * D)]]
    scratch += [pltpu.VMEM((part, D), F32), pltpu.VMEM((part, D), F32), pltpu.VMEM((part, D), BF)]
    return group_call(
        encoder_attention_back_kernel,
        steps,
        (tile_rows, vis_len),
        [
            (gathered, "any"),
            (vector, "whole"),
            (gproj, "rows"),
            (grad, "rows"),
            (qkv, "rows"),
            (lse, "rows"),
            (x0, "rows"),
        ],
        outs,
        scratch + [pltpu.SemaphoreType.DMA((2,))],
        "encoder_attention_back",
        2 * rows * 4 * D * D,
    )


def weight_grad_kernel(parts, cut, extra, index_ref, x_ref, g_ref, *refs):
    outs = refs[extra : extra + min(parts, 2)]
    total = refs[-1]
    col_tiles = g_ref.shape[1] // BS
    x_t = x_ref[...].T

    def body(j, cols):
        total[:, cols] = mm(x_t, g_ref[:, cols])

    col_loop(col_tiles, body)
    for p in range(parts):
        start = pl.multiple_of((p ^ index_ref[0]) * cut, cut)
        for j in range(col_tiles):
            outs[p % 2][p // 2, j] = total[pl.ds(start, cut), j * BS : (j + 1) * BS].astype(BF)


def weight_grad(index, parts, count, first, x, g, buffers):
    cut = BS // parts
    rows, width = x.shape
    col_tiles = g.shape[1] // BS
    assert first % col_tiles == 0
    held = min(parts, 2)
    shape = jax.ShapeDtypeStruct((parts // held, count, cut, BS), BF)
    given = list(buffers or [])
    out_spec = pl.BlockSpec(
        (parts // held, col_tiles, cut, BS), lambda i, *_: (0, first // col_tiles + i, 0, 0)
    )
    return pl.pallas_call(
        functools.partial(weight_grad_kernel, parts, cut, len(given)),
        grid_spec=pltpu.PrefetchScalarGridSpec(
            num_scalar_prefetch=1,
            grid=(width // BS,),
            in_specs=[
                pl.BlockSpec((rows, BS), lambda i, *_: (0, i)),
                pl.BlockSpec(g.shape, lambda i, *_: (0, 0)),
            ]
            + [pl.BlockSpec(memory_space=pl.ANY)] * len(given),
            out_specs=[out_spec] * held,
            scratch_shapes=[pltpu.VMEM((BS, g.shape[1]), F32)],
        ),
        out_shape=[shape] * held,
        input_output_aliases={3 + i: i for i in range(len(given))},
        compiler_params=pltpu.CompilerParams(vmem_limit_bytes=VMEM_LIMIT),
        cost_estimate=pl.CostEstimate(
            flops=2 * rows * width * g.shape[1],
            bytes_accessed=2 * rows * (width + g.shape[1]) + 2 * width * g.shape[1],
            transcendentals=0,
        ),
        name="weight_grad",
    )(index, x, g, *given)


def seed_kernel(parts, index_ref, vec_ref, *outs):
    at = pl.program_id(0)
    for p in range(parts):
        got = vec_ref[p ^ index_ref[0]]
        outs[p % 2][p // 2, 0] = jnp.where(at == 0, got, 0.0).astype(BF)


def seed_buffers(index, parts, count, first, vector_tile):
    cut = BS // parts
    held = min(parts, 2)
    shape = jax.ShapeDtypeStruct((parts // held, count, cut, BS), BF)
    return pl.pallas_call(
        functools.partial(seed_kernel, parts),
        grid_spec=pltpu.PrefetchScalarGridSpec(
            num_scalar_prefetch=1,
            grid=(count - first,),
            in_specs=[pl.BlockSpec(vector_tile.shape, lambda i, *_: (0, 0, 0))],
            out_specs=[pl.BlockSpec((parts // held, 1, cut, BS), lambda i, *_: (0, first + i, 0, 0))] * held,
        ),
        out_shape=[shape] * held,
        name="seed_buffers",
    )(index, vector_tile)


def low_sum(a, b):
    return (a.astype(F32) + b.astype(F32)).astype(BF)


def swap_bit(x, bit, size):
    return lax.ppermute(x, "dp", [(i, i ^ (1 << bit)) for i in range(size)])


def reduce_dp(buffers, parts):
    if parts == 1:
        return buffers[0][0]
    bits = parts.bit_length() - 1
    whole = low_sum(buffers[0], swap_bit(buffers[1], 0, parts))
    count = whole.shape[1]
    whole = whole.reshape((2,) * (bits - 1) + whole.shape[1:])
    results = []
    for half in range(2):
        lo, hi = (0, count // 2) if half == 0 else (count // 2, count)
        current = whole[..., lo:hi, :, :]
        left = list(range(bits - 1, 0, -1))
        order = left[::-1] if half == 0 else left
        for bit in order:
            axis = left.index(bit)
            left = [b for b in left if b != bit]
            keep = lax.index_in_dim(current, 0, axis, keepdims=False)
            send = lax.index_in_dim(current, 1, axis, keepdims=False)
            current = low_sum(keep, swap_bit(send, bit, parts))
        results.append(current)
    return jnp.concatenate(results, axis=0)


def shift_patch(x, shift, size):
    return lax.ppermute(x, "patch", [(i, (i + shift) % size) for i in range(size)])


def reduce_patch(x, groups):
    if groups == 1:
        return x
    me = lax.axis_index("patch")
    pieces = x.reshape((groups, x.shape[0] // groups) + x.shape[1:])
    total = lax.dynamic_index_in_dim(pieces, me, 0, keepdims=False).astype(F32)
    for k in range(1, groups):
        piece = lax.dynamic_index_in_dim(pieces, (me + k) % groups, 0, keepdims=False)
        total = total + shift_patch(piece, k, groups).astype(F32)
    total = total.astype(BF)
    return jnp.concatenate([total] + [shift_patch(total, k, groups) for k in range(1, groups)], axis=0)


def place_after(position, count, groups):
    if groups == 1:
        return position
    size = count // groups
    me = lax.axis_index("patch")
    return (me - position // size) % groups * size + position % size


def sum_all(x, parts, groups):
    for bit in range(groups.bit_length() - 1):
        x = x + lax.ppermute(x, "patch", [(i, i ^ (1 << bit)) for i in range(groups)])
    return sum_dp(x, parts)


def sum_dp(x, parts):
    for bit in range(parts.bit_length() - 1):
        x = x + swap_bit(x, bit, parts)
    return x


def split_low(x):
    high = x.astype(BF)
    return high, (x - high.astype(F32)).astype(BF)


def tile_kernel(
    scale_ref, grad_ref, w_ref, left_stat_ref, right_stat_ref, left_root_ref, right_root_ref,
    clipped_ref, left_new_ref, right_new_ref, w_new_ref,
):
    scale = scale_ref[0]
    for t in range(w_ref.shape[0]):
        grad = grad_ref[:, t].reshape(BS, BS)
        clipped_ref[t] = grad.astype(F32) * scale
        square = (1.0 - BETA_STAT) * scale * scale
        left_new_ref[t] = BETA_STAT * left_stat_ref[t] + square * mm_nt(grad, grad)
        right_new_ref[t] = BETA_STAT * right_stat_ref[t] + square * mm_tn(grad, grad)
        high, low = split_low(left_root_ref[t])
        half = (mm(high, grad) + mm(low, grad)) * scale
        half_high, half_low = split_low(half)
        high, low = split_low(right_root_ref[t])
        direction = mm(half_high, high) + (mm(half_high, low) + mm(half_low, high))
        direction = direction * lax.rsqrt(jnp.mean(direction * direction) + EPS_ROOT)
        w_new_ref[t] = w_ref[t] - RATE_MATRIX * (direction + DECAY_MATRIX * w_ref[t])


def tile_update(scale, grads, states):
    parts, slots, cut, _ = grads.shape
    per = 2 if slots % 2 == 0 else 1
    tile = pl.BlockSpec((per, BS, BS), lambda i, *_: (i, 0, 0))
    return pl.pallas_call(
        tile_kernel,
        grid_spec=pltpu.PrefetchScalarGridSpec(
            num_scalar_prefetch=1,
            grid=(slots // per,),
            in_specs=[pl.BlockSpec((parts, per, cut, BS), lambda i, *_: (0, i, 0, 0))] + [tile] * 5,
            out_specs=[tile] * 4,
        ),
        out_shape=[jax.ShapeDtypeStruct((slots, BS, BS), F32)] * 4,
        compiler_params=pltpu.CompilerParams(vmem_limit_bytes=VMEM_LIMIT),
        name="tile_update",
    )(scale.reshape(1), grads, *states)


def vector_update(clipped, vectors, moment, second):
    moment_new = BETA_FIRST * moment + (1.0 - BETA_FIRST) * clipped
    second_new = BETA_SECOND * second + (1.0 - BETA_SECOND) * clipped * clipped
    corrected = moment_new / (1.0 - BETA_FIRST**STEP)
    scaled = second_new / (1.0 - BETA_SECOND**STEP)
    vectors_new = vectors - RATE_VECTOR * corrected / (jnp.sqrt(scaled) + EPS_ADAM)
    return moment_new, second_new, vectors_new


ENC_ORDER = [(T_EUP, 3, 12), (T_EDOWN, 12, 3)]
CHUNKS = [
    [(T_DUP, 2, 8), (T_DDOWN, 8, 2), (T_DOUT, 2, 2), (T_DQKV, 2, 6), (T_HEAD, 2, 3), (T_PROJ, 3, 2)],
    [(T_EUP, 3, 12), (T_EDOWN, 12, 3)],
    [(T_EQKV, 3, 9), (T_EOUT, 3, 3), (T_EMBED, 3, 3)],
]


def chunk_sizes(groups):
    unit = max(2, groups)
    sizes = []
    for i, chunk in enumerate(CHUNKS):
        used = sum(r * c for _, r, c in chunk) + (2 if i == len(CHUNKS) - 1 else 0)
        sizes.append(-(-used // unit) * unit)
    return sizes


def tile_places(sizes):
    chunk_of = np.zeros(NBLK + 2, np.int32)
    place_of = np.zeros(NBLK + 2, np.int32)
    for i, chunk in enumerate(CHUNKS):
        at = 0
        for first, row_tiles, col_tiles in chunk:
            for t in range(row_tiles * col_tiles):
                chunk_of[first + t], place_of[first + t] = i, at + t
            at += row_tiles * col_tiles
    chunk_of[NBLK:] = len(CHUNKS) - 1
    place_of[NBLK + 1] = at
    place_of[NBLK] = at + 1
    return chunk_of, place_of, at


def shards(parts, groups, pixels, shuffle, vis_len, block_owner, weights, vectors, vec_moment, vec_second,
           left_stat, right_stat, left_root, right_root):
    slots = weights.shape[0]
    own = vectors.shape[0]
    index = lax.axis_index("dp").astype(jnp.int32).reshape(1)
    images = pixels.shape[0]

    vector_rows = -(-own // (16 * BS)) * 16
    mine = jnp.concatenate(
        [
            weights.astype(BF).reshape(slots * BS, BS),
            jnp.pad(vectors.astype(BF), (0, vector_rows * BS - own)).reshape(vector_rows, BS),
        ]
    )
    gathered = lax.all_gather(mine, "dp", axis=0, tiled=True)
    stride = mine.shape[0]
    slot_index = jnp.arange(block_owner.shape[0], dtype=jnp.int32)
    slot_of_block = jnp.sum(
        jnp.where(block_owner[None, :] == jnp.arange(NBLK, dtype=jnp.int32)[:, None], slot_index[None, :], 0),
        axis=1,
    )
    tile_rows = slot_of_block // slots * stride + slot_of_block % slots * BS
    vector = gathered.reshape(parts, stride, BS)[:, slots * BS :].reshape(parts, vector_rows * BS)
    vector = vector[:, :own].reshape(-1).astype(F32)
    enc_key, dec_key = 4 * D, 4 * D + (8 * D + FE - 3 * D) + 2 * D + 2 * E + 3 * E
    vector = jnp.concatenate(
        [vector[:enc_key], jnp.zeros(D, F32), vector[enc_key:dec_key], jnp.zeros(E, F32), vector[dec_key:]]
    ).reshape(1, V_ALL)

    ordered, visible_pix, pos_d, pos_e = order_patches(pixels, shuffle)
    (x0, h1, qkv, lse, att, mid, h2, act, slope, x1, hn, latent) = encoder_forward(
        tile_rows, vis_len, gathered, vector, visible_pix, pos_d, 2
    )
    (d_h1, d_dqkv, d_att, d_gproj, d_h2, d_du, d_act, d_gdown, d_hn, d_gpred, glat, d_sums) = decoder(
        tile_rows, vis_len, gathered, vector, latent, pos_e, ordered, 4
    )
    sizes = chunk_sizes(groups)
    chunk_of, place_of, vector_place = tile_places(sizes)

    def gradients(chunk, pairs, buffers=None):
        at = 0
        for x, g in pairs:
            buffers = weight_grad(index, parts, sizes[chunk], at, x, g, buffers)
            at += x.shape[1] // BS * (g.shape[1] // BS)
        return reduce_patch(reduce_dp(buffers, parts), groups)

    first = gradients(
        0, [(d_h2, d_du), (d_act, d_gdown), (d_att, d_gproj), (d_h1, d_dqkv), (d_hn, d_gpred), (hn, glat)]
    )
    gdown, du, grad_mid, gproj, m_sums = encoder_mlp_back(tile_rows, gathered, vector, glat, x1, mid, slope, 2)
    second = gradients(1, [(h2, du), (act, gdown)])
    dqkv, gembed, a_sums = encoder_attention_back(
        tile_rows, vis_len, gathered, vector, gproj, grad_mid, qkv, lse, x0, 2
    )

    d_sums, m_sums, a_sums = (jnp.sum(s, axis=0) for s in (d_sums, m_sums, a_sums))

    def cut(sums, start, size):
        return sums[start : start + size]

    grad_vector = jnp.concatenate(
        [
            cut(a_sums, EA_EMBED, D),
            cut(a_sums, EA_G1, 2 * D),
            cut(a_sums, EA_QKV, D),
            cut(a_sums, EA_QKV + 2 * D, D),
            cut(m_sums, EM_BO, D),
            cut(m_sums, EM_G2, 2 * D),
            cut(m_sums, EM_BU, FE),
            cut(m_sums, EM_BD, D),
            cut(m_sums, EM_NORM, 2 * D),
            cut(m_sums, EM_PROJ, E),
            cut(d_sums, DS_MASK, E),
            cut(d_sums, DS["g1"], 2 * E),
            cut(d_sums, DS["bqkv"], E),
            cut(d_sums, DS["bqkv"] + 2 * E, E),
            cut(d_sums, DS["bo"], E),
            cut(d_sums, DS["g2"], 2 * E),
            cut(d_sums, DS["bu"], FD),
            cut(d_sums, DS["bd"], E),
            cut(d_sums, DS_NORM, 2 * E),
            cut(d_sums, DS_HEAD, PIX),
        ]
    )
    rows_cut = BS // parts
    vector_tile = jnp.pad(grad_vector.reshape(parts, own), ((0, 0), (0, rows_cut * BS - own)))
    seeded = seed_buffers(index, parts, sizes[2], vector_place, vector_tile.reshape(parts, rows_cut, BS))
    third = gradients(2, [(h1, dqkv), (att, gproj), (visible_pix.reshape(-1, PIX), gembed)], seeded)

    reduced = jnp.concatenate([first, second, third], axis=0)
    starts = np.cumsum([0] + sizes)
    where = jnp.zeros(NBLK + 2, jnp.int32)
    for i, size in enumerate(sizes):
        here = starts[i] + place_after(jnp.asarray(place_of), size, groups)
        where = jnp.where(jnp.asarray(chunk_of == i), here, where)
    wide = reduced.astype(F32)
    squares = sum_dp(jnp.sum(wide * wide), parts)
    totals = jnp.stack([jnp.sum(cut(d_sums, DS_LOSS, PIX)) / PIX, jnp.sum(POS - vis_len).astype(F32)])
    totals = sum_all(totals, parts, groups)
    loss_sum, masked_count = totals[0], totals[1]
    grad_norm = jnp.sqrt(squares) / masked_count
    scale = jnp.minimum(1.0, CLIP_NORM / grad_norm) / masked_count

    slot_rows = reduced[where[jnp.minimum(block_owner, NBLK)]]
    if parts > 1:
        slot_rows = lax.all_to_all(slot_rows, "dp", 0, 0, tiled=True)
    grads = slot_rows.reshape(parts, slots, rows_cut, BS)
    clipped, left_new, right_new, weights_new = tile_update(
        scale, grads, (weights, left_stat, right_stat, left_root, right_root)
    )
    own_vector = lax.dynamic_index_in_dim(reduced, where[NBLK + 1], 0, keepdims=False)
    own_vector = own_vector.reshape(-1)[:own].astype(F32) * scale
    moment_new, second_new, vectors_new = vector_update(own_vector, vectors, vec_moment, vec_second)
    return (
        loss_sum,
        masked_count,
        grad_norm,
        clipped,
        left_new,
        right_new,
        weights_new,
        moment_new,
        second_new,
        vectors_new,
    )


def solution(mesh):
    both = ("dp", "patch")
    tiles = P("dp", None, None)
    return jax.shard_map(
        functools.partial(shards, mesh.shape["dp"], mesh.shape["patch"]),
        mesh=mesh,
        in_specs=(P(both, None, None), P(both, None), P(both), P())
        + (tiles, P("dp"), P("dp"), P("dp"))
        + (tiles,) * 4,
        out_specs=(P(), P(), P()) + (tiles,) * 4 + (P("dp"),) * 3,
        check_vma=False,
    )
```

time: 1330 us -> 954 us (0.72)
  Pallas kernels: 0 us -> 504 us
  local copies, waits for them, and re-layouts: 348 us -> 13.9 us
  blocking collectives: 331 us -> 0 us
  matrix products: 286 us -> 0 us
  other arithmetic: 159 us -> 30 us
  waiting for transfers between devices: 177 us -> 279 us
  starting transfers between devices: 0.08 us -> 91.3 us
    pallas_call x0 -> x18, Pallas kernels: none -> 504 us  [the longest x4 369 us: group_call(): pl.pallas_call(kernel, grid_spec=pltpu.PrefetchScalarGridSpec(num_scalar_...]
    psum x3 -> x0, blocking collectives: 297 us -> none  [the longest x1 217 us: shards(): grad_shard, vec_shard = lax.psum((grad_shard, vec_shard), 'patch')]
    dot_general x48 -> x0, matrix products: 286 us -> none  [the longest x10 56.8 us: matmul_back(): lax.dot_general(grads_low, matrix, (((2,), (1,)), ((), ())), preferred_el...]
    ppermute x0 -> x41, waiting for transfers between devices: none -> 164 us  [the longest x21 90.5 us: swap_bit(): return lax.ppermute(x, 'dp', [(i, i ^ 1 << bit) for i in range(size)])]
    reduce_scatter x1 -> x0, waiting for transfers between devices: 125 us -> none  [shards(): lax.psum_scatter(grad_slots.astype(jnp.bfloat16), 'dp', scatter_dimension...]
    reshape x29 -> x3, local copies, waits for them, and re-layouts: 104 us -> 0.72 us  [the longest x1 0.69 us: shards(): vector = jnp.concatenate([vector[:enc_key], jnp.zeros(D, F32), vector[enc...]
    ppermute x0 -> x41, starting transfers between devices: none -> 86.7 us  [the longest x18 62.2 us: shift_patch(): lax.ppermute(x, 'patch', [(i, (i + shift) % size) for i in range(size)])]
    gather x9 -> x2, local copies, waits for them, and re-layouts: 87.9 us -> 4.48 us  [shards(): slot_rows = reduced[where[jnp.minimum(block_owner, NBLK)]]]
  transfers between devices with their start and end apart: 2 -> 43, of which waited for: 2 -> 22; matrix products, arithmetic and copies ran while one was open for 2% -> 3% of each run, Pallas kernels for 0% -> 9%
where the time goes in v1:
time: 954 us; the launch traced here: 943 us
  Pallas kernels  504 us (53%)
  waiting for transfers between devices  279 us (29%)
  starting transfers between devices  91.3 us (10%)
  other arithmetic  30 us (3%)
  between operations  24.6 us (3%)
  local copies, waits for them, and re-layouts  13.9 us (1%)
    pallas_call x4, Pallas kernels, group_call(): pl.pallas_call(kernel, grid_spec=pltpu.PrefetchScalarGridSpec(num_scalar_...  369 us
    all_gather x1, waiting for transfers between devices, shards(): gathered = lax.all_gather(mine, 'dp', axis=0, tiled=True)  115 us
    pallas_call x11, Pallas kernels, weight_grad(): pl.pallas_call(functools.partial(weight_grad_kernel, parts, cut, len(give...  98.8 us
    ppermute x21, waiting for transfers between devices, swap_bit(): return lax.ppermute(x, 'dp', [(i, i ^ 1 << bit) for i in range(size)])  90.5 us
    ppermute x18, waiting for transfers between devices, shift_patch(): lax.ppermute(x, 'patch', [(i, (i + shift) % size) for i in range(size)])  68.5 us
    ppermute x18, starting transfers between devices, shift_patch(): lax.ppermute(x, 'patch', [(i, (i + shift) % size) for i in range(size)])  62.2 us
    pallas_call x1, Pallas kernels, tile_update(): pl.pallas_call(tile_kernel, grid_spec=pltpu.PrefetchScalarGridSpec(num_sc...  24.9 us
    ppermute x21, starting transfers between devices, swap_bit(): return lax.ppermute(x, 'dp', [(i, i ^ 1 << bit) for i in range(size)])  19.7 us
  transfers between devices with their start and end apart: 43, of which 22 were waited for; matrix products, arithmetic and copies ran while one was open for 3% of the time, Pallas kernels for 9%

profile of v1, /device:TPU:0, one launch (start us, length us, event | category | flops | bytes accessed | tf_op | source)
XLA Modules:
  0.0 942.9 jit_solution(17831292486938389566)
XLA Ops:
  8.0 3.2 convert_element_type.251
  16.9 8.7 order_patches.1
  26.3 115.3 %all-gather.2.cloned.1.call-done.wg_ref = bf16[49280,256]{1,0:T(8,128)(2,1)} async-done(((bf16[6160,256]{1,0:T(8,128)(2,1)}), bf16[49280,256]{1,0:T(8,128)(2,1)}) %all-gather.2.cloned.1.call-update) | async-done | bytes 25231376 | tf_op jit(solution)/shard_map/all_gather | solution.py:1059
  143.2 63.6 %encoder_forward.1 = (f32[640,768]{1,0:T(8,128)}, bf16[640,768]{1,0:T(8,128)(2,1)}, bf16[640,2304]{1,0:T(8,128)(2,1)}, f32[8,3,4,80]{3,2,1,0:T(4,128)}, bf16[640...) custom-call(s32[177]{0:T(256)} %fusion.37.row_ref, ...), custom_call_target="tpu_custom_call" | custom-call | flops 10317987840 | bytes 43970560 | tf_op jit(solution)/shard_map/encoder_forward/pallas_call | solution.py:373
  206.8 229.5 %decoder.1 = (bf16[1664,512]{1,0:T(8,128)(2,1)}, bf16[1664,1536]{1,0:T(8,128)(2,1)}, bf16[1664,512]{1,0:T(8,128)(2,1)}, bf16[1664,512]{1,0:T(8,128)(2,1)}, bf16[...) custom-call(s32[177]{0:T(256)} %fusion.37.row_ref, ...), custom_call_target="tpu_custom_call" | custom-call | flops 23555211264 | bytes 64978944 | tf_op jit(solution)/shard_map/decoder/pallas_call | solution.py:373
  437.4 33.1 %encoder_mlp_back.1 = (bf16[640,768]{1,0:T(8,128)(2,1)}, bf16[640,3072]{1,0:T(8,128)(2,1)}, f32[640,768]{1,0:T(8,128)}, bf16[640,768]{1,0:T(8,128)(2,1)}, f32[8,8192]{1,0:T(8,128)}) custom-call(s32[177]{0:T(256)} %fusion.37.row_ref, bf16[49280,256]{1,0:T(8,128)(2,1)} %all-gather.2.cloned.1.call-done.wg_ref, f32[1,21760]{1,0:T(1,128)} %reshape.138.vec_ref, ...), custom_call_target="tpu_custom_call" | custom-call | flops 6543114240 | bytes 16252928 | tf_op jit(solution)/shard_map/encoder_mlp_back/pallas_call | solution.py:373
  470.5 42.9 %encoder_attention_back.1 = (bf16[640,2304]{1,0:T(8,128)(2,1)}, bf16[640,768]{1,0:T(8,128)(2,1)}, f32[8,4608]{1,0:T(8,128)}) custom-call(s32[177]{0:T(256)} %fusion.37.row_ref, s32[8]{0:T(128)} %len_ref.5, bf16[49280,256]{1,0:T(8,128)(2,1)} %all-gather.2.cloned.1.call-done.wg_ref, f32[1,21760]{1,0:T(1,128)} %reshape.138.vec_ref, ...), custom_call_target="tpu_custom_call" | custom-call | flops 3019898880 | bytes 8159232 | tf_op jit(solution)/shard_map/encoder_attention_back/pallas_call | solution.py:373
  515.5 2.3 seed_buffers.1
  517.8 11.2 %weight_grad.19 = (bf16[4,48,32,256]{3,2,1,0:T(8,128)(2,1)}, bf16[4,48,32,256]{3,2,1,0:T(8,128)(2,1)}) custom-call(s32[1]{0:T(128)} %bitcast.11.index_ref, bf16[640,768]{1,0:T(8,128)(2,1)} %get-tuple-element.122.x_ref, bf16[640,2304]{1,0:T(8,128)(2,1)} %get-tuple-element.123.g_ref, ...), custom_call_target="tpu_custom_call", output_to_operand_aliasing={{0}: (3, {}), {1}: (4, {})} | custom-call | flops 2264924160 | bytes 7471104 | tf_op jit(solution)/shard_map/weight_grad/pallas_call | solution.py:844
  529.0 5.2 weight_grad.20
  534.2 5.2 weight_grad.21
  539.7 11.9 %weight_grad.11 = (bf16[4,60,32,256]{3,2,1,0:T(8,128)(2,1)}, bf16[4,60,32,256]{3,2,1,0:T(8,128)(2,1)}) custom-call(s32[1]{0:T(128)} %bitcast.11.index_ref, bf16[1664,512]{1,0:T(8,128)(2,1)} %get-tuple-element.90.x_ref, bf16[1664,2048]{1,0:T(8,128)(2,1)} %get-tuple-element.91.g_ref), custom_call_target="tpu_custom_call" | custom-call | flops 3489660928 | bytes 10616832 | tf_op jit(solution)/shard_map/weight_grad/pallas_call | solution.py:844
  551.6 12.0 %weight_grad.12 = (bf16[4,60,32,256]{3,2,1,0:T(8,128)(2,1)}, bf16[4,60,32,256]{3,2,1,0:T(8,128)(2,1)}) custom-call(s32[1]{0:T(128)} %bitcast.11.index_ref, bf16[1664,2048]{1,0:T(8,128)(2,1)} %get-tuple-element.88.x_ref, bf16[1664,512]{1,0:T(8,128)(2,1)} %get-tuple-element.89.g_ref, ...), custom_call_target="tpu_custom_call", output_to_operand_aliasing={{0}: (3, {}), {1}: (4, {})} | custom-call | flops 3489660928 | bytes 10616832 | tf_op jit(solution)/shard_map/weight_grad/pallas_call | solution.py:844
  563.6 4.7 weight_grad.13
  568.3 9.4 weight_grad.14
  577.6 5.9 weight_grad.15
  583.5 4.4 weight_grad.16
  588.2 14.0 %weight_grad.17 = (bf16[4,72,32,256]{3,2,1,0:T(8,128)(2,1)}, bf16[4,72,32,256]{3,2,1,0:T(8,128)(2,1)}) custom-call(s32[1]{0:T(128)} %bitcast.11.index_ref, bf16[640,768]{1,0:T(8,128)(2,1)} %get-tuple-element.109.x_ref, bf16[640,3072]{1,0:T(8,128)(2,1)} %get-tuple-element.110.g_ref), custom_call_target="tpu_custom_call" | custom-call | flops 3019898880 | bytes 9633792 | tf_op jit(solution)/shard_map/weight_grad/pallas_call | solution.py:844
  602.3 14.9 %weight_grad.18 = (bf16[4,72,32,256]{3,2,1,0:T(8,128)(2,1)}, bf16[4,72,32,256]{3,2,1,0:T(8,128)(2,1)}) custom-call(s32[1]{0:T(128)} %bitcast.11.index_ref, bf16[640,3072]{1,0:T(8,128)(2,1)} %get-tuple-element.104.x_ref, bf16[640,768]{1,0:T(8,128)(2,1)} %get-tuple-element.108.g_ref, ...), custom_call_target="tpu_custom_call", output_to_operand_aliasing={{0}: (3, {}), {1}: (4, {})} | custom-call | flops 3019898880 | bytes 9633792 | tf_op jit(solution)/shard_map/weight_grad/pallas_call | solution.py:844
  619.5 3.6 add_convert_fusion.2
  625.4 4.2 add_convert_fusion.1
  632.8 10.8 %collective-permute-done.28 = bf16[2,24,32,256]{3,2,1,0:T(8,128)(2,1)S(1)} collective-permute-done((bf16[2,24,32,256]{3,2,1,0:T(8,128)(2,1)S(1)}, bf16[2,24,32,256]{3,2,1,0:T(8,128)(2,1)S(1)}, u32[]{:S(2)}, u32[]{:S(2)}) %collective-permute-start.28) | collective-permute-done | bytes 786464 | tf_op jit(solution)/shard_map/ppermute | solution.py:898
  646.5 4.8 add_convert_fusion
  653.7 11.0 %collective-permute-done.6 = bf16[2,30,32,256]{3,2,1,0:T(8,128)(2,1)S(1)} collective-permute-done((bf16[2,30,32,256]{3,2,1,0:T(8,128)(2,1)S(1)}, bf16[2,30,32,256]{3,2,1,0:T(8,128)(2,1)S(1)}, u32[]{:S(2)}, u32[]{:S(2)}) %collective-permute-start.6) | collective-permute-done | bytes 983072 | tf_op jit(solution)/shard_map/ppermute | solution.py:898
  668.3 39.8 %collective-permute-done.9 = bf16[30,32,256]{2,1,0:T(8,128)(2,1)S(1)} collective-permute-done((bf16[30,32,256]{2,1,0:T(8,128)(2,1)S(1)}, bf16[30,32,256]{2,1,0:T(8,128)(2,1)S(1)}, u32[]{:S(2)}, u32[]{:S(2)}) %collective-permute-start.9) | collective-permute-done | bytes 491552 | tf_op jit(solution)/shard_map/ppermute | solution.py:898
  708.7 3.4 collective-permute-start.12
  718.5 14.2 %collective-permute-done.11 = bf16[15,32,256]{2,1,0:T(8,128)(2,1)S(1)} collective-permute-done((bf16[15,32,256]{2,1,0:T(8,128)(2,1)S(1)}, bf16[15,32,256]{2,1,0:T(8,128)(2,1)S(1)}, u32[]{:S(2)}, u32[]{:S(2)}) %collective-permute-start.11) | collective-permute-done | bytes 245792 | tf_op jit(solution)/shard_map/ppermute | solution.py:925
  733.8 2.0 collective-permute-start.14
  735.8 3.1 collective-permute-start.15
  740.2 3.6 collective-permute-done.13
  743.8 22.1 %collective-permute-start.21 = (bf16[18,32,256]{2,1,0:T(8,128)(2,1)S(1)}, bf16[18,32,256]{2,1,0:T(8,128)(2,1)S(1)}, u32[]{:S(2)}, u32[]{:S(2)}) collective-permute-start(bf16[18,32,256]{2,1,0:T(8,128)(2,1)S(1)} %get-tuple-element.153), channel_id=1, source_target_pairs={{0,1},{1,2},{2,3},{3,0},{4,5},{5,6},{6,7},{7,4},{8,9},{9,10},{10,1... | collective-permute-start | bytes 884744 | tf_op jit(solution)/shard_map/ppermute | solution.py:925
  766.6 15.7 %collective-permute-done.22 = bf16[18,32,256]{2,1,0:T(8,128)(2,1)S(1)} collective-permute-done((bf16[18,32,256]{2,1,0:T(8,128)(2,1)S(1)}, bf16[18,32,256]{2,1,0:T(8,128)(2,1)S(1)}, u32[]{:S(2)}, u32[]{:S(2)}) %collective-permute-start.22) | collective-permute-done | bytes 294944 | tf_op jit(solution)/shard_map/ppermute | solution.py:925
  784.6 3.0 collective-permute-start.26
  788.9 5.5 collective-permute-done.24
  794.4 19.0 %collective-permute-start.32 = (bf16[12,32,256]{2,1,0:T(8,128)(2,1)S(1)}, bf16[12,32,256]{2,1,0:T(8,128)(2,1)S(1)}, u32[]{:S(2)}, u32[]{:S(2)}) collective-permute-start(bf16[12,32,256]{2,1,0:T(8,128)(2,1)S(1)} %get-tuple-element.159), channel_id=1, source_target_pairs={{0,1},{1,2},{2,3},{3,0},{4,5},{5,6},{6,7},{7,4},{8,9},{9,10},{10,1... | collective-permute-start | bytes 589832 | tf_op jit(solution)/shard_map/ppermute | solution.py:925
  813.5 15.0 %collective-permute-done.33 = bf16[12,32,256]{2,1,0:T(8,128)(2,1)S(1)} collective-permute-done((bf16[12,32,256]{2,1,0:T(8,128)(2,1)S(1)}, bf16[12,32,256]{2,1,0:T(8,128)(2,1)S(1)}, u32[]{:S(2)}, u32[]{:S(2)}) %collective-permute-start.33) | collective-permute-done | bytes 196640 | tf_op jit(solution)/shard_map/ppermute | solution.py:925
  828.8 3.8 collective-permute-start.37
  832.6 5.8 collective-permute-done.35
  838.4 6.8 collective-permute-done.36
  845.3 2.7 gather_fusion.1
  848.0 4.6 all-to-all-start
  857.8 3.8 collective-permute-start
  864.1 3.4 collective-permute-done.1
  870.7 18.8 %collective-permute-done.3 = f32[2]{0:T(128)S(1)} collective-permute-done((f32[2]{0:T(128)S(1)}, f32[2]{0:T(128)S(1)}, u32[]{:S(2)}, u32[]{:S(2)}) %collective-permute-start.3) | collective-permute-done | bytes 40 | tf_op jit(solution)/shard_map/ppermute | solution.py:898
  890.9 2.1 collective-permute-done.4
  894.2 2.1 multiply_reduce_fusion
  903.1 2.8 collective-permute-start.40
  909.5 24.9 %tile_update.1 = (f32[24,256,256]{2,1,0:T(8,128)}, f32[24,256,256]{2,1,0:T(8,128)}, f32[24,256,256]{2,1,0:T(8,128)}, f32[24,256,256]{2,1,0:T(8,128)}) custom-call(f32[1]{0:T(128)} %bitcast.54.scale_ref, bf16[8,24,32,256]{3,2,1,0:T(8,128)(2,1)} %bitcast.57.grad_ref, f32[24,256,256]{2,1,0:T(8,128)} %w_ref.1, f32[24,256,256]{2,1,0:T(8,128)} %left_stat_ref.1, ...), custom_call_target="tpu_custom_call" | custom-call | tf_op jit(solution)/shard_map/tile_update/pallas_call | solution.py:990
  (202 shorter events, 58.5 us)
Async XLA Ops:
  7.2 134.3 %all-gather.2.cloned.1.call-start = ((), (), s32[]{:S(2)}) async-start(), calls=%async_computation.1 | async-start | bytes 28385280 | tf_op jit(solution)/shard_map/all_gather | solution.py:1059
  470.5 44.0 %copy-start.3 = (f32[8,8192]{1,0:T(8,128)S(1)}, f32[8,8192]{1,0:T(8,128)}, u32[]{:S(2)}) copy-start(f32[8,8192]{1,0:T(8,128)} %get-tuple-element.125) | copy-start | bytes 786436
  539.4 80.1 %collective-permute-start.27 = (bf16[4,48,32,256]{3,2,1,0:T(8,128)(2,1)}, bf16[4,48,32,256]{3,2,1,0:T(8,128)(2,1)}, u32[]{:S(2)}, u32[]{:S(2)}) collective-permute-start(bf16[4,48,32,256]{3,2,1,0:T(8,128)(2,1)} %get-tuple-element.133), channel_id=1, source_target_pairs={{0,4},{4,0},{8,12},{12,8},{16,20},{20,16},{24,28},{28,24},{1,5},{5... | collective-permute-start | bytes 9437192 | tf_op jit(solution)/shard_map/ppermute | solution.py:898
  587.9 37.4 %collective-permute-start.5 = (bf16[4,60,32,256]{3,2,1,0:T(8,128)(2,1)}, bf16[4,60,32,256]{3,2,1,0:T(8,128)(2,1)}, u32[]{:S(2)}, u32[]{:S(2)}) collective-permute-start(bf16[4,60,32,256]{3,2,1,0:T(8,128)(2,1)} %get-tuple-element.103), channel_id=1, source_target_pairs={{0,4},{4,0},{8,12},{12,8},{16,20},{20,16},{24,28},{28,24},{1,5},{5... | collective-permute-start | bytes 11796488 | tf_op jit(solution)/shard_map/ppermute | solution.py:898
  617.2 29.3 %collective-permute-start.16 = (bf16[4,72,32,256]{3,2,1,0:T(8,128)(2,1)}, bf16[4,72,32,256]{3,2,1,0:T(8,128)(2,1)}, u32[]{:S(2)}, u32[]{:S(2)}) collective-permute-start(bf16[4,72,32,256]{3,2,1,0:T(8,128)(2,1)} %get-tuple-element.114), channel_id=1, source_target_pairs={{0,4},{4,0},{8,12},{12,8},{16,20},{20,16},{24,28},{28,24},{1,5},{5... | collective-permute-start | bytes 14155784 | tf_op jit(solution)/shard_map/ppermute | solution.py:898
  623.1 20.4 %collective-permute-start.28 = (bf16[2,24,32,256]{3,2,1,0:T(8,128)(2,1)S(1)}, bf16[2,24,32,256]{3,2,1,0:T(8,128)(2,1)S(1)}, u32[]{:S(2)}, u32[]{:S(2)}) collective-permute-start(bf16[2,24,32,256]{3,2,1,0:T(8,128)(2,1)S(1)} %slice_bitcast_fusion.10), channel_id=1, source_target_pairs={{0,8},{4,12},{8,0},{12,4},{16,24},{20,28},{24,16},{28,20},{1,9},{5... | collective-permute-start | bytes 2359304 | tf_op jit(solution)/shard_map/ppermute | solution.py:898
  624.7 20.5 %collective-permute-start.30 = (bf16[2,24,32,256]{3,2,1,0:T(8,128)(2,1)S(1)}, bf16[2,24,32,256]{3,2,1,0:T(8,128)(2,1)S(1)}, u32[]{:S(2)}, u32[]{:S(2)}) collective-permute-start(bf16[2,24,32,256]{3,2,1,0:T(8,128)(2,1)S(1)} %slice_bitcast_fusion.8), channel_id=1, source_target_pairs={{0,16},{4,20},{8,24},{12,28},{16,0},{20,4},{24,8},{28,12},{1,17},{... | collective-permute-start | bytes 2359304 | tf_op jit(solution)/shard_map/ppermute | solution.py:898
  625.3 21.2 %slice-start = ((s8[4718592]{0:T(1024)(128)(4,1)}), s8[4194304]{0:T(1024)(128)(4,1)S(1)}, s32[]{:S(2)}) async-start(s8[4718592]{0:T(1024)(128)(4,1)} %bitcast.161), calls=%async_computation.2 | async-start | bytes 8388608
  629.7 34.9 %collective-permute-start.6 = (bf16[2,30,32,256]{3,2,1,0:T(8,128)(2,1)S(1)}, bf16[2,30,32,256]{3,2,1,0:T(8,128)(2,1)S(1)}, u32[]{:S(2)}, u32[]{:S(2)}) collective-permute-start(bf16[2,30,32,256]{3,2,1,0:T(8,128)(2,1)S(1)} %slice_bitcast_fusion.6), channel_id=1, source_target_pairs={{0,8},{4,12},{8,0},{12,4},{16,24},{20,28},{24,16},{28,20},{1,9},{5... | collective-permute-start | bytes 2949128 | tf_op jit(solution)/shard_map/ppermute | solution.py:898
  631.1 35.1 %collective-permute-start.8 = (bf16[2,30,32,256]{3,2,1,0:T(8,128)(2,1)}, bf16[2,30,32,256]{3,2,1,0:T(8,128)(2,1)S(1)}, u32[]{:S(2)}, u32[]{:S(2)}) collective-permute-start(bf16[2,30,32,256]{3,2,1,0:T(8,128)(2,1)} %slice_bitcast_fusion.4), channel_id=1, source_target_pairs={{0,16},{4,20},{8,24},{12,28},{16,0},{20,4},{24,8},{28,12},{1,17},{... | collective-permute-start | bytes 2949128 | tf_op jit(solution)/shard_map/ppermute | solution.py:898
  645.9 70.1 %collective-permute-start.31 = (bf16[24,32,256]{2,1,0:T(8,128)(2,1)S(1)}, bf16[24,32,256]{2,1,0:T(8,128)(2,1)S(1)}, u32[]{:S(2)}, u32[]{:S(2)}) collective-permute-start(bf16[24,32,256]{2,1,0:T(8,128)(2,1)S(1)} %slice_bitcast_fusion.20), channel_id=1, source_target_pairs={{0,8},{4,12},{8,0},{12,4},{16,24},{20,28},{24,16},{28,20},{1,9},{5... | collective-permute-start | bytes 1179656 | tf_op jit(solution)/shard_map/ppermute | solution.py:898
  651.4 60.7 %collective-permute-start.17 = (bf16[2,36,32,256]{3,2,1,0:T(8,128)(2,1)S(1)}, bf16[2,36,32,256]{3,2,1,0:T(8,128)(2,1)S(1)}, u32[]{:S(2)}, u32[]{:S(2)}) collective-permute-start(bf16[2,36,32,256]{3,2,1,0:T(8,128)(2,1)S(1)} %slice_bitcast_fusion.2), channel_id=1, source_target_pairs={{0,8},{4,12},{8,0},{12,4},{16,24},{20,28},{24,16},{28,20},{1,9},{5... | collective-permute-start | bytes 3538952 | tf_op jit(solution)/shard_map/ppermute | solution.py:898
  653.0 60.2 %collective-permute-start.19 = (bf16[2,36,32,256]{3,2,1,0:T(8,128)(2,1)S(1)}, bf16[2,36,32,256]{3,2,1,0:T(8,128)(2,1)S(1)}, u32[]{:S(2)}, u32[]{:S(2)}) collective-permute-start(bf16[2,36,32,256]{3,2,1,0:T(8,128)(2,1)S(1)} %slice_bitcast_fusion), channel_id=1, source_target_pairs={{0,16},{4,20},{8,24},{12,28},{16,0},{20,4},{24,8},{28,12},{1,17},{... | collective-permute-start | bytes 3538952 | tf_op jit(solution)/shard_map/ppermute | solution.py:898
  667.2 41.0 %collective-permute-start.9 = (bf16[30,32,256]{2,1,0:T(8,128)(2,1)S(1)}, bf16[30,32,256]{2,1,0:T(8,128)(2,1)S(1)}, u32[]{:S(2)}, u32[]{:S(2)}) collective-permute-start(bf16[30,32,256]{2,1,0:T(8,128)(2,1)S(1)} %slice_bitcast_fusion.16), channel_id=1, source_target_pairs={{0,8},{4,12},{8,0},{12,4},{16,24},{20,28},{24,16},{28,20},{1,9},{5... | collective-permute-start | bytes 1474568 | tf_op jit(solution)/shard_map/ppermute | solution.py:898
  667.9 40.5 %collective-permute-start.7 = (bf16[30,32,256]{2,1,0:T(8,128)(2,1)S(1)}, bf16[30,32,256]{2,1,0:T(8,128)(2,1)S(1)}, u32[]{:S(2)}, u32[]{:S(2)}) collective-permute-start(bf16[30,32,256]{2,1,0:T(8,128)(2,1)S(1)} %slice_bitcast_fusion.18), channel_id=1, source_target_pairs={{0,16},{4,20},{8,24},{12,28},{16,0},{20,4},{24,8},{28,12},{1,17},{... | collective-permute-start | bytes 1474568 | tf_op jit(solution)/shard_map/ppermute | solution.py:898
  708.7 9.8 %collective-permute-start.12 = (bf16[15,32,256]{2,1,0:T(8,128)(2,1)S(1)}, bf16[15,32,256]{2,1,0:T(8,128)(2,1)S(1)}, u32[]{:S(2)}, u32[]{:S(2)}) collective-permute-start(bf16[15,32,256]{2,1,0:T(8,128)(2,1)S(1)} %get-tuple-element.157), channel_id=1, source_target_pairs={{0,3},{1,0},{2,1},{3,2},{4,7},{5,4},{6,5},{7,6},{8,11},{9,8},{10,9... | collective-permute-start | bytes 737288 | tf_op jit(solution)/shard_map/ppermute | solution.py:925
  712.1 20.7 %collective-permute-start.11 = (bf16[15,32,256]{2,1,0:T(8,128)(2,1)S(1)}, bf16[15,32,256]{2,1,0:T(8,128)(2,1)S(1)}, u32[]{:S(2)}, u32[]{:S(2)}) collective-permute-start(bf16[15,32,256]{2,1,0:T(8,128)(2,1)S(1)} %get-tuple-element.158), channel_id=1, source_target_pairs={{0,2},{1,3},{2,0},{3,1},{4,6},{5,7},{6,4},{7,5},{8,10},{9,11},{10,... | collective-permute-start | bytes 737288 | tf_op jit(solution)/shard_map/ppermute | solution.py:925
  712.1 20.7 %collective-permute-start.10 = (bf16[15,32,256]{2,1,0:T(8,128)(2,1)S(1)}, bf16[15,32,256]{2,1,0:T(8,128)(2,1)S(1)}, u32[]{:S(2)}, u32[]{:S(2)}) collective-permute-start(bf16[15,32,256]{2,1,0:T(8,128)(2,1)S(1)} %get-tuple-element.156), channel_id=1, source_target_pairs={{0,1},{1,2},{2,3},{3,0},{4,5},{5,6},{6,7},{7,4},{8,9},{9,10},{10,1... | collective-permute-start | bytes 737288 | tf_op jit(solution)/shard_map/ppermute | solution.py:925
  714.4 24.4 %collective-permute-start.20 = (bf16[36,32,256]{2,1,0:T(8,128)(2,1)S(1)}, bf16[36,32,256]{2,1,0:T(8,128)(2,1)S(1)}, u32[]{:S(2)}, u32[]{:S(2)}) collective-permute-start(bf16[36,32,256]{2,1,0:T(8,128)(2,1)S(1)} %slice_bitcast_fusion.12), channel_id=1, source_target_pairs={{0,8},{4,12},{8,0},{12,4},{16,24},{20,28},{24,16},{28,20},{1,9},{5... | collective-permute-start | bytes 1769480 | tf_op jit(solution)/shard_map/ppermute | solution.py:898
  716.0 23.1 %collective-permute-start.18 = (bf16[36,32,256]{2,1,0:T(8,128)(2,1)S(1)}, bf16[36,32,256]{2,1,0:T(8,128)(2,1)S(1)}, u32[]{:S(2)}, u32[]{:S(2)}) collective-permute-start(bf16[36,32,256]{2,1,0:T(8,128)(2,1)S(1)} %slice_bitcast_fusion.14), channel_id=1, source_target_pairs={{0,16},{4,20},{8,24},{12,28},{16,0},{20,4},{24,8},{28,12},{1,17},{... | collective-permute-start | bytes 1769480 | tf_op jit(solution)/shard_map/ppermute | solution.py:898
  733.0 10.8 %collective-permute-start.13 = (bf16[15,32,256]{2,1,0:T(8,128)(2,1)S(1)}, bf16[15,32,256]{2,1,0:T(8,128)(2,1)S(1)}, u32[]{:S(2)}, u32[]{:S(2)}) collective-permute-start(bf16[15,32,256]{2,1,0:T(8,128)(2,1)S(1)} %get-tuple-element.146), channel_id=1, source_target_pairs={{0,1},{1,2},{2,3},{3,0},{4,5},{5,6},{6,7},{7,4},{8,9},{9,10},{10,1... | collective-permute-start | bytes 737288 | tf_op jit(solution)/shard_map/ppermute | solution.py:925
  733.8 32.1 %collective-permute-start.14 = (bf16[15,32,256]{2,1,0:T(8,128)(2,1)S(1)}, bf16[15,32,256]{2,1,0:T(8,128)(2,1)S(1)}, u32[]{:S(2)}, u32[]{:S(2)}) collective-permute-start(bf16[15,32,256]{2,1,0:T(8,128)(2,1)S(1)} %get-tuple-element.146), channel_id=1, source_target_pairs={{0,2},{1,3},{2,0},{3,1},{4,6},{5,7},{6,4},{7,5},{8,10},{9,11},{10,... | collective-permute-start | bytes 737288 | tf_op jit(solution)/shard_map/ppermute | solution.py:925
  735.8 30.7 %collective-permute-start.15 = (bf16[15,32,256]{2,1,0:T(8,128)(2,1)S(1)}, bf16[15,32,256]{2,1,0:T(8,128)(2,1)S(1)}, u32[]{:S(2)}, u32[]{:S(2)}) collective-permute-start(bf16[15,32,256]{2,1,0:T(8,128)(2,1)S(1)} %get-tuple-element.146), channel_id=1, source_target_pairs={{0,3},{1,0},{2,1},{3,2},{4,7},{5,4},{6,5},{7,6},{8,11},{9,8},{10,9... | collective-permute-start | bytes 737288 | tf_op jit(solution)/shard_map/ppermute | solution.py:925
  739.5 27.0 %collective-permute-start.23 = (bf16[18,32,256]{2,1,0:T(8,128)(2,1)S(1)}, bf16[18,32,256]{2,1,0:T(8,128)(2,1)S(1)}, u32[]{:S(2)}, u32[]{:S(2)}) collective-permute-start(bf16[18,32,256]{2,1,0:T(8,128)(2,1)S(1)} %get-tuple-element.154), channel_id=1, source_target_pairs={{0,3},{1,0},{2,1},{3,2},{4,7},{5,4},{6,5},{7,6},{8,11},{9,8},{10,9... | collective-permute-start | bytes 884744 | tf_op jit(solution)/shard_map/ppermute | solution.py:925
  739.6 42.7 %collective-permute-start.22 = (bf16[18,32,256]{2,1,0:T(8,128)(2,1)S(1)}, bf16[18,32,256]{2,1,0:T(8,128)(2,1)S(1)}, u32[]{:S(2)}, u32[]{:S(2)}) collective-permute-start(bf16[18,32,256]{2,1,0:T(8,128)(2,1)S(1)} %get-tuple-element.155), channel_id=1, source_target_pairs={{0,2},{1,3},{2,0},{3,1},{4,6},{5,7},{6,4},{7,5},{8,10},{9,11},{10,... | collective-permute-start | bytes 884744 | tf_op jit(solution)/shard_map/ppermute | solution.py:925
  743.8 38.5 %collective-permute-start.21 = (bf16[18,32,256]{2,1,0:T(8,128)(2,1)S(1)}, bf16[18,32,256]{2,1,0:T(8,128)(2,1)S(1)}, u32[]{:S(2)}, u32[]{:S(2)}) collective-permute-start(bf16[18,32,256]{2,1,0:T(8,128)(2,1)S(1)} %get-tuple-element.153), channel_id=1, source_target_pairs={{0,1},{1,2},{2,3},{3,0},{4,5},{5,6},{6,7},{7,4},{8,9},{9,10},{10,1... | collective-permute-start | bytes 884744 | tf_op jit(solution)/shard_map/ppermute | solution.py:925
  765.9 16.7 %collective-permute-start.29 = (bf16[24,32,256]{2,1,0:T(8,128)(2,1)S(1)}, bf16[24,32,256]{2,1,0:T(8,128)(2,1)S(1)}, u32[]{:S(2)}, u32[]{:S(2)}) collective-permute-start(bf16[24,32,256]{2,1,0:T(8,128)(2,1)S(1)} %slice_bitcast_fusion.22), channel_id=1, source_target_pairs={{0,16},{4,20},{8,24},{12,28},{16,0},{20,4},{24,8},{28,12},{1,17},{... | collective-permute-start | bytes 1179656 | tf_op jit(solution)/shard_map/ppermute | solution.py:898
  782.5 11.9 %collective-permute-start.24 = (bf16[18,32,256]{2,1,0:T(8,128)(2,1)S(1)}, bf16[18,32,256]{2,1,0:T(8,128)(2,1)S(1)}, u32[]{:S(2)}, u32[]{:S(2)}) collective-permute-start(bf16[18,32,256]{2,1,0:T(8,128)(2,1)S(1)} %get-tuple-element.144), channel_id=1, source_target_pairs={{0,1},{1,2},{2,3},{3,0},{4,5},{5,6},{6,7},{7,4},{8,9},{9,10},{10,1... | collective-permute-start | bytes 884744 | tf_op jit(solution)/shard_map/ppermute | solution.py:925
  782.7 30.7 %collective-permute-start.25 = (bf16[18,32,256]{2,1,0:T(8,128)(2,1)S(1)}, bf16[18,32,256]{2,1,0:T(8,128)(2,1)S(1)}, u32[]{:S(2)}, u32[]{:S(2)}) collective-permute-start(bf16[18,32,256]{2,1,0:T(8,128)(2,1)S(1)} %get-tuple-element.144), channel_id=1, source_target_pairs={{0,2},{1,3},{2,0},{3,1},{4,6},{5,7},{6,4},{7,5},{8,10},{9,11},{10,... | collective-permute-start | bytes 884744 | tf_op jit(solution)/shard_map/ppermute | solution.py:925
  784.6 28.9 %collective-permute-start.26 = (bf16[18,32,256]{2,1,0:T(8,128)(2,1)S(1)}, bf16[18,32,256]{2,1,0:T(8,128)(2,1)S(1)}, u32[]{:S(2)}, u32[]{:S(2)}) collective-permute-start(bf16[18,32,256]{2,1,0:T(8,128)(2,1)S(1)} %get-tuple-element.144), channel_id=1, source_target_pairs={{0,3},{1,0},{2,1},{3,2},{4,7},{5,4},{6,5},{7,6},{8,11},{9,8},{10,9... | collective-permute-start | bytes 884744 | tf_op jit(solution)/shard_map/ppermute | solution.py:925
  787.6 25.9 %collective-permute-start.34 = (bf16[12,32,256]{2,1,0:T(8,128)(2,1)S(1)}, bf16[12,32,256]{2,1,0:T(8,128)(2,1)S(1)}, u32[]{:S(2)}, u32[]{:S(2)}) collective-permute-start(bf16[12,32,256]{2,1,0:T(8,128)(2,1)S(1)} %get-tuple-element.160), channel_id=1, source_target_pairs={{0,3},{1,0},{2,1},{3,2},{4,7},{5,4},{6,5},{7,6},{8,11},{9,8},{10,9... | collective-permute-start | bytes 589832 | tf_op jit(solution)/shard_map/ppermute | solution.py:925
  787.6 40.9 %collective-permute-start.33 = (bf16[12,32,256]{2,1,0:T(8,128)(2,1)S(1)}, bf16[12,32,256]{2,1,0:T(8,128)(2,1)S(1)}, u32[]{:S(2)}, u32[]{:S(2)}) collective-permute-start(bf16[12,32,256]{2,1,0:T(8,128)(2,1)S(1)} %get-tuple-element.161), channel_id=1, source_target_pairs={{0,2},{1,3},{2,0},{3,1},{4,6},{5,7},{6,4},{7,5},{8,10},{9,11},{10,... | collective-permute-start | bytes 589832 | tf_op jit(solution)/shard_map/ppermute | solution.py:925
  794.4 34.1 %collective-permute-start.32 = (bf16[12,32,256]{2,1,0:T(8,128)(2,1)S(1)}, bf16[12,32,256]{2,1,0:T(8,128)(2,1)S(1)}, u32[]{:S(2)}, u32[]{:S(2)}) collective-permute-start(bf16[12,32,256]{2,1,0:T(8,128)(2,1)S(1)} %get-tuple-element.159), channel_id=1, source_target_pairs={{0,1},{1,2},{2,3},{3,0},{4,5},{5,6},{6,7},{7,4},{8,9},{9,10},{10,1... | collective-permute-start | bytes 589832 | tf_op jit(solution)/shard_map/ppermute | solution.py:925
  828.6 9.8 %collective-permute-start.35 = (bf16[12,32,256]{2,1,0:T(8,128)(2,1)S(1)}, bf16[12,32,256]{2,1,0:T(8,128)(2,1)S(1)}, u32[]{:S(2)}, u32[]{:S(2)}) collective-permute-start(bf16[12,32,256]{2,1,0:T(8,128)(2,1)S(1)} %get-tuple-element.142), channel_id=1, source_target_pairs={{0,1},{1,2},{2,3},{3,0},{4,5},{5,6},{6,7},{7,4},{8,9},{9,10},{10,1... | collective-permute-start | bytes 589832 | tf_op jit(solution)/shard_map/ppermute | solution.py:925
  828.7 16.6 %collective-permute-start.36 = (bf16[12,32,256]{2,1,0:T(8,128)(2,1)S(1)}, bf16[12,32,256]{2,1,0:T(8,128)(2,1)S(1)}, u32[]{:S(2)}, u32[]{:S(2)}) collective-permute-start(bf16[12,32,256]{2,1,0:T(8,128)(2,1)S(1)} %get-tuple-element.142), channel_id=1, source_target_pairs={{0,2},{1,3},{2,0},{3,1},{4,6},{5,7},{6,4},{7,5},{8,10},{9,11},{10,... | collective-permute-start | bytes 589832 | tf_op jit(solution)/shard_map/ppermute | solution.py:925
  828.8 16.5 %collective-permute-start.37 = (bf16[12,32,256]{2,1,0:T(8,128)(2,1)S(1)}, bf16[12,32,256]{2,1,0:T(8,128)(2,1)S(1)}, u32[]{:S(2)}, u32[]{:S(2)}) collective-permute-start(bf16[12,32,256]{2,1,0:T(8,128)(2,1)S(1)} %get-tuple-element.142), channel_id=1, source_target_pairs={{0,3},{1,0},{2,1},{3,2},{4,7},{5,4},{6,5},{7,6},{8,11},{9,8},{10,9... | collective-permute-start | bytes 589832 | tf_op jit(solution)/shard_map/ppermute | solution.py:925
  848.0 61.5 %all-to-all-start = ((bf16[192,32,256]{2,1,0:T(8,128)(2,1)}), bf16[192,32,256]{2,1,0:T(8,128)(2,1)}, u32[]{:S(2)}, u32[]{:S(2)}) async-start(bf16[192,32,256]{2,1,0:T(8,128)(2,1)} %gather_fusion.1), calls=%async_computation | async-start | bytes 6291456 | tf_op jit(solution)/shard_map/all_to_all | solution.py:1150
  852.6 56.3 %copy-start.4 = (f32[2560]{0:T(1024)S(1)}, f32[2560]{0:T(1024)}, u32[]{:S(2)}) copy-start(f32[2560]{0:T(1024)} %param.23) | copy-start | bytes 30724
  852.6 56.3 %copy-start.5 = (f32[2560]{0:T(1024)S(1)}, f32[2560]{0:T(1024)}, u32[]{:S(2)}) copy-start(f32[2560]{0:T(1024)} %param.25) | copy-start | bytes 30724
  852.6 56.3 %copy-start.6 = (f32[2560]{0:T(1024)S(1)}, f32[2560]{0:T(1024)}, u32[]{:S(2)}) copy-start(f32[2560]{0:T(1024)} %param.24) | copy-start | bytes 30724
  857.8 5.3 collective-permute-start
  863.1 4.4 collective-permute-start.1
  867.7 1.1 collective-permute-start.2
  868.8 20.6 %collective-permute-start.3 = (f32[2]{0:T(128)S(1)}, f32[2]{0:T(128)S(1)}, u32[]{:S(2)}, u32[]{:S(2)}) collective-permute-start(f32[2]{0:T(128)S(1)} %add.257), channel_id=1, source_target_pairs={{0,8},{4,12},{8,0},{12,4},{16,24},{20,28},{24,16},{28,20},{1,9},{5... | collective-permute-start | bytes 32 | tf_op jit(solution)/shard_map/ppermute | solution.py:898
  889.4 3.5 collective-permute-start.4
  896.3 1.2 collective-permute-start.38
  898.9 3.6 collective-permute-start.39
  903.1 3.6 collective-permute-start.40
  (16 other events, 198.8 us)
Sparse Core Ops, SparseCore 0:
  13.2 128.2 all-gather.1

commit v2 on v1

--- a/solution.py
+++ b/solution.py
@@ -100,13 +100,19 @@
     return centred * inverse, inverse
 
 
-def row_loop(rows, step, body, carry=0, unroll=2):
+def loop(lower, upper, body, carry, most=26):
+    count = upper - lower
+    unroll = max(u for u in range(1, min(most, count) + 1) if count % u == 0)
+    return lax.fori_loop(lower, upper, body, carry, unroll=unroll)
+
+
+def row_loop(rows, step, body, carry=0):
     count = rows // step
 
     def one(i, c):
         return body(pl.ds(pl.multiple_of(i * step, step), step), c)
 
-    return lax.fori_loop(0, count, one, carry, unroll=unroll if count % unroll == 0 else 1)
+    return loop(0, count, one, carry)
 
 
 def norm_forward(x_ref, gain, shift, out_ref):
@@ -141,7 +147,7 @@
         body(j, pl.ds(pl.multiple_of(j * BS, BS), BS))
         return c
 
-    lax.fori_loop(0, count, one, 0)
+    loop(0, count, one, 0, 4)
 
 
 def vec_at(vec_ref, start, j):
@@ -182,7 +188,7 @@
         lse_ref[image, g] = jnp.concatenate(logs, axis=0)
         return c
 
-    lax.fori_loop(0, width // BS, group, 0)
+    loop(0, width // BS, group, 0)
 
 
 def attention_backward(qkv_ref, datt_ref, lse_ref, dqkv_ref, image, seq, width, head_size, valid):
@@ -214,7 +220,7 @@
         dqkv_ref[rows, cols(2)] = jnp.concatenate(d_v, axis=0).T.astype(BF)
         return c
 
-    lax.fori_loop(0, width // BS, group, 0)
+    loop(0, width // BS, group, 0)
 
 
 def fetch_tiles(row_ref, wg_ref, first, dst, sem):
@@ -533,8 +539,8 @@
             x0[at, :] = token + pos_ref[at, :]
             return c
 
-        lax.fori_loop(0, VMAX // chunk, head_rows, 0)
-        lax.fori_loop(VMAX // chunk, SD // chunk, tail_rows, 0)
+        loop(0, VMAX // chunk, head_rows, 0)
+        loop(VMAX // chunk, SD // chunk, tail_rows, 0)
         return c
 
     lax.fori_loop(0, images, place, 0)
@@ -575,7 +581,7 @@
             gpred_ref[at, :] = low
             return (loss + fold8(residual * residual), bias + fold8(low.astype(F32)))
 
-        return lax.fori_loop(0, SD // chunk, one, c)
+        return loop(0, SD // chunk, one, c)
 
     zero = jnp.zeros((8, PIX), F32)
     loss, bias = lax.fori_loop(0, images, errors, (zero, zero))
@@ -622,8 +628,8 @@
             got = grad[pl.ds(pl.multiple_of(image * SD + i * chunk, chunk), chunk), :]
             return c + fold8(jnp.where(i * chunk + order < POS, got, 0.0))
 
-        c = lax.fori_loop(0, VMAX // chunk, head_rows, c)
-        return lax.fori_loop(VMAX // chunk, SD // chunk, tail_rows, c)
+        c = loop(0, VMAX // chunk, head_rows, c)
+        return loop(VMAX // chunk, SD // chunk, tail_rows, c)
 
     add_sum(sum_ref, DS_MASK, lax.fori_loop(0, images, unplace, jnp.zeros((8, E), F32)))
 
@@ -816,43 +822,50 @@
 
 def weight_grad_kernel(parts, cut, extra, index_ref, x_ref, g_ref, *refs):
     outs = refs[extra : extra + min(parts, 2)]
-    total = refs[-1]
-    col_tiles = g_ref.shape[1] // BS
-    x_t = x_ref[...].T
-
-    def body(j, cols):
-        total[:, cols] = mm(x_t, g_ref[:, cols])
-
-    col_loop(col_tiles, body)
+    x_t, total = refs[-2:]
+    row_tiles, col_tiles = x_ref.shape[1] // BS, g_ref.shape[1] // BS
+
+    @pl.when(pl.program_id(1) == 0)
+    def _():
+        x_t[...] = x_ref[...].T
+
+    total[...] = mm(x_t[...], g_ref[...])
     for p in range(parts):
-        start = pl.multiple_of((p ^ index_ref[0]) * cut, cut)
-        for j in range(col_tiles):
-            outs[p % 2][p // 2, j] = total[pl.ds(start, cut), j * BS : (j + 1) * BS].astype(BF)
-
-
-def weight_grad(index, parts, count, first, x, g, buffers):
+        for i in range(row_tiles):
+            start = pl.multiple_of(i * BS + (p ^ index_ref[0]) * cut, cut)
+            for j in range(col_tiles):
+                got = total[pl.ds(start, cut), j * BS : (j + 1) * BS]
+                outs[p % 2][p // 2, i * col_tiles + j] = got.astype(BF)
+
+
+def weight_grad(index, parts, count, first, x, g, block, buffers):
     cut = BS // parts
     rows, width = x.shape
-    col_tiles = g.shape[1] // BS
-    assert first % col_tiles == 0
+    row_tiles, col_tiles = block
+    size = row_tiles * col_tiles
+    across = g.shape[1] // (col_tiles * BS)
+    assert first % size == 0
     held = min(parts, 2)
     shape = jax.ShapeDtypeStruct((parts // held, count, cut, BS), BF)
     given = list(buffers or [])
     out_spec = pl.BlockSpec(
-        (parts // held, col_tiles, cut, BS), lambda i, *_: (0, first // col_tiles + i, 0, 0)
+        (parts // held, size, cut, BS), lambda i, j, *_: (0, first // size + i * across + j, 0, 0)
     )
     return pl.pallas_call(
         functools.partial(weight_grad_kernel, parts, cut, len(given)),
         grid_spec=pltpu.PrefetchScalarGridSpec(
             num_scalar_prefetch=1,
-            grid=(width // BS,),
+            grid=(width // (row_tiles * BS), across),
             in_specs=[
-                pl.BlockSpec((rows, BS), lambda i, *_: (0, i)),
-                pl.BlockSpec(g.shape, lambda i, *_: (0, 0)),
+                pl.BlockSpec((rows, row_tiles * BS), lambda i, j, *_: (0, i)),
+                pl.BlockSpec((rows, col_tiles * BS), lambda i, j, *_: (0, j)),
             ]
             + [pl.BlockSpec(memory_space=pl.ANY)] * len(given),
             out_specs=[out_spec] * held,
-            scratch_shapes=[pltpu.VMEM((BS, g.shape[1]), F32)],
+            scratch_shapes=[
+                pltpu.VMEM((row_tiles * BS, rows), BF),
+                pltpu.VMEM((row_tiles * BS, col_tiles * BS), F32),
+            ],
         ),
         out_shape=[shape] * held,
         input_output_aliases={3 + i: i for i in range(len(given))},
@@ -898,27 +911,33 @@
     return lax.ppermute(x, "dp", [(i, i ^ (1 << bit)) for i in range(size)])
 
 
-def reduce_dp(buffers, parts):
+def reduce_core(buffers, parts):
     if parts == 1:
-        return buffers[0][0]
-    bits = parts.bit_length() - 1
+        return [buffers[0][0]] * 2, []
     whole = low_sum(buffers[0], swap_bit(buffers[1], 0, parts))
-    count = whole.shape[1]
-    whole = whole.reshape((2,) * (bits - 1) + whole.shape[1:])
-    results = []
-    for half in range(2):
-        lo, hi = (0, count // 2) if half == 0 else (count // 2, count)
-        current = whole[..., lo:hi, :, :]
-        left = list(range(bits - 1, 0, -1))
-        order = left[::-1] if half == 0 else left
-        for bit in order:
-            axis = left.index(bit)
-            left = [b for b in left if b != bit]
-            keep = lax.index_in_dim(current, 0, axis, keepdims=False)
-            send = lax.index_in_dim(current, 1, axis, keepdims=False)
-            current = low_sum(keep, swap_bit(send, bit, parts))
-        results.append(current)
-    return jnp.concatenate(results, axis=0)
+    bits = list(range(parts.bit_length() - 2, 0, -1))
+    whole = whole.reshape((2,) * len(bits) + whole.shape[1:])
+    count = whole.shape[-3]
+    return [whole[..., : count // 2, :, :], whole[..., count // 2 :, :, :]], [bits, bits]
+
+
+def reduce_chips(state, parts, steps):
+    halves, left = list(state[0]), list(state[1])
+    for half in range(2 if parts > 1 else 0):
+        for _ in range(min(steps, len(left[half]))):
+            bit = left[half][-1 if half == 0 else 0]
+            axis = left[half].index(bit)
+            keep = lax.index_in_dim(halves[half], 0, axis, keepdims=False)
+            send = lax.index_in_dim(halves[half], 1, axis, keepdims=False)
+            halves[half] = low_sum(keep, swap_bit(send, bit, parts))
+            left[half] = [b for b in left[half] if b != bit]
+    return halves, left
+
+
+def reduce_end(state, parts, groups):
+    halves, _ = reduce_chips(state, parts, 99)
+    whole = jnp.concatenate(halves, axis=0) if parts > 1 else halves[0]
+    return reduce_patch(whole, groups)
 
 
 def shift_patch(x, shift, size):
@@ -1010,11 +1029,17 @@
     return moment_new, second_new, vectors_new
 
 
-ENC_ORDER = [(T_EUP, 3, 12), (T_EDOWN, 12, 3)]
 CHUNKS = [
-    [(T_DUP, 2, 8), (T_DDOWN, 8, 2), (T_DOUT, 2, 2), (T_DQKV, 2, 6), (T_HEAD, 2, 3), (T_PROJ, 3, 2)],
-    [(T_EUP, 3, 12), (T_EDOWN, 12, 3)],
-    [(T_EQKV, 3, 9), (T_EOUT, 3, 3), (T_EMBED, 3, 3)],
+    [
+        (T_DUP, 2, 8, (2, 4)),
+        (T_DDOWN, 8, 2, (4, 2)),
+        (T_DOUT, 2, 2, (2, 2)),
+        (T_DQKV, 2, 6, (2, 3)),
+        (T_HEAD, 2, 3, (2, 3)),
+        (T_PROJ, 3, 2, (3, 2)),
+    ],
+    [(T_EUP, 3, 12, (3, 4)), (T_EDOWN, 12, 3, (4, 3)), (T_EOUT, 3, 3, (3, 3))],
+    [(T_EQKV, 3, 9, (3, 3)), (T_EMBED, 3, 3, (3, 3))],
 ]
 
 
@@ -1022,7 +1047,7 @@
     unit = max(2, groups)
     sizes = []
     for i, chunk in enumerate(CHUNKS):
-        used = sum(r * c for _, r, c in chunk) + (2 if i == len(CHUNKS) - 1 else 0)
+        used = sum(r * c for _, r, c, _ in chunk) + (2 if i == len(CHUNKS) - 1 else 0)
         sizes.append(-(-used // unit) * unit)
     return sizes
 
@@ -1032,14 +1057,17 @@
     place_of = np.zeros(NBLK + 2, np.int32)
     for i, chunk in enumerate(CHUNKS):
         at = 0
-        for first, row_tiles, col_tiles in chunk:
-            for t in range(row_tiles * col_tiles):
-                chunk_of[first + t], place_of[first + t] = i, at + t
+        for first, row_tiles, col_tiles, (high, wide) in chunk:
+            for r in range(row_tiles):
+                for c in range(col_tiles):
+                    block = r // high * (col_tiles // wide) + c // wide
+                    chunk_of[first + r * col_tiles + c] = i
+                    place_of[first + r * col_tiles + c] = at + block * high * wide + r % high * wide + c % wide
             at += row_tiles * col_tiles
     chunk_of[NBLK:] = len(CHUNKS) - 1
     place_of[NBLK + 1] = at
     place_of[NBLK] = at + 1
-    return chunk_of, place_of, at
+    return chunk_of, place_of
 
 
 def shards(parts, groups, pixels, shuffle, vis_len, block_owner, weights, vectors, vec_moment, vec_second,
@@ -1079,23 +1107,39 @@
         tile_rows, vis_len, gathered, vector, latent, pos_e, ordered, 4
     )
     sizes = chunk_sizes(groups)
-    chunk_of, place_of, vector_place = tile_places(sizes)
-
-    def gradients(chunk, pairs, buffers=None):
-        at = 0
-        for x, g in pairs:
-            buffers = weight_grad(index, parts, sizes[chunk], at, x, g, buffers)
-            at += x.shape[1] // BS * (g.shape[1] // BS)
-        return reduce_patch(reduce_dp(buffers, parts), groups)
-
-    first = gradients(
+    chunk_of, place_of = tile_places(sizes)
+
+    rows_cut = BS // parts
+
+    def gradients(chunk, pairs, vector_tile=None):
+        used = sum(r * c for _, r, c, _ in CHUNKS[chunk])
+        at, buffers = 0, None
+        if sizes[chunk] > used:
+            if vector_tile is None:
+                vector_tile = jnp.zeros((parts, rows_cut, BS), F32)
+            buffers = seed_buffers(index, parts, sizes[chunk], used, vector_tile)
+        for (x, g), (_, row_tiles, col_tiles, block) in zip(pairs, CHUNKS[chunk]):
+            buffers = weight_grad(index, parts, sizes[chunk], at, x, g, block, buffers)
+            at += row_tiles * col_tiles
+        return buffers
+
+    buffers0 = gradients(
         0, [(d_h2, d_du), (d_act, d_gdown), (d_att, d_gproj), (d_h1, d_dqkv), (d_hn, d_gpred), (hn, glat)]
     )
+    glat, buffers0 = lax.optimization_barrier((glat, buffers0))
     gdown, du, grad_mid, gproj, m_sums = encoder_mlp_back(tile_rows, gathered, vector, glat, x1, mid, slope, 2)
-    second = gradients(1, [(h2, du), (act, gdown)])
+    state0 = reduce_core(buffers0, parts)
+    gdown, du, gproj, halves = lax.optimization_barrier((gdown, du, gproj, state0[0]))
+    state0 = (halves, state0[1])
+    buffers1 = gradients(1, [(h2, du), (act, gdown), (att, gproj)])
+    state0 = reduce_chips(state0, parts, 1)
+    gproj, buffers1 = lax.optimization_barrier((gproj, buffers1))
     dqkv, gembed, a_sums = encoder_attention_back(
         tile_rows, vis_len, gathered, vector, gproj, grad_mid, qkv, lse, x0, 2
     )
+    state1 = reduce_core(buffers1, parts)
+    dqkv, gembed, halves0, halves1 = lax.optimization_barrier((dqkv, gembed, state0[0], state1[0]))
+    state0, state1 = (halves0, state0[1]), (halves1, state1[1])
 
     d_sums, m_sums, a_sums = (jnp.sum(s, axis=0) for s in (d_sums, m_sums, a_sums))
 
@@ -1126,10 +1170,12 @@
             cut(d_sums, DS_HEAD, PIX),
         ]
     )
-    rows_cut = BS // parts
     vector_tile = jnp.pad(grad_vector.reshape(parts, own), ((0, 0), (0, rows_cut * BS - own)))
-    seeded = seed_buffers(index, parts, sizes[2], vector_place, vector_tile.reshape(parts, rows_cut, BS))
-    third = gradients(2, [(h1, dqkv), (att, gproj), (visible_pix.reshape(-1, PIX), gembed)], seeded)
+    vector_tile = vector_tile.reshape(parts, rows_cut, BS)
+    buffers2 = gradients(2, [(h1, dqkv), (visible_pix.reshape(-1, PIX), gembed)], vector_tile)
+    first = reduce_end(state0, parts, groups)
+    second = reduce_end(state1, parts, groups)
+    third = reduce_end(reduce_core(buffers2, parts), parts, groups)
 
     reduced = jnp.concatenate([first, second, third], axis=0)
     starts = np.cumsum([0] + sizes)

time: 954 us -> 745 us (0.78)
  Pallas kernels: 504 us -> 326 us
  waiting for transfers between devices: 279 us -> 235 us
  local copies, waits for them, and re-layouts: 13.9 us -> 27.4 us
  other arithmetic: 30 us -> 41.2 us
    pallas_call x4, Pallas kernels: 369 us -> 222 us  [group_call(): pl.pallas_call(kernel, grid_spec=pltpu.PrefetchScalarGridSpec(num_scalar_...]
    ppermute x21, waiting for transfers between devices: 90.5 us -> 55 us  [swap_bit(): return lax.ppermute(x, 'dp', [(i, i ^ 1 << bit) for i in range(size)])]
    pallas_call x11, Pallas kernels: 98.8 us -> 65.6 us  [weight_grad(): pl.pallas_call(functools.partial(weight_grad_kernel, parts, cut, len(give...]
    ppermute x18, starting transfers between devices: 62.2 us -> 51.1 us  [shift_patch(): lax.ppermute(x, 'patch', [(i, (i + shift) % size) for i in range(size)])]
    convert_element_type x12 -> x14, other arithmetic: 16.4 us -> 27.3 us  [low_sum(): return (a.astype(F32) + b.astype(F32)).astype(BF)]
  transfers between devices with their start and end apart: 43 -> 43, of which waited for: 22 -> 20; matrix products, arithmetic and copies ran while one was open for 3% -> 6% of each run, Pallas kernels for 9% -> 10%
where the time goes in v2:
time: 745 us; the launch traced here: 737 us
  Pallas kernels  326 us (44%)
  waiting for transfers between devices  235 us (32%)
  starting transfers between devices  82.7 us (11%)
  other arithmetic  41.2 us (6%)
  local copies, waits for them, and re-layouts  27.4 us (4%)
  between operations  24.5 us (3%)
    pallas_call x4, Pallas kernels, group_call(): pl.pallas_call(kernel, grid_spec=pltpu.PrefetchScalarGridSpec(num_scalar_...  222 us
    all_gather x1, waiting for transfers between devices, shards(): gathered = lax.all_gather(mine, 'dp', axis=0, tiled=True)  115 us
    pallas_call x11, Pallas kernels, weight_grad(): pl.pallas_call(functools.partial(weight_grad_kernel, parts, cut, len(give...  65.6 us
    ppermute x18, waiting for transfers between devices, shift_patch(): lax.ppermute(x, 'patch', [(i, (i + shift) % size) for i in range(size)])  59.9 us
    ppermute x21, waiting for transfers between devices, swap_bit(): return lax.ppermute(x, 'dp', [(i, i ^ 1 << bit) for i in range(size)])  55 us
    ppermute x18, starting transfers between devices, shift_patch(): lax.ppermute(x, 'patch', [(i, (i + shift) % size) for i in range(size)])  51.1 us
    convert_element_type x14, other arithmetic, low_sum(): return (a.astype(F32) + b.astype(F32)).astype(BF)  27.3 us
    pallas_call x1, Pallas kernels, tile_update(): pl.pallas_call(tile_kernel, grid_spec=pltpu.PrefetchScalarGridSpec(num_sc...  24.9 us
  transfers between devices with their start and end apart: 43, of which 20 were waited for; matrix products, arithmetic and copies ran while one was open for 6% of the time, Pallas kernels for 10%

profile of v2, /device:TPU:0, one launch (start us, length us, event | category | flops | bytes accessed | tf_op | source)
XLA Modules:
  0.0 737.2 jit_solution(850013643376283683)
XLA Ops:
  8.0 3.2 convert_element_type.251
  16.9 8.7 %order_patches.1 = (bf16[8,208,768]{2,1,0:T(8,128)(2,1)}, bf16[8,80,768]{2,1,0:T(8,128)(2,1)}, f32[8,80,768]{2,1,0:T(8,128)}, f32[8,208,512]{2,1,0:T(8,128)}) custom-call(s32[8,208,1]{2,1,0:T(8,128)} %copy.59.shuffle_ref, bf16[8,196,768]{2,1,0:T(8,128)(2,1)} %copy.60.pixels_ref, bf16[2,196,768]{2,1,0:T(8,128)(2,1)} %constant.225.clone.sin_d_ref, ...), custom_call_target="tpu_custom_call" | custom-call | tf_op jit(solution)/shard_map/order_patches/pallas_call | solution.py:354
  26.3 115.2 %all-gather.2.cloned.1.call-done.wg_ref = bf16[49280,256]{1,0:T(8,128)(2,1)} async-done(((bf16[6160,256]{1,0:T(8,128)(2,1)}), bf16[49280,256]{1,0:T(8,128)(2,1)}) %all-gather.2.cloned.1.call-update) | async-done | bytes 25231376 | tf_op jit(solution)/shard_map/all_gather | solution.py:1087
  143.2 42.7 %encoder_forward.1 = (f32[640,768]{1,0:T(8,128)}, bf16[640,768]{1,0:T(8,128)(2,1)}, bf16[640,2304]{1,0:T(8,128)(2,1)}, f32[8,3,4,80]{3,2,1,0:T(4,128)}, bf16[640...) custom-call(s32[177]{0:T(256)} %fusion.37.row_ref, ...), custom_call_target="tpu_custom_call" | custom-call | flops 10317987840 | bytes 43970560 | tf_op jit(solution)/shard_map/encoder_forward/pallas_call | solution.py:379
  185.9 129.7 %decoder.1 = (bf16[1664,512]{1,0:T(8,128)(2,1)}, bf16[1664,1536]{1,0:T(8,128)(2,1)}, bf16[1664,512]{1,0:T(8,128)(2,1)}, bf16[1664,512]{1,0:T(8,128)(2,1)}, bf16[...) custom-call(s32[177]{0:T(256)} %fusion.37.row_ref, ...), custom_call_target="tpu_custom_call" | custom-call | flops 23555211264 | bytes 64978944 | tf_op jit(solution)/shard_map/decoder/pallas_call | solution.py:379
  315.6 8.3 %weight_grad.11 = (bf16[4,60,32,256]{3,2,1,0:T(8,128)(2,1)}, bf16[4,60,32,256]{3,2,1,0:T(8,128)(2,1)}) custom-call(s32[1]{0:T(128)} %bitcast.11.index_ref, bf16[1664,512]{1,0:T(8,128)(2,1)} %get-tuple-element.109.x_ref, bf16[1664,2048]{1,0:T(8,128)(2,1)} %get-tuple-element.110.g_ref), custom_call_target="tpu_custom_call" | custom-call | flops 3489660928 | bytes 10616832 | tf_op jit(solution)/shard_map/weight_grad/pallas_call | solution.py:854
  323.9 7.9 %weight_grad.12 = (bf16[4,60,32,256]{3,2,1,0:T(8,128)(2,1)}, bf16[4,60,32,256]{3,2,1,0:T(8,128)(2,1)}) custom-call(s32[1]{0:T(128)} %bitcast.11.index_ref, bf16[1664,2048]{1,0:T(8,128)(2,1)} %get-tuple-element.107.x_ref, bf16[1664,512]{1,0:T(8,128)(2,1)} %get-tuple-element.108.g_ref, ...), custom_call_target="tpu_custom_call", output_to_operand_aliasing={{0}: (3, {}), {1}: (4, {})} | custom-call | flops 3489660928 | bytes 10616832 | tf_op jit(solution)/shard_map/weight_grad/pallas_call | solution.py:854
  331.8 4.0 weight_grad.13
  335.8 7.0 weight_grad.14
  342.8 4.8 weight_grad.15
  347.7 3.2 weight_grad.16
  351.8 2.3 seed_buffers.2
  354.1 18.1 %encoder_mlp_back.1 = (bf16[640,768]{1,0:T(8,128)(2,1)}, bf16[640,3072]{1,0:T(8,128)(2,1)}, f32[640,768]{1,0:T(8,128)}, bf16[640,768]{1,0:T(8,128)(2,1)}, f32[8,8192]{1,0:T(8,128)}) custom-call(s32[177]{0:T(256)} %fusion.37.row_ref, bf16[49280,256]{1,0:T(8,128)(2,1)} %all-gather.2.cloned.1.call-done.wg_ref, f32[1,21760]{1,0:T(1,128)} %reshape.138.vec_ref, ...), custom_call_target="tpu_custom_call" | custom-call | flops 6543114240 | bytes 16252928 | tf_op jit(solution)/shard_map/encoder_mlp_back/pallas_call | solution.py:379
  372.2 4.2 add_convert_fusion.1
  378.3 8.1 %weight_grad.17 = (bf16[4,84,32,256]{3,2,1,0:T(8,128)(2,1)}, bf16[4,84,32,256]{3,2,1,0:T(8,128)(2,1)}) custom-call(s32[1]{0:T(128)} %bitcast.11.index_ref, bf16[640,768]{1,0:T(8,128)(2,1)} %get-tuple-element.136.x_ref, bf16[640,3072]{1,0:T(8,128)(2,1)} %get-tuple-element.137.g_ref, ...), custom_call_target="tpu_custom_call", output_to_operand_aliasing={{0}: (3, {}), {1}: (4, {})} | custom-call | flops 3019898880 | bytes 9633792 | tf_op jit(solution)/shard_map/weight_grad/pallas_call | solution.py:854
  386.4 7.9 %weight_grad.18 = (bf16[4,84,32,256]{3,2,1,0:T(8,128)(2,1)}, bf16[4,84,32,256]{3,2,1,0:T(8,128)(2,1)}) custom-call(s32[1]{0:T(128)} %bitcast.11.index_ref, bf16[640,3072]{1,0:T(8,128)(2,1)} %get-tuple-element.134.x_ref, bf16[640,768]{1,0:T(8,128)(2,1)} %get-tuple-element.135.g_ref, ...), custom_call_target="tpu_custom_call", output_to_operand_aliasing={{0}: (3, {}), {1}: (4, {})} | custom-call | flops 3019898880 | bytes 9633792 | tf_op jit(solution)/shard_map/weight_grad/pallas_call | solution.py:854
  394.4 3.8 weight_grad.19
  401.2 2.2 slice_bitcast_fusion.2
  404.0 31.8 %encoder_attention_back.1 = (bf16[640,2304]{1,0:T(8,128)(2,1)}, bf16[640,768]{1,0:T(8,128)(2,1)}, f32[8,4608]{1,0:T(8,128)}) custom-call(s32[177]{0:T(256)} %fusion.37.row_ref, s32[8]{0:T(128)} %len_ref.5, bf16[49280,256]{1,0:T(8,128)(2,1)} %all-gather.2.cloned.1.call-done.wg_ref, f32[1,21760]{1,0:T(1,128)} %reshape.138.vec_ref, ...), custom_call_target="tpu_custom_call" | custom-call | flops 3019898880 | bytes 8159232 | tf_op jit(solution)/shard_map/encoder_attention_back/pallas_call | solution.py:379
  437.8 2.5 seed_buffers.3
  443.6 7.1 add_convert_fusion
  461.5 6.9 weight_grad.20
  468.4 3.8 weight_grad.21
  473.5 24.5 %collective-permute-done.9 = bf16[30,32,256]{2,1,0:T(8,128)(2,1)S(1)} collective-permute-done((bf16[30,32,256]{2,1,0:T(8,128)(2,1)}, bf16[30,32,256]{2,1,0:T(8,128)(2,1)S(1)}, u32[]{:S(2)}, u32[]{:S(2)}) %collective-permute-start.9) | collective-permute-done | bytes 491552 | tf_op jit(solution)/shard_map/ppermute | solution.py:911
  499.4 3.6 collective-permute-start.13
  514.8 8.1 %collective-permute-done.12 = bf16[15,32,256]{2,1,0:T(8,128)(2,1)} collective-permute-done((bf16[15,32,256]{2,1,0:T(8,128)(2,1)S(1)}, bf16[15,32,256]{2,1,0:T(8,128)(2,1)}, u32[]{:S(2)}, u32[]{:S(2)}) %collective-permute-start.12) | collective-permute-done | bytes 245792 | tf_op jit(solution)/shard_map/ppermute | solution.py:944
  527.1 3.1 collective-permute-start.16
  533.3 3.0 add_convert_fusion.2
  539.4 3.3 collective-permute-done.15
  542.8 14.7 %collective-permute-start.22 = (bf16[21,32,256]{2,1,0:T(8,128)(2,1)S(1)}, bf16[21,32,256]{2,1,0:T(8,128)(2,1)S(1)}, u32[]{:S(2)}, u32[]{:S(2)}) collective-permute-start(bf16[21,32,256]{2,1,0:T(8,128)(2,1)S(1)} %get-tuple-element.193), channel_id=1, source_target_pairs={{0,2},{1,3},{2,0},{3,1},{4,6},{5,7},{6,4},{7,5},{8,10},{9,11},{10,... | collective-permute-start | bytes 1032200 | tf_op jit(solution)/shard_map/ppermute | solution.py:944
  557.5 5.0 collective-permute-start.21
  562.6 26.3 %collective-permute-done.22 = bf16[21,32,256]{2,1,0:T(8,128)(2,1)S(1)} collective-permute-done((bf16[21,32,256]{2,1,0:T(8,128)(2,1)S(1)}, bf16[21,32,256]{2,1,0:T(8,128)(2,1)S(1)}, u32[]{:S(2)}, u32[]{:S(2)}) %collective-permute-start.22) | collective-permute-done | bytes 344096 | tf_op jit(solution)/shard_map/ppermute | solution.py:944
  589.3 3.7 collective-permute-start.26
  598.6 2.1 collective-permute-done.31
  603.1 10.3 %collective-permute-start.33 = (bf16[10,32,256]{2,1,0:T(8,128)(2,1)S(1)}, bf16[10,32,256]{2,1,0:T(8,128)(2,1)S(1)}, u32[]{:S(2)}, u32[]{:S(2)}) collective-permute-start(bf16[10,32,256]{2,1,0:T(8,128)(2,1)S(1)} %get-tuple-element.199), channel_id=1, source_target_pairs={{0,2},{1,3},{2,0},{3,1},{4,6},{5,7},{6,4},{7,5},{8,10},{9,11},{10,... | collective-permute-start | bytes 491528 | tf_op jit(solution)/shard_map/ppermute | solution.py:944
  616.2 13.4 %collective-permute-done.33 = bf16[10,32,256]{2,1,0:T(8,128)(2,1)S(1)} collective-permute-done((bf16[10,32,256]{2,1,0:T(8,128)(2,1)S(1)}, bf16[10,32,256]{2,1,0:T(8,128)(2,1)S(1)}, u32[]{:S(2)}, u32[]{:S(2)}) %collective-permute-start.33) | collective-permute-done | bytes 163872 | tf_op jit(solution)/shard_map/ppermute | solution.py:944
  630.0 3.8 collective-permute-start.37
  633.7 3.4 collective-permute-done.35
  637.2 2.5 collective-permute-done.36
  639.7 2.7 gather_fusion.1
  642.4 4.6 all-to-all-start
  652.1 2.3 collective-permute-start
  657.2 3.3 collective-permute-done.1
  663.6 20.3 %collective-permute-done.3 = f32[2]{0:T(128)S(1)} collective-permute-done((f32[2]{0:T(128)S(1)}, f32[2]{0:T(128)S(1)}, u32[]{:S(2)}, u32[]{:S(2)}) %collective-permute-start.3) | collective-permute-done | bytes 40 | tf_op jit(solution)/shard_map/ppermute | solution.py:911
  685.3 2.1 collective-permute-done.4
  688.6 2.1 multiply_reduce_fusion
  697.5 2.8 collective-permute-start.40
  703.8 24.9 %tile_update.1 = (f32[24,256,256]{2,1,0:T(8,128)}, f32[24,256,256]{2,1,0:T(8,128)}, f32[24,256,256]{2,1,0:T(8,128)}, f32[24,256,256]{2,1,0:T(8,128)}) custom-call(f32[1]{0:T(128)} %bitcast.54.scale_ref, bf16[8,24,32,256]{3,2,1,0:T(8,128)(2,1)} %bitcast.57.grad_ref, f32[24,256,256]{2,1,0:T(8,128)} %w_ref.1, f32[24,256,256]{2,1,0:T(8,128)} %left_stat_ref.1, ...), custom_call_target="tpu_custom_call" | custom-call | tf_op jit(solution)/shard_map/tile_update/pallas_call | solution.py:1009
  (225 shorter events, 83.3 us)
Async XLA Ops:
  7.2 134.3 %all-gather.2.cloned.1.call-start = ((), (), s32[]{:S(2)}) async-start(), calls=%async_computation.1 | async-start | bytes 28385280 | tf_op jit(solution)/shard_map/all_gather | solution.py:1087
  350.8 21.4 %collective-permute-start.5 = (bf16[4,60,32,256]{3,2,1,0:T(8,128)(2,1)}, bf16[4,60,32,256]{3,2,1,0:T(8,128)(2,1)}, u32[]{:S(2)}, u32[]{:S(2)}) collective-permute-start(bf16[4,60,32,256]{3,2,1,0:T(8,128)(2,1)} %get-tuple-element.131), channel_id=1, source_target_pairs={{0,4},{4,0},{8,12},{12,8},{16,20},{20,16},{24,28},{28,24},{1,5},{5... | collective-permute-start | bytes 11796488 | tf_op jit(solution)/shard_map/ppermute | solution.py:911
  354.1 18.1 %copy-start = (bf16[4,60,32,256]{3,2,1,0:T(8,128)(2,1)S(1)}, bf16[4,60,32,256]{3,2,1,0:T(8,128)(2,1)}, u32[]{:S(2)}) copy-start(bf16[4,60,32,256]{3,2,1,0:T(8,128)(2,1)} %get-tuple-element.130) | copy-start | bytes 11796484
  398.2 45.4 %collective-permute-start.8 = (bf16[4,84,32,256]{3,2,1,0:T(8,128)(2,1)}, bf16[4,84,32,256]{3,2,1,0:T(8,128)(2,1)}, u32[]{:S(2)}, u32[]{:S(2)}) collective-permute-start(bf16[4,84,32,256]{3,2,1,0:T(8,128)(2,1)} %get-tuple-element.156), channel_id=1, source_target_pairs={{0,4},{4,0},{8,12},{12,8},{16,20},{20,16},{24,28},{28,24},{1,5},{5... | collective-permute-start | bytes 16515080 | tf_op jit(solution)/shard_map/ppermute | solution.py:911
  399.8 40.6 %collective-permute-start.6 = (bf16[2,30,32,256]{3,2,1,0:T(8,128)(2,1)}, bf16[2,30,32,256]{3,2,1,0:T(8,128)(2,1)}, u32[]{:S(2)}, u32[]{:S(2)}) collective-permute-start(bf16[2,30,32,256]{3,2,1,0:T(8,128)(2,1)} %slice_bitcast_fusion.3), channel_id=1, source_target_pairs={{0,8},{4,12},{8,0},{12,4},{16,24},{20,28},{24,16},{28,20},{1,9},{5... | collective-permute-start | bytes 2949128 | tf_op jit(solution)/shard_map/ppermute | solution.py:911
  403.5 38.6 %collective-permute-start.7 = (bf16[2,30,32,256]{3,2,1,0:T(8,128)(2,1)}, bf16[2,30,32,256]{3,2,1,0:T(8,128)(2,1)S(1)}, u32[]{:S(2)}, u32[]{:S(2)}) collective-permute-start(bf16[2,30,32,256]{3,2,1,0:T(8,128)(2,1)} %slice_bitcast_fusion.2), channel_id=1, source_target_pairs={{0,16},{4,20},{8,24},{12,28},{16,0},{20,4},{24,8},{28,12},{1,17},{... | collective-permute-start | bytes 2949128 | tf_op jit(solution)/shard_map/ppermute | solution.py:911
  454.2 17.9 %collective-permute-start.10 = (bf16[30,32,256]{2,1,0:T(8,128)(2,1)}, bf16[30,32,256]{2,1,0:T(8,128)(2,1)S(1)}, u32[]{:S(2)}, u32[]{:S(2)}) collective-permute-start(bf16[30,32,256]{2,1,0:T(8,128)(2,1)} %slice_bitcast_fusion.12), channel_id=1, source_target_pairs={{0,8},{4,12},{8,0},{12,4},{16,24},{20,28},{24,16},{28,20},{1,9},{5... | collective-permute-start | bytes 1474568 | tf_op jit(solution)/shard_map/ppermute | solution.py:911
  455.8 47.2 %collective-permute-start.19 = (bf16[2,42,32,256]{3,2,1,0:T(8,128)(2,1)}, bf16[2,42,32,256]{3,2,1,0:T(8,128)(2,1)}, u32[]{:S(2)}, u32[]{:S(2)}) collective-permute-start(bf16[2,42,32,256]{3,2,1,0:T(8,128)(2,1)} %slice_bitcast_fusion), channel_id=1, source_target_pairs={{0,16},{4,20},{8,24},{12,28},{16,0},{20,4},{24,8},{28,12},{1,17},{... | collective-permute-start | bytes 4128776 | tf_op jit(solution)/shard_map/ppermute | solution.py:911
  458.3 39.7 %collective-permute-start.9 = (bf16[30,32,256]{2,1,0:T(8,128)(2,1)}, bf16[30,32,256]{2,1,0:T(8,128)(2,1)S(1)}, u32[]{:S(2)}, u32[]{:S(2)}) collective-permute-start(bf16[30,32,256]{2,1,0:T(8,128)(2,1)} %slice_bitcast_fusion.13), channel_id=1, source_target_pairs={{0,16},{4,20},{8,24},{12,28},{16,0},{20,4},{24,8},{28,12},{1,17},{... | collective-permute-start | bytes 1474568 | tf_op jit(solution)/shard_map/ppermute | solution.py:911
  459.8 47.2 %collective-permute-start.17 = (bf16[2,42,32,256]{3,2,1,0:T(8,128)(2,1)}, bf16[2,42,32,256]{3,2,1,0:T(8,128)(2,1)}, u32[]{:S(2)}, u32[]{:S(2)}) collective-permute-start(bf16[2,42,32,256]{3,2,1,0:T(8,128)(2,1)} %slice_bitcast_fusion.1), channel_id=1, source_target_pairs={{0,8},{4,12},{8,0},{12,4},{16,24},{20,28},{24,16},{28,20},{1,9},{5... | collective-permute-start | bytes 4128776 | tf_op jit(solution)/shard_map/ppermute | solution.py:911
  472.1 31.9 %copy-start.3 = (bf16[2,2,42,32,256]{4,3,2,1,0:T(8,128)(2,1)S(1)}, bf16[2,2,42,32,256]{4,3,2,1,0:T(8,128)(2,1)}, u32[]{:S(2)}) copy-start(bf16[2,2,42,32,256]{4,3,2,1,0:T(8,128)(2,1)} %copy-done.2) | copy-start | bytes 8257540
  472.1 61.1 %collective-permute-start.27 = (bf16[4,40,32,256]{3,2,1,0:T(8,128)(2,1)}, bf16[4,40,32,256]{3,2,1,0:T(8,128)(2,1)}, u32[]{:S(2)}, u32[]{:S(2)}) collective-permute-start(bf16[4,40,32,256]{3,2,1,0:T(8,128)(2,1)} %get-tuple-element.171), channel_id=1, source_target_pairs={{0,4},{4,0},{8,12},{12,8},{16,20},{20,16},{24,28},{28,24},{1,5},{5... | collective-permute-start | bytes 7864328 | tf_op jit(solution)/shard_map/ppermute | solution.py:911
  499.4 12.0 %collective-permute-start.13 = (bf16[15,32,256]{2,1,0:T(8,128)(2,1)S(1)}, bf16[15,32,256]{2,1,0:T(8,128)(2,1)S(1)}, u32[]{:S(2)}, u32[]{:S(2)}) collective-permute-start(bf16[15,32,256]{2,1,0:T(8,128)(2,1)S(1)} %get-tuple-element.195), channel_id=1, source_target_pairs={{0,3},{1,0},{2,1},{3,2},{4,7},{5,4},{6,5},{7,6},{8,11},{9,8},{10,9... | collective-permute-start | bytes 737288 | tf_op jit(solution)/shard_map/ppermute | solution.py:944
  502.9 19.9 %collective-permute-start.12 = (bf16[15,32,256]{2,1,0:T(8,128)(2,1)S(1)}, bf16[15,32,256]{2,1,0:T(8,128)(2,1)}, u32[]{:S(2)}, u32[]{:S(2)}) collective-permute-start(bf16[15,32,256]{2,1,0:T(8,128)(2,1)S(1)} %get-tuple-element.196), channel_id=1, source_target_pairs={{0,2},{1,3},{2,0},{3,1},{4,6},{5,7},{6,4},{7,5},{8,10},{9,11},{10,... | collective-permute-start | bytes 737288 | tf_op jit(solution)/shard_map/ppermute | solution.py:944
  502.9 19.9 %collective-permute-start.11 = (bf16[15,32,256]{2,1,0:T(8,128)(2,1)S(1)}, bf16[15,32,256]{2,1,0:T(8,128)(2,1)}, u32[]{:S(2)}, u32[]{:S(2)}) collective-permute-start(bf16[15,32,256]{2,1,0:T(8,128)(2,1)S(1)} %get-tuple-element.194), channel_id=1, source_target_pairs={{0,1},{1,2},{2,3},{3,0},{4,5},{5,6},{6,7},{7,4},{8,9},{9,10},{10,1... | collective-permute-start | bytes 737288 | tf_op jit(solution)/shard_map/ppermute | solution.py:944
  507.0 20.1 %collective-permute-start.20 = (bf16[42,32,256]{2,1,0:T(8,128)(2,1)}, bf16[42,32,256]{2,1,0:T(8,128)(2,1)}, u32[]{:S(2)}, u32[]{:S(2)}) collective-permute-start(bf16[42,32,256]{2,1,0:T(8,128)(2,1)} %slice_bitcast_fusion.4), channel_id=1, source_target_pairs={{0,8},{4,12},{8,0},{12,4},{16,24},{20,28},{24,16},{28,20},{1,9},{5... | collective-permute-start | bytes 2064392 | tf_op jit(solution)/shard_map/ppermute | solution.py:911
  511.7 20.1 %collective-permute-start.18 = (bf16[42,32,256]{2,1,0:T(8,128)(2,1)}, bf16[42,32,256]{2,1,0:T(8,128)(2,1)}, u32[]{:S(2)}, u32[]{:S(2)}) collective-permute-start(bf16[42,32,256]{2,1,0:T(8,128)(2,1)} %slice_bitcast_fusion.6), channel_id=1, source_target_pairs={{0,16},{4,20},{8,24},{12,28},{16,0},{20,4},{24,8},{28,12},{1,17},{... | collective-permute-start | bytes 2064392 | tf_op jit(solution)/shard_map/ppermute | solution.py:911
  524.2 15.1 %collective-permute-start.14 = (bf16[15,32,256]{2,1,0:T(8,128)(2,1)S(1)}, bf16[15,32,256]{2,1,0:T(8,128)(2,1)S(1)}, u32[]{:S(2)}, u32[]{:S(2)}) collective-permute-start(bf16[15,32,256]{2,1,0:T(8,128)(2,1)S(1)} %get-tuple-element.184), channel_id=1, source_target_pairs={{0,1},{1,2},{2,3},{3,0},{4,5},{5,6},{6,7},{7,4},{8,9},{9,10},{10,1... | collective-permute-start | bytes 737288 | tf_op jit(solution)/shard_map/ppermute | solution.py:944
  525.1 17.7 %collective-permute-start.15 = (bf16[15,32,256]{2,1,0:T(8,128)(2,1)S(1)}, bf16[15,32,256]{2,1,0:T(8,128)(2,1)S(1)}, u32[]{:S(2)}, u32[]{:S(2)}) collective-permute-start(bf16[15,32,256]{2,1,0:T(8,128)(2,1)S(1)} %get-tuple-element.184), channel_id=1, source_target_pairs={{0,2},{1,3},{2,0},{3,1},{4,6},{5,7},{6,4},{7,5},{8,10},{9,11},{10,... | collective-permute-start | bytes 737288 | tf_op jit(solution)/shard_map/ppermute | solution.py:944
  527.1 30.4 %collective-permute-start.16 = (bf16[15,32,256]{2,1,0:T(8,128)(2,1)S(1)}, bf16[15,32,256]{2,1,0:T(8,128)(2,1)S(1)}, u32[]{:S(2)}, u32[]{:S(2)}) collective-permute-start(bf16[15,32,256]{2,1,0:T(8,128)(2,1)S(1)} %get-tuple-element.184), channel_id=1, source_target_pairs={{0,3},{1,0},{2,1},{3,2},{4,7},{5,4},{6,5},{7,6},{8,11},{9,8},{10,9... | collective-permute-start | bytes 737288 | tf_op jit(solution)/shard_map/ppermute | solution.py:944
  536.4 56.6 %collective-permute-start.28 = (bf16[2,20,32,256]{3,2,1,0:T(8,128)(2,1)S(1)}, bf16[2,20,32,256]{3,2,1,0:T(8,128)(2,1)S(1)}, u32[]{:S(2)}, u32[]{:S(2)}) collective-permute-start(bf16[2,20,32,256]{3,2,1,0:T(8,128)(2,1)S(1)} %slice_bitcast_fusion.10), channel_id=1, source_target_pairs={{0,8},{4,12},{8,0},{12,4},{16,24},{20,28},{24,16},{28,20},{1,9},{5... | collective-permute-start | bytes 1966088 | tf_op jit(solution)/shard_map/ppermute | solution.py:911
  537.8 55.2 %collective-permute-start.30 = (bf16[2,20,32,256]{3,2,1,0:T(8,128)(2,1)S(1)}, bf16[2,20,32,256]{3,2,1,0:T(8,128)(2,1)S(1)}, u32[]{:S(2)}, u32[]{:S(2)}) collective-permute-start(bf16[2,20,32,256]{3,2,1,0:T(8,128)(2,1)S(1)} %slice_bitcast_fusion.8), channel_id=1, source_target_pairs={{0,16},{4,20},{8,24},{12,28},{16,0},{20,4},{24,8},{28,12},{1,17},{... | collective-permute-start | bytes 1966088 | tf_op jit(solution)/shard_map/ppermute | solution.py:911
  539.3 23.2 %collective-permute-start.23 = (bf16[21,32,256]{2,1,0:T(8,128)(2,1)S(1)}, bf16[21,32,256]{2,1,0:T(8,128)(2,1)S(1)}, u32[]{:S(2)}, u32[]{:S(2)}) collective-permute-start(bf16[21,32,256]{2,1,0:T(8,128)(2,1)S(1)} %get-tuple-element.192), channel_id=1, source_target_pairs={{0,3},{1,0},{2,1},{3,2},{4,7},{5,4},{6,5},{7,6},{8,11},{9,8},{10,9... | collective-permute-start | bytes 1032200 | tf_op jit(solution)/shard_map/ppermute | solution.py:944
  542.8 46.1 %collective-permute-start.22 = (bf16[21,32,256]{2,1,0:T(8,128)(2,1)S(1)}, bf16[21,32,256]{2,1,0:T(8,128)(2,1)S(1)}, u32[]{:S(2)}, u32[]{:S(2)}) collective-permute-start(bf16[21,32,256]{2,1,0:T(8,128)(2,1)S(1)} %get-tuple-element.193), channel_id=1, source_target_pairs={{0,2},{1,3},{2,0},{3,1},{4,6},{5,7},{6,4},{7,5},{8,10},{9,11},{10,... | collective-permute-start | bytes 1032200 | tf_op jit(solution)/shard_map/ppermute | solution.py:944
  557.5 31.4 %collective-permute-start.21 = (bf16[21,32,256]{2,1,0:T(8,128)(2,1)S(1)}, bf16[21,32,256]{2,1,0:T(8,128)(2,1)S(1)}, u32[]{:S(2)}, u32[]{:S(2)}) collective-permute-start(bf16[21,32,256]{2,1,0:T(8,128)(2,1)S(1)} %get-tuple-element.191), channel_id=1, source_target_pairs={{0,1},{1,2},{2,3},{3,0},{4,5},{5,6},{6,7},{7,4},{8,9},{9,10},{10,1... | collective-permute-start | bytes 1032200 | tf_op jit(solution)/shard_map/ppermute | solution.py:944
  589.1 9.5 %collective-permute-start.24 = (bf16[21,32,256]{2,1,0:T(8,128)(2,1)S(1)}, bf16[21,32,256]{2,1,0:T(8,128)(2,1)S(1)}, u32[]{:S(2)}, u32[]{:S(2)}) collective-permute-start(bf16[21,32,256]{2,1,0:T(8,128)(2,1)S(1)} %get-tuple-element.182), channel_id=1, source_target_pairs={{0,1},{1,2},{2,3},{3,0},{4,5},{5,6},{6,7},{7,4},{8,9},{9,10},{10,1... | collective-permute-start | bytes 1032200 | tf_op jit(solution)/shard_map/ppermute | solution.py:944
  589.2 26.2 %collective-permute-start.25 = (bf16[21,32,256]{2,1,0:T(8,128)(2,1)S(1)}, bf16[21,32,256]{2,1,0:T(8,128)(2,1)S(1)}, u32[]{:S(2)}, u32[]{:S(2)}) collective-permute-start(bf16[21,32,256]{2,1,0:T(8,128)(2,1)S(1)} %get-tuple-element.182), channel_id=1, source_target_pairs={{0,2},{1,3},{2,0},{3,1},{4,6},{5,7},{6,4},{7,5},{8,10},{9,11},{10,... | collective-permute-start | bytes 1032200 | tf_op jit(solution)/shard_map/ppermute | solution.py:944
  589.3 26.1 %collective-permute-start.26 = (bf16[21,32,256]{2,1,0:T(8,128)(2,1)S(1)}, bf16[21,32,256]{2,1,0:T(8,128)(2,1)S(1)}, u32[]{:S(2)}, u32[]{:S(2)}) collective-permute-start(bf16[21,32,256]{2,1,0:T(8,128)(2,1)S(1)} %get-tuple-element.182), channel_id=1, source_target_pairs={{0,3},{1,0},{2,1},{3,2},{4,7},{5,4},{6,5},{7,6},{8,11},{9,8},{10,9... | collective-permute-start | bytes 1032200 | tf_op jit(solution)/shard_map/ppermute | solution.py:944
  593.6 7.1 collective-permute-start.31
  595.1 7.1 collective-permute-start.29
  602.4 13.8 %collective-permute-start.34 = (bf16[10,32,256]{2,1,0:T(8,128)(2,1)S(1)}, bf16[10,32,256]{2,1,0:T(8,128)(2,1)S(1)}, u32[]{:S(2)}, u32[]{:S(2)}) collective-permute-start(bf16[10,32,256]{2,1,0:T(8,128)(2,1)S(1)} %get-tuple-element.198), channel_id=1, source_target_pairs={{0,3},{1,0},{2,1},{3,2},{4,7},{5,4},{6,5},{7,6},{8,11},{9,8},{10,9... | collective-permute-start | bytes 491528 | tf_op jit(solution)/shard_map/ppermute | solution.py:944
  603.1 26.5 %collective-permute-start.33 = (bf16[10,32,256]{2,1,0:T(8,128)(2,1)S(1)}, bf16[10,32,256]{2,1,0:T(8,128)(2,1)S(1)}, u32[]{:S(2)}, u32[]{:S(2)}) collective-permute-start(bf16[10,32,256]{2,1,0:T(8,128)(2,1)S(1)} %get-tuple-element.199), channel_id=1, source_target_pairs={{0,2},{1,3},{2,0},{3,1},{4,6},{5,7},{6,4},{7,5},{8,10},{9,11},{10,... | collective-permute-start | bytes 491528 | tf_op jit(solution)/shard_map/ppermute | solution.py:944
  613.4 16.2 %collective-permute-start.32 = (bf16[10,32,256]{2,1,0:T(8,128)(2,1)S(1)}, bf16[10,32,256]{2,1,0:T(8,128)(2,1)S(1)}, u32[]{:S(2)}, u32[]{:S(2)}) collective-permute-start(bf16[10,32,256]{2,1,0:T(8,128)(2,1)S(1)} %get-tuple-element.197), channel_id=1, source_target_pairs={{0,1},{1,2},{2,3},{3,0},{4,5},{5,6},{6,7},{7,4},{8,9},{9,10},{10,1... | collective-permute-start | bytes 491528 | tf_op jit(solution)/shard_map/ppermute | solution.py:944
  629.8 7.4 %collective-permute-start.35 = (bf16[10,32,256]{2,1,0:T(8,128)(2,1)S(1)}, bf16[10,32,256]{2,1,0:T(8,128)(2,1)S(1)}, u32[]{:S(2)}, u32[]{:S(2)}) collective-permute-start(bf16[10,32,256]{2,1,0:T(8,128)(2,1)S(1)} %get-tuple-element.180), channel_id=1, source_target_pairs={{0,1},{1,2},{2,3},{3,0},{4,5},{5,6},{6,7},{7,4},{8,9},{9,10},{10,1... | collective-permute-start | bytes 491528 | tf_op jit(solution)/shard_map/ppermute | solution.py:944
  629.9 9.8 %collective-permute-start.36 = (bf16[10,32,256]{2,1,0:T(8,128)(2,1)S(1)}, bf16[10,32,256]{2,1,0:T(8,128)(2,1)S(1)}, u32[]{:S(2)}, u32[]{:S(2)}) collective-permute-start(bf16[10,32,256]{2,1,0:T(8,128)(2,1)S(1)} %get-tuple-element.180), channel_id=1, source_target_pairs={{0,2},{1,3},{2,0},{3,1},{4,6},{5,7},{6,4},{7,5},{8,10},{9,11},{10,... | collective-permute-start | bytes 491528 | tf_op jit(solution)/shard_map/ppermute | solution.py:944
  630.0 9.7 %collective-permute-start.37 = (bf16[10,32,256]{2,1,0:T(8,128)(2,1)S(1)}, bf16[10,32,256]{2,1,0:T(8,128)(2,1)S(1)}, u32[]{:S(2)}, u32[]{:S(2)}) collective-permute-start(bf16[10,32,256]{2,1,0:T(8,128)(2,1)S(1)} %get-tuple-element.180), channel_id=1, source_target_pairs={{0,3},{1,0},{2,1},{3,2},{4,7},{5,4},{6,5},{7,6},{8,11},{9,8},{10,9... | collective-permute-start | bytes 491528 | tf_op jit(solution)/shard_map/ppermute | solution.py:944
  642.4 61.4 %all-to-all-start = ((bf16[192,32,256]{2,1,0:T(8,128)(2,1)}), bf16[192,32,256]{2,1,0:T(8,128)(2,1)}, u32[]{:S(2)}, u32[]{:S(2)}) async-start(bf16[192,32,256]{2,1,0:T(8,128)(2,1)} %gather_fusion.1), calls=%async_computation | async-start | bytes 6291456 | tf_op jit(solution)/shard_map/all_to_all | solution.py:1196
  647.0 56.2 %copy-start.14 = (f32[2560]{0:T(1024)S(1)}, f32[2560]{0:T(1024)}, u32[]{:S(2)}) copy-start(f32[2560]{0:T(1024)} %param.23) | copy-start | bytes 30724
  647.0 56.2 %copy-start.15 = (f32[2560]{0:T(1024)S(1)}, f32[2560]{0:T(1024)}, u32[]{:S(2)}) copy-start(f32[2560]{0:T(1024)} %param.25) | copy-start | bytes 30724
  647.0 56.2 %copy-start.16 = (f32[2560]{0:T(1024)S(1)}, f32[2560]{0:T(1024)}, u32[]{:S(2)}) copy-start(f32[2560]{0:T(1024)} %param.24) | copy-start | bytes 30724
  652.1 3.8 collective-permute-start
  656.0 4.4 collective-permute-start.1
  660.6 1.1 collective-permute-start.2
  661.7 22.1 %collective-permute-start.3 = (f32[2]{0:T(128)S(1)}, f32[2]{0:T(128)S(1)}, u32[]{:S(2)}, u32[]{:S(2)}) collective-permute-start(f32[2]{0:T(128)S(1)} %add.257), channel_id=1, source_target_pairs={{0,8},{4,12},{8,0},{12,4},{16,24},{20,28},{24,16},{28,20},{1,9},{5... | collective-permute-start | bytes 32 | tf_op jit(solution)/shard_map/ppermute | solution.py:911
  683.8 3.5 collective-permute-start.4
  690.8 1.2 collective-permute-start.38
  693.3 3.6 collective-permute-start.39
  697.5 3.6 collective-permute-start.40
  (24 other events, 121.2 us)
Sparse Core Ops, SparseCore 0:
  13.2 128.2 all-gather.1

commit v3 on v2

--- a/solution.py
+++ b/solution.py
@@ -490,18 +490,19 @@
     )
 
 
-DS = layer_offsets(0, E, FD)
-DS_NORM = 9 * E + FD
-DS_HEAD = DS_NORM + 2 * E
-DS_MASK = DS_HEAD + PIX
-DS_LOSS = DS_MASK + E
-DS_ALL = DS_LOSS + PIX
+DM_BO, DM_G2, DM_S2, DM_BU, DM_BD = 0, E, 2 * E, 3 * E, 3 * E + FD
+DM_NORM = 4 * E + FD
+DM_HEAD = DM_NORM + 2 * E
+DM_LOSS = DM_HEAD + PIX
+DM_ALL = DM_LOSS + PIX
+DA_QKV, DA_G1, DA_S1, DA_MASK, DA_ALL = 0, 3 * E, 4 * E, 5 * E, 6 * E
+CHUNK = 16
 
 
 def decoder_kernel(
     row_ref, len_ref, wg_ref, vec_ref, latent_ref, pos_ref, pix_ref,
-    h1_ref, dqkv_ref, att_ref, gproj_ref, h2_ref, du_ref, act_ref, gdown_ref, hn_ref, gpred_ref, glat_ref, sum_ref,
-    w_qkv, w_out, w_up, w_down, w_head, x0, qkv, lse, mid, slope, x1, pred, dy, grad, datt, sems,
+    x0, h1_ref, qkv, lse, att_ref, gproj_ref, grad, h2_ref, du_ref, act_ref, gdown_ref, hn_ref, gpred_ref, sum_ref,
+    w_qkv, w_out, w_up, w_down, w_head, mid, slope, x1, pred, dy, sems,
 ):
     step = pl.program_id(0)
     images = lse.shape[0]
@@ -523,24 +524,23 @@
     def length(image):
         return len_ref[step * images + image]
 
-    chunk = 16
-    order = lax.broadcasted_iota(jnp.int32, (chunk, 1), 0)
+    order = lax.broadcasted_iota(jnp.int32, (CHUNK, 1), 0)
     token = vec(V_MASK)
 
     def place(image, c):
         def head_rows(i, c):
-            at = pl.ds(pl.multiple_of(image * SD + i * chunk, chunk), chunk)
-            got = latent_ref[pl.ds(pl.multiple_of(image * VMAX + i * chunk, chunk), chunk), :]
-            x0[at, :] = jnp.where(i * chunk + order < length(image), got, token) + pos_ref[at, :]
+            at = pl.ds(pl.multiple_of(image * SD + i * CHUNK, CHUNK), CHUNK)
+            got = latent_ref[pl.ds(pl.multiple_of(image * VMAX + i * CHUNK, CHUNK), CHUNK), :]
+            x0[at, :] = jnp.where(i * CHUNK + order < length(image), got, token) + pos_ref[at, :]
             return c
 
         def tail_rows(i, c):
-            at = pl.ds(pl.multiple_of(image * SD + i * chunk, chunk), chunk)
+            at = pl.ds(pl.multiple_of(image * SD + i * CHUNK, CHUNK), CHUNK)
             x0[at, :] = token + pos_ref[at, :]
             return c
 
-        loop(0, VMAX // chunk, head_rows, 0)
-        loop(VMAX // chunk, SD // chunk, tail_rows, 0)
+        loop(0, VMAX // CHUNK, head_rows, 0)
+        loop(VMAX // CHUNK, SD // CHUNK, tail_rows, 0)
         return c
 
     lax.fori_loop(0, images, place, 0)
@@ -572,66 +572,33 @@
     def errors(image, c):
         def one(i, c):
             loss, bias = c
-            at = pl.ds(pl.multiple_of(image * SD + i * chunk, chunk), chunk)
+            at = pl.ds(pl.multiple_of(image * SD + i * CHUNK, CHUNK), CHUNK)
             target, _ = norm_parts(pix_ref[at, :].astype(F32))
-            place_in = i * chunk + order
+            place_in = i * CHUNK + order
             masked = (place_in >= length(image)) & (place_in < POS)
             residual = jnp.where(masked, pred[at, :] - target, 0.0)
             low = (residual * (2.0 / PIX)).astype(BF)
             gpred_ref[at, :] = low
             return (loss + fold8(residual * residual), bias + fold8(low.astype(F32)))
 
-        return loop(0, SD // chunk, one, c)
+        return loop(0, SD // CHUNK, one, c)
 
     zero = jnp.zeros((8, PIX), F32)
     loss, bias = lax.fori_loop(0, images, errors, (zero, zero))
-    add_sum(sum_ref, DS_LOSS, loss)
-    add_sum(sum_ref, DS_HEAD, bias)
+    add_sum(sum_ref, DM_LOSS, loss)
+    add_sum(sum_ref, DM_HEAD, bias)
 
     back_linear(gpred_ref, w_head, dy)
     d_gain, d_shift = norm_backward(x1, dy, vec(V_DNORM), grad, False)
-    add_sum(sum_ref, DS_NORM, d_gain)
-    add_sum(sum_ref, DS_NORM + E, d_shift)
-    round_and_sum(grad, gdown_ref, sum_ref, DS["bd"])
-    back_up(gdown_ref, w_down, slope, du_ref, sum_ref, DS["bu"])
+    add_sum(sum_ref, DM_NORM, d_gain)
+    add_sum(sum_ref, DM_NORM + E, d_shift)
+    round_and_sum(grad, gdown_ref, sum_ref, DM_BD)
+    back_up(gdown_ref, w_down, slope, du_ref, sum_ref, DM_BU)
     back_linear(du_ref, w_up, dy)
     d_gain, d_shift = norm_backward(mid, dy, vec(DEC["g2"]), grad, True)
-    add_sum(sum_ref, DS["g2"], d_gain)
-    add_sum(sum_ref, DS["s2"], d_shift)
-    round_and_sum(grad, gproj_ref, sum_ref, DS["bo"])
-
-    def back_out(j, cols):
-        datt[:, cols] = mm_nt(gproj_ref[...], w_out[cols, :]).astype(BF)
-
-    col_loop(E // BS, back_out)
-
-    def attend_back(image, c):
-        attention_backward(qkv, datt, lse, dqkv_ref, image, SD, E, E // HD, valid)
-        return c
-
-    lax.fori_loop(0, images, attend_back, 0)
-    sum_rows(dqkv_ref, sum_ref, DS["bqkv"])
-    back_linear(dqkv_ref, w_qkv, dy)
-    d_gain, d_shift = norm_backward(x0, dy, vec(DEC["g1"]), grad, True)
-    add_sum(sum_ref, DS["g1"], d_gain)
-    add_sum(sum_ref, DS["s1"], d_shift)
-
-    def unplace(image, c):
-        def head_rows(i, c):
-            got = grad[pl.ds(pl.multiple_of(image * SD + i * chunk, chunk), chunk), :]
-            seen = i * chunk + order < length(image)
-            at = pl.ds(pl.multiple_of(image * VMAX + i * chunk, chunk), chunk)
-            glat_ref[at, :] = jnp.where(seen, got, 0.0).astype(BF)
-            return c + fold8(jnp.where(seen, 0.0, got))
-
-        def tail_rows(i, c):
-            got = grad[pl.ds(pl.multiple_of(image * SD + i * chunk, chunk), chunk), :]
-            return c + fold8(jnp.where(i * chunk + order < POS, got, 0.0))
-
-        c = loop(0, VMAX // chunk, head_rows, c)
-        return loop(VMAX // chunk, SD // chunk, tail_rows, c)
-
-    add_sum(sum_ref, DS_MASK, lax.fori_loop(0, images, unplace, jnp.zeros((8, E), F32)))
+    add_sum(sum_ref, DM_G2, d_gain)
+    add_sum(sum_ref, DM_S2, d_shift)
+    round_and_sum(grad, gproj_ref, sum_ref, DM_BO)
 
 
 def decoder(tile_rows, vis_len, gathered, vector, latent, pos_e, ordered, steps):
@@ -639,31 +606,28 @@
     rows = images * SD
     part = rows // steps
     outs = [
+        ((rows, E), F32, "rows"),
         ((rows, E), BF, "rows"),
         ((rows, 3 * E), BF, "rows"),
+        ((images, E // BS, BS * HD // E, SD), F32, "rows"),
         ((rows, E), BF, "rows"),
         ((rows, E), BF, "rows"),
+        ((rows, E), F32, "rows"),
         ((rows, E), BF, "rows"),
         ((rows, FD), BF, "rows"),
         ((rows, FD), BF, "rows"),
         ((rows, E), BF, "rows"),
         ((rows, E), BF, "rows"),
         ((rows, PIX), BF, "rows"),
-        ((images * VMAX, E), BF, "rows"),
-        ((8, DS_ALL), F32, "whole"),
+        ((8, DM_ALL), F32, "whole"),
     ]
     scratch = [pltpu.VMEM(s, BF) for s in [(E, 3 * E), (E, E), (E, FD), (FD, E), (E, PIX)]]
     scratch += [
-        pltpu.VMEM((part, E), F32),
-        pltpu.VMEM((part, 3 * E), BF),
-        pltpu.VMEM((images // steps, E // BS, BS * HD // E, SD), F32),
         pltpu.VMEM((part, E), F32),
         pltpu.VMEM((part, FD), BF),
         pltpu.VMEM((part, E), F32),
         pltpu.VMEM((part, PIX), F32),
         pltpu.VMEM((part, E), F32),
-        pltpu.VMEM((part, E), F32),
-        pltpu.VMEM((part, E), BF),
         pltpu.SemaphoreType.DMA((5,)),
     ]
     return group_call(
@@ -680,7 +644,94 @@
         outs,
         scratch,
         "decoder",
-        4 * rows * (4 * E * E + 2 * E * FD + E * PIX),
+        2 * rows * (4 * E * E + 4 * E * FD + 2 * E * PIX),
+    )
+
+
+def decoder_attention_back_kernel(
+    row_ref, len_ref, wg_ref, vec_ref, gproj_ref, grad_in_ref, qkv_ref, lse_ref, x0_ref,
+    dqkv_ref, glat_ref, sum_ref,
+    w_out, w_qkv, dy, grad, datt, sems,
+):
+    step = pl.program_id(0)
+    images = lse_ref.shape[0]
+    ready = fetch_all(step == 0, row_ref, wg_ref, sems, [(T_DOUT, w_out), (T_DQKV, w_qkv)])
+
+    @pl.when(step == 0)
+    def _():
+        sum_ref[...] = jnp.zeros_like(sum_ref)
+
+    valid = lax.broadcasted_iota(jnp.int32, (SD, 1), 0) < POS
+    order = lax.broadcasted_iota(jnp.int32, (CHUNK, 1), 0)
+    ready(0)
+
+    def back_out(j, cols):
+        datt[:, cols] = mm_nt(gproj_ref[...], w_out[cols, :]).astype(BF)
+
+    col_loop(E // BS, back_out)
+
+    def attend_back(image, c):
+        attention_backward(qkv_ref, datt, lse_ref, dqkv_ref, image, SD, E, E // HD, valid)
+        return c
+
+    lax.fori_loop(0, images, attend_back, 0)
+    sum_rows(dqkv_ref, sum_ref, DA_QKV)
+    ready(1)
+    back_linear(dqkv_ref, w_qkv, dy)
+    grad[...] = grad_in_ref[...]
+    gain = vec_ref[:, DEC["g1"] : DEC["g1"] + E]
+    d_gain, d_shift = norm_backward(x0_ref, dy, gain, grad, True)
+    add_sum(sum_ref, DA_G1, d_gain)
+    add_sum(sum_ref, DA_S1, d_shift)
+
+    def unplace(image, c):
+        length = len_ref[step * images + image]
+
+        def head_rows(i, c):
+            got = grad[pl.ds(pl.multiple_of(image * SD + i * CHUNK, CHUNK), CHUNK), :]
+            seen = i * CHUNK + order < length
+            at = pl.ds(pl.multiple_of(image * VMAX + i * CHUNK, CHUNK), CHUNK)
+            glat_ref[at, :] = jnp.where(seen, got, 0.0).astype(BF)
+            return c + fold8(jnp.where(seen, 0.0, got))
+
+        def tail_rows(i, c):
+            got = grad[pl.ds(pl.multiple_of(image * SD + i * CHUNK, CHUNK), CHUNK), :]
+            return c + fold8(jnp.where(i * CHUNK + order < POS, got, 0.0))
+
+        c = loop(0, VMAX // CHUNK, head_rows, c)
+        return loop(VMAX // CHUNK, SD // CHUNK, tail_rows, c)
+
+    add_sum(sum_ref, DA_MASK, lax.fori_loop(0, images, unplace, jnp.zeros((8, E), F32)))
+
+
+def decoder_attention_back(tile_rows, vis_len, gathered, vector, gproj, grad, qkv, lse, x0, steps):
+    images = vis_len.shape[0]
+    rows = x0.shape[0]
+    part = rows // steps
+    outs = [
+        ((rows, 3 * E), BF, "rows"),
+        ((images * VMAX, E), BF, "rows"),
+        ((8, DA_ALL), F32, "whole"),
+    ]
+    scratch = [pltpu.VMEM(s, BF) for s in [(E, E), (E, 3 * E)]]
+    scratch += [pltpu.VMEM((part, E), F32), pltpu.VMEM((part, E), F32), pltpu.VMEM((part, E), BF)]
+    return group_call(
+        decoder_attention_back_kernel,
+        steps,
+        (tile_rows, vis_len),
+        [
+            (gathered, "any"),
+            (vector, "whole"),
+            (gproj, "rows"),
+            (grad, "rows"),
+            (qkv, "rows"),
+            (lse, "rows"),
+            (x0, "rows"),
+        ],
+        outs,
+        scratch + [pltpu.SemaphoreType.DMA((2,))],
+        "decoder_attention_back",
+        2 * rows * 4 * E * E,
     )
 
 
@@ -880,23 +931,27 @@
 
 
 def seed_kernel(parts, index_ref, vec_ref, *outs):
-    at = pl.program_id(0)
+    first = pl.program_id(0) == 0
     for p in range(parts):
         got = vec_ref[p ^ index_ref[0]]
-        outs[p % 2][p // 2, 0] = jnp.where(at == 0, got, 0.0).astype(BF)
+        out = outs[p % 2]
+        for t in range(out.shape[1]):
+            out[p // 2, t] = (jnp.where(first, got, 0.0) if t == 0 else jnp.zeros_like(got)).astype(BF)
 
 
 def seed_buffers(index, parts, count, first, vector_tile):
     cut = BS // parts
     held = min(parts, 2)
+    size = math.gcd(first, count - first)
     shape = jax.ShapeDtypeStruct((parts // held, count, cut, BS), BF)
+    block = (parts // held, size, cut, BS)
     return pl.pallas_call(
         functools.partial(seed_kernel, parts),
         grid_spec=pltpu.PrefetchScalarGridSpec(
             num_scalar_prefetch=1,
-            grid=(count - first,),
+            grid=((count - first) // size,),
             in_specs=[pl.BlockSpec(vector_tile.shape, lambda i, *_: (0, 0, 0))],
-            out_specs=[pl.BlockSpec((parts // held, 1, cut, BS), lambda i, *_: (0, first + i, 0, 0))] * held,
+            out_specs=[pl.BlockSpec(block, lambda i, *_: (0, first // size + i, 0, 0))] * held,
         ),
         out_shape=[shape] * held,
         name="seed_buffers",
@@ -934,17 +989,16 @@
     return halves, left
 
 
-def reduce_end(state, parts, groups):
+def reduce_join(state, parts):
     halves, _ = reduce_chips(state, parts, 99)
-    whole = jnp.concatenate(halves, axis=0) if parts > 1 else halves[0]
-    return reduce_patch(whole, groups)
+    return jnp.concatenate(halves, axis=0) if parts > 1 else halves[0]
 
 
 def shift_patch(x, shift, size):
     return lax.ppermute(x, "patch", [(i, (i + shift) % size) for i in range(size)])
 
 
-def reduce_patch(x, groups):
+def scatter_patch(x, groups):
     if groups == 1:
         return x
     me = lax.axis_index("patch")
@@ -953,7 +1007,10 @@
     for k in range(1, groups):
         piece = lax.dynamic_index_in_dim(pieces, (me + k) % groups, 0, keepdims=False)
         total = total + shift_patch(piece, k, groups).astype(F32)
-    total = total.astype(BF)
+    return total.astype(BF)
+
+
+def gather_patch(total, groups):
     return jnp.concatenate([total] + [shift_patch(total, k, groups) for k in range(1, groups)], axis=0)
 
 
@@ -1030,15 +1087,10 @@
 
 
 CHUNKS = [
-    [
-        (T_DUP, 2, 8, (2, 4)),
-        (T_DDOWN, 8, 2, (4, 2)),
-        (T_DOUT, 2, 2, (2, 2)),
-        (T_DQKV, 2, 6, (2, 3)),
-        (T_HEAD, 2, 3, (2, 3)),
-        (T_PROJ, 3, 2, (3, 2)),
-    ],
-    [(T_EUP, 3, 12, (3, 4)), (T_EDOWN, 12, 3, (4, 3)), (T_EOUT, 3, 3, (3, 3))],
+    [(T_DUP, 2, 8, (2, 4)), (T_DDOWN, 8, 2, (4, 2)), (T_DOUT, 2, 2, (2, 2))],
+    [(T_DQKV, 2, 6, (2, 3)), (T_HEAD, 2, 3, (2, 3)), (T_PROJ, 3, 2, (3, 2))],
+    [(T_EUP, 3, 12, (3, 4))],
+    [(T_EDOWN, 12, 3, (4, 3)), (T_EOUT, 3, 3, (3, 3))],
     [(T_EQKV, 3, 9, (3, 3)), (T_EMBED, 3, 3, (3, 3))],
 ]
 
@@ -1103,9 +1155,9 @@
     (x0, h1, qkv, lse, att, mid, h2, act, slope, x1, hn, latent) = encoder_forward(
         tile_rows, vis_len, gathered, vector, visible_pix, pos_d, 2
     )
-    (d_h1, d_dqkv, d_att, d_gproj, d_h2, d_du, d_act, d_gdown, d_hn, d_gpred, glat, d_sums) = decoder(
-        tile_rows, vis_len, gathered, vector, latent, pos_e, ordered, 4
-    )
+    (
+        d_x0, d_h1, d_qkv, d_lse, d_att, d_gproj, d_grad, d_h2, d_du, d_act, d_gdown, d_hn, d_gpred, dm_sums,
+    ) = decoder(tile_rows, vis_len, gathered, vector, latent, pos_e, ordered, 4)
     sizes = chunk_sizes(groups)
     chunk_of, place_of = tile_places(sizes)
 
@@ -1123,25 +1175,45 @@
             at += row_tiles * col_tiles
         return buffers
 
-    buffers0 = gradients(
-        0, [(d_h2, d_du), (d_act, d_gdown), (d_att, d_gproj), (d_h1, d_dqkv), (d_hn, d_gpred), (hn, glat)]
-    )
-    glat, buffers0 = lax.optimization_barrier((glat, buffers0))
+    def core(buffers):
+        return reduce_core(buffers, parts)
+
+    def chips(state, steps=1):
+        return reduce_chips(state, parts, steps)
+
+    after = lax.optimization_barrier
+    buf0 = gradients(0, [(d_h2, d_du), (d_act, d_gdown), (d_att, d_gproj)])
+    d_grad, buf0 = after((d_grad, buf0))
+    d_dqkv, glat, da_sums = decoder_attention_back(
+        tile_rows, vis_len, gathered, vector, d_gproj, d_grad, d_qkv, d_lse, d_x0, 4
+    )
+    half0, left0 = core(buf0)
+    d_dqkv, glat, half0 = after((d_dqkv, glat, half0))
+    buf1 = gradients(1, [(d_h1, d_dqkv), (d_hn, d_gpred), (hn, glat)])
+    half0, left0 = chips((half0, left0))
+    glat, buf1 = after((glat, buf1))
     gdown, du, grad_mid, gproj, m_sums = encoder_mlp_back(tile_rows, gathered, vector, glat, x1, mid, slope, 2)
-    state0 = reduce_core(buffers0, parts)
-    gdown, du, gproj, halves = lax.optimization_barrier((gdown, du, gproj, state0[0]))
-    state0 = (halves, state0[1])
-    buffers1 = gradients(1, [(h2, du), (act, gdown), (att, gproj)])
-    state0 = reduce_chips(state0, parts, 1)
-    gproj, buffers1 = lax.optimization_barrier((gproj, buffers1))
+    half1, left1 = core(buf1)
+    du, half0, half1 = after((du, half0, half1))
+    buf2 = gradients(2, [(h2, du)])
+    half0, left0 = chips((half0, left0), 99)
+    half1, left1 = chips((half1, left1))
+    gdown, buf2, half0, half1 = after((gdown, buf2, half0, half1))
+    buf3 = gradients(3, [(act, gdown), (att, gproj)])
+    own0 = scatter_patch(reduce_join((half0, left0), parts), groups)
+    half1, left1 = chips((half1, left1), 99)
+    half2, left2 = core(buf2)
+    grad_mid, buf3, half1, half2, own0 = after((grad_mid, buf3, half1, half2, own0))
     dqkv, gembed, a_sums = encoder_attention_back(
         tile_rows, vis_len, gathered, vector, gproj, grad_mid, qkv, lse, x0, 2
     )
-    state1 = reduce_core(buffers1, parts)
-    dqkv, gembed, halves0, halves1 = lax.optimization_barrier((dqkv, gembed, state0[0], state1[0]))
-    state0, state1 = (halves0, state0[1]), (halves1, state1[1])
-
-    d_sums, m_sums, a_sums = (jnp.sum(s, axis=0) for s in (d_sums, m_sums, a_sums))
+    own1 = scatter_patch(reduce_join((half1, left1), parts), groups)
+    full0 = gather_patch(own0, groups)
+    half2, left2 = chips((half2, left2))
+    half3, left3 = core(buf3)
+    dqkv, gembed, half2, half3, own1 = after((dqkv, gembed, half2, half3, own1))
+
+    dm_sums, da_sums, m_sums, a_sums = (jnp.sum(s, axis=0) for s in (dm_sums, da_sums, m_sums, a_sums))
 
     def cut(sums, start, size):
         return sums[start : start + size]
@@ -1158,39 +1230,50 @@
             cut(m_sums, EM_BD, D),
             cut(m_sums, EM_NORM, 2 * D),
             cut(m_sums, EM_PROJ, E),
-            cut(d_sums, DS_MASK, E),
-            cut(d_sums, DS["g1"], 2 * E),
-            cut(d_sums, DS["bqkv"], E),
-            cut(d_sums, DS["bqkv"] + 2 * E, E),
-            cut(d_sums, DS["bo"], E),
-            cut(d_sums, DS["g2"], 2 * E),
-            cut(d_sums, DS["bu"], FD),
-            cut(d_sums, DS["bd"], E),
-            cut(d_sums, DS_NORM, 2 * E),
-            cut(d_sums, DS_HEAD, PIX),
+            cut(da_sums, DA_MASK, E),
+            cut(da_sums, DA_G1, 2 * E),
+            cut(da_sums, DA_QKV, E),
+            cut(da_sums, DA_QKV + 2 * E, E),
+            cut(dm_sums, DM_BO, E),
+            cut(dm_sums, DM_G2, 2 * E),
+            cut(dm_sums, DM_BU, FD),
+            cut(dm_sums, DM_BD, E),
+            cut(dm_sums, DM_NORM, 2 * E),
+            cut(dm_sums, DM_HEAD, PIX),
         ]
     )
     vector_tile = jnp.pad(grad_vector.reshape(parts, own), ((0, 0), (0, rows_cut * BS - own)))
     vector_tile = vector_tile.reshape(parts, rows_cut, BS)
-    buffers2 = gradients(2, [(h1, dqkv), (visible_pix.reshape(-1, PIX), gembed)], vector_tile)
-    first = reduce_end(state0, parts, groups)
-    second = reduce_end(state1, parts, groups)
-    third = reduce_end(reduce_core(buffers2, parts), parts, groups)
-
-    reduced = jnp.concatenate([first, second, third], axis=0)
+    buf4 = gradients(4, [(h1, dqkv), (visible_pix.reshape(-1, PIX), gembed)], vector_tile)
+    own2 = scatter_patch(reduce_join((half2, left2), parts), groups)
+    own3 = scatter_patch(reduce_join((half3, left3), parts), groups)
+    own4 = scatter_patch(reduce_join(core(buf4), parts), groups)
+    owns = [own0, own1, own2, own3, own4]
+    fulls = [full0] + [gather_patch(o, groups) for o in owns[1:]]
+
+    def squares(x):
+        wide = x.astype(F32)
+        return jnp.sum(wide * wide)
+
+    totals = jnp.stack(
+        [
+            jnp.sum(cut(dm_sums, DM_LOSS, PIX)) / PIX,
+            jnp.sum(POS - vis_len).astype(F32),
+            sum(squares(o) for o in owns),
+        ]
+    )
+    totals = sum_all(totals, parts, groups)
+    loss_sum, masked_count = totals[0], totals[1]
+    grad_norm = jnp.sqrt(totals[2]) / masked_count
+    scale = jnp.minimum(1.0, CLIP_NORM / grad_norm) / masked_count
+
+    reduced = jnp.concatenate(fulls, axis=0)
     starts = np.cumsum([0] + sizes)
     where = jnp.zeros(NBLK + 2, jnp.int32)
     for i, size in enumerate(sizes):
         here = starts[i] + place_after(jnp.asarray(place_of), size, groups)
         where = jnp.where(jnp.asarray(chunk_of == i), here, where)
-    wide = reduced.astype(F32)
-    squares = sum_dp(jnp.sum(wide * wide), parts)
-    totals = jnp.stack([jnp.sum(cut(d_sums, DS_LOSS, PIX)) / PIX, jnp.sum(POS - vis_len).astype(F32)])
-    totals = sum_all(totals, parts, groups)
-    loss_sum, masked_count = totals[0], totals[1]
-    grad_norm = jnp.sqrt(squares) / masked_count
-    scale = jnp.minimum(1.0, CLIP_NORM / grad_norm) / masked_count
-
+    reduced, scale = after((reduced, scale))
     slot_rows = reduced[where[jnp.minimum(block_owner, NBLK)]]
     if parts > 1:
         slot_rows = lax.all_to_all(slot_rows, "dp", 0, 0, tiled=True)

time: 745 us -> 769 us (1.032)
  local copies, waits for them, and re-layouts: 27.4 us -> 52.8 us
  waiting for transfers between devices: 235 us -> 214 us
  other arithmetic: 41.2 us -> 57.4 us
    ppermute x18 -> x30, waiting for transfers between devices: 59.9 us -> 22.7 us  [shift_patch(): lax.ppermute(x, 'patch', [(i, (i + shift) % size) for i in range(size)])]
    all_to_all x1, waiting for transfers between devices: 0.01 us -> 33.3 us  [shards(): slot_rows = lax.all_to_all(slot_rows, 'dp', 0, 0, tiled=True)]
    unnamed x85 -> x125, local copies, waits for them, and re-layouts: 6.62 us -> 27.3 us
    ppermute x21 -> x28, waiting for transfers between devices: 55 us -> 35.7 us  [swap_bit(): return lax.ppermute(x, 'dp', [(i, i ^ 1 << bit) for i in range(size)])]
    convert_element_type x14 -> x24, other arithmetic: 27.3 us -> 33.2 us  [low_sum(): return (a.astype(F32) + b.astype(F32)).astype(BF)]
    pallas_call x4 -> x5, Pallas kernels: 222 us -> 228 us  [group_call(): pl.pallas_call(kernel, grid_spec=pltpu.PrefetchScalarGridSpec(num_scalar_...]
    ppermute x18 -> x30, starting transfers between devices: 51.1 us -> 48.6 us  [shift_patch(): lax.ppermute(x, 'patch', [(i, (i + shift) % size) for i in range(size)])]
    ppermute x21 -> x28, starting transfers between devices: 23.5 us -> 22.1 us  [swap_bit(): return lax.ppermute(x, 'dp', [(i, i ^ 1 << bit) for i in range(size)])]
  transfers between devices with their start and end apart: 43 -> 62, of which waited for: 20 -> 22; matrix products, arithmetic and copies ran while one was open for 6% -> 10% of each run, Pallas kernels for 10% -> 15%
where the time goes in v3:
time: 769 us; the launch traced here: 761 us
  Pallas kernels  332 us (43%)
  waiting for transfers between devices  214 us (28%)
  starting transfers between devices  78.8 us (10%)
  other arithmetic  57.4 us (7%)
  local copies, waits for them, and re-layouts  52.8 us (7%)
  between operations  26.2 us (3%)
    pallas_call x5, Pallas kernels, group_call(): pl.pallas_call(kernel, grid_spec=pltpu.PrefetchScalarGridSpec(num_scalar_...  228 us
    all_gather x1, waiting for transfers between devices, shards(): gathered = lax.all_gather(mine, 'dp', axis=0, tiled=True)  114 us
    pallas_call x11, Pallas kernels, weight_grad(): pl.pallas_call(functools.partial(weight_grad_kernel, parts, cut, len(give...  66.9 us
    ppermute x30, starting transfers between devices, shift_patch(): lax.ppermute(x, 'patch', [(i, (i + shift) % size) for i in range(size)])  48.6 us
    ppermute x28, waiting for transfers between devices, swap_bit(): return lax.ppermute(x, 'dp', [(i, i ^ 1 << bit) for i in range(size)])  35.7 us
    all_to_all x1, waiting for transfers between devices, shards(): slot_rows = lax.all_to_all(slot_rows, 'dp', 0, 0, tiled=True)  33.3 us
    convert_element_type x24, other arithmetic, low_sum(): return (a.astype(F32) + b.astype(F32)).astype(BF)  33.2 us
    unnamed x125, local copies, waits for them, and re-layouts  27.3 us
  transfers between devices with their start and end apart: 62, of which 22 were waited for; matrix products, arithmetic and copies ran while one was open for 10% of the time, Pallas kernels for 15%

profile of v3, /device:TPU:0, one launch (start us, length us, event | category | flops | bytes accessed | tf_op | source)
XLA Modules:
  0.0 760.8 jit_solution(10912299592530386099)
XLA Ops:
  7.2 3.2 convert_element_type.413
  17.2 8.8 %order_patches.1 = (bf16[8,208,768]{2,1,0:T(8,128)(2,1)}, bf16[8,80,768]{2,1,0:T(8,128)(2,1)}, f32[8,80,768]{2,1,0:T(8,128)}, f32[8,208,512]{2,1,0:T(8,128)}) custom-call(s32[8,208,1]{2,1,0:T(8,128)} %copy.61.shuffle_ref, bf16[8,196,768]{2,1,0:T(8,128)(2,1)} %copy.62.pixels_ref, bf16[2,196,768]{2,1,0:T(8,128)(2,1)} %constant.289.clone.sin_d_ref, ...), custom_call_target="tpu_custom_call" | custom-call | tf_op jit(solution)/shard_map/order_patches/pallas_call | solution.py:354
  26.7 114.1 %all-gather.2.cloned.1.call-done.wg_ref = bf16[49280,256]{1,0:T(8,128)(2,1)} async-done(((bf16[6160,256]{1,0:T(8,128)(2,1)}), bf16[49280,256]{1,0:T(8,128)(2,1)}) %all-gather.2.cloned.1.call-update) | async-done | bytes 25231376 | tf_op jit(solution)/shard_map/all_gather | solution.py:1139
  142.5 42.8 %encoder_forward.1 = (f32[640,768]{1,0:T(8,128)}, bf16[640,768]{1,0:T(8,128)(2,1)}, bf16[640,2304]{1,0:T(8,128)(2,1)}, f32[8,3,4,80]{3,2,1,0:T(4,128)}, bf16[640...) custom-call(s32[177]{0:T(256)} %fusion.56.row_ref, ...), custom_call_target="tpu_custom_call" | custom-call | flops 10317987840 | bytes 43970560 | tf_op jit(solution)/shard_map/encoder_forward/pallas_call | solution.py:379
  185.3 81.3 %decoder.1 = (f32[1664,512]{1,0:T(8,128)}, bf16[1664,512]{1,0:T(8,128)(2,1)}, bf16[1664,1536]{1,0:T(8,128)(2,1)}, f32[8,2,8,208]{3,2,1,0:T(8,128)}, bf16[1664,51...) custom-call(s32[177]{0:T(256)} %fusion.56.row_ref, ...), custom_call_target="tpu_custom_call" | custom-call | flops 20065550336 | bytes 77316096 | tf_op jit(solution)/shard_map/decoder/pallas_call | solution.py:379
  266.6 8.4 %weight_grad.11 = (bf16[4,36,32,256]{3,2,1,0:T(8,128)(2,1)}, bf16[4,36,32,256]{3,2,1,0:T(8,128)(2,1)}) custom-call(s32[1]{0:T(128)} %bitcast.9.index_ref, bf16[1664,512]{1,0:T(8,128)(2,1)} %get-tuple-element.131.x_ref, bf16[1664,2048]{1,0:T(8,128)(2,1)} %get-tuple-element.132.g_ref), custom_call_target="tpu_custom_call" | custom-call | flops 3489660928 | bytes 10616832 | tf_op jit(solution)/shard_map/weight_grad/pallas_call | solution.py:905
  275.0 8.4 %weight_grad.12 = (bf16[4,36,32,256]{3,2,1,0:T(8,128)(2,1)}, bf16[4,36,32,256]{3,2,1,0:T(8,128)(2,1)}) custom-call(s32[1]{0:T(128)} %bitcast.9.index_ref, bf16[1664,2048]{1,0:T(8,128)(2,1)} %get-tuple-element.129.x_ref, bf16[1664,512]{1,0:T(8,128)(2,1)} %get-tuple-element.130.g_ref, ...), custom_call_target="tpu_custom_call", output_to_operand_aliasing={{0}: (3, {}), {1}: (4, {})} | custom-call | flops 3489660928 | bytes 10616832 | tf_op jit(solution)/shard_map/weight_grad/pallas_call | solution.py:905
  283.5 4.0 weight_grad.13
  288.0 54.3 %decoder_attention_back.1 = (bf16[1664,1536]{1,0:T(8,128)(2,1)}, bf16[640,512]{1,0:T(8,128)(2,1)}, f32[8,3072]{1,0:T(8,128)}) custom-call(s32[177]{0:T(256)} %fusion.56.row_ref, s32[8]{0:T(128)} %len_ref.7, bf16[49280,256]{1,0:T(8,128)(2,1)} %all-gather.2.cloned.1.call-done.wg_ref, f32[1,21760]{1,0:T(1,128)} %reshape.171.vec_ref, ...), custom_call_target="tpu_custom_call" | custom-call | flops 3489660928 | bytes 11730944 | tf_op jit(solution)/shard_map/decoder_attention_back/pallas_call | solution.py:379
  342.3 2.8 add_convert_fusion.3
  345.4 7.1 weight_grad.14
  352.6 4.9 weight_grad.15
  357.4 3.1 weight_grad.16
  363.8 17.4 %encoder_mlp_back.1 = (bf16[640,768]{1,0:T(8,128)(2,1)}, bf16[640,3072]{1,0:T(8,128)(2,1)}, f32[640,768]{1,0:T(8,128)}, bf16[640,768]{1,0:T(8,128)(2,1)}, f32[8,8192]{1,0:T(8,128)}) custom-call(s32[177]{0:T(256)} %fusion.56.row_ref, bf16[49280,256]{1,0:T(8,128)(2,1)} %all-gather.2.cloned.1.call-done.wg_ref, f32[1,21760]{1,0:T(1,128)} %reshape.171.vec_ref, ...), custom_call_target="tpu_custom_call" | custom-call | flops 6543114240 | bytes 16252928 | tf_op jit(solution)/shard_map/encoder_mlp_back/pallas_call | solution.py:379
  390.2 8.0 %weight_grad.17 = (bf16[4,36,32,256]{3,2,1,0:T(8,128)(2,1)}, bf16[4,36,32,256]{3,2,1,0:T(8,128)(2,1)}) custom-call(s32[1]{0:T(128)} %bitcast.9.index_ref, bf16[640,768]{1,0:T(8,128)(2,1)} %get-tuple-element.168.x_ref, bf16[640,3072]{1,0:T(8,128)(2,1)} %get-tuple-element.174.g_ref), custom_call_target="tpu_custom_call" | custom-call | flops 3019898880 | bytes 9633792 | tf_op jit(solution)/shard_map/weight_grad/pallas_call | solution.py:905
  398.2 5.4 collective-permute-done.5
  425.7 8.1 %weight_grad.18 = (bf16[4,48,32,256]{3,2,1,0:T(8,128)(2,1)}, bf16[4,48,32,256]{3,2,1,0:T(8,128)(2,1)}) custom-call(s32[1]{0:T(128)} %bitcast.9.index_ref, bf16[640,3072]{1,0:T(8,128)(2,1)} %get-tuple-element.166.x_ref, bf16[640,768]{1,0:T(8,128)(2,1)} %get-tuple-element.181.g_ref, ...), custom_call_target="tpu_custom_call", output_to_operand_aliasing={{0}: (3, {}), {1}: (4, {})} | custom-call | flops 3019898880 | bytes 9633792 | tf_op jit(solution)/shard_map/weight_grad/pallas_call | solution.py:905
  434.4 3.9 weight_grad.19
  445.5 2.8 add_convert_fusion.2
  448.6 32.1 %encoder_attention_back.1 = (bf16[640,2304]{1,0:T(8,128)(2,1)}, bf16[640,768]{1,0:T(8,128)(2,1)}, f32[8,4608]{1,0:T(8,128)}) custom-call(s32[177]{0:T(256)} %fusion.56.row_ref, s32[8]{0:T(128)} %len_ref.7, bf16[49280,256]{1,0:T(8,128)(2,1)} %all-gather.2.cloned.1.call-done.wg_ref, f32[1,21760]{1,0:T(1,128)} %reshape.171.vec_ref, ...), custom_call_target="tpu_custom_call" | custom-call | flops 3019898880 | bytes 8159232 | tf_op jit(solution)/shard_map/encoder_attention_back/pallas_call | solution.py:379
  483.7 2.7 collective-permute-start.19
  498.0 2.9 collective-permute-start.47
  506.9 3.5 collective-permute-done.46
  513.2 5.6 collective-permute-done.14
  520.1 3.6 add_convert_fusion
  526.8 2.8 collective-permute-start.50
  540.3 7.2 weight_grad.20
  547.5 3.8 weight_grad.21
  556.5 3.3 collective-permute-start.24
  564.2 4.3 collective-permute-done.23
  569.3 3.6 collective-permute-start.51
  575.0 8.5 %collective-permute-done.27 = bf16[2,24,32,256]{3,2,1,0:T(8,128)(2,1)S(1)} collective-permute-done((bf16[2,24,32,256]{3,2,1,0:T(8,128)(2,1)S(1)}, bf16[2,24,32,256]{3,2,1,0:T(8,128)(2,1)S(1)}, u32[]{:S(2)}, u32[]{:S(2)}) %collective-permute-start.27) | collective-permute-done | bytes 786464 | tf_op jit(solution)/shard_map/ppermute | solution.py:966
  593.9 2.9 add_convert_fusion.1
  601.2 3.4 collective-permute-start.31
  608.9 4.9 collective-permute-done.30
  614.7 3.8 collective-permute-start.54
  627.9 4.5 collective-permute-done.34
  634.0 2.4 collective-permute-start.38
  636.4 2.8 collective-permute-start.39
  642.9 3.6 collective-permute-done.38
  648.0 3.4 collective-permute-start.57
  656.6 5.0 collective-permute-done.40
  663.9 2.7 collective-permute-done.41
  667.8 3.5 collective-permute-done.43
  679.6 4.6 gather_fusion.1
  684.3 3.8 all-to-all-start
  692.6 33.3 %all-to-all-done = bf16[192,32,256]{2,1,0:T(8,128)(2,1)S(1)} async-done(((bf16[192,32,256]{2,1,0:T(8,128)(2,1)}), bf16[192,32,256]{2,1,0:T(8,128)(2,1)S(1)}, u32[]{:S(2)}, u32[]{:S(2)}) %all-to-all-start) | async-done | bytes 3145760 | tf_op jit(solution)/shard_map/all_to_all | solution.py:1279
  727.5 24.9 %tile_update.1 = (f32[24,256,256]{2,1,0:T(8,128)}, f32[24,256,256]{2,1,0:T(8,128)}, f32[24,256,256]{2,1,0:T(8,128)}, f32[24,256,256]{2,1,0:T(8,128)}) custom-call(f32[1]{0:T(128)} %bitcast.84.scale_ref, bf16[8,24,32,256]{3,2,1,0:T(8,128)(2,1)} %bitcast.202, f32[24,256,256]{2,1,0:T(8,128)} %w_ref.1, f32[24,256,256]{2,1,0:T(8,128)} %left_stat_ref.1, ...), custom_call_target="tpu_custom_call" | custom-call | tf_op jit(solution)/shard_map/tile_update/pallas_call | solution.py:1066
  (337 shorter events, 152.0 us)
Async XLA Ops:
  7.2 133.7 %all-gather.2.cloned.1.call-start = ((), (), s32[]{:S(2)}) async-start(), calls=%async_computation.1 | async-start | bytes 28385280 | tf_op jit(solution)/shard_map/all_gather | solution.py:1139
  287.6 54.8 %collective-permute-start = (bf16[4,36,32,256]{3,2,1,0:T(8,128)(2,1)}, bf16[4,36,32,256]{3,2,1,0:T(8,128)(2,1)}, u32[]{:S(2)}, u32[]{:S(2)}) collective-permute-start(bf16[4,36,32,256]{3,2,1,0:T(8,128)(2,1)} %get-tuple-element.146), channel_id=1, source_target_pairs={{0,4},{4,0},{8,12},{12,8},{16,20},{20,16},{24,28},{28,24},{1,5},{5... | collective-permute-start | bytes 7077896 | tf_op jit(solution)/shard_map/ppermute | solution.py:966
  360.6 22.4 %collective-permute-start.3 = (bf16[4,24,32,256]{3,2,1,0:T(8,128)(2,1)}, bf16[4,24,32,256]{3,2,1,0:T(8,128)(2,1)}, u32[]{:S(2)}, u32[]{:S(2)}) collective-permute-start(bf16[4,24,32,256]{3,2,1,0:T(8,128)(2,1)} %get-tuple-element.173), channel_id=1, source_target_pairs={{0,4},{4,0},{8,12},{12,8},{16,20},{20,16},{24,28},{28,24},{1,5},{5... | collective-permute-start | bytes 4718600 | tf_op jit(solution)/shard_map/ppermute | solution.py:966
  360.9 20.4 %collective-permute-start.2 = (bf16[2,18,32,256]{3,2,1,0:T(8,128)(2,1)S(1)}, bf16[2,18,32,256]{3,2,1,0:T(8,128)(2,1)}, u32[]{:S(2)}, u32[]{:S(2)}) collective-permute-start(bf16[2,18,32,256]{3,2,1,0:T(8,128)(2,1)S(1)} %slice_bitcast_fusion.8), channel_id=1, source_target_pairs={{0,16},{4,20},{8,24},{12,28},{16,0},{20,4},{24,8},{28,12},{1,17},{... | collective-permute-start | bytes 1769480 | tf_op jit(solution)/shard_map/ppermute | solution.py:966
  362.2 20.5 %collective-permute-start.1 = (bf16[2,18,32,256]{3,2,1,0:T(8,128)(2,1)}, bf16[2,18,32,256]{3,2,1,0:T(8,128)(2,1)S(1)}, u32[]{:S(2)}, u32[]{:S(2)}) collective-permute-start(bf16[2,18,32,256]{3,2,1,0:T(8,128)(2,1)} %slice_bitcast_fusion.9), channel_id=1, source_target_pairs={{0,8},{4,12},{8,0},{12,4},{16,24},{20,28},{24,16},{28,20},{1,9},{5... | collective-permute-start | bytes 1769480 | tf_op jit(solution)/shard_map/ppermute | solution.py:966
  385.2 21.4 %collective-permute-start.7 = (bf16[2,12,32,256]{3,2,1,0:T(8,128)(2,1)S(1)}, bf16[2,12,32,256]{3,2,1,0:T(8,128)(2,1)}, u32[]{:S(2)}, u32[]{:S(2)}) collective-permute-start(bf16[2,12,32,256]{3,2,1,0:T(8,128)(2,1)S(1)} %slice_bitcast_fusion.14), channel_id=1, source_target_pairs={{0,16},{4,20},{8,24},{12,28},{16,0},{20,4},{24,8},{28,12},{1,17},{... | collective-permute-start | bytes 1179656 | tf_op jit(solution)/shard_map/ppermute | solution.py:966
  386.8 21.0 %collective-permute-start.6 = (bf16[2,12,32,256]{3,2,1,0:T(8,128)(2,1)S(1)}, bf16[2,12,32,256]{3,2,1,0:T(8,128)(2,1)}, u32[]{:S(2)}, u32[]{:S(2)}) collective-permute-start(bf16[2,12,32,256]{3,2,1,0:T(8,128)(2,1)S(1)} %slice_bitcast_fusion.15), channel_id=1, source_target_pairs={{0,8},{4,12},{8,0},{12,4},{16,24},{20,28},{24,16},{28,20},{1,9},{5... | collective-permute-start | bytes 1179656 | tf_op jit(solution)/shard_map/ppermute | solution.py:966
  387.4 16.3 %collective-permute-start.5 = (bf16[18,32,256]{2,1,0:T(8,128)(2,1)S(1)}, bf16[18,32,256]{2,1,0:T(8,128)(2,1)}, u32[]{:S(2)}, u32[]{:S(2)}) collective-permute-start(bf16[18,32,256]{2,1,0:T(8,128)(2,1)S(1)} %slice_bitcast_fusion.22), channel_id=1, source_target_pairs={{0,8},{4,12},{8,0},{12,4},{16,24},{20,28},{24,16},{28,20},{1,9},{5... | collective-permute-start | bytes 884744 | tf_op jit(solution)/shard_map/ppermute | solution.py:966
  389.7 15.1 %collective-permute-start.4 = (bf16[18,32,256]{2,1,0:T(8,128)(2,1)}, bf16[18,32,256]{2,1,0:T(8,128)(2,1)}, u32[]{:S(2)}, u32[]{:S(2)}) collective-permute-start(bf16[18,32,256]{2,1,0:T(8,128)(2,1)} %slice_bitcast_fusion.23), channel_id=1, source_target_pairs={{0,16},{4,20},{8,24},{12,28},{16,0},{20,4},{24,8},{28,12},{1,17},{... | collective-permute-start | bytes 884744 | tf_op jit(solution)/shard_map/ppermute | solution.py:966
  408.8 36.6 %collective-permute-start.10 = (bf16[4,36,32,256]{3,2,1,0:T(8,128)(2,1)}, bf16[4,36,32,256]{3,2,1,0:T(8,128)(2,1)}, u32[]{:S(2)}, u32[]{:S(2)}) collective-permute-start(bf16[4,36,32,256]{3,2,1,0:T(8,128)(2,1)} %get-tuple-element.191), channel_id=1, source_target_pairs={{0,4},{4,0},{8,12},{12,8},{16,20},{20,16},{24,28},{28,24},{1,5},{5... | collective-permute-start | bytes 7077896 | tf_op jit(solution)/shard_map/ppermute | solution.py:966
  419.7 18.6 %collective-permute-start.11 = (bf16[9,32,256]{2,1,0:T(8,128)(2,1)}, bf16[9,32,256]{2,1,0:T(8,128)(2,1)}, u32[]{:S(2)}, u32[]{:S(2)}) collective-permute-start(bf16[9,32,256]{2,1,0:T(8,128)(2,1)} %get-tuple-element.258), channel_id=1, source_target_pairs={{0,1},{1,2},{2,3},{3,0},{4,5},{5,6},{6,7},{7,4},{8,9},{9,10},{10,1... | collective-permute-start | bytes 442376 | tf_op jit(solution)/shard_map/ppermute | solution.py:998
  421.2 17.7 %collective-permute-start.12 = (bf16[9,32,256]{2,1,0:T(8,128)(2,1)}, bf16[9,32,256]{2,1,0:T(8,128)(2,1)}, u32[]{:S(2)}, u32[]{:S(2)}) collective-permute-start(bf16[9,32,256]{2,1,0:T(8,128)(2,1)} %get-tuple-element.260), channel_id=1, source_target_pairs={{0,2},{1,3},{2,0},{3,1},{4,6},{5,7},{6,4},{7,5},{8,10},{9,11},{10,... | collective-permute-start | bytes 442376 | tf_op jit(solution)/shard_map/ppermute | solution.py:998
  423.6 15.3 %collective-permute-start.13 = (bf16[9,32,256]{2,1,0:T(8,128)(2,1)}, bf16[9,32,256]{2,1,0:T(8,128)(2,1)}, u32[]{:S(2)}, u32[]{:S(2)}) collective-permute-start(bf16[9,32,256]{2,1,0:T(8,128)(2,1)} %get-tuple-element.259), channel_id=1, source_target_pairs={{0,3},{1,0},{2,1},{3,2},{4,7},{5,4},{6,5},{7,6},{8,11},{9,8},{10,9... | collective-permute-start | bytes 442376 | tf_op jit(solution)/shard_map/ppermute | solution.py:998
  425.1 15.6 %collective-permute-start.9 = (bf16[12,32,256]{2,1,0:T(8,128)(2,1)S(1)}, bf16[12,32,256]{2,1,0:T(8,128)(2,1)}, u32[]{:S(2)}, u32[]{:S(2)}) collective-permute-start(bf16[12,32,256]{2,1,0:T(8,128)(2,1)S(1)} %slice_bitcast_fusion.24), channel_id=1, source_target_pairs={{0,8},{4,12},{8,0},{12,4},{16,24},{20,28},{24,16},{28,20},{1,9},{5... | collective-permute-start | bytes 589832 | tf_op jit(solution)/shard_map/ppermute | solution.py:966
  482.6 13.3 %collective-permute-start.17 = (bf16[6,32,256]{2,1,0:T(8,128)(2,1)}, bf16[6,32,256]{2,1,0:T(8,128)(2,1)}, u32[]{:S(2)}, u32[]{:S(2)}) collective-permute-start(bf16[6,32,256]{2,1,0:T(8,128)(2,1)} %get-tuple-element.261), channel_id=1, source_target_pairs={{0,1},{1,2},{2,3},{3,0},{4,5},{5,6},{6,7},{7,4},{8,9},{9,10},{10,1... | collective-permute-start | bytes 294920 | tf_op jit(solution)/shard_map/ppermute | solution.py:998
  483.2 13.3 %collective-permute-start.18 = (bf16[6,32,256]{2,1,0:T(8,128)(2,1)}, bf16[6,32,256]{2,1,0:T(8,128)(2,1)}, u32[]{:S(2)}, u32[]{:S(2)}) collective-permute-start(bf16[6,32,256]{2,1,0:T(8,128)(2,1)} %get-tuple-element.263), channel_id=1, source_target_pairs={{0,2},{1,3},{2,0},{3,1},{4,6},{5,7},{6,4},{7,5},{8,10},{9,11},{10,... | collective-permute-start | bytes 294920 | tf_op jit(solution)/shard_map/ppermute | solution.py:998
  483.7 14.3 %collective-permute-start.19 = (bf16[6,32,256]{2,1,0:T(8,128)(2,1)}, bf16[6,32,256]{2,1,0:T(8,128)(2,1)}, u32[]{:S(2)}, u32[]{:S(2)}) collective-permute-start(bf16[6,32,256]{2,1,0:T(8,128)(2,1)} %get-tuple-element.262), channel_id=1, source_target_pairs={{0,3},{1,0},{2,1},{3,2},{4,7},{5,4},{6,5},{7,6},{8,11},{9,8},{10,9... | collective-permute-start | bytes 294920 | tf_op jit(solution)/shard_map/ppermute | solution.py:998
  486.5 33.6 %collective-permute-start.16 = (bf16[4,48,32,256]{3,2,1,0:T(8,128)(2,1)}, bf16[4,48,32,256]{3,2,1,0:T(8,128)(2,1)}, u32[]{:S(2)}, u32[]{:S(2)}) collective-permute-start(bf16[4,48,32,256]{3,2,1,0:T(8,128)(2,1)} %get-tuple-element.204), channel_id=1, source_target_pairs={{0,4},{4,0},{8,12},{12,8},{16,20},{20,16},{24,28},{28,24},{1,5},{5... | collective-permute-start | bytes 9437192 | tf_op jit(solution)/shard_map/ppermute | solution.py:966
  487.3 24.4 %collective-permute-start.15 = (bf16[2,18,32,256]{3,2,1,0:T(8,128)(2,1)}, bf16[2,18,32,256]{3,2,1,0:T(8,128)(2,1)}, u32[]{:S(2)}, u32[]{:S(2)}) collective-permute-start(bf16[2,18,32,256]{3,2,1,0:T(8,128)(2,1)} %slice_bitcast_fusion.6), channel_id=1, source_target_pairs={{0,16},{4,20},{8,24},{12,28},{16,0},{20,4},{24,8},{28,12},{1,17},{... | collective-permute-start | bytes 1769480 | tf_op jit(solution)/shard_map/ppermute | solution.py:966
  496.5 13.9 %collective-permute-start.46 = (bf16[9,32,256]{2,1,0:T(8,128)(2,1)}, bf16[9,32,256]{2,1,0:T(8,128)(2,1)S(1)}, u32[]{:S(2)}, u32[]{:S(2)}) collective-permute-start(bf16[9,32,256]{2,1,0:T(8,128)(2,1)} %fusion.31), channel_id=1, source_target_pairs={{0,2},{1,3},{2,0},{3,1},{4,6},{5,7},{6,4},{7,5},{8,10},{9,11},{10,... | collective-permute-start | bytes 442376 | tf_op jit(solution)/shard_map/ppermute | solution.py:998
  498.0 13.0 %collective-permute-start.47 = (bf16[9,32,256]{2,1,0:T(8,128)(2,1)}, bf16[9,32,256]{2,1,0:T(8,128)(2,1)S(1)}, u32[]{:S(2)}, u32[]{:S(2)}) collective-permute-start(bf16[9,32,256]{2,1,0:T(8,128)(2,1)} %fusion.31), channel_id=1, source_target_pairs={{0,3},{1,0},{2,1},{3,2},{4,7},{5,4},{6,5},{7,6},{8,11},{9,8},{10,9... | collective-permute-start | bytes 442376 | tf_op jit(solution)/shard_map/ppermute | solution.py:998
  504.8 14.0 %collective-permute-start.14 = (bf16[2,18,32,256]{3,2,1,0:T(8,128)(2,1)}, bf16[2,18,32,256]{3,2,1,0:T(8,128)(2,1)S(1)}, u32[]{:S(2)}, u32[]{:S(2)}) collective-permute-start(bf16[2,18,32,256]{3,2,1,0:T(8,128)(2,1)} %slice_bitcast_fusion.7), channel_id=1, source_target_pairs={{0,8},{4,12},{8,0},{12,4},{16,24},{20,28},{24,16},{28,20},{1,9},{5... | collective-permute-start | bytes 1769480 | tf_op jit(solution)/shard_map/ppermute | solution.py:966
  524.2 30.2 %collective-permute-start.48 = (bf16[6,32,256]{2,1,0:T(8,128)(2,1)}, bf16[6,32,256]{2,1,0:T(8,128)(2,1)}, u32[]{:S(2)}, u32[]{:S(2)}) collective-permute-start(bf16[6,32,256]{2,1,0:T(8,128)(2,1)} %fusion.34), channel_id=1, source_target_pairs={{0,1},{1,2},{2,3},{3,0},{4,5},{5,6},{6,7},{7,4},{8,9},{9,10},{10,1... | collective-permute-start | bytes 294920 | tf_op jit(solution)/shard_map/ppermute | solution.py:998
  524.9 31.1 %collective-permute-start.49 = (bf16[6,32,256]{2,1,0:T(8,128)(2,1)}, bf16[6,32,256]{2,1,0:T(8,128)(2,1)}, u32[]{:S(2)}, u32[]{:S(2)}) collective-permute-start(bf16[6,32,256]{2,1,0:T(8,128)(2,1)} %fusion.34), channel_id=1, source_target_pairs={{0,2},{1,3},{2,0},{3,1},{4,6},{5,7},{6,4},{7,5},{8,10},{9,11},{10,... | collective-permute-start | bytes 294920 | tf_op jit(solution)/shard_map/ppermute | solution.py:998
  526.8 29.8 %collective-permute-start.50 = (bf16[6,32,256]{2,1,0:T(8,128)(2,1)}, bf16[6,32,256]{2,1,0:T(8,128)(2,1)S(1)}, u32[]{:S(2)}, u32[]{:S(2)}) collective-permute-start(bf16[6,32,256]{2,1,0:T(8,128)(2,1)} %fusion.34), channel_id=1, source_target_pairs={{0,3},{1,0},{2,1},{3,2},{4,7},{5,4},{6,5},{7,6},{8,11},{9,8},{10,9... | collective-permute-start | bytes 294920 | tf_op jit(solution)/shard_map/ppermute | solution.py:998
  533.8 17.5 %collective-permute-start.20 = (bf16[18,32,256]{2,1,0:T(8,128)(2,1)}, bf16[18,32,256]{2,1,0:T(8,128)(2,1)}, u32[]{:S(2)}, u32[]{:S(2)}) collective-permute-start(bf16[18,32,256]{2,1,0:T(8,128)(2,1)} %slice_bitcast_fusion.21), channel_id=1, source_target_pairs={{0,16},{4,20},{8,24},{12,28},{16,0},{20,4},{24,8},{28,12},{1,17},{... | collective-permute-start | bytes 884744 | tf_op jit(solution)/shard_map/ppermute | solution.py:966
  536.0 16.5 %collective-permute-start.21 = (bf16[18,32,256]{2,1,0:T(8,128)(2,1)}, bf16[18,32,256]{2,1,0:T(8,128)(2,1)S(1)}, u32[]{:S(2)}, u32[]{:S(2)}) collective-permute-start(bf16[18,32,256]{2,1,0:T(8,128)(2,1)} %slice_bitcast_fusion.20), channel_id=1, source_target_pairs={{0,8},{4,12},{8,0},{12,4},{16,24},{20,28},{24,16},{28,20},{1,9},{5... | collective-permute-start | bytes 884744 | tf_op jit(solution)/shard_map/ppermute | solution.py:966
  551.3 42.6 %collective-permute-start.32 = (bf16[4,40,32,256]{3,2,1,0:T(8,128)(2,1)}, bf16[4,40,32,256]{3,2,1,0:T(8,128)(2,1)}, u32[]{:S(2)}, u32[]{:S(2)}) collective-permute-start(bf16[4,40,32,256]{3,2,1,0:T(8,128)(2,1)} %get-tuple-element.223), channel_id=1, source_target_pairs={{0,4},{4,0},{8,12},{12,8},{16,20},{20,16},{24,28},{28,24},{1,5},{5... | collective-permute-start | bytes 7864328 | tf_op jit(solution)/shard_map/ppermute | solution.py:966
  552.6 20.7 %collective-permute-start.25 = (bf16[2,24,32,256]{3,2,1,0:T(8,128)(2,1)}, bf16[2,24,32,256]{3,2,1,0:T(8,128)(2,1)S(1)}, u32[]{:S(2)}, u32[]{:S(2)}) collective-permute-start(bf16[2,24,32,256]{3,2,1,0:T(8,128)(2,1)} %slice_bitcast_fusion.1), channel_id=1, source_target_pairs={{0,8},{4,12},{8,0},{12,4},{16,24},{20,28},{24,16},{28,20},{1,9},{5... | collective-permute-start | bytes 2359304 | tf_op jit(solution)/shard_map/ppermute | solution.py:966
  556.0 12.5 %collective-permute-start.23 = (bf16[9,32,256]{2,1,0:T(8,128)(2,1)S(1)}, bf16[9,32,256]{2,1,0:T(8,128)(2,1)S(1)}, u32[]{:S(2)}, u32[]{:S(2)}) collective-permute-start(bf16[9,32,256]{2,1,0:T(8,128)(2,1)S(1)} %get-tuple-element.257), channel_id=1, source_target_pairs={{0,2},{1,3},{2,0},{3,1},{4,6},{5,7},{6,4},{7,5},{8,10},{9,11},{10,... | collective-permute-start | bytes 442376 | tf_op jit(solution)/shard_map/ppermute | solution.py:998
  556.5 12.0 %collective-permute-start.24 = (bf16[9,32,256]{2,1,0:T(8,128)(2,1)S(1)}, bf16[9,32,256]{2,1,0:T(8,128)(2,1)S(1)}, u32[]{:S(2)}, u32[]{:S(2)}) collective-permute-start(bf16[9,32,256]{2,1,0:T(8,128)(2,1)S(1)} %get-tuple-element.256), channel_id=1, source_target_pairs={{0,3},{1,0},{2,1},{3,2},{4,7},{5,4},{6,5},{7,6},{8,11},{9,8},{10,9... | collective-permute-start | bytes 442376 | tf_op jit(solution)/shard_map/ppermute | solution.py:998
  563.0 20.5 %collective-permute-start.27 = (bf16[2,24,32,256]{3,2,1,0:T(8,128)(2,1)S(1)}, bf16[2,24,32,256]{3,2,1,0:T(8,128)(2,1)S(1)}, u32[]{:S(2)}, u32[]{:S(2)}) collective-permute-start(bf16[2,24,32,256]{3,2,1,0:T(8,128)(2,1)S(1)} %copy-done.16), channel_id=1, source_target_pairs={{0,16},{4,20},{8,24},{12,28},{16,0},{20,4},{24,8},{28,12},{1,17},{... | collective-permute-start | bytes 2359304 | tf_op jit(solution)/shard_map/ppermute | solution.py:966
  569.3 19.0 %collective-permute-start.51 = (bf16[9,32,256]{2,1,0:T(8,128)(2,1)}, bf16[9,32,256]{2,1,0:T(8,128)(2,1)}, u32[]{:S(2)}, u32[]{:S(2)}) collective-permute-start(bf16[9,32,256]{2,1,0:T(8,128)(2,1)} %get-tuple-element.238), channel_id=1, source_target_pairs={{0,1},{1,2},{2,3},{3,0},{4,5},{5,6},{6,7},{7,4},{8,9},{9,10},{10,1... | collective-permute-start | bytes 442376 | tf_op jit(solution)/shard_map/ppermute | solution.py:998
  573.0 27.9 %collective-permute-start.52 = (bf16[9,32,256]{2,1,0:T(8,128)(2,1)}, bf16[9,32,256]{2,1,0:T(8,128)(2,1)}, u32[]{:S(2)}, u32[]{:S(2)}) collective-permute-start(bf16[9,32,256]{2,1,0:T(8,128)(2,1)} %get-tuple-element.238), channel_id=1, source_target_pairs={{0,2},{1,3},{2,0},{3,1},{4,6},{5,7},{6,4},{7,5},{8,10},{9,11},{10,... | collective-permute-start | bytes 442376 | tf_op jit(solution)/shard_map/ppermute | solution.py:998
  574.4 15.5 %collective-permute-start.26 = (bf16[24,32,256]{2,1,0:T(8,128)(2,1)}, bf16[24,32,256]{2,1,0:T(8,128)(2,1)}, u32[]{:S(2)}, u32[]{:S(2)}) collective-permute-start(bf16[24,32,256]{2,1,0:T(8,128)(2,1)} %slice_bitcast_fusion.12), channel_id=1, source_target_pairs={{0,16},{4,20},{8,24},{12,28},{16,0},{20,4},{24,8},{28,12},{1,17},{... | collective-permute-start | bytes 1179656 | tf_op jit(solution)/shard_map/ppermute | solution.py:966
  588.3 12.9 %collective-permute-start.53 = (bf16[9,32,256]{2,1,0:T(8,128)(2,1)}, bf16[9,32,256]{2,1,0:T(8,128)(2,1)S(1)}, u32[]{:S(2)}, u32[]{:S(2)}) collective-permute-start(bf16[9,32,256]{2,1,0:T(8,128)(2,1)} %get-tuple-element.238), channel_id=1, source_target_pairs={{0,3},{1,0},{2,1},{3,2},{4,7},{5,4},{6,5},{7,6},{8,11},{9,8},{10,9... | collective-permute-start | bytes 442376 | tf_op jit(solution)/shard_map/ppermute | solution.py:998
  598.6 23.6 %collective-permute-start.33 = (bf16[2,20,32,256]{3,2,1,0:T(8,128)(2,1)}, bf16[2,20,32,256]{3,2,1,0:T(8,128)(2,1)}, u32[]{:S(2)}, u32[]{:S(2)}) collective-permute-start(bf16[2,20,32,256]{3,2,1,0:T(8,128)(2,1)} %slice_bitcast_fusion.4), channel_id=1, source_target_pairs={{0,8},{4,12},{8,0},{12,4},{16,24},{20,28},{24,16},{28,20},{1,9},{5... | collective-permute-start | bytes 1966088 | tf_op jit(solution)/shard_map/ppermute | solution.py:966
  600.2 22.1 %collective-permute-start.35 = (bf16[2,20,32,256]{3,2,1,0:T(8,128)(2,1)S(1)}, bf16[2,20,32,256]{3,2,1,0:T(8,128)(2,1)}, u32[]{:S(2)}, u32[]{:S(2)}) collective-permute-start(bf16[2,20,32,256]{3,2,1,0:T(8,128)(2,1)S(1)} %slice_bitcast_fusion.2), channel_id=1, source_target_pairs={{0,16},{4,20},{8,24},{12,28},{16,0},{20,4},{24,8},{28,12},{1,17},{... | collective-permute-start | bytes 1966088 | tf_op jit(solution)/shard_map/ppermute | solution.py:966
  600.8 13.1 %collective-permute-start.30 = (bf16[12,32,256]{2,1,0:T(8,128)(2,1)S(1)}, bf16[12,32,256]{2,1,0:T(8,128)(2,1)S(1)}, u32[]{:S(2)}, u32[]{:S(2)}) collective-permute-start(bf16[12,32,256]{2,1,0:T(8,128)(2,1)S(1)} %get-tuple-element.251), channel_id=1, source_target_pairs={{0,2},{1,3},{2,0},{3,1},{4,6},{5,7},{6,4},{7,5},{8,10},{9,11},{10,... | collective-permute-start | bytes 589832 | tf_op jit(solution)/shard_map/ppermute | solution.py:998
  601.2 12.6 %collective-permute-start.31 = (bf16[12,32,256]{2,1,0:T(8,128)(2,1)S(1)}, bf16[12,32,256]{2,1,0:T(8,128)(2,1)S(1)}, u32[]{:S(2)}, u32[]{:S(2)}) collective-permute-start(bf16[12,32,256]{2,1,0:T(8,128)(2,1)S(1)} %get-tuple-element.250), channel_id=1, source_target_pairs={{0,3},{1,0},{2,1},{3,2},{4,7},{5,4},{6,5},{7,6},{8,11},{9,8},{10,9... | collective-permute-start | bytes 589832 | tf_op jit(solution)/shard_map/ppermute | solution.py:998
  614.7 11.6 %collective-permute-start.54 = (bf16[12,32,256]{2,1,0:T(8,128)(2,1)S(1)}, bf16[12,32,256]{2,1,0:T(8,128)(2,1)}, u32[]{:S(2)}, u32[]{:S(2)}) collective-permute-start(bf16[12,32,256]{2,1,0:T(8,128)(2,1)S(1)} %get-tuple-element.236), channel_id=1, source_target_pairs={{0,1},{1,2},{2,3},{3,0},{4,5},{5,6},{6,7},{7,4},{8,9},{9,10},{10,1... | collective-permute-start | bytes 589832 | tf_op jit(solution)/shard_map/ppermute | solution.py:998
  618.5 20.8 %collective-permute-start.55 = (bf16[12,32,256]{2,1,0:T(8,128)(2,1)S(1)}, bf16[12,32,256]{2,1,0:T(8,128)(2,1)}, u32[]{:S(2)}, u32[]{:S(2)}) collective-permute-start(bf16[12,32,256]{2,1,0:T(8,128)(2,1)S(1)} %get-tuple-element.236), channel_id=1, source_target_pairs={{0,2},{1,3},{2,0},{3,1},{4,6},{5,7},{6,4},{7,5},{8,10},{9,11},{10,... | collective-permute-start | bytes 589832 | tf_op jit(solution)/shard_map/ppermute | solution.py:998
  619.6 21.3 %collective-permute-start.56 = (bf16[12,32,256]{2,1,0:T(8,128)(2,1)S(1)}, bf16[12,32,256]{2,1,0:T(8,128)(2,1)}, u32[]{:S(2)}, u32[]{:S(2)}) collective-permute-start(bf16[12,32,256]{2,1,0:T(8,128)(2,1)S(1)} %get-tuple-element.236), channel_id=1, source_target_pairs={{0,3},{1,0},{2,1},{3,2},{4,7},{5,4},{6,5},{7,6},{8,11},{9,8},{10,9... | collective-permute-start | bytes 589832 | tf_op jit(solution)/shard_map/ppermute | solution.py:998
  634.0 12.6 %collective-permute-start.38 = (bf16[10,32,256]{2,1,0:T(8,128)(2,1)S(1)}, bf16[10,32,256]{2,1,0:T(8,128)(2,1)S(1)}, u32[]{:S(2)}, u32[]{:S(2)}) collective-permute-start(bf16[10,32,256]{2,1,0:T(8,128)(2,1)S(1)} %get-tuple-element.254), channel_id=1, source_target_pairs={{0,2},{1,3},{2,0},{3,1},{4,6},{5,7},{6,4},{7,5},{8,10},{9,11},{10,... | collective-permute-start | bytes 491528 | tf_op jit(solution)/shard_map/ppermute | solution.py:998
  648.0 29.5 %collective-permute-start.57 = (bf16[10,32,256]{2,1,0:T(8,128)(2,1)S(1)}, bf16[10,32,256]{2,1,0:T(8,128)(2,1)S(1)}, u32[]{:S(2)}, u32[]{:S(2)}) collective-permute-start(bf16[10,32,256]{2,1,0:T(8,128)(2,1)S(1)} %get-tuple-element.234), channel_id=1, source_target_pairs={{0,1},{1,2},{2,3},{3,0},{4,5},{5,6},{6,7},{7,4},{8,9},{9,10},{10,1... | collective-permute-start | bytes 491528 | tf_op jit(solution)/shard_map/ppermute | solution.py:998
  651.4 26.9 %collective-permute-start.58 = (bf16[10,32,256]{2,1,0:T(8,128)(2,1)S(1)}, bf16[10,32,256]{2,1,0:T(8,128)(2,1)S(1)}, u32[]{:S(2)}, u32[]{:S(2)}) collective-permute-start(bf16[10,32,256]{2,1,0:T(8,128)(2,1)S(1)} %get-tuple-element.234), channel_id=1, source_target_pairs={{0,2},{1,3},{2,0},{3,1},{4,6},{5,7},{6,4},{7,5},{8,10},{9,11},{10,... | collective-permute-start | bytes 491528 | tf_op jit(solution)/shard_map/ppermute | solution.py:998
  653.8 25.2 %collective-permute-start.59 = (bf16[10,32,256]{2,1,0:T(8,128)(2,1)S(1)}, bf16[10,32,256]{2,1,0:T(8,128)(2,1)S(1)}, u32[]{:S(2)}, u32[]{:S(2)}) collective-permute-start(bf16[10,32,256]{2,1,0:T(8,128)(2,1)S(1)} %get-tuple-element.234), channel_id=1, source_target_pairs={{0,3},{1,0},{2,1},{3,2},{4,7},{5,4},{6,5},{7,6},{8,11},{9,8},{10,9... | collective-permute-start | bytes 491528 | tf_op jit(solution)/shard_map/ppermute | solution.py:998
  684.3 41.6 %all-to-all-start = ((bf16[192,32,256]{2,1,0:T(8,128)(2,1)}), bf16[192,32,256]{2,1,0:T(8,128)(2,1)S(1)}, u32[]{:S(2)}, u32[]{:S(2)}) async-start(bf16[192,32,256]{2,1,0:T(8,128)(2,1)} %gather_fusion.1), calls=%async_computation | async-start | bytes 6291456 | tf_op jit(solution)/shard_map/all_to_all | solution.py:1279
  (58 other events, 765.2 us)
Sparse Core Ops, SparseCore 0:
  12.5 128.2 all-gather.1

commit v4 on v2

--- a/solution.py
+++ b/solution.py
@@ -160,12 +160,33 @@
     return jnp.where(inside, 1.0, 0.0).astype(BF)
 
 
-def scores_of(k_masked, q, head_size, valid):
-    scores = mm_nt(k_masked, q) * (head_size**-0.5 * LOG2E)
-    return jnp.where(valid, scores, NEG_LARGE)
-
-
-def attention_forward(qkv_ref, att_ref, lse_ref, image, seq, width, head_size, valid):
+def masked_scores(k_masked, q, head_size, count):
+    scores = mm(k_masked, q) * (head_size**-0.5 * LOG2E)
+    if isinstance(count, int):
+        whole = count // 8 * 8
+        tail = scores[whole:]
+        row = lax.broadcasted_iota(jnp.int32, tail.shape, 0) + whole
+        return jnp.concatenate([scores[:whole], jnp.where(row < count, tail, NEG_LARGE)], axis=0)
+    row = lax.broadcasted_iota(jnp.int32, (scores.shape[0], 1), 0)
+    return jnp.where(row < count, scores, NEG_LARGE)
+
+
+def scores_bounded(qkv_ref, width, head_size):
+    lane = lax.broadcasted_iota(jnp.int32, (BS, 128), 0) // head_size
+    pick = jnp.where(lane == lax.broadcasted_iota(jnp.int32, (BS, 128), 1), 1.0, 0.0).astype(BF)
+    tops = []
+    for which in range(2):
+        top = None
+        for g in range(width // BS):
+            x = qkv_ref[:, which * width + g * BS : which * width + (g + 1) * BS]
+            norms = mm(x * x, pick)
+            top = norms if top is None else jnp.maximum(top, norms)
+        tops.append(jnp.max(top))
+    limit = 60.0 / (1.05 * head_size**-0.5 * LOG2E)
+    return tops[0] * tops[1] < limit * limit
+
+
+def attention_forward(qkv_ref, att_ref, out_t_ref, lse_ref, image, seq, width, head_size, count, bounded):
     rows = pl.ds(pl.multiple_of(image * seq, 16), seq)
     per = BS // head_size
 
@@ -175,23 +196,52 @@
 
         q, k, v = part(0), part(1), part(2)
         v_t = v.T
+        q = q.T
+        ones = jnp.ones((16, seq), BF)
         outs, logs = [], []
         for h in range(per):
-            scores = scores_of(k * head_mask(h, head_size), q, head_size, valid)
-            top = jnp.max(scores, axis=0, keepdims=True)
-            e = jnp.exp2(scores - top)
-            total = jnp.sum(e, axis=0, keepdims=True)
-            out = mm(v_t[h * head_size : (h + 1) * head_size, :], e.astype(BF))
-            outs.append(out * (1.0 / total))
+            scores = masked_scores(k * head_mask(h, head_size), q, head_size, count)
+            top = 0.0
+            if not bounded:
+                top = jnp.max(scores, axis=0, keepdims=True)
+                scores = scores - top
+            e = jnp.exp2(scores).astype(BF)
+            both = mm(jnp.concatenate([v_t[h * head_size : (h + 1) * head_size, :], ones], axis=0), e)
+            total = both[head_size : head_size + 1, :]
+            outs.append(both[:head_size, :] * (1.0 / total))
             logs.append(top + jnp.log2(total))
-        att_ref[rows, pl.ds(pl.multiple_of(g * BS, BS), BS)] = jnp.concatenate(outs, axis=0).T.astype(BF)
+        out_t = jnp.concatenate(outs, axis=0)
+        out_t_ref[image, g] = out_t
+        att_ref[rows, pl.ds(pl.multiple_of(g * BS, BS), BS)] = out_t.T.astype(BF)
         lse_ref[image, g] = jnp.concatenate(logs, axis=0)
         return c
 
     loop(0, width // BS, group, 0)
 
 
-def attention_backward(qkv_ref, datt_ref, lse_ref, dqkv_ref, image, seq, width, head_size, valid):
+def attend_all(qkv_ref, att_ref, out_t_ref, lse_ref, images, seq, width, head_size, count_of):
+    safe = scores_bounded(qkv_ref, width, head_size)
+
+    def run(bounded):
+        def one(image, c):
+            count = count_of(image)
+            attention_forward(
+                qkv_ref, att_ref, out_t_ref, lse_ref, image, seq, width, head_size, count, bounded
+            )
+            return c
+
+        lax.fori_loop(0, images, one, 0)
+
+    @pl.when(safe)
+    def _():
+        run(True)
+
+    @pl.when(jnp.logical_not(safe))
+    def _():
+        run(False)
+
+
+def attention_backward(qkv_ref, datt_ref, out_t_ref, lse_ref, dqkv_ref, image, seq, width, head_size, count):
     rows = pl.ds(pl.multiple_of(image * seq, 16), seq)
     per = BS // head_size
     scale = head_size**-0.5
@@ -204,20 +254,20 @@
         d_out = datt_ref[rows, cols(0)]
         lse = lse_ref[image, g]
         q_t, k_t, d_out_t = q.T, k.T, d_out.T
-        d_q, d_k, d_v = [], [], []
+        along = d_out_t.astype(F32) * out_t_ref[image, g]
+        d_q, d_k, d_v = [], jnp.zeros((seq, BS), F32), jnp.zeros((seq, BS), F32)
         for h in range(per):
             mask = head_mask(h, head_size)
             part = slice(h * head_size, (h + 1) * head_size)
-            probs = jnp.exp2(scores_of(k * mask, q, head_size, valid) - lse[h : h + 1, :])
-            d_probs = mm_nt(v * mask, d_out)
-            delta = jnp.sum(probs * d_probs, axis=0, keepdims=True)
-            d_scores = (probs * (d_probs - delta)).astype(BF)
-            d_v.append(mm_nt(d_out_t[part, :], probs.astype(BF)))
-            d_k.append(mm_nt(q_t[part, :], d_scores))
+            delta = jnp.sum(along[part, :], axis=0, keepdims=True)
+            probs = jnp.exp2(masked_scores(k * mask, q_t, head_size, count) - lse[h : h + 1, :])
+            d_scores = (probs * (mm(v * mask, d_out_t) - delta)).astype(BF)
+            d_v = d_v + mm(probs.astype(BF), d_out * mask)
+            d_k = d_k + mm(d_scores, q * mask)
             d_q.append(mm(k_t[part, :], d_scores))
         dqkv_ref[rows, cols(0)] = (jnp.concatenate(d_q, axis=0).T * scale).astype(BF)
-        dqkv_ref[rows, cols(1)] = (jnp.concatenate(d_k, axis=0).T * scale).astype(BF)
-        dqkv_ref[rows, cols(2)] = jnp.concatenate(d_v, axis=0).T.astype(BF)
+        dqkv_ref[rows, cols(1)] = (d_k * scale).astype(BF)
+        dqkv_ref[rows, cols(2)] = d_v.astype(BF)
         return c
 
     loop(0, width // BS, group, 0)
@@ -367,35 +417,40 @@
     )(ids, pixels, jnp.asarray(sinusoid_parts(POS, D)), jnp.asarray(sinusoid_parts(POS, E)))
 
 
-def group_call(kernel, steps, prefetch, in_arrays, out_list, scratch, name, flops):
+def group_call(kernel, steps, prefetch, in_arrays, out_list, scratch, name, flops, share=(0, 1), given=()):
+    count = steps // share[1]
+    start = share[0] * count
+
     def spec(shape, kind):
         if kind == "any":
             return pl.BlockSpec(memory_space=pl.ANY)
         if kind == "rows":
             block = (shape[0] // steps,) + tuple(shape[1:])
-            return pl.BlockSpec(block, lambda i, *_: (i,) + (0,) * (len(shape) - 1))
+            return pl.BlockSpec(block, lambda i, *_: (start + i,) + (0,) * (len(shape) - 1))
         return pl.BlockSpec(tuple(shape), lambda i, *_: (0,) * len(shape))
 
+    first_given = len(prefetch) + len(in_arrays)
     return pl.pallas_call(
-        kernel,
+        functools.partial(kernel, start, len(given)),
         grid_spec=pltpu.PrefetchScalarGridSpec(
             num_scalar_prefetch=len(prefetch),
-            grid=(steps,),
-            in_specs=[spec(a.shape, kind) for a, kind in in_arrays],
+            grid=(count,),
+            in_specs=[spec(a.shape, kind) for a, kind in in_arrays] + [pl.BlockSpec(memory_space=pl.ANY)] * len(given),
             out_specs=[spec(shape, kind) for shape, _, kind in out_list],
             scratch_shapes=scratch,
         ),
         out_shape=[jax.ShapeDtypeStruct(shape, dtype) for shape, dtype, _ in out_list],
+        input_output_aliases={first_given + i: i for i in range(len(given))},
         compiler_params=pltpu.CompilerParams(
             vmem_limit_bytes=VMEM_LIMIT, dimension_semantics=("arbitrary",)
         ),
         cost_estimate=pl.CostEstimate(
-            flops=flops,
-            bytes_accessed=sum(math.prod(s) * jnp.dtype(t).itemsize for s, t, _ in out_list) * 2,
+            flops=flops // share[1],
+            bytes_accessed=sum(math.prod(s) * jnp.dtype(t).itemsize for s, t, _ in out_list) * 2 // share[1],
             transcendentals=0,
         ),
         name=name,
-    )(*prefetch, *[a for a, _ in in_arrays])
+    )(*prefetch, *[a for a, _ in in_arrays], *given)
 
 
 ENC = layer_offsets(V_ENC, D, FE)
@@ -403,8 +458,8 @@
 
 
 def encoder_forward_kernel(
-    row_ref, len_ref, wg_ref, vec_ref, pix_ref, pos_ref,
-    x0_ref, h1_ref, qkv_ref, lse_ref, att_ref, mid_ref, h2_ref, act_ref, slope_ref, x1_ref, hn_ref, latent_ref,
+    start, given, row_ref, len_ref, wg_ref, vec_ref, pix_ref, pos_ref,
+    x0_ref, h1_ref, qkv_ref, lse_ref, out_t_ref, att_ref, mid_ref, h2_ref, act_ref, slope_ref, x1_ref, hn_ref, latent_ref,
     w_embed, w_qkv, w_out, w_up, w_down, w_proj, sems,
 ):
     step = pl.program_id(0)
@@ -433,12 +488,9 @@
     ready(1)
     qkv_forward(h1_ref, w_qkv, vec_ref, ENC["bqkv"], qkv_ref)
 
-    def one(image, c):
-        valid = lax.broadcasted_iota(jnp.int32, (VMAX, 1), 0) < len_ref[step * images + image]
-        attention_forward(qkv_ref, att_ref, lse_ref, image, VMAX, D, D // HE, valid)
-        return c
-
-    lax.fori_loop(0, images, one, 0)
+    attend_all(
+        qkv_ref, att_ref, out_t_ref, lse_ref, images, VMAX, D, D // HE, lambda i: len_ref[step * images + i]
+    )
     ready(2)
     add_linear(x0_ref, att_ref, w_out, vec_ref, ENC["bo"], mid_ref)
     norm_forward(mid_ref, vec(ENC["g2"]), vec(ENC["s2"]), h2_ref)
@@ -463,6 +515,7 @@
         ((rows, D), BF, "rows"),
         ((rows, 3 * D), BF, "rows"),
         ((images, D // BS, BS * HE // D, VMAX), F32, "rows"),
+        ((images, D // BS, BS, VMAX), F32, "rows"),
         ((rows, D), BF, "rows"),
         ((rows, D), F32, "rows"),
         ((rows, D), BF, "rows"),
@@ -499,9 +552,9 @@
 
 
 def decoder_kernel(
-    row_ref, len_ref, wg_ref, vec_ref, latent_ref, pos_ref, pix_ref,
+    start, given, row_ref, len_ref, wg_ref, vec_ref, latent_ref, pos_ref, pix_ref,
     h1_ref, dqkv_ref, att_ref, gproj_ref, h2_ref, du_ref, act_ref, gdown_ref, hn_ref, gpred_ref, glat_ref, sum_ref,
-    w_qkv, w_out, w_up, w_down, w_head, x0, qkv, lse, mid, slope, x1, pred, dy, grad, datt, sems,
+    w_qkv, w_out, w_up, w_down, w_head, x0, qkv, lse, out_t, mid, slope, x1, pred, dy, grad, datt, sems,
 ):
     step = pl.program_id(0)
     images = lse.shape[0]
@@ -547,13 +600,7 @@
     norm_forward(x0, vec(DEC["g1"]), vec(DEC["s1"]), h1_ref)
     ready(0)
     qkv_forward(h1_ref, w_qkv, vec_ref, DEC["bqkv"], qkv)
-    valid = lax.broadcasted_iota(jnp.int32, (SD, 1), 0) < POS
-
-    def attend(image, c):
-        attention_forward(qkv, att_ref, lse, image, SD, E, E // HD, valid)
-        return c
-
-    lax.fori_loop(0, images, attend, 0)
+    attend_all(qkv, att_ref, out_t, lse, images, SD, E, E // HD, lambda i: POS)
     ready(1)
     add_linear(x0, att_ref, w_out, vec_ref, DEC["bo"], mid)
     norm_forward(mid, vec(DEC["g2"]), vec(DEC["s2"]), h2_ref)
@@ -606,7 +653,7 @@
     col_loop(E // BS, back_out)
 
     def attend_back(image, c):
-        attention_backward(qkv, datt, lse, dqkv_ref, image, SD, E, E // HD, valid)
+        attention_backward(qkv, datt, out_t, lse, dqkv_ref, image, SD, E, E // HD, POS)
         return c
 
     lax.fori_loop(0, images, attend_back, 0)
@@ -657,6 +704,7 @@
         pltpu.VMEM((part, E), F32),
         pltpu.VMEM((part, 3 * E), BF),
         pltpu.VMEM((images // steps, E // BS, BS * HD // E, SD), F32),
+        pltpu.VMEM((images // steps, E // BS, BS, SD), F32),
         pltpu.VMEM((part, E), F32),
         pltpu.VMEM((part, FD), BF),
         pltpu.VMEM((part, E), F32),
@@ -693,7 +741,7 @@
 
 
 def encoder_mlp_back_kernel(
-    row_ref, wg_ref, vec_ref, glat_ref, x1_ref, mid_ref, slope_ref,
+    start, given, row_ref, wg_ref, vec_ref, glat_ref, x1_ref, mid_ref, slope_ref,
     gdown_ref, du_ref, grad_ref, gproj_ref, sum_ref,
     w_proj, w_down, w_up, dy, sems,
 ):
@@ -758,10 +806,9 @@
 
 
 def encoder_attention_back_kernel(
-    row_ref, len_ref, wg_ref, vec_ref, gproj_ref, grad_in_ref, qkv_ref, lse_ref, x0_ref,
-    dqkv_ref, gembed_ref, sum_ref,
-    w_out, w_qkv, dy, grad, datt, sems,
+    start, given, row_ref, len_ref, wg_ref, vec_ref, gproj_ref, grad_in_ref, qkv_ref, lse_ref, out_t_ref, x0_ref, *refs
 ):
+    dqkv_ref, gembed_ref, sum_ref, w_out, w_qkv, dy, grad, datt, sems = refs[given:]
     step = pl.program_id(0)
     images = lse_ref.shape[0]
     ready = fetch_all(step == 0, row_ref, wg_ref, sems, [(T_EOUT, w_out), (T_EQKV, w_qkv)])
@@ -778,8 +825,8 @@
     col_loop(D // BS, back_out)
 
     def attend_back(image, c):
-        valid = lax.broadcasted_iota(jnp.int32, (VMAX, 1), 0) < len_ref[step * images + image]
-        attention_backward(qkv_ref, datt, lse_ref, dqkv_ref, image, VMAX, D, D // HE, valid)
+        count = len_ref[(start + step) * images + image]
+        attention_backward(qkv_ref, datt, out_t_ref, lse_ref, dqkv_ref, image, VMAX, D, D // HE, count)
         return c
 
     lax.fori_loop(0, images, attend_back, 0)
@@ -794,7 +841,7 @@
     round_and_sum(grad, gembed_ref, sum_ref, EA_EMBED)
 
 
-def encoder_attention_back(tile_rows, vis_len, gathered, vector, gproj, grad, qkv, lse, x0, steps):
+def encoder_attention_back(tile_rows, vis_len, gathered, vector, gproj, grad, qkv, lse, out_t, x0, steps, share, given):
     rows = x0.shape[0]
     part = rows // steps
     outs = [((rows, 3 * D), BF, "rows"), ((rows, D), BF, "rows"), ((8, EA_ALL), F32, "whole")]
@@ -811,12 +858,15 @@
             (grad, "rows"),
             (qkv, "rows"),
             (lse, "rows"),
+            (out_t, "rows"),
             (x0, "rows"),
         ],
         outs,
         scratch + [pltpu.SemaphoreType.DMA((2,))],
         "encoder_attention_back",
         2 * rows * 4 * D * D,
+        share,
+        given,
     )
 
 
@@ -934,35 +984,23 @@
     return halves, left
 
 
-def reduce_end(state, parts, groups):
+def reduce_join(state, parts):
     halves, _ = reduce_chips(state, parts, 99)
-    whole = jnp.concatenate(halves, axis=0) if parts > 1 else halves[0]
-    return reduce_patch(whole, groups)
-
-
-def shift_patch(x, shift, size):
-    return lax.ppermute(x, "patch", [(i, (i + shift) % size) for i in range(size)])
-
-
-def reduce_patch(x, groups):
+    return jnp.concatenate(halves, axis=0) if parts > 1 else halves[0]
+
+
+def scatter_patch(x, groups):
     if groups == 1:
         return x
-    me = lax.axis_index("patch")
-    pieces = x.reshape((groups, x.shape[0] // groups) + x.shape[1:])
-    total = lax.dynamic_index_in_dim(pieces, me, 0, keepdims=False).astype(F32)
-    for k in range(1, groups):
-        piece = lax.dynamic_index_in_dim(pieces, (me + k) % groups, 0, keepdims=False)
-        total = total + shift_patch(piece, k, groups).astype(F32)
-    total = total.astype(BF)
-    return jnp.concatenate([total] + [shift_patch(total, k, groups) for k in range(1, groups)], axis=0)
-
-
-def place_after(position, count, groups):
+    pieces = lax.all_to_all(x, "patch", 0, 0, tiled=True).reshape((groups, x.shape[0] // groups) + x.shape[1:])
+    return jnp.sum(pieces.astype(F32), axis=0).astype(BF)
+
+
+def gather_patch(own, groups):
     if groups == 1:
-        return position
-    size = count // groups
-    me = lax.axis_index("patch")
-    return (me - position // size) % groups * size + position % size
+        return own
+    copies = jnp.broadcast_to(own[None], (groups,) + own.shape).reshape((groups * own.shape[0],) + own.shape[1:])
+    return lax.all_to_all(copies, "patch", 0, 0, tiled=True)
 
 
 def sum_all(x, parts, groups):
@@ -1004,7 +1042,7 @@
 
 def tile_update(scale, grads, states):
     parts, slots, cut, _ = grads.shape
-    per = 2 if slots % 2 == 0 else 1
+    per = max(p for p in range(1, 7) if slots % p == 0)
     tile = pl.BlockSpec((per, BS, BS), lambda i, *_: (i, 0, 0))
     return pl.pallas_call(
         tile_kernel,
@@ -1100,7 +1138,7 @@
     ).reshape(1, V_ALL)
 
     ordered, visible_pix, pos_d, pos_e = order_patches(pixels, shuffle)
-    (x0, h1, qkv, lse, att, mid, h2, act, slope, x1, hn, latent) = encoder_forward(
+    (x0, h1, qkv, lse, out_t, att, mid, h2, act, slope, x1, hn, latent) = encoder_forward(
         tile_rows, vis_len, gathered, vector, visible_pix, pos_d, 2
     )
     (d_h1, d_dqkv, d_att, d_gproj, d_h2, d_du, d_act, d_gdown, d_hn, d_gpred, glat, d_sums) = decoder(
@@ -1123,24 +1161,32 @@
             at += row_tiles * col_tiles
         return buffers
 
-    buffers0 = gradients(
+    after = lax.optimization_barrier
+    buf0 = gradients(
         0, [(d_h2, d_du), (d_act, d_gdown), (d_att, d_gproj), (d_h1, d_dqkv), (d_hn, d_gpred), (hn, glat)]
     )
-    glat, buffers0 = lax.optimization_barrier((glat, buffers0))
+    glat, buf0 = after((glat, buf0))
     gdown, du, grad_mid, gproj, m_sums = encoder_mlp_back(tile_rows, gathered, vector, glat, x1, mid, slope, 2)
-    state0 = reduce_core(buffers0, parts)
-    gdown, du, gproj, halves = lax.optimization_barrier((gdown, du, gproj, state0[0]))
-    state0 = (halves, state0[1])
-    buffers1 = gradients(1, [(h2, du), (act, gdown), (att, gproj)])
-    state0 = reduce_chips(state0, parts, 1)
-    gproj, buffers1 = lax.optimization_barrier((gproj, buffers1))
-    dqkv, gembed, a_sums = encoder_attention_back(
-        tile_rows, vis_len, gathered, vector, gproj, grad_mid, qkv, lse, x0, 2
-    )
-    state1 = reduce_core(buffers1, parts)
-    dqkv, gembed, halves0, halves1 = lax.optimization_barrier((dqkv, gembed, state0[0], state1[0]))
-    state0, state1 = (halves0, state0[1]), (halves1, state1[1])
-
+    half0, left0 = reduce_core(buf0, parts)
+    gdown, du, gproj, half0 = after((gdown, du, gproj, half0))
+    buf1 = gradients(1, [(h2, du), (act, gdown), (att, gproj)])
+    half0, left0 = reduce_chips((half0, left0), parts, 1)
+    gproj, buf1, half0 = after((gproj, buf1, half0))
+
+    def attention_back(gproj, k, given):
+        return encoder_attention_back(
+            tile_rows, vis_len, gathered, vector, gproj, grad_mid, qkv, lse, out_t, x0, 2, (k, 2), given
+        )
+
+    dqkv, gembed, a_sums = attention_back(gproj, 0, ())
+    sum0 = reduce_join((half0, left0), parts)
+    half1, left1 = reduce_core(buf1, parts)
+    gproj, dqkv, gembed, sum0, half1 = after((gproj, dqkv, gembed, sum0, half1))
+    dqkv, gembed, b_sums = attention_back(gproj, 1, (dqkv, gembed))
+    own0 = scatter_patch(sum0, groups)
+    half1, left1 = reduce_chips((half1, left1), parts, 1)
+    dqkv, gembed, own0, half1 = after((dqkv, gembed, own0, half1))
+    a_sums = a_sums + b_sums
     d_sums, m_sums, a_sums = (jnp.sum(s, axis=0) for s in (d_sums, m_sums, a_sums))
 
     def cut(sums, start, size):
@@ -1172,25 +1218,29 @@
     )
     vector_tile = jnp.pad(grad_vector.reshape(parts, own), ((0, 0), (0, rows_cut * BS - own)))
     vector_tile = vector_tile.reshape(parts, rows_cut, BS)
-    buffers2 = gradients(2, [(h1, dqkv), (visible_pix.reshape(-1, PIX), gembed)], vector_tile)
-    first = reduce_end(state0, parts, groups)
-    second = reduce_end(state1, parts, groups)
-    third = reduce_end(reduce_core(buffers2, parts), parts, groups)
-
-    reduced = jnp.concatenate([first, second, third], axis=0)
-    starts = np.cumsum([0] + sizes)
-    where = jnp.zeros(NBLK + 2, jnp.int32)
-    for i, size in enumerate(sizes):
-        here = starts[i] + place_after(jnp.asarray(place_of), size, groups)
-        where = jnp.where(jnp.asarray(chunk_of == i), here, where)
-    wide = reduced.astype(F32)
-    squares = sum_dp(jnp.sum(wide * wide), parts)
-    totals = jnp.stack([jnp.sum(cut(d_sums, DS_LOSS, PIX)) / PIX, jnp.sum(POS - vis_len).astype(F32)])
+    buf2 = gradients(2, [(h1, dqkv), (visible_pix.reshape(-1, PIX), gembed)], vector_tile)
+    own1 = scatter_patch(reduce_join((half1, left1), parts), groups)
+    own2 = scatter_patch(reduce_join(reduce_core(buf2, parts), parts), groups)
+    owns = [own0, own1, own2]
+
+    def squares(x):
+        wide = x.astype(F32)
+        return jnp.sum(wide * wide)
+
+    totals = jnp.stack(
+        [
+            jnp.sum(cut(d_sums, DS_LOSS, PIX)) / PIX,
+            jnp.sum(POS - vis_len).astype(F32),
+            sum(squares(o) for o in owns),
+        ]
+    )
     totals = sum_all(totals, parts, groups)
     loss_sum, masked_count = totals[0], totals[1]
-    grad_norm = jnp.sqrt(squares) / masked_count
+    grad_norm = jnp.sqrt(totals[2]) / masked_count
     scale = jnp.minimum(1.0, CLIP_NORM / grad_norm) / masked_count
 
+    reduced = jnp.concatenate([gather_patch(o, groups) for o in owns], axis=0)
+    where = jnp.asarray(np.cumsum([0] + sizes)[chunk_of] + place_of, jnp.int32)
     slot_rows = reduced[where[jnp.minimum(block_owner, NBLK)]]
     if parts > 1:
         slot_rows = lax.all_to_all(slot_rows, "dp", 0, 0, tiled=True)

time: 745 us -> 746 us (level)
  starting transfers between devices: 82.7 us -> 46.3 us
  waiting for transfers between devices: 235 us -> 265 us
  other arithmetic: 41.2 us -> 54.8 us
  Pallas kernels: 326 us -> 317 us
    all_to_all x0 -> x6, waiting for transfers between devices: none -> 82.4 us  [the longest x3 51.9 us: gather_patch(): return lax.all_to_all(copies, 'patch', 0, 0, tiled=True)]
    ppermute x18 -> x0, waiting for transfers between devices: 59.9 us -> none  [shift_patch(): lax.ppermute(x, 'patch', [(i, (i + shift) % size) for i in range(size)])]
    ppermute x18 -> x0, starting transfers between devices: 51.1 us -> none  [shift_patch(): lax.ppermute(x, 'patch', [(i, (i + shift) % size) for i in range(size)])]
    all_to_all x0 -> x6, starting transfers between devices: none -> 25.3 us  [the longest x3 12.7 us: gather_patch(): return lax.all_to_all(copies, 'patch', 0, 0, tiled=True)]
    pallas_call x4 -> x5, Pallas kernels: 222 us -> 215 us  [group_call(): pl.pallas_call(functools.partial(kernel, start, len(given)), grid_spec=pl...]
    ppermute x21 -> x18, starting transfers between devices: 23.5 us -> 17 us  [swap_bit(): return lax.ppermute(x, 'dp', [(i, i ^ 1 << bit) for i in range(size)])]
    ppermute x21 -> x18, waiting for transfers between devices: 55 us -> 60.6 us  [swap_bit(): return lax.ppermute(x, 'dp', [(i, i ^ 1 << bit) for i in range(size)])]
  transfers between devices with their start and end apart: 43 -> 28, of which waited for: 20 -> 17; matrix products, arithmetic and copies ran while one was open for 6% -> 6% of each run, Pallas kernels for 10% -> 9%
where the time goes in v4:
time: 746 us; the launch traced here: 735 us
  Pallas kernels  317 us (42%)
  waiting for transfers between devices  265 us (36%)
  other arithmetic  54.8 us (7%)
  starting transfers between devices  46.3 us (6%)
  local copies, waits for them, and re-layouts  30.4 us (4%)
  between operations  22.2 us (3%)
    pallas_call x5, Pallas kernels, group_call(): pl.pallas_call(functools.partial(kernel, start, len(given)), grid_spec=pl...  215 us
    all_gather x1, waiting for transfers between devices, shards(): gathered = lax.all_gather(mine, 'dp', axis=0, tiled=True)  114 us
    pallas_call x11, Pallas kernels, weight_grad(): pl.pallas_call(functools.partial(weight_grad_kernel, parts, cut, len(give...  65.7 us
    ppermute x18, waiting for transfers between devices, swap_bit(): return lax.ppermute(x, 'dp', [(i, i ^ 1 << bit) for i in range(size)])  60.6 us
    all_to_all x3, waiting for transfers between devices, gather_patch(): return lax.all_to_all(copies, 'patch', 0, 0, tiled=True)  51.9 us
    all_to_all x3, waiting for transfers between devices, scatter_patch(): lax.all_to_all(x, 'patch', 0, 0, tiled=True)  30.5 us
    convert_element_type x14, other arithmetic, low_sum(): return (a.astype(F32) + b.astype(F32)).astype(BF)  29.3 us
    pallas_call x1, Pallas kernels, tile_update(): pl.pallas_call(tile_kernel, grid_spec=pltpu.PrefetchScalarGridSpec(num_sc...  22.1 us
  transfers between devices with their start and end apart: 28, of which 17 were waited for; matrix products, arithmetic and copies ran while one was open for 6% of the time, Pallas kernels for 9%

profile of v4, /device:TPU:0, one launch (start us, length us, event | category | flops | bytes accessed | tf_op | source)
XLA Modules:
  0.0 735.3 jit_solution(6981660629243833753)
XLA Ops:
  7.2 3.2 convert_element_type.209
  17.2 8.8 %order_patches.1 = (bf16[8,208,768]{2,1,0:T(8,128)(2,1)}, bf16[8,80,768]{2,1,0:T(8,128)(2,1)}, f32[8,80,768]{2,1,0:T(8,128)}, f32[8,208,512]{2,1,0:T(8,128)}) custom-call(s32[8,208,1]{2,1,0:T(8,128)} %copy.58.shuffle_ref, bf16[8,196,768]{2,1,0:T(8,128)(2,1)} %copy.59.pixels_ref, bf16[2,196,768]{2,1,0:T(8,128)(2,1)} %constant.86.clone.sin_d_ref, ...), custom_call_target="tpu_custom_call" | custom-call | tf_op jit(solution)/shard_map/order_patches/pallas_call | solution.py:404
  26.7 114.1 %all-gather.2.cloned.1.call-done.wg_ref = bf16[49280,256]{1,0:T(8,128)(2,1)} async-done(((bf16[6160,256]{1,0:T(8,128)(2,1)}), bf16[49280,256]{1,0:T(8,128)(2,1)}) %all-gather.2.cloned.1.call-update) | async-done | bytes 25231376 | tf_op jit(solution)/shard_map/all_gather | solution.py:1125
  142.5 37.7 %encoder_forward.1 = (f32[640,768]{1,0:T(8,128)}, bf16[640,768]{1,0:T(8,128)(2,1)}, bf16[640,2304]{1,0:T(8,128)(2,1)}, f32[8,3,4,80]{3,2,1,0:T(4,128)}, f32[8,3,...) custom-call(s32[177]{0:T(256)} %fusion.14.row_ref, ...), custom_call_target="tpu_custom_call" | custom-call | flops 10317987840 | bytes 47902720 | tf_op jit(solution)/shard_map/encoder_forward/pallas_call | solution.py:433
  180.2 124.9 %decoder.1 = (bf16[1664,512]{1,0:T(8,128)(2,1)}, bf16[1664,1536]{1,0:T(8,128)(2,1)}, bf16[1664,512]{1,0:T(8,128)(2,1)}, bf16[1664,512]{1,0:T(8,128)(2,1)}, bf16[...) custom-call(s32[177]{0:T(256)} %fusion.14.row_ref, ...), custom_call_target="tpu_custom_call" | custom-call | flops 23555211264 | bytes 64978944 | tf_op jit(solution)/shard_map/decoder/pallas_call | solution.py:433
  305.1 8.4 %weight_grad.11 = (bf16[4,60,32,256]{3,2,1,0:T(8,128)(2,1)}, bf16[4,60,32,256]{3,2,1,0:T(8,128)(2,1)}) custom-call(s32[1]{0:T(128)} %bitcast.9.index_ref, bf16[1664,512]{1,0:T(8,128)(2,1)} %get-tuple-element.120.x_ref, bf16[1664,2048]{1,0:T(8,128)(2,1)} %get-tuple-element.121.g_ref), custom_call_target="tpu_custom_call" | custom-call | flops 3489660928 | bytes 10616832 | tf_op jit(solution)/shard_map/weight_grad/pallas_call | solution.py:904
  313.5 7.9 %weight_grad.12 = (bf16[4,60,32,256]{3,2,1,0:T(8,128)(2,1)}, bf16[4,60,32,256]{3,2,1,0:T(8,128)(2,1)}) custom-call(s32[1]{0:T(128)} %bitcast.9.index_ref, bf16[1664,2048]{1,0:T(8,128)(2,1)} %get-tuple-element.118.x_ref, bf16[1664,512]{1,0:T(8,128)(2,1)} %get-tuple-element.119.g_ref, ...), custom_call_target="tpu_custom_call", output_to_operand_aliasing={{0}: (3, {}), {1}: (4, {})} | custom-call | flops 3489660928 | bytes 10616832 | tf_op jit(solution)/shard_map/weight_grad/pallas_call | solution.py:904
  321.4 4.0 weight_grad.13
  325.3 7.0 weight_grad.14
  332.3 4.8 weight_grad.15
  337.2 3.2 weight_grad.16
  340.6 18.1 %encoder_mlp_back.1 = (bf16[640,768]{1,0:T(8,128)(2,1)}, bf16[640,3072]{1,0:T(8,128)(2,1)}, f32[640,768]{1,0:T(8,128)}, bf16[640,768]{1,0:T(8,128)(2,1)}, f32[8,8192]{1,0:T(8,128)}) custom-call(s32[177]{0:T(256)} %fusion.14.row_ref, bf16[49280,256]{1,0:T(8,128)(2,1)} %all-gather.2.cloned.1.call-done.wg_ref, f32[1,21760]{1,0:T(1,128)} %reshape.145.vec_ref, ...), custom_call_target="tpu_custom_call" | custom-call | flops 6543114240 | bytes 16252928 | tf_op jit(solution)/shard_map/encoder_mlp_back/pallas_call | solution.py:433
  358.7 4.2 add_convert_fusion.1
  370.7 8.0 %weight_grad.17 = (bf16[4,84,32,256]{3,2,1,0:T(8,128)(2,1)}, bf16[4,84,32,256]{3,2,1,0:T(8,128)(2,1)}) custom-call(s32[1]{0:T(128)} %bitcast.9.index_ref, bf16[640,768]{1,0:T(8,128)(2,1)} %get-tuple-element.147.x_ref, bf16[640,3072]{1,0:T(8,128)(2,1)} %get-tuple-element.148.g_ref, ...), custom_call_target="tpu_custom_call", output_to_operand_aliasing={{0}: (3, {}), {1}: (4, {})} | custom-call | flops 3019898880 | bytes 9633792 | tf_op jit(solution)/shard_map/weight_grad/pallas_call | solution.py:904
  378.7 7.9 %weight_grad.18 = (bf16[4,84,32,256]{3,2,1,0:T(8,128)(2,1)}, bf16[4,84,32,256]{3,2,1,0:T(8,128)(2,1)}) custom-call(s32[1]{0:T(128)} %bitcast.9.index_ref, bf16[640,3072]{1,0:T(8,128)(2,1)} %get-tuple-element.145.x_ref, bf16[640,768]{1,0:T(8,128)(2,1)} %get-tuple-element.146.g_ref, ...), custom_call_target="tpu_custom_call", output_to_operand_aliasing={{0}: (3, {}), {1}: (4, {})} | custom-call | flops 3019898880 | bytes 9633792 | tf_op jit(solution)/shard_map/weight_grad/pallas_call | solution.py:904
  386.6 3.7 weight_grad.19
  399.1 17.5 %encoder_attention_back.2 = (bf16[640,2304]{1,0:T(8,128)(2,1)}, bf16[640,768]{1,0:T(8,128)(2,1)}, f32[8,4608]{1,0:T(8,128)}) custom-call(s32[177]{0:T(256)} %fusion.14.row_ref, s32[8]{0:T(128)} %len_ref.7, bf16[49280,256]{1,0:T(8,128)(2,1)} %all-gather.2.cloned.1.call-done.wg_ref, f32[1,21760]{1,0:T(1,128)} %reshape.145.vec_ref, ...), custom_call_target="tpu_custom_call" | custom-call | flops 1509949440 | bytes 4079616 | tf_op jit(solution)/shard_map/encoder_attention_back/pallas_call | solution.py:433
  418.0 7.1 add_convert_fusion
  427.5 17.1 %encoder_attention_back.3 = (bf16[640,2304]{1,0:T(8,128)(2,1)}, bf16[640,768]{1,0:T(8,128)(2,1)}, f32[8,4608]{1,0:T(8,128)}) custom-call(s32[177]{0:T(256)} %fusion.14.row_ref, s32[8]{0:T(128)} %len_ref.7, bf16[49280,256]{1,0:T(8,128)(2,1)} %all-gather.2.cloned.1.call-done.wg_ref, ...), custom_call_target="tpu_custom_call", output_to_operand_aliasing={{0}: (10, {}), {1}: (11, {})} | custom-call | flops 1509949440 | bytes 4079616 | tf_op jit(solution)/shard_map/encoder_attention_back/pallas_call | solution.py:433
  445.7 2.5 slice_bitcast_fusion
  451.6 4.8 all-to-all-start
  457.3 2.4 seed_buffers.3
  459.7 20.1 %collective-permute-done.7 = bf16[2,42,32,256]{3,2,1,0:T(8,128)(2,1)} collective-permute-done((bf16[2,42,32,256]{3,2,1,0:T(8,128)(2,1)}, bf16[2,42,32,256]{3,2,1,0:T(8,128)(2,1)}, u32[]{:S(2)}, u32[]{:S(2)}) %collective-permute-start.7) | collective-permute-done | bytes 1376288 | tf_op jit(solution)/shard_map/ppermute | solution.py:961
  479.8 3.4 fusion
  483.2 3.0 fusion.1
  487.5 7.0 weight_grad.20
  494.5 3.9 weight_grad.21
  503.3 4.8 all-to-all-start.3
  508.2 9.3 %collective-permute-done.8 = bf16[42,32,256]{2,1,0:T(8,128)(2,1)} collective-permute-done((bf16[42,32,256]{2,1,0:T(8,128)(2,1)}, bf16[42,32,256]{2,1,0:T(8,128)(2,1)}, u32[]{:S(2)}, u32[]{:S(2)}) %collective-permute-start.8) | collective-permute-done | bytes 688160 | tf_op jit(solution)/shard_map/ppermute | solution.py:961
  520.4 2.9 add_convert_fusion.2
  528.0 4.7 all-to-all-done.3
  532.7 4.3 all-to-all-start.1
  537.0 3.0 collective-permute-done.11
  540.0 2.5 collective-permute-done.13
  546.7 6.0 collective-permute-done.12
  554.0 15.4 %all-to-all-done.1 = bf16[84,32,256]{2,1,0:T(8,128)(2,1)} async-done(((bf16[84,32,256]{2,1,0:T(8,128)(2,1)}), bf16[84,32,256]{2,1,0:T(8,128)(2,1)}, u32[]{:S(2)}, u32[]{:S(2)}) %all-to-all-start.1) | async-done | bytes 1376288 | tf_op jit(solution)/shard_map/all_to_all | solution.py:995
  569.4 3.5 all-to-all-start.2
  574.5 15.1 %all-to-all-done.2 = bf16[40,32,256]{2,1,0:T(8,128)(2,1)S(1)} async-done(((bf16[40,32,256]{2,1,0:T(8,128)(2,1)}), bf16[40,32,256]{2,1,0:T(8,128)(2,1)S(1)}, u32[]{:S(2)}, u32[]{:S(2)}) %all-to-all-start.2) | async-done | bytes 655392 | tf_op jit(solution)/shard_map/all_to_all | solution.py:995
  590.9 3.7 all-to-all-start.4
  594.7 32.1 %all-to-all-done.4 = bf16[84,32,256]{2,1,0:T(8,128)(2,1)S(1)} async-done(((bf16[84,32,256]{2,1,0:T(8,128)(2,1)}), bf16[84,32,256]{2,1,0:T(8,128)(2,1)S(1)}, u32[]{:S(2)}, u32[]{:S(2)}) %all-to-all-start.4) | async-done | bytes 1376288 | tf_op jit(solution)/shard_map/all_to_all | solution.py:1003
  627.7 4.2 all-to-all-start.5
  633.6 15.2 %all-to-all-done.5 = bf16[40,32,256]{2,1,0:T(8,128)(2,1)} async-done(((bf16[40,32,256]{2,1,0:T(8,128)(2,1)}), bf16[40,32,256]{2,1,0:T(8,128)(2,1)}, u32[]{:S(2)}, u32[]{:S(2)}) %all-to-all-start.5) | async-done | bytes 655392 | tf_op jit(solution)/shard_map/all_to_all | solution.py:1003
  650.9 2.7 gather_fusion.1
  653.6 4.0 all-to-all-start.6
  666.9 3.5 collective-permute-done.15
  670.5 4.4 collective-permute-done.16
  678.1 16.3 %collective-permute-done.18 = f32[3]{0:T(128)S(1)} collective-permute-done((f32[3]{0:T(128)S(1)}, f32[3]{0:T(128)S(1)}, u32[]{:S(2)}, u32[]{:S(2)}) %collective-permute-start.18) | collective-permute-done | bytes 44 | tf_op jit(solution)/shard_map/ppermute | solution.py:961
  705.1 22.1 %tile_update.1 = (f32[24,256,256]{2,1,0:T(8,128)}, f32[24,256,256]{2,1,0:T(8,128)}, f32[24,256,256]{2,1,0:T(8,128)}, f32[24,256,256]{2,1,0:T(8,128)}) custom-call(f32[1]{0:T(128)} %bitcast.44.scale_ref, bf16[8,24,32,256]{3,2,1,0:T(8,128)(2,1)} %bitcast.110, f32[24,256,256]{2,1,0:T(8,128)} %w_ref.1, f32[24,256,256]{2,1,0:T(8,128)} %left_stat_ref.1, ...), custom_call_target="tpu_custom_call" | custom-call | tf_op jit(solution)/shard_map/tile_update/pallas_call | solution.py:1047
  (174 shorter events, 79.0 us)
Async XLA Ops:
  7.2 3.3 copy-start.17
  7.2 133.7 %all-gather.2.cloned.1.call-start = ((), (), s32[]{:S(2)}) async-start(), calls=%async_computation.7 | async-start | bytes 28385280 | tf_op jit(solution)/shard_map/all_gather | solution.py:1125
  12.4 1.7 copy-start.12
  12.4 3.6 copy-start.20
  15.9 10.1 %copy-start.21 = (s32[192]{0:T(256)S(1)}, s32[192]{0:T(256)}, u32[]{:S(2)}) copy-start(s32[192]{0:T(256)} %param.18) | copy-start | bytes 2308
  340.3 18.4 %collective-permute-start = (bf16[4,60,32,256]{3,2,1,0:T(8,128)(2,1)}, bf16[4,60,32,256]{3,2,1,0:T(8,128)(2,1)}, u32[]{:S(2)}, u32[]{:S(2)}) collective-permute-start(bf16[4,60,32,256]{3,2,1,0:T(8,128)(2,1)} %get-tuple-element.142), channel_id=1, source_target_pairs={{0,4},{4,0},{8,12},{12,8},{16,20},{20,16},{24,28},{28,24},{1,5},{5... | collective-permute-start | bytes 11796488 | tf_op jit(solution)/shard_map/ppermute | solution.py:961
  340.6 18.1 %copy-start.1 = (bf16[4,60,32,256]{3,2,1,0:T(8,128)(2,1)S(1)}, bf16[4,60,32,256]{3,2,1,0:T(8,128)(2,1)}, u32[]{:S(2)}) copy-start(bf16[4,60,32,256]{3,2,1,0:T(8,128)(2,1)} %get-tuple-element.141) | copy-start | bytes 11796484
  364.6 25.7 %collective-permute-start.2 = (bf16[2,30,32,256]{3,2,1,0:T(8,128)(2,1)S(1)}, bf16[2,30,32,256]{3,2,1,0:T(8,128)(2,1)}, u32[]{:S(2)}, u32[]{:S(2)}) collective-permute-start(bf16[2,30,32,256]{3,2,1,0:T(8,128)(2,1)S(1)} %slice_bitcast_fusion.2), channel_id=1, source_target_pairs={{0,16},{4,20},{8,24},{12,28},{16,0},{20,4},{24,8},{28,12},{1,17},{... | collective-permute-start | bytes 2949128 | tf_op jit(solution)/shard_map/ppermute | solution.py:961
  366.0 26.2 %collective-permute-start.1 = (bf16[2,30,32,256]{3,2,1,0:T(8,128)(2,1)}, bf16[2,30,32,256]{3,2,1,0:T(8,128)(2,1)}, u32[]{:S(2)}, u32[]{:S(2)}) collective-permute-start(bf16[2,30,32,256]{3,2,1,0:T(8,128)(2,1)} %slice_bitcast_fusion.3), channel_id=1, source_target_pairs={{0,8},{4,12},{8,0},{12,4},{16,24},{20,28},{24,16},{28,20},{1,9},{5... | collective-permute-start | bytes 2949128 | tf_op jit(solution)/shard_map/ppermute | solution.py:961
  393.8 24.2 %collective-permute-start.5 = (bf16[4,84,32,256]{3,2,1,0:T(8,128)(2,1)}, bf16[4,84,32,256]{3,2,1,0:T(8,128)(2,1)}, u32[]{:S(2)}, u32[]{:S(2)}) collective-permute-start(bf16[4,84,32,256]{3,2,1,0:T(8,128)(2,1)} %get-tuple-element.170), channel_id=1, source_target_pairs={{0,4},{4,0},{8,12},{12,8},{16,20},{20,16},{24,28},{28,24},{1,5},{5... | collective-permute-start | bytes 16515080 | tf_op jit(solution)/shard_map/ppermute | solution.py:961
  394.8 21.8 %collective-permute-start.3 = (bf16[30,32,256]{2,1,0:T(8,128)(2,1)S(1)}, bf16[30,32,256]{2,1,0:T(8,128)(2,1)S(1)}, u32[]{:S(2)}, u32[]{:S(2)}) collective-permute-start(bf16[30,32,256]{2,1,0:T(8,128)(2,1)S(1)} %slice_bitcast_fusion.11), channel_id=1, source_target_pairs={{0,16},{4,20},{8,24},{12,28},{16,0},{20,4},{24,8},{28,12},{1,17},{... | collective-permute-start | bytes 1474568 | tf_op jit(solution)/shard_map/ppermute | solution.py:961
  396.4 20.4 %collective-permute-start.4 = (bf16[30,32,256]{2,1,0:T(8,128)(2,1)S(1)}, bf16[30,32,256]{2,1,0:T(8,128)(2,1)S(1)}, u32[]{:S(2)}, u32[]{:S(2)}) collective-permute-start(bf16[30,32,256]{2,1,0:T(8,128)(2,1)S(1)} %slice_bitcast_fusion.10), channel_id=1, source_target_pairs={{0,8},{4,12},{8,0},{12,4},{16,24},{20,28},{24,16},{28,20},{1,9},{5... | collective-permute-start | bytes 1474568 | tf_op jit(solution)/shard_map/ppermute | solution.py:961
  399.1 17.6 %copy-start.11 = (bf16[2,30,32,256]{3,2,1,0:T(8,128)(2,1)S(1)}, bf16[2,30,32,256]{3,2,1,0:T(8,128)(2,1)}, u32[]{:S(2)}) copy-start(bf16[2,30,32,256]{3,2,1,0:T(8,128)(2,1)} %copy-done.10) | copy-start | bytes 2949124
  427.5 17.2 %copy-start.15 = (f32[8,4608]{1,0:T(8,128)S(1)}, f32[8,4608]{1,0:T(8,128)}, u32[]{:S(2)}) copy-start(f32[8,4608]{1,0:T(8,128)} %get-tuple-element.185) | copy-start | bytes 442372
  427.5 18.1 %copy-start.16 = (f32[20480]{0:T(1024)S(1)}, f32[20480]{0:T(1024)}, u32[]{:S(2)}) copy-start(f32[20480]{0:T(1024)} %custom-call) | copy-start | bytes 245764
  448.2 31.5 %collective-permute-start.7 = (bf16[2,42,32,256]{3,2,1,0:T(8,128)(2,1)}, bf16[2,42,32,256]{3,2,1,0:T(8,128)(2,1)}, u32[]{:S(2)}, u32[]{:S(2)}) collective-permute-start(bf16[2,42,32,256]{3,2,1,0:T(8,128)(2,1)} %slice_bitcast_fusion), channel_id=1, source_target_pairs={{0,16},{4,20},{8,24},{12,28},{16,0},{20,4},{24,8},{28,12},{1,17},{... | collective-permute-start | bytes 4128776 | tf_op jit(solution)/shard_map/ppermute | solution.py:961
  449.8 33.4 %collective-permute-start.6 = (bf16[2,42,32,256]{3,2,1,0:T(8,128)(2,1)}, bf16[2,42,32,256]{3,2,1,0:T(8,128)(2,1)}, u32[]{:S(2)}, u32[]{:S(2)}) collective-permute-start(bf16[2,42,32,256]{3,2,1,0:T(8,128)(2,1)} %slice_bitcast_fusion.1), channel_id=1, source_target_pairs={{0,8},{4,12},{8,0},{12,4},{16,24},{20,28},{24,16},{28,20},{1,9},{5... | collective-permute-start | bytes 4128776 | tf_op jit(solution)/shard_map/ppermute | solution.py:961
  451.6 34.6 %all-to-all-start = ((bf16[60,32,256]{2,1,0:T(8,128)(2,1)}), bf16[60,32,256]{2,1,0:T(8,128)(2,1)}, u32[]{:S(2)}, u32[]{:S(2)}) async-start(bf16[60,32,256]{2,1,0:T(8,128)(2,1)} %pad_maximum_fusion.3), calls=%async_computation | async-start | bytes 1966080 | tf_op jit(solution)/shard_map/all_to_all | solution.py:995
  487.5 14.7 %copy-start.13 = (bf16[15,32,256]{2,1,0:T(8,128)(2,1)}, bf16[15,32,256]{2,1,0:T(8,128)(2,1)S(1)}, u32[]{:S(2)}) copy-start(bf16[15,32,256]{2,1,0:T(8,128)(2,1)S(1)} %reduce_sum.121) | copy-start | bytes 737284
  494.5 3.9 copy-start.8
  494.5 5.2 copy-start.7
  498.4 22.0 %collective-permute-start.10 = (bf16[4,40,32,256]{3,2,1,0:T(8,128)(2,1)}, bf16[4,40,32,256]{3,2,1,0:T(8,128)(2,1)}, u32[]{:S(2)}, u32[]{:S(2)}) collective-permute-start(bf16[4,40,32,256]{3,2,1,0:T(8,128)(2,1)} %get-tuple-element.193), channel_id=1, source_target_pairs={{0,4},{4,0},{8,12},{12,8},{16,20},{20,16},{24,28},{28,24},{1,5},{5... | collective-permute-start | bytes 7864328 | tf_op jit(solution)/shard_map/ppermute | solution.py:961
  499.3 18.2 %collective-permute-start.8 = (bf16[42,32,256]{2,1,0:T(8,128)(2,1)}, bf16[42,32,256]{2,1,0:T(8,128)(2,1)}, u32[]{:S(2)}, u32[]{:S(2)}) collective-permute-start(bf16[42,32,256]{2,1,0:T(8,128)(2,1)} %slice_bitcast_fusion.5), channel_id=1, source_target_pairs={{0,16},{4,20},{8,24},{12,28},{16,0},{20,4},{24,8},{28,12},{1,17},{... | collective-permute-start | bytes 2064392 | tf_op jit(solution)/shard_map/ppermute | solution.py:961
  500.6 18.4 %collective-permute-start.9 = (bf16[42,32,256]{2,1,0:T(8,128)(2,1)}, bf16[42,32,256]{2,1,0:T(8,128)(2,1)S(1)}, u32[]{:S(2)}, u32[]{:S(2)}) collective-permute-start(bf16[42,32,256]{2,1,0:T(8,128)(2,1)} %slice_bitcast_fusion.4), channel_id=1, source_target_pairs={{0,8},{4,12},{8,0},{12,4},{16,24},{20,28},{24,16},{28,20},{1,9},{5... | collective-permute-start | bytes 2064392 | tf_op jit(solution)/shard_map/ppermute | solution.py:961
  503.3 17.1 %copy-start.2 = (bf16[4,40,32,256]{3,2,1,0:T(8,128)(2,1)S(1)}, bf16[4,40,32,256]{3,2,1,0:T(8,128)(2,1)}, u32[]{:S(2)}) copy-start(bf16[4,40,32,256]{3,2,1,0:T(8,128)(2,1)} %get-tuple-element.192) | copy-start | bytes 7864324
  503.3 29.4 %all-to-all-start.3 = ((bf16[60,32,256]{2,1,0:T(8,128)(2,1)}), bf16[60,32,256]{2,1,0:T(8,128)(2,1)}, u32[]{:S(2)}, u32[]{:S(2)}) async-start(bf16[60,32,256]{2,1,0:T(8,128)(2,1)} %bitcast.115), calls=%async_computation.3 | async-start | bytes 1966080 | tf_op jit(solution)/shard_map/all_to_all | solution.py:1003
  523.4 1.6 copy-start.4
  523.5 16.5 %collective-permute-start.11 = (bf16[2,20,32,256]{3,2,1,0:T(8,128)(2,1)S(1)}, bf16[2,20,32,256]{3,2,1,0:T(8,128)(2,1)}, u32[]{:S(2)}, u32[]{:S(2)}) collective-permute-start(bf16[2,20,32,256]{3,2,1,0:T(8,128)(2,1)S(1)} %slice_bitcast_fusion.8), channel_id=1, source_target_pairs={{0,8},{4,12},{8,0},{12,4},{16,24},{20,28},{24,16},{28,20},{1,9},{5... | collective-permute-start | bytes 1966088 | tf_op jit(solution)/shard_map/ppermute | solution.py:961
  525.9 16.6 %copy-start.5 = (bf16[4,40,32,256]{3,2,1,0:T(8,128)(2,1)S(1)}, bf16[4,40,32,256]{3,2,1,0:T(8,128)(2,1)}, u32[]{:S(2)}) copy-start(bf16[4,40,32,256]{3,2,1,0:T(8,128)(2,1)} %copy-done.4) | copy-start | bytes 7864324
  525.9 16.6 %collective-permute-start.13 = (bf16[2,20,32,256]{3,2,1,0:T(8,128)(2,1)}, bf16[2,20,32,256]{3,2,1,0:T(8,128)(2,1)}, u32[]{:S(2)}, u32[]{:S(2)}) collective-permute-start(bf16[2,20,32,256]{3,2,1,0:T(8,128)(2,1)} %slice_bitcast_fusion.6), channel_id=1, source_target_pairs={{0,16},{4,20},{8,24},{12,28},{16,0},{20,4},{24,8},{28,12},{1,17},{... | collective-permute-start | bytes 1966088 | tf_op jit(solution)/shard_map/ppermute | solution.py:961
  532.7 36.6 %all-to-all-start.1 = ((bf16[84,32,256]{2,1,0:T(8,128)(2,1)}), bf16[84,32,256]{2,1,0:T(8,128)(2,1)}, u32[]{:S(2)}, u32[]{:S(2)}) async-start(bf16[84,32,256]{2,1,0:T(8,128)(2,1)} %pad_maximum_fusion.2), calls=%async_computation.1 | async-start | bytes 2752512 | tf_op jit(solution)/shard_map/all_to_all | solution.py:995
  544.3 8.4 %collective-permute-start.12 = (bf16[20,32,256]{2,1,0:T(8,128)(2,1)S(1)}, bf16[20,32,256]{2,1,0:T(8,128)(2,1)S(1)}, u32[]{:S(2)}, u32[]{:S(2)}) collective-permute-start(bf16[20,32,256]{2,1,0:T(8,128)(2,1)S(1)} %slice_bitcast_fusion.14), channel_id=1, source_target_pairs={{0,16},{4,20},{8,24},{12,28},{16,0},{20,4},{24,8},{28,12},{1,17},{... | collective-permute-start | bytes 983048 | tf_op jit(solution)/shard_map/ppermute | solution.py:961
  545.1 7.9 %collective-permute-start.14 = (bf16[20,32,256]{2,1,0:T(8,128)(2,1)S(1)}, bf16[20,32,256]{2,1,0:T(8,128)(2,1)S(1)}, u32[]{:S(2)}, u32[]{:S(2)}) collective-permute-start(bf16[20,32,256]{2,1,0:T(8,128)(2,1)S(1)} %slice_bitcast_fusion.12), channel_id=1, source_target_pairs={{0,8},{4,12},{8,0},{12,4},{16,24},{20,28},{24,16},{28,20},{1,9},{5... | collective-permute-start | bytes 983048 | tf_op jit(solution)/shard_map/ppermute | solution.py:961
  569.4 20.2 %all-to-all-start.2 = ((bf16[40,32,256]{2,1,0:T(8,128)(2,1)}), bf16[40,32,256]{2,1,0:T(8,128)(2,1)S(1)}, u32[]{:S(2)}, u32[]{:S(2)}) async-start(bf16[40,32,256]{2,1,0:T(8,128)(2,1)} %pad_maximum_fusion.4), calls=%async_computation.2 | async-start | bytes 1310720 | tf_op jit(solution)/shard_map/all_to_all | solution.py:995
  590.9 41.1 %copy-start = (s32[179]{0:T(256)S(1)}, s32[179]{0:T(256)}, u32[]{:S(2)}) copy-start(s32[179]{0:T(256)} %constant.88.clone) | copy-start | bytes 2152
  590.9 35.9 %all-to-all-start.4 = ((bf16[84,32,256]{2,1,0:T(8,128)(2,1)}), bf16[84,32,256]{2,1,0:T(8,128)(2,1)S(1)}, u32[]{:S(2)}, u32[]{:S(2)}) async-start(bf16[84,32,256]{2,1,0:T(8,128)(2,1)} %bitcast.46), calls=%async_computation.4 | async-start | bytes 2752512 | tf_op jit(solution)/shard_map/all_to_all | solution.py:1003
  594.7 38.9 %copy-start.14 = (bf16[10,32,256]{2,1,0:T(8,128)(2,1)}, bf16[10,32,256]{2,1,0:T(8,128)(2,1)S(1)}, u32[]{:S(2)}) copy-start(bf16[10,32,256]{2,1,0:T(8,128)(2,1)S(1)} %reduce_sum.127) | copy-start | bytes 491524
  626.7 6.9 copy-start.9
  627.7 21.0 %all-to-all-start.5 = ((bf16[40,32,256]{2,1,0:T(8,128)(2,1)}), bf16[40,32,256]{2,1,0:T(8,128)(2,1)}, u32[]{:S(2)}, u32[]{:S(2)}) async-start(bf16[40,32,256]{2,1,0:T(8,128)(2,1)} %bitcast.47), calls=%async_computation.5 | async-start | bytes 1310720 | tf_op jit(solution)/shard_map/all_to_all | solution.py:1003
  653.6 48.5 %copy-start.18 = (f32[2560]{0:T(1024)S(1)}, f32[2560]{0:T(1024)}, u32[]{:S(2)}) copy-start(f32[2560]{0:T(1024)} %param.20) | copy-start | bytes 30724
  653.6 48.5 %copy-start.19 = (f32[2560]{0:T(1024)S(1)}, f32[2560]{0:T(1024)}, u32[]{:S(2)}) copy-start(f32[2560]{0:T(1024)} %param.22) | copy-start | bytes 30724
  653.6 49.8 %all-to-all-start.6 = ((bf16[192,32,256]{2,1,0:T(8,128)(2,1)}), bf16[192,32,256]{2,1,0:T(8,128)(2,1)S(1)}, u32[]{:S(2)}, u32[]{:S(2)}) async-start(bf16[192,32,256]{2,1,0:T(8,128)(2,1)} %gather_fusion.1), calls=%async_computation.6 | async-start | bytes 6291456 | tf_op jit(solution)/shard_map/all_to_all | solution.py:1246
  666.9 3.5 collective-permute-start.15
  670.5 4.4 collective-permute-start.16
  675.0 1.1 collective-permute-start.17
  676.2 18.3 %collective-permute-start.18 = (f32[3]{0:T(128)S(1)}, f32[3]{0:T(128)S(1)}, u32[]{:S(2)}, u32[]{:S(2)}) collective-permute-start(f32[3]{0:T(128)S(1)} %add.142), channel_id=1, source_target_pairs={{0,8},{4,12},{8,0},{12,4},{16,24},{20,28},{24,16},{28,20},{1,9},{5... | collective-permute-start | bytes 44 | tf_op jit(solution)/shard_map/ppermute | solution.py:961
  694.5 3.5 collective-permute-start.19
  703.4 1.6 copy-start.3
  (2 other events, 2.2 us)
Sparse Core Ops, SparseCore 0:
  12.5 128.2 all-gather.1

commit v5 on v4

--- a/solution.py
+++ b/solution.py
@@ -40,6 +40,7 @@
 BF = jnp.bfloat16
 F32 = jnp.float32
 VMEM_LIMIT = 60 * 1024 * 1024
+SMALL = pl.CostEstimate(flops=1000, bytes_accessed=1000, transcendentals=0)
 
 T_EMBED, T_EQKV, T_EOUT, T_EUP, T_EDOWN, T_PROJ = 0, 9, 36, 45, 81, 117
 T_DQKV, T_DOUT, T_DUP, T_DDOWN, T_HEAD = 123, 135, 139, 155, 171
@@ -417,7 +418,7 @@
     )(ids, pixels, jnp.asarray(sinusoid_parts(POS, D)), jnp.asarray(sinusoid_parts(POS, E)))
 
 
-def group_call(kernel, steps, prefetch, in_arrays, out_list, scratch, name, flops, share=(0, 1), given=()):
+def group_call(kernel, steps, prefetch, in_arrays, out_list, scratch, name, share=(0, 1), given=()):
     count = steps // share[1]
     start = share[0] * count
 
@@ -444,11 +445,7 @@
         compiler_params=pltpu.CompilerParams(
             vmem_limit_bytes=VMEM_LIMIT, dimension_semantics=("arbitrary",)
         ),
-        cost_estimate=pl.CostEstimate(
-            flops=flops // share[1],
-            bytes_accessed=sum(math.prod(s) * jnp.dtype(t).itemsize for s, t, _ in out_list) * 2 // share[1],
-            transcendentals=0,
-        ),
+        cost_estimate=SMALL,
         name=name,
     )(*prefetch, *[a for a, _ in in_arrays], *given)
 
@@ -539,7 +536,6 @@
         outs,
         scratch + [pltpu.SemaphoreType.DMA((6,))],
         "encoder_forward",
-        2 * rows * (PIX * D + 4 * D * D + 2 * D * FE + D * E),
     )
 
 
@@ -728,7 +724,6 @@
         outs,
         scratch,
         "decoder",
-        4 * rows * (4 * E * E + 2 * E * FD + E * PIX),
     )
 
 
@@ -801,7 +796,6 @@
         outs,
         scratch,
         "encoder_mlp_back",
-        2 * rows * (D * E + 2 * D * FE),
     )
 
 
@@ -864,7 +858,6 @@
         outs,
         scratch + [pltpu.SemaphoreType.DMA((2,))],
         "encoder_attention_back",
-        2 * rows * 4 * D * D,
         share,
         given,
     )
@@ -920,11 +913,7 @@
         out_shape=[shape] * held,
         input_output_aliases={3 + i: i for i in range(len(given))},
         compiler_params=pltpu.CompilerParams(vmem_limit_bytes=VMEM_LIMIT),
-        cost_estimate=pl.CostEstimate(
-            flops=2 * rows * width * g.shape[1],
-            bytes_accessed=2 * rows * (width + g.shape[1]) + 2 * width * g.shape[1],
-            transcendentals=0,
-        ),
+        cost_estimate=SMALL,
         name="weight_grad",
     )(index, x, g, *given)
 
@@ -963,7 +952,8 @@
 
 def reduce_core(buffers, parts):
     if parts == 1:
-        return [buffers[0][0]] * 2, []
+        whole, count = buffers[0][0], buffers[0].shape[1]
+        return [whole[: count // 2], whole[count // 2 :]], [[], []]
     whole = low_sum(buffers[0], swap_bit(buffers[1], 0, parts))
     bits = list(range(parts.bit_length() - 2, 0, -1))
     whole = whole.reshape((2,) * len(bits) + whole.shape[1:])
@@ -973,7 +963,7 @@
 
 def reduce_chips(state, parts, steps):
     halves, left = list(state[0]), list(state[1])
-    for half in range(2 if parts > 1 else 0):
+    for half in range(2):
         for _ in range(min(steps, len(left[half]))):
             bit = left[half][-1 if half == 0 else 0]
             axis = left[half].index(bit)
@@ -984,23 +974,30 @@
     return halves, left
 
 
-def reduce_join(state, parts):
-    halves, _ = reduce_chips(state, parts, 99)
-    return jnp.concatenate(halves, axis=0) if parts > 1 else halves[0]
-
-
-def scatter_patch(x, groups):
+def patch_steps(groups):
+    middle = groups // 2 - 1
+
+    def inwards(k, x):
+        return low_sum(x, lax.ppermute(x, "patch", [(k, k + 1), (groups - 1 - k, groups - 2 - k)]))
+
+    def across(x):
+        return low_sum(x, lax.ppermute(x, "patch", [(middle, middle + 1), (middle + 1, middle)]))
+
+    def outwards(k, x):
+        got = lax.ppermute(x, "patch", [(k + 1, k), (groups - 2 - k, groups - 1 - k)])
+        me = lax.axis_index("patch")
+        return jnp.where((me == k) | (me == groups - 1 - k), got, x)
+
     if groups == 1:
-        return x
-    pieces = lax.all_to_all(x, "patch", 0, 0, tiled=True).reshape((groups, x.shape[0] // groups) + x.shape[1:])
-    return jnp.sum(pieces.astype(F32), axis=0).astype(BF)
-
-
-def gather_patch(own, groups):
-    if groups == 1:
-        return own
-    copies = jnp.broadcast_to(own[None], (groups,) + own.shape).reshape((groups * own.shape[0],) + own.shape[1:])
-    return lax.all_to_all(copies, "patch", 0, 0, tiled=True)
+        return []
+    steps = [functools.partial(inwards, k) for k in range(middle)] + [across]
+    return steps + [functools.partial(outwards, k) for k in reversed(range(middle))]
+
+
+def sum_patch(x, steps):
+    for step in steps:
+        x = step(x)
+    return x
 
 
 def sum_all(x, parts, groups):
@@ -1179,13 +1176,12 @@
         )
 
     dqkv, gembed, a_sums = attention_back(gproj, 0, ())
-    sum0 = reduce_join((half0, left0), parts)
+    half0, left0 = reduce_chips((half0, left0), parts, 99)
     half1, left1 = reduce_core(buf1, parts)
-    gproj, dqkv, gembed, sum0, half1 = after((gproj, dqkv, gembed, sum0, half1))
+    gproj, dqkv, gembed, half0, half1 = after((gproj, dqkv, gembed, half0, half1))
     dqkv, gembed, b_sums = attention_back(gproj, 1, (dqkv, gembed))
-    own0 = scatter_patch(sum0, groups)
     half1, left1 = reduce_chips((half1, left1), parts, 1)
-    dqkv, gembed, own0, half1 = after((dqkv, gembed, own0, half1))
+    dqkv, gembed, b_sums, half0, half1 = after((dqkv, gembed, b_sums, half0, half1))
     a_sums = a_sums + b_sums
     d_sums, m_sums, a_sums = (jnp.sum(s, axis=0) for s in (d_sums, m_sums, a_sums))
 
@@ -1219,9 +1215,13 @@
     vector_tile = jnp.pad(grad_vector.reshape(parts, own), ((0, 0), (0, rows_cut * BS - own)))
     vector_tile = vector_tile.reshape(parts, rows_cut, BS)
     buf2 = gradients(2, [(h1, dqkv), (visible_pix.reshape(-1, PIX), gembed)], vector_tile)
-    own1 = scatter_patch(reduce_join((half1, left1), parts), groups)
-    own2 = scatter_patch(reduce_join(reduce_core(buf2, parts), parts), groups)
-    owns = [own0, own1, own2]
+    half1, _ = reduce_chips((half1, left1), parts, 99)
+    steps = patch_steps(groups)
+    half0 = [sum_patch(x, steps[:1]) for x in half0]
+    buf2, half0, half1 = after((buf2, half0, half1))
+    half2, _ = reduce_chips(reduce_core(buf2, parts), parts, 99)
+    pieces = [sum_patch(x, steps[1:]) for x in half0] + [sum_patch(x, steps) for x in half1 + half2]
+    mine = jnp.where(lax.axis_index("patch") == 0, 1.0, 0.0)
 
     def squares(x):
         wide = x.astype(F32)
@@ -1231,7 +1231,7 @@
         [
             jnp.sum(cut(d_sums, DS_LOSS, PIX)) / PIX,
             jnp.sum(POS - vis_len).astype(F32),
-            sum(squares(o) for o in owns),
+            sum(squares(x) for x in pieces) * mine,
         ]
     )
     totals = sum_all(totals, parts, groups)
@@ -1239,7 +1239,7 @@
     grad_norm = jnp.sqrt(totals[2]) / masked_count
     scale = jnp.minimum(1.0, CLIP_NORM / grad_norm) / masked_count
 
-    reduced = jnp.concatenate([gather_patch(o, groups) for o in owns], axis=0)
+    reduced = jnp.concatenate(pieces, axis=0)
     where = jnp.asarray(np.cumsum([0] + sizes)[chunk_of] + place_of, jnp.int32)
     slot_rows = reduced[where[jnp.minimum(block_owner, NBLK)]]
     if parts > 1:

time: 746 us -> 695 us (0.932)
  waiting for transfers between devices: 265 us -> 203 us
  local copies, waits for them, and re-layouts: 30.4 us -> 38.5 us
  Pallas kernels: 317 us -> 309 us
    all_to_all x6 -> x0, waiting for transfers between devices: 82.4 us -> none  [the longest x3 51.9 us: gather_patch(): return lax.all_to_all(copies, 'patch', 0, 0, tiled=True)]
    ppermute x0 -> x18, waiting for transfers between devices: none -> 44 us  [the longest x6 23.4 us: inwards(): lax.ppermute(x, 'patch', [(k, k + 1), (groups - 1 - k, groups - 2 - k)])]
    ppermute x0 -> x18, starting transfers between devices: none -> 30.5 us  [the longest x6 17 us: inwards(): lax.ppermute(x, 'patch', [(k, k + 1), (groups - 1 - k, groups - 2 - k)])]
    all_to_all x6 -> x0, starting transfers between devices: 25.3 us -> none  [the longest x3 12.7 us: gather_patch(): return lax.all_to_all(copies, 'patch', 0, 0, tiled=True)]
    ppermute x18, waiting for transfers between devices: 60.6 us -> 37.4 us  [swap_bit(): return lax.ppermute(x, 'dp', [(i, i ^ 1 << bit) for i in range(size)])]
    unnamed x63 -> x79, local copies, waits for them, and re-layouts: 8.88 us -> 23.5 us
    pallas_call x5, Pallas kernels: 215 us -> 207 us  [group_call(): pl.pallas_call(functools.partial(kernel, start, len(given)), grid_spec=pl...]
    convert_element_type x14 -> x26, other arithmetic: 29.3 us -> 35.3 us  [low_sum(): return (a.astype(F32) + b.astype(F32)).astype(BF)]
  transfers between devices with their start and end apart: 28 -> 40, of which waited for: 17 -> 17; matrix products, arithmetic and copies ran while one was open for 6% -> 9% of each run, Pallas kernels for 9% -> 14%
where the time goes in v5:
time: 695 us; the launch traced here: 686 us
  Pallas kernels  309 us (44%)
  waiting for transfers between devices  203 us (29%)
  other arithmetic  59.3 us (9%)
  starting transfers between devices  52.3 us (8%)
  local copies, waits for them, and re-layouts  38.5 us (6%)
  between operations  24.4 us (4%)
    pallas_call x5, Pallas kernels, group_call(): pl.pallas_call(functools.partial(kernel, start, len(given)), grid_spec=pl...  207 us
    all_gather x1, waiting for transfers between devices, shards(): gathered = lax.all_gather(mine, 'dp', axis=0, tiled=True)  114 us
    pallas_call x11, Pallas kernels, weight_grad(): pl.pallas_call(functools.partial(weight_grad_kernel, parts, cut, len(give...  65.4 us
    ppermute x18, waiting for transfers between devices, swap_bit(): return lax.ppermute(x, 'dp', [(i, i ^ 1 << bit) for i in range(size)])  37.4 us
    convert_element_type x26, other arithmetic, low_sum(): return (a.astype(F32) + b.astype(F32)).astype(BF)  35.3 us
    unnamed x79, local copies, waits for them, and re-layouts  23.5 us
    ppermute x6, waiting for transfers between devices, inwards(): lax.ppermute(x, 'patch', [(k, k + 1), (groups - 1 - k, groups - 2 - k)])  23.4 us
    pallas_call x1, Pallas kernels, tile_update(): pl.pallas_call(tile_kernel, grid_spec=pltpu.PrefetchScalarGridSpec(num_sc...  22.1 us
  transfers between devices with their start and end apart: 40, of which 17 were waited for; matrix products, arithmetic and copies ran while one was open for 9% of the time, Pallas kernels for 14%

profile of v5, /device:TPU:0, one launch (start us, length us, event | category | flops | bytes accessed | tf_op | source)
XLA Modules:
  0.0 685.6 jit_solution(707538530102109110)
XLA Ops:
  7.2 3.2 convert_element_type.320
  17.2 8.8 %order_patches.1 = (bf16[8,208,768]{2,1,0:T(8,128)(2,1)}, bf16[8,80,768]{2,1,0:T(8,128)(2,1)}, f32[8,80,768]{2,1,0:T(8,128)}, f32[8,208,512]{2,1,0:T(8,128)}) custom-call(s32[8,208,1]{2,1,0:T(8,128)} %copy.57.shuffle_ref, bf16[8,196,768]{2,1,0:T(8,128)(2,1)} %copy.58.pixels_ref, bf16[2,196,768]{2,1,0:T(8,128)(2,1)} %constant.88.clone.sin_d_ref, ...), custom_call_target="tpu_custom_call" | custom-call | tf_op jit(solution)/shard_map/order_patches/pallas_call | solution.py:405
  26.7 114.1 %all-gather.2.cloned.1.call-done.wg_ref = bf16[49280,256]{1,0:T(8,128)(2,1)} async-done(((bf16[6160,256]{1,0:T(8,128)(2,1)}), bf16[49280,256]{1,0:T(8,128)(2,1)}) %all-gather.2.cloned.1.call-update) | async-done | bytes 25231376 | tf_op jit(solution)/shard_map/all_gather | solution.py:1122
  142.5 37.7 %encoder_forward.1 = (f32[640,768]{1,0:T(8,128)}, bf16[640,768]{1,0:T(8,128)(2,1)}, bf16[640,2304]{1,0:T(8,128)(2,1)}, f32[8,3,4,80]{3,2,1,0:T(4,128)}, f32[8,3,...) custom-call(s32[177]{0:T(256)} %fusion.19.row_ref, ...), custom_call_target="tpu_custom_call" | custom-call | flops 1000 | bytes 1000 | tf_op jit(solution)/shard_map/encoder_forward/pallas_call | solution.py:434
  180.2 117.1 %decoder.1 = (bf16[1664,512]{1,0:T(8,128)(2,1)}, bf16[1664,1536]{1,0:T(8,128)(2,1)}, bf16[1664,512]{1,0:T(8,128)(2,1)}, bf16[1664,512]{1,0:T(8,128)(2,1)}, bf16[...) custom-call(s32[177]{0:T(256)} %fusion.19.row_ref, ...), custom_call_target="tpu_custom_call" | custom-call | flops 1000 | bytes 1000 | tf_op jit(solution)/shard_map/decoder/pallas_call | solution.py:434
  297.3 8.3 %weight_grad.11 = (bf16[4,60,32,256]{3,2,1,0:T(8,128)(2,1)}, bf16[4,60,32,256]{3,2,1,0:T(8,128)(2,1)}) custom-call(s32[1]{0:T(128)} %bitcast.9.index_ref, bf16[1664,512]{1,0:T(8,128)(2,1)} %get-tuple-element.129.x_ref, bf16[1664,2048]{1,0:T(8,128)(2,1)} %get-tuple-element.130.g_ref), custom_call_target="tpu_custom_call" | custom-call | flops 1000 | bytes 1000 | tf_op jit(solution)/shard_map/weight_grad/pallas_call | solution.py:897
  305.6 7.9 %weight_grad.12 = (bf16[4,60,32,256]{3,2,1,0:T(8,128)(2,1)}, bf16[4,60,32,256]{3,2,1,0:T(8,128)(2,1)}) custom-call(s32[1]{0:T(128)} %bitcast.9.index_ref, bf16[1664,2048]{1,0:T(8,128)(2,1)} %get-tuple-element.127.x_ref, bf16[1664,512]{1,0:T(8,128)(2,1)} %get-tuple-element.128.g_ref, ...), custom_call_target="tpu_custom_call", output_to_operand_aliasing={{0}: (3, {}), {1}: (4, {})} | custom-call | flops 1000 | bytes 1000 | tf_op jit(solution)/shard_map/weight_grad/pallas_call | solution.py:897
  313.5 4.0 weight_grad.13
  317.5 7.0 %weight_grad.14 = (bf16[4,60,32,256]{3,2,1,0:T(8,128)(2,1)}, bf16[4,60,32,256]{3,2,1,0:T(8,128)(2,1)}) custom-call(s32[1]{0:T(128)} %bitcast.9.index_ref, bf16[1664,512]{1,0:T(8,128)(2,1)} %get-tuple-element.123.x_ref, bf16[1664,1536]{1,0:T(8,128)(2,1)} %get-tuple-element.124.g_ref, ...), custom_call_target="tpu_custom_call", output_to_operand_aliasing={{0}: (3, {}), {1}: (4, {})} | custom-call | flops 1000 | bytes 1000 | tf_op jit(solution)/shard_map/weight_grad/pallas_call | solution.py:897
  324.5 4.8 weight_grad.15
  329.3 3.1 weight_grad.16
  332.7 18.1 %encoder_mlp_back.1 = (bf16[640,768]{1,0:T(8,128)(2,1)}, bf16[640,3072]{1,0:T(8,128)(2,1)}, f32[640,768]{1,0:T(8,128)}, bf16[640,768]{1,0:T(8,128)(2,1)}, f32[8,8192]{1,0:T(8,128)}) custom-call(s32[177]{0:T(256)} %fusion.19.row_ref, bf16[49280,256]{1,0:T(8,128)(2,1)} %all-gather.2.cloned.1.call-done.wg_ref, f32[1,21760]{1,0:T(1,128)} %reshape.124.vec_ref, ...), custom_call_target="tpu_custom_call" | custom-call | flops 1000 | bytes 1000 | tf_op jit(solution)/shard_map/encoder_mlp_back/pallas_call | solution.py:434
  350.8 4.2 add_convert_fusion.1
  360.7 2.3 seed_buffers.2
  363.0 8.1 %weight_grad.17 = (bf16[4,84,32,256]{3,2,1,0:T(8,128)(2,1)}, bf16[4,84,32,256]{3,2,1,0:T(8,128)(2,1)}) custom-call(s32[1]{0:T(128)} %bitcast.9.index_ref, bf16[640,768]{1,0:T(8,128)(2,1)} %get-tuple-element.156.x_ref, bf16[640,3072]{1,0:T(8,128)(2,1)} %get-tuple-element.157.g_ref, ...), custom_call_target="tpu_custom_call", output_to_operand_aliasing={{0}: (3, {}), {1}: (4, {})} | custom-call | flops 1000 | bytes 1000 | tf_op jit(solution)/shard_map/weight_grad/pallas_call | solution.py:897
  371.0 7.9 %weight_grad.18 = (bf16[4,84,32,256]{3,2,1,0:T(8,128)(2,1)}, bf16[4,84,32,256]{3,2,1,0:T(8,128)(2,1)}) custom-call(s32[1]{0:T(128)} %bitcast.9.index_ref, bf16[640,3072]{1,0:T(8,128)(2,1)} %get-tuple-element.154.x_ref, bf16[640,768]{1,0:T(8,128)(2,1)} %get-tuple-element.155.g_ref, ...), custom_call_target="tpu_custom_call", output_to_operand_aliasing={{0}: (3, {}), {1}: (4, {})} | custom-call | flops 1000 | bytes 1000 | tf_op jit(solution)/shard_map/weight_grad/pallas_call | solution.py:897
  378.9 3.7 weight_grad.19
  388.6 17.6 %encoder_attention_back.2 = (bf16[640,2304]{1,0:T(8,128)(2,1)}, bf16[640,768]{1,0:T(8,128)(2,1)}, f32[8,4608]{1,0:T(8,128)}) custom-call(s32[177]{0:T(256)} %fusion.19.row_ref, s32[8]{0:T(128)} %len_ref.7, bf16[49280,256]{1,0:T(8,128)(2,1)} %all-gather.2.cloned.1.call-done.wg_ref, f32[1,21760]{1,0:T(1,128)} %reshape.124.vec_ref, ...), custom_call_target="tpu_custom_call" | custom-call | flops 1000 | bytes 1000 | tf_op jit(solution)/shard_map/encoder_attention_back/pallas_call | solution.py:434
  407.3 7.1 %add_convert_fusion = bf16[4,84,32,256]{3,2,1,0:T(8,128)(2,1)S(1)} fusion(bf16[4,84,32,256]{3,2,1,0:T(8,128)(2,1)} %collective-permute-done.5, bf16[4,84,32,256]{3,2,1,0:T(8,128)(2,1)} %get-tuple-element.178), kind=kLoop, calls=%fused_computation.2 | loop fusion | flops 11010048 | bytes 16515072 | tf_op jit(solution)/shard_map/convert_element_type | solution.py:946
  423.0 17.0 %encoder_attention_back.3 = (bf16[640,2304]{1,0:T(8,128)(2,1)}, bf16[640,768]{1,0:T(8,128)(2,1)}, f32[8,4608]{1,0:T(8,128)}) custom-call(s32[177]{0:T(256)} %fusion.19.row_ref, s32[8]{0:T(128)} %len_ref.7, bf16[49280,256]{1,0:T(8,128)(2,1)} %all-gather.2.cloned.1.call-done.wg_ref, ...), custom_call_target="tpu_custom_call", output_to_operand_aliasing={{0}: (10, {}), {1}: (11, {})} | custom-call | flops 1000 | bytes 1000 | tf_op jit(solution)/shard_map/encoder_attention_back/pallas_call | solution.py:434
  440.0 10.0 %collective-permute-done.7 = bf16[2,42,32,256]{3,2,1,0:T(8,128)(2,1)} collective-permute-done((bf16[2,42,32,256]{3,2,1,0:T(8,128)(2,1)}, bf16[2,42,32,256]{3,2,1,0:T(8,128)(2,1)}, u32[]{:S(2)}, u32[]{:S(2)}) %collective-permute-start.7) | collective-permute-done | bytes 1376288 | tf_op jit(solution)/shard_map/ppermute | solution.py:950
  450.0 2.3 fusion
  452.4 2.4 fusion.1
  457.1 4.1 collective-permute-start.9
  480.1 2.5 seed_buffers.3
  482.6 6.9 %weight_grad.20 = (bf16[4,40,32,256]{3,2,1,0:T(8,128)(2,1)}, bf16[4,40,32,256]{3,2,1,0:T(8,128)(2,1)}) custom-call(s32[1]{0:T(128)} %bitcast.9.index_ref, bf16[640,768]{1,0:T(8,128)(2,1)} %get-tuple-element.191.x_ref, bf16[640,2304]{1,0:T(8,128)(2,1)} %get-tuple-element.192.g_ref, ...), custom_call_target="tpu_custom_call", output_to_operand_aliasing={{0}: (3, {}), {1}: (4, {})} | custom-call | flops 1000 | bytes 1000 | tf_op jit(solution)/shard_map/weight_grad/pallas_call | solution.py:897
  489.5 3.7 weight_grad.21
  493.2 2.1 add_convert_fusion.9
  495.4 2.2 add_convert_fusion.10
  503.7 3.7 collective-permute-start.16
  514.0 8.6 %collective-permute-done.16 = bf16[42,32,256]{2,1,0:T(8,128)(2,1)} collective-permute-done((bf16[42,32,256]{2,1,0:T(8,128)(2,1)}, bf16[42,32,256]{2,1,0:T(8,128)(2,1)}, u32[]{:S(2)}, u32[]{:S(2)}) %collective-permute-start.16) | collective-permute-done | bytes 688160 | tf_op jit(solution)/shard_map/ppermute | solution.py:981
  524.9 2.9 add_convert_fusion.2
  528.9 7.3 %collective-permute-done.19 = bf16[42,32,256]{2,1,0:T(8,128)(2,1)S(1)} collective-permute-done((bf16[42,32,256]{2,1,0:T(8,128)(2,1)S(1)}, bf16[42,32,256]{2,1,0:T(8,128)(2,1)S(1)}, u32[]{:S(2)}, u32[]{:S(2)}) %collective-permute-start.19) | collective-permute-done | bytes 688160 | tf_op jit(solution)/shard_map/ppermute | solution.py:981
  539.1 3.6 collective-permute-done.23
  542.7 9.3 %collective-permute-done.28 = bf16[2,20,32,256]{3,2,1,0:T(8,128)(2,1)S(1)} collective-permute-done((bf16[2,20,32,256]{3,2,1,0:T(8,128)(2,1)S(1)}, bf16[2,20,32,256]{3,2,1,0:T(8,128)(2,1)S(1)}, u32[]{:S(2)}, u32[]{:S(2)}) %collective-permute-start.28) | collective-permute-done | bytes 655392 | tf_op jit(solution)/shard_map/ppermute | solution.py:950
  556.7 3.7 collective-permute-done.24
  560.5 4.4 collective-permute-start.25
  567.9 4.8 collective-permute-done.25
  573.6 2.7 collective-permute-done.30
  580.2 10.2 %collective-permute-done.21 = bf16[42,32,256]{2,1,0:T(8,128)(2,1)S(1)} collective-permute-done((bf16[42,32,256]{2,1,0:T(8,128)(2,1)S(1)}, bf16[42,32,256]{2,1,0:T(8,128)(2,1)S(1)}, u32[]{:S(2)}, u32[]{:S(2)}) %collective-permute-start.21) | collective-permute-done | bytes 688160 | tf_op jit(solution)/shard_map/ppermute | solution.py:987
  590.6 6.7 collective-permute-done.27
  597.5 3.6 collective-permute-done.32
  602.0 2.7 gather_fusion.1
  604.6 4.0 all-to-all-start
  626.7 3.5 collective-permute-done.33
  631.2 3.5 collective-permute-done.34
  637.9 7.6 %collective-permute-done.36 = f32[3]{0:T(128)S(1)} collective-permute-done((f32[3]{0:T(128)S(1)}, f32[3]{0:T(128)S(1)}, u32[]{:S(2)}, u32[]{:S(2)}) %collective-permute-start.36) | collective-permute-done | bytes 44 | tf_op jit(solution)/shard_map/ppermute | solution.py:950
  655.4 22.1 %tile_update.1 = (f32[24,256,256]{2,1,0:T(8,128)}, f32[24,256,256]{2,1,0:T(8,128)}, f32[24,256,256]{2,1,0:T(8,128)}, f32[24,256,256]{2,1,0:T(8,128)}) custom-call(f32[1]{0:T(128)} %bitcast.41.scale_ref, bf16[8,24,32,256]{3,2,1,0:T(8,128)(2,1)} %bitcast.104, f32[24,256,256]{2,1,0:T(8,128)} %w_ref.1, f32[24,256,256]{2,1,0:T(8,128)} %left_stat_ref.1, ...), custom_call_target="tpu_custom_call" | custom-call | tf_op jit(solution)/shard_map/tile_update/pallas_call | solution.py:1044
  (224 shorter events, 108.0 us)
Async XLA Ops:
  7.2 133.7 %all-gather.2.cloned.1.call-start = ((), (), s32[]{:S(2)}) async-start(), calls=%async_computation.1 | async-start | bytes 28385280 | tf_op jit(solution)/shard_map/all_gather | solution.py:1122
  332.4 18.4 %collective-permute-start = (bf16[4,60,32,256]{3,2,1,0:T(8,128)(2,1)}, bf16[4,60,32,256]{3,2,1,0:T(8,128)(2,1)}, u32[]{:S(2)}, u32[]{:S(2)}) collective-permute-start(bf16[4,60,32,256]{3,2,1,0:T(8,128)(2,1)} %get-tuple-element.151), channel_id=1, source_target_pairs={{0,4},{4,0},{8,12},{12,8},{16,20},{20,16},{24,28},{28,24},{1,5},{5... | collective-permute-start | bytes 11796488 | tf_op jit(solution)/shard_map/ppermute | solution.py:950
  332.7 18.1 %copy-start.1 = (bf16[4,60,32,256]{3,2,1,0:T(8,128)(2,1)S(1)}, bf16[4,60,32,256]{3,2,1,0:T(8,128)(2,1)}, u32[]{:S(2)}) copy-start(bf16[4,60,32,256]{3,2,1,0:T(8,128)(2,1)} %get-tuple-element.150) | copy-start | bytes 11796484
  356.8 25.8 %collective-permute-start.2 = (bf16[2,30,32,256]{3,2,1,0:T(8,128)(2,1)S(1)}, bf16[2,30,32,256]{3,2,1,0:T(8,128)(2,1)}, u32[]{:S(2)}, u32[]{:S(2)}) collective-permute-start(bf16[2,30,32,256]{3,2,1,0:T(8,128)(2,1)S(1)} %slice_bitcast_fusion.3), channel_id=1, source_target_pairs={{0,16},{4,20},{8,24},{12,28},{16,0},{20,4},{24,8},{28,12},{1,17},{... | collective-permute-start | bytes 2949128 | tf_op jit(solution)/shard_map/ppermute | solution.py:950
  358.3 26.2 %collective-permute-start.1 = (bf16[2,30,32,256]{3,2,1,0:T(8,128)(2,1)}, bf16[2,30,32,256]{3,2,1,0:T(8,128)(2,1)}, u32[]{:S(2)}, u32[]{:S(2)}) collective-permute-start(bf16[2,30,32,256]{3,2,1,0:T(8,128)(2,1)} %slice_bitcast_fusion.4), channel_id=1, source_target_pairs={{0,8},{4,12},{8,0},{12,4},{16,24},{20,28},{24,16},{28,20},{1,9},{5... | collective-permute-start | bytes 2949128 | tf_op jit(solution)/shard_map/ppermute | solution.py:950
  386.1 21.2 %collective-permute-start.5 = (bf16[4,84,32,256]{3,2,1,0:T(8,128)(2,1)}, bf16[4,84,32,256]{3,2,1,0:T(8,128)(2,1)}, u32[]{:S(2)}, u32[]{:S(2)}) collective-permute-start(bf16[4,84,32,256]{3,2,1,0:T(8,128)(2,1)} %get-tuple-element.179), channel_id=1, source_target_pairs={{0,4},{4,0},{8,12},{12,8},{16,20},{20,16},{24,28},{28,24},{1,5},{5... | collective-permute-start | bytes 16515080 | tf_op jit(solution)/shard_map/ppermute | solution.py:950
  386.2 19.9 %collective-permute-start.4 = (bf16[30,32,256]{2,1,0:T(8,128)(2,1)S(1)}, bf16[30,32,256]{2,1,0:T(8,128)(2,1)S(1)}, u32[]{:S(2)}, u32[]{:S(2)}) collective-permute-start(bf16[30,32,256]{2,1,0:T(8,128)(2,1)S(1)} %slice_bitcast_fusion.11), channel_id=1, source_target_pairs={{0,8},{4,12},{8,0},{12,4},{16,24},{20,28},{24,16},{28,20},{1,9},{5... | collective-permute-start | bytes 1474568 | tf_op jit(solution)/shard_map/ppermute | solution.py:950
  387.1 19.2 %collective-permute-start.3 = (bf16[30,32,256]{2,1,0:T(8,128)(2,1)S(1)}, bf16[30,32,256]{2,1,0:T(8,128)(2,1)S(1)}, u32[]{:S(2)}, u32[]{:S(2)}) collective-permute-start(bf16[30,32,256]{2,1,0:T(8,128)(2,1)S(1)} %slice_bitcast_fusion.12), channel_id=1, source_target_pairs={{0,16},{4,20},{8,24},{12,28},{16,0},{20,4},{24,8},{28,12},{1,17},{... | collective-permute-start | bytes 1474568 | tf_op jit(solution)/shard_map/ppermute | solution.py:950
  417.9 32.1 %collective-permute-start.7 = (bf16[2,42,32,256]{3,2,1,0:T(8,128)(2,1)}, bf16[2,42,32,256]{3,2,1,0:T(8,128)(2,1)}, u32[]{:S(2)}, u32[]{:S(2)}) collective-permute-start(bf16[2,42,32,256]{3,2,1,0:T(8,128)(2,1)} %slice_bitcast_fusion), channel_id=1, source_target_pairs={{0,16},{4,20},{8,24},{12,28},{16,0},{20,4},{24,8},{28,12},{1,17},{... | collective-permute-start | bytes 4128776 | tf_op jit(solution)/shard_map/ppermute | solution.py:950
  419.7 32.7 %collective-permute-start.6 = (bf16[2,42,32,256]{3,2,1,0:T(8,128)(2,1)}, bf16[2,42,32,256]{3,2,1,0:T(8,128)(2,1)}, u32[]{:S(2)}, u32[]{:S(2)}) collective-permute-start(bf16[2,42,32,256]{3,2,1,0:T(8,128)(2,1)} %slice_bitcast_fusion.1), channel_id=1, source_target_pairs={{0,8},{4,12},{8,0},{12,4},{16,24},{20,28},{24,16},{28,20},{1,9},{5... | collective-permute-start | bytes 4128776 | tf_op jit(solution)/shard_map/ppermute | solution.py:950
  454.9 42.7 %collective-permute-start.11 = (bf16[42,32,256]{2,1,0:T(8,128)(2,1)S(1)}, bf16[42,32,256]{2,1,0:T(8,128)(2,1)S(1)}, u32[]{:S(2)}, u32[]{:S(2)}) collective-permute-start(bf16[42,32,256]{2,1,0:T(8,128)(2,1)S(1)} %slice_bitcast_fusion.5), channel_id=1, source_target_pairs={{0,8},{4,12},{8,0},{12,4},{16,24},{20,28},{24,16},{28,20},{1,9},{5... | collective-permute-start | bytes 2064392 | tf_op jit(solution)/shard_map/ppermute | solution.py:950
  456.5 41.4 %collective-permute-start.10 = (bf16[42,32,256]{2,1,0:T(8,128)(2,1)S(1)}, bf16[42,32,256]{2,1,0:T(8,128)(2,1)S(1)}, u32[]{:S(2)}, u32[]{:S(2)}) collective-permute-start(bf16[42,32,256]{2,1,0:T(8,128)(2,1)S(1)} %slice_bitcast_fusion.6), channel_id=1, source_target_pairs={{0,16},{4,20},{8,24},{12,28},{16,0},{20,4},{24,8},{28,12},{1,17},{... | collective-permute-start | bytes 2064392 | tf_op jit(solution)/shard_map/ppermute | solution.py:950
  457.1 36.1 %collective-permute-start.9 = (bf16[30,32,256]{2,1,0:T(8,128)(2,1)S(1)}, bf16[30,32,256]{2,1,0:T(8,128)(2,1)}, u32[]{:S(2)}, u32[]{:S(2)}) collective-permute-start(bf16[30,32,256]{2,1,0:T(8,128)(2,1)S(1)} %fusion.8), channel_id=1, source_target_pairs={{0,1},{3,2},{4,5},{7,6},{8,9},{11,10},{12,13},{15,14},{16,17},{19,... | collective-permute-start | bytes 1474568 | tf_op jit(solution)/shard_map/ppermute | solution.py:981
  461.3 34.1 %collective-permute-start.8 = (bf16[30,32,256]{2,1,0:T(8,128)(2,1)}, bf16[30,32,256]{2,1,0:T(8,128)(2,1)}, u32[]{:S(2)}, u32[]{:S(2)}) collective-permute-start(bf16[30,32,256]{2,1,0:T(8,128)(2,1)} %fusion.9), channel_id=1, source_target_pairs={{0,1},{3,2},{4,5},{7,6},{8,9},{11,10},{12,13},{15,14},{16,17},{19,... | collective-permute-start | bytes 1474568 | tf_op jit(solution)/shard_map/ppermute | solution.py:981
  499.0 25.9 %collective-permute-start.22 = (bf16[4,40,32,256]{3,2,1,0:T(8,128)(2,1)}, bf16[4,40,32,256]{3,2,1,0:T(8,128)(2,1)}, u32[]{:S(2)}, u32[]{:S(2)}) collective-permute-start(bf16[4,40,32,256]{3,2,1,0:T(8,128)(2,1)} %get-tuple-element.211), channel_id=1, source_target_pairs={{0,4},{4,0},{8,12},{12,8},{16,20},{20,16},{24,28},{28,24},{1,5},{5... | collective-permute-start | bytes 7864328 | tf_op jit(solution)/shard_map/ppermute | solution.py:950
  499.0 9.7 %collective-permute-start.12 = (bf16[30,32,256]{2,1,0:T(8,128)(2,1)}, bf16[30,32,256]{2,1,0:T(8,128)(2,1)}, u32[]{:S(2)}, u32[]{:S(2)}) collective-permute-start(bf16[30,32,256]{2,1,0:T(8,128)(2,1)} %add_convert_fusion.10), channel_id=1, source_target_pairs={{1,2},{2,1},{5,6},{6,5},{9,10},{10,9},{13,14},{14,13},{17,18},{18,... | collective-permute-start | bytes 1474568 | tf_op jit(solution)/shard_map/ppermute | solution.py:984
  502.0 22.8 %copy-start.2 = (bf16[4,40,32,256]{3,2,1,0:T(8,128)(2,1)S(1)}, bf16[4,40,32,256]{3,2,1,0:T(8,128)(2,1)}, u32[]{:S(2)}) copy-start(bf16[4,40,32,256]{3,2,1,0:T(8,128)(2,1)} %get-tuple-element.210) | copy-start | bytes 7864324
  502.1 9.3 %collective-permute-start.14 = (bf16[30,32,256]{2,1,0:T(8,128)(2,1)}, bf16[30,32,256]{2,1,0:T(8,128)(2,1)}, u32[]{:S(2)}, u32[]{:S(2)}) collective-permute-start(bf16[30,32,256]{2,1,0:T(8,128)(2,1)} %add_convert_fusion.9), channel_id=1, source_target_pairs={{1,2},{2,1},{5,6},{6,5},{9,10},{10,9},{13,14},{14,13},{17,18},{18,... | collective-permute-start | bytes 1474568 | tf_op jit(solution)/shard_map/ppermute | solution.py:984
  503.7 18.9 %collective-permute-start.16 = (bf16[42,32,256]{2,1,0:T(8,128)(2,1)}, bf16[42,32,256]{2,1,0:T(8,128)(2,1)}, u32[]{:S(2)}, u32[]{:S(2)}) collective-permute-start(bf16[42,32,256]{2,1,0:T(8,128)(2,1)} %fusion.5), channel_id=1, source_target_pairs={{0,1},{3,2},{4,5},{7,6},{8,9},{11,10},{12,13},{15,14},{16,17},{19,... | collective-permute-start | bytes 2064392 | tf_op jit(solution)/shard_map/ppermute | solution.py:981
  507.3 28.9 %collective-permute-start.19 = (bf16[42,32,256]{2,1,0:T(8,128)(2,1)S(1)}, bf16[42,32,256]{2,1,0:T(8,128)(2,1)S(1)}, u32[]{:S(2)}, u32[]{:S(2)}) collective-permute-start(bf16[42,32,256]{2,1,0:T(8,128)(2,1)S(1)} %fusion.4), channel_id=1, source_target_pairs={{0,1},{3,2},{4,5},{7,6},{8,9},{11,10},{12,13},{15,14},{16,17},{19,... | collective-permute-start | bytes 2064392 | tf_op jit(solution)/shard_map/ppermute | solution.py:981
  510.0 28.6 %copy-start.12 = (bf16[30,32,256]{2,1,0:T(8,128)(2,1)}, bf16[30,32,256]{2,1,0:T(8,128)(2,1)S(1)}, u32[]{:S(2)}) copy-start(bf16[30,32,256]{2,1,0:T(8,128)(2,1)S(1)} %add_convert_fusion.8) | copy-start | bytes 1474564
  510.0 27.9 %collective-permute-start.13 = (bf16[30,32,256]{2,1,0:T(8,128)(2,1)S(1)}, bf16[30,32,256]{2,1,0:T(8,128)(2,1)S(1)}, u32[]{:S(2)}, u32[]{:S(2)}) collective-permute-start(bf16[30,32,256]{2,1,0:T(8,128)(2,1)S(1)} %add_convert_fusion.8), channel_id=1, source_target_pairs={{1,0},{2,3},{5,4},{6,7},{9,8},{10,11},{13,12},{14,15},{17,16},{18,... | collective-permute-start | bytes 1474568 | tf_op jit(solution)/shard_map/ppermute | solution.py:987
  512.7 26.2 %copy-start.13 = (bf16[30,32,256]{2,1,0:T(8,128)(2,1)}, bf16[30,32,256]{2,1,0:T(8,128)(2,1)S(1)}, u32[]{:S(2)}) copy-start(bf16[30,32,256]{2,1,0:T(8,128)(2,1)S(1)} %add_convert_fusion.7) | copy-start | bytes 1474564
  512.7 26.1 %collective-permute-start.15 = (bf16[30,32,256]{2,1,0:T(8,128)(2,1)S(1)}, bf16[30,32,256]{2,1,0:T(8,128)(2,1)S(1)}, u32[]{:S(2)}, u32[]{:S(2)}) collective-permute-start(bf16[30,32,256]{2,1,0:T(8,128)(2,1)S(1)} %add_convert_fusion.7), channel_id=1, source_target_pairs={{1,0},{2,3},{5,4},{6,7},{9,8},{10,11},{13,12},{14,15},{17,16},{18,... | collective-permute-start | bytes 1474568 | tf_op jit(solution)/shard_map/ppermute | solution.py:987
  524.2 30.9 %collective-permute-start.17 = (bf16[42,32,256]{2,1,0:T(8,128)(2,1)S(1)}, bf16[42,32,256]{2,1,0:T(8,128)(2,1)S(1)}, u32[]{:S(2)}, u32[]{:S(2)}) collective-permute-start(bf16[42,32,256]{2,1,0:T(8,128)(2,1)S(1)} %add_convert_fusion.6), channel_id=1, source_target_pairs={{1,2},{2,1},{5,6},{6,5},{9,10},{10,9},{13,14},{14,13},{17,18},{18,... | collective-permute-start | bytes 2064392 | tf_op jit(solution)/shard_map/ppermute | solution.py:984
  527.9 14.8 %collective-permute-start.23 = (bf16[2,20,32,256]{3,2,1,0:T(8,128)(2,1)S(1)}, bf16[2,20,32,256]{3,2,1,0:T(8,128)(2,1)S(1)}, u32[]{:S(2)}, u32[]{:S(2)}) collective-permute-start(bf16[2,20,32,256]{3,2,1,0:T(8,128)(2,1)S(1)} %slice_bitcast_fusion.9), channel_id=1, source_target_pairs={{0,8},{4,12},{8,0},{12,4},{16,24},{20,28},{24,16},{28,20},{1,9},{5... | collective-permute-start | bytes 1966088 | tf_op jit(solution)/shard_map/ppermute | solution.py:950
  536.2 15.7 %collective-permute-start.28 = (bf16[2,20,32,256]{3,2,1,0:T(8,128)(2,1)S(1)}, bf16[2,20,32,256]{3,2,1,0:T(8,128)(2,1)S(1)}, u32[]{:S(2)}, u32[]{:S(2)}) collective-permute-start(bf16[2,20,32,256]{3,2,1,0:T(8,128)(2,1)S(1)} %slice_bitcast_fusion.7), channel_id=1, source_target_pairs={{0,16},{4,20},{8,24},{12,28},{16,0},{20,4},{24,8},{28,12},{1,17},{... | collective-permute-start | bytes 1966088 | tf_op jit(solution)/shard_map/ppermute | solution.py:950
  537.9 28.4 %collective-permute-start.20 = (bf16[42,32,256]{2,1,0:T(8,128)(2,1)S(1)}, bf16[42,32,256]{2,1,0:T(8,128)(2,1)S(1)}, u32[]{:S(2)}, u32[]{:S(2)}) collective-permute-start(bf16[42,32,256]{2,1,0:T(8,128)(2,1)S(1)} %add_convert_fusion.4), channel_id=1, source_target_pairs={{1,2},{2,1},{5,6},{6,5},{9,10},{10,9},{13,14},{14,13},{17,18},{18,... | collective-permute-start | bytes 2064392 | tf_op jit(solution)/shard_map/ppermute | solution.py:984
  552.5 7.8 %collective-permute-start.24 = (bf16[20,32,256]{2,1,0:T(8,128)(2,1)S(1)}, bf16[20,32,256]{2,1,0:T(8,128)(2,1)S(1)}, u32[]{:S(2)}, u32[]{:S(2)}) collective-permute-start(bf16[20,32,256]{2,1,0:T(8,128)(2,1)S(1)} %slice_bitcast_fusion.15), channel_id=1, source_target_pairs={{0,16},{4,20},{8,24},{12,28},{16,0},{20,4},{24,8},{28,12},{1,17},{... | collective-permute-start | bytes 983048 | tf_op jit(solution)/shard_map/ppermute | solution.py:950
  554.1 10.8 %collective-permute-start.29 = (bf16[20,32,256]{2,1,0:T(8,128)(2,1)S(1)}, bf16[20,32,256]{2,1,0:T(8,128)(2,1)S(1)}, u32[]{:S(2)}, u32[]{:S(2)}) collective-permute-start(bf16[20,32,256]{2,1,0:T(8,128)(2,1)S(1)} %slice_bitcast_fusion.13), channel_id=1, source_target_pairs={{0,8},{4,12},{8,0},{12,4},{16,24},{20,28},{24,16},{28,20},{1,9},{5... | collective-permute-start | bytes 983048 | tf_op jit(solution)/shard_map/ppermute | solution.py:950
  555.3 21.7 %copy-start.6 = (bf16[42,32,256]{2,1,0:T(8,128)(2,1)}, bf16[42,32,256]{2,1,0:T(8,128)(2,1)S(1)}, u32[]{:S(2)}) copy-start(bf16[42,32,256]{2,1,0:T(8,128)(2,1)S(1)} %add_convert_fusion.5) | copy-start | bytes 2064388
  555.4 21.7 %collective-permute-start.18 = (bf16[42,32,256]{2,1,0:T(8,128)(2,1)S(1)}, bf16[42,32,256]{2,1,0:T(8,128)(2,1)S(1)}, u32[]{:S(2)}, u32[]{:S(2)}) collective-permute-start(bf16[42,32,256]{2,1,0:T(8,128)(2,1)S(1)} %add_convert_fusion.5), channel_id=1, source_target_pairs={{1,0},{2,3},{5,4},{6,7},{9,8},{10,11},{13,12},{14,15},{17,16},{18,... | collective-permute-start | bytes 2064392 | tf_op jit(solution)/shard_map/ppermute | solution.py:987
  560.5 12.3 %collective-permute-start.25 = (bf16[20,32,256]{2,1,0:T(8,128)(2,1)S(1)}, bf16[20,32,256]{2,1,0:T(8,128)(2,1)S(1)}, u32[]{:S(2)}, u32[]{:S(2)}) collective-permute-start(bf16[20,32,256]{2,1,0:T(8,128)(2,1)S(1)} %fusion.11), channel_id=1, source_target_pairs={{0,1},{3,2},{4,5},{7,6},{8,9},{11,10},{12,13},{15,14},{16,17},{19,... | collective-permute-start | bytes 983048 | tf_op jit(solution)/shard_map/ppermute | solution.py:981
  565.0 11.2 %collective-permute-start.30 = (bf16[20,32,256]{2,1,0:T(8,128)(2,1)S(1)}, bf16[20,32,256]{2,1,0:T(8,128)(2,1)S(1)}, u32[]{:S(2)}, u32[]{:S(2)}) collective-permute-start(bf16[20,32,256]{2,1,0:T(8,128)(2,1)S(1)} %fusion.10), channel_id=1, source_target_pairs={{0,1},{3,2},{4,5},{7,6},{8,9},{11,10},{12,13},{15,14},{16,17},{19,... | collective-permute-start | bytes 983048 | tf_op jit(solution)/shard_map/ppermute | solution.py:981
  566.6 23.8 %copy-start.7 = (bf16[42,32,256]{2,1,0:T(8,128)(2,1)}, bf16[42,32,256]{2,1,0:T(8,128)(2,1)S(1)}, u32[]{:S(2)}) copy-start(bf16[42,32,256]{2,1,0:T(8,128)(2,1)S(1)} %add_convert_fusion.3) | copy-start | bytes 2064388
  566.6 23.7 %collective-permute-start.21 = (bf16[42,32,256]{2,1,0:T(8,128)(2,1)S(1)}, bf16[42,32,256]{2,1,0:T(8,128)(2,1)S(1)}, u32[]{:S(2)}, u32[]{:S(2)}) collective-permute-start(bf16[42,32,256]{2,1,0:T(8,128)(2,1)S(1)} %add_convert_fusion.3), channel_id=1, source_target_pairs={{1,0},{2,3},{5,4},{6,7},{9,8},{10,11},{13,12},{14,15},{17,16},{18,... | collective-permute-start | bytes 2064392 | tf_op jit(solution)/shard_map/ppermute | solution.py:987
  572.9 4.5 collective-permute-start.26
  576.4 2.4 collective-permute-start.31
  577.5 19.9 %collective-permute-start.27 = (bf16[20,32,256]{2,1,0:T(8,128)(2,1)S(1)}, bf16[20,32,256]{2,1,0:T(8,128)(2,1)S(1)}, u32[]{:S(2)}, u32[]{:S(2)}) collective-permute-start(bf16[20,32,256]{2,1,0:T(8,128)(2,1)S(1)} %add_convert_fusion.13), channel_id=1, source_target_pairs={{1,0},{2,3},{5,4},{6,7},{9,8},{10,11},{13,12},{14,15},{17,16},{18,... | collective-permute-start | bytes 983048 | tf_op jit(solution)/shard_map/ppermute | solution.py:987
  578.9 22.2 %collective-permute-start.32 = (bf16[20,32,256]{2,1,0:T(8,128)(2,1)S(1)}, bf16[20,32,256]{2,1,0:T(8,128)(2,1)S(1)}, u32[]{:S(2)}, u32[]{:S(2)}) collective-permute-start(bf16[20,32,256]{2,1,0:T(8,128)(2,1)S(1)} %add_convert_fusion.11), channel_id=1, source_target_pairs={{1,0},{2,3},{5,4},{6,7},{9,8},{10,11},{13,12},{14,15},{17,16},{18,... | collective-permute-start | bytes 983048 | tf_op jit(solution)/shard_map/ppermute | solution.py:987
  604.6 49.1 %all-to-all-start = ((bf16[192,32,256]{2,1,0:T(8,128)(2,1)}), bf16[192,32,256]{2,1,0:T(8,128)(2,1)S(1)}, u32[]{:S(2)}, u32[]{:S(2)}) async-start(bf16[192,32,256]{2,1,0:T(8,128)(2,1)} %gather_fusion.1), calls=%async_computation | async-start | bytes 6291456 | tf_op jit(solution)/shard_map/all_to_all | solution.py:1246
  611.2 41.9 %copy-start.25 = (f32[2560]{0:T(1024)S(1)}, f32[2560]{0:T(1024)}, u32[]{:S(2)}) copy-start(f32[2560]{0:T(1024)} %param.22) | copy-start | bytes 30724
  611.2 41.9 %copy-start.26 = (f32[2560]{0:T(1024)S(1)}, f32[2560]{0:T(1024)}, u32[]{:S(2)}) copy-start(f32[2560]{0:T(1024)} %param.21) | copy-start | bytes 30724
  626.7 3.5 collective-permute-start.33
  630.3 4.4 collective-permute-start.34
  634.8 1.1 collective-permute-start.35
  635.9 9.6 %collective-permute-start.36 = (f32[3]{0:T(128)S(1)}, f32[3]{0:T(128)S(1)}, u32[]{:S(2)}, u32[]{:S(2)}) collective-permute-start(f32[3]{0:T(128)S(1)} %add.202), channel_id=1, source_target_pairs={{0,8},{4,12},{8,0},{12,4},{16,24},{20,28},{24,16},{28,20},{1,9},{5... | collective-permute-start | bytes 44 | tf_op jit(solution)/shard_map/ppermute | solution.py:950
  645.5 3.5 collective-permute-start.37
  (22 other events, 143.9 us)
Sparse Core Ops, SparseCore 0:
  12.5 128.2 all-gather.1

commit v6 on v5

--- a/solution.py
+++ b/solution.py
@@ -175,16 +175,17 @@
 def scores_bounded(qkv_ref, width, head_size):
     lane = lax.broadcasted_iota(jnp.int32, (BS, 128), 0) // head_size
     pick = jnp.where(lane == lax.broadcasted_iota(jnp.int32, (BS, 128), 1), 1.0, 0.0).astype(BF)
-    tops = []
-    for which in range(2):
-        top = None
-        for g in range(width // BS):
+    score, value = None, None
+    for g in range(width // BS):
+        tops = []
+        for which in range(3):
             x = qkv_ref[:, which * width + g * BS : which * width + (g + 1) * BS]
-            norms = mm(x * x, pick)
-            top = norms if top is None else jnp.maximum(top, norms)
-        tops.append(jnp.max(top))
-    limit = 60.0 / (1.05 * head_size**-0.5 * LOG2E)
-    return tops[0] * tops[1] < limit * limit
+            tops.append(jnp.max(mm(x * x, pick), axis=0, keepdims=True))
+        one = tops[0] * tops[1]
+        score = one if score is None else jnp.maximum(score, one)
+        value = tops[2] if value is None else jnp.maximum(value, tops[2])
+    limit = 90.0 / (1.05 * head_size**-0.5 * LOG2E)
+    return (jnp.max(score) < limit * limit) & (jnp.max(value) < 2.0**40)
 
 
 def attention_forward(qkv_ref, att_ref, out_t_ref, lse_ref, image, seq, width, head_size, count, bounded):
@@ -918,28 +919,42 @@
     )(index, x, g, *given)
 
 
-def seed_kernel(parts, index_ref, vec_ref, *outs):
-    at = pl.program_id(0)
+def seed_kernel(parts, parcels, own, index_ref, *refs):
+    sums, outs, rows = refs[: -1 - min(parts, 2)], refs[-1 - min(parts, 2) : -1], refs[-1]
+    rows[...] = jnp.zeros_like(rows)
+    at = 0
+    for source, start, size in parcels:
+        for k in range(0, size, 128):
+            piece = sum(jnp.sum(sums[i][:, start + k : start + k + 128], axis=0, keepdims=True) for i in source)
+            row, col = at % own // BS, at % own % BS
+            rows[at // own, row : row + 1, col : col + 128] = piece
+            at += 128
     for p in range(parts):
-        got = vec_ref[p ^ index_ref[0]]
-        outs[p % 2][p // 2, 0] = jnp.where(at == 0, got, 0.0).astype(BF)
-
-
-def seed_buffers(index, parts, count, first, vector_tile):
+        out = outs[p % 2]
+        out[p // 2, 0] = rows[p ^ index_ref[0]].astype(BF)
+        for t in range(1, out.shape[1]):
+            out[p // 2, t] = jnp.zeros(rows.shape[1:], BF)
+
+
+def seed_buffers(index, parts, count, first, sums=(), parcels=(), own=1):
     cut = BS // parts
     held = min(parts, 2)
+    size = count - first
+    assert first % size == 0
     shape = jax.ShapeDtypeStruct((parts // held, count, cut, BS), BF)
     return pl.pallas_call(
-        functools.partial(seed_kernel, parts),
+        functools.partial(seed_kernel, parts, parcels, own),
         grid_spec=pltpu.PrefetchScalarGridSpec(
             num_scalar_prefetch=1,
-            grid=(count - first,),
-            in_specs=[pl.BlockSpec(vector_tile.shape, lambda i, *_: (0, 0, 0))],
-            out_specs=[pl.BlockSpec((parts // held, 1, cut, BS), lambda i, *_: (0, first + i, 0, 0))] * held,
+            grid=(1,),
+            in_specs=[pl.BlockSpec(x.shape, lambda i, *_: (0, 0)) for x in sums],
+            out_specs=[pl.BlockSpec((parts // held, size, cut, BS), lambda i, *_: (0, first // size, 0, 0))] * held,
+            scratch_shapes=[pltpu.VMEM((parts, cut, BS), F32)],
         ),
         out_shape=[shape] * held,
+        cost_estimate=SMALL,
         name="seed_buffers",
-    )(index, vector_tile)
+    )(index, *sums)
 
 
 def low_sum(a, b):
@@ -1078,13 +1093,9 @@
 ]
 
 
-def chunk_sizes(groups):
-    unit = max(2, groups)
-    sizes = []
-    for i, chunk in enumerate(CHUNKS):
-        used = sum(r * c for _, r, c, _ in chunk) + (2 if i == len(CHUNKS) - 1 else 0)
-        sizes.append(-(-used // unit) * unit)
-    return sizes
+def chunk_sizes():
+    sizes = [sum(r * c for _, r, c, _ in chunk) for chunk in CHUNKS]
+    return sizes[:-1] + [sizes[-1] + 2]
 
 
 def tile_places(sizes):
@@ -1141,18 +1152,16 @@
     (d_h1, d_dqkv, d_att, d_gproj, d_h2, d_du, d_act, d_gdown, d_hn, d_gpred, glat, d_sums) = decoder(
         tile_rows, vis_len, gathered, vector, latent, pos_e, ordered, 4
     )
-    sizes = chunk_sizes(groups)
+    sizes = chunk_sizes()
     chunk_of, place_of = tile_places(sizes)
 
     rows_cut = BS // parts
 
-    def gradients(chunk, pairs, vector_tile=None):
+    def gradients(chunk, pairs, *vector):
         used = sum(r * c for _, r, c, _ in CHUNKS[chunk])
         at, buffers = 0, None
         if sizes[chunk] > used:
-            if vector_tile is None:
-                vector_tile = jnp.zeros((parts, rows_cut, BS), F32)
-            buffers = seed_buffers(index, parts, sizes[chunk], used, vector_tile)
+            buffers = seed_buffers(index, parts, sizes[chunk], used, *vector)
         for (x, g), (_, row_tiles, col_tiles, block) in zip(pairs, CHUNKS[chunk]):
             buffers = weight_grad(index, parts, sizes[chunk], at, x, g, block, buffers)
             at += row_tiles * col_tiles
@@ -1182,44 +1191,38 @@
     dqkv, gembed, b_sums = attention_back(gproj, 1, (dqkv, gembed))
     half1, left1 = reduce_chips((half1, left1), parts, 1)
     dqkv, gembed, b_sums, half0, half1 = after((dqkv, gembed, b_sums, half0, half1))
-    a_sums = a_sums + b_sums
-    d_sums, m_sums, a_sums = (jnp.sum(s, axis=0) for s in (d_sums, m_sums, a_sums))
-
-    def cut(sums, start, size):
-        return sums[start : start + size]
-
-    grad_vector = jnp.concatenate(
-        [
-            cut(a_sums, EA_EMBED, D),
-            cut(a_sums, EA_G1, 2 * D),
-            cut(a_sums, EA_QKV, D),
-            cut(a_sums, EA_QKV + 2 * D, D),
-            cut(m_sums, EM_BO, D),
-            cut(m_sums, EM_G2, 2 * D),
-            cut(m_sums, EM_BU, FE),
-            cut(m_sums, EM_BD, D),
-            cut(m_sums, EM_NORM, 2 * D),
-            cut(m_sums, EM_PROJ, E),
-            cut(d_sums, DS_MASK, E),
-            cut(d_sums, DS["g1"], 2 * E),
-            cut(d_sums, DS["bqkv"], E),
-            cut(d_sums, DS["bqkv"] + 2 * E, E),
-            cut(d_sums, DS["bo"], E),
-            cut(d_sums, DS["g2"], 2 * E),
-            cut(d_sums, DS["bu"], FD),
-            cut(d_sums, DS["bd"], E),
-            cut(d_sums, DS_NORM, 2 * E),
-            cut(d_sums, DS_HEAD, PIX),
-        ]
-    )
-    vector_tile = jnp.pad(grad_vector.reshape(parts, own), ((0, 0), (0, rows_cut * BS - own)))
-    vector_tile = vector_tile.reshape(parts, rows_cut, BS)
-    buf2 = gradients(2, [(h1, dqkv), (visible_pix.reshape(-1, PIX), gembed)], vector_tile)
+
+    late, early, dec = (0, 1), (2,), (3,)
+    parcels = [
+        (late, EA_EMBED, D),
+        (late, EA_G1, 2 * D),
+        (late, EA_QKV, D),
+        (late, EA_QKV + 2 * D, D),
+        (early, EM_BO, D),
+        (early, EM_G2, 2 * D),
+        (early, EM_BU, FE),
+        (early, EM_BD, D),
+        (early, EM_NORM, 2 * D),
+        (early, EM_PROJ, E),
+        (dec, DS_MASK, E),
+        (dec, DS["g1"], 2 * E),
+        (dec, DS["bqkv"], E),
+        (dec, DS["bqkv"] + 2 * E, E),
+        (dec, DS["bo"], E),
+        (dec, DS["g2"], 2 * E),
+        (dec, DS["bu"], FD),
+        (dec, DS["bd"], E),
+        (dec, DS_NORM, 2 * E),
+        (dec, DS_HEAD, PIX),
+    ]
+    buf2 = gradients(2, [(h1, dqkv), (visible_pix.reshape(-1, PIX), gembed)], (a_sums, b_sums, m_sums, d_sums), parcels, own)
     half1, _ = reduce_chips((half1, left1), parts, 99)
     steps = patch_steps(groups)
     half0 = [sum_patch(x, steps[:1]) for x in half0]
     buf2, half0, half1 = after((buf2, half0, half1))
-    half2, _ = reduce_chips(reduce_core(buf2, parts), parts, 99)
+    half2, left2 = reduce_core(buf2, parts)
+    half1, half2 = after((half1, half2))
+    half2, _ = reduce_chips((half2, left2), parts, 99)
     pieces = [sum_patch(x, steps[1:]) for x in half0] + [sum_patch(x, steps) for x in half1 + half2]
     mine = jnp.where(lax.axis_index("patch") == 0, 1.0, 0.0)
 
@@ -1229,7 +1232,7 @@
 
     totals = jnp.stack(
         [
-            jnp.sum(cut(d_sums, DS_LOSS, PIX)) / PIX,
+            jnp.sum(d_sums[:, DS_LOSS : DS_LOSS + PIX]) / PIX,
             jnp.sum(POS - vis_len).astype(F32),
             sum(squares(x) for x in pieces) * mine,
         ]

time: 695 us -> 704 us (1.013)
  waiting for transfers between devices: 203 us -> 244 us
  local copies, waits for them, and re-layouts: 38.5 us -> 20.2 us
  other arithmetic: 59.3 us -> 51.7 us
    ppermute x6, waiting for transfers between devices: 20.5 us -> 70.8 us  [outwards(): lax.ppermute(x, 'patch', [(k + 1, k), (groups - 2 - k, groups - 1 - k)])]
    unnamed x79 -> x69, local copies, waits for them, and re-layouts: 23.5 us -> 6.19 us
    ppermute x18, waiting for transfers between devices: 37.4 us -> 24 us  [swap_bit(): return lax.ppermute(x, 'dp', [(i, i ^ 1 << bit) for i in range(size)])]
    convert_element_type x26 -> x27, other arithmetic: 35.3 us -> 30.9 us  [low_sum(): return (a.astype(F32) + b.astype(F32)).astype(BF)]
  transfers between devices with their start and end apart: 40 -> 40, of which waited for: 17 -> 19; matrix products, arithmetic and copies ran while one was open for 9% -> 5% of each run, Pallas kernels for 14% -> 14%
where the time goes in v6:
time: 704 us; the launch traced here: 695 us
  Pallas kernels  307 us (44%)
  waiting for transfers between devices  244 us (35%)
  other arithmetic  51.7 us (7%)
  starting transfers between devices  47.9 us (7%)
  between operations  24.5 us (3%)
  local copies, waits for them, and re-layouts  20.2 us (3%)
    pallas_call x5, Pallas kernels, group_call(): pl.pallas_call(functools.partial(kernel, start, len(given)), grid_spec=pl...  208 us
    all_gather x1, waiting for transfers between devices, shards(): gathered = lax.all_gather(mine, 'dp', axis=0, tiled=True)  114 us
    ppermute x6, waiting for transfers between devices, outwards(): lax.ppermute(x, 'patch', [(k + 1, k), (groups - 2 - k, groups - 1 - k)])  70.8 us
    pallas_call x11, Pallas kernels, weight_grad(): pl.pallas_call(functools.partial(weight_grad_kernel, parts, cut, len(give...  65.6 us
    convert_element_type x27, other arithmetic, low_sum(): return (a.astype(F32) + b.astype(F32)).astype(BF)  30.9 us
    ppermute x6, waiting for transfers between devices, inwards(): lax.ppermute(x, 'patch', [(k, k + 1), (groups - 1 - k, groups - 2 - k)])  27.4 us
    ppermute x18, waiting for transfers between devices, swap_bit(): return lax.ppermute(x, 'dp', [(i, i ^ 1 << bit) for i in range(size)])  24 us
    pallas_call x1, Pallas kernels, tile_update(): pl.pallas_call(tile_kernel, grid_spec=pltpu.PrefetchScalarGridSpec(num_sc...  22.1 us
  transfers between devices with their start and end apart: 40, of which 19 were waited for; matrix products, arithmetic and copies ran while one was open for 5% of the time, Pallas kernels for 14%

profile of v6, /device:TPU:0, one launch (start us, length us, event | category | flops | bytes accessed | tf_op | source)
XLA Modules:
  0.0 695.4 jit_solution(17234251138210503018)
XLA Ops:
  7.2 3.2 convert_element_type.318
  17.2 8.8 %order_patches.1 = (bf16[8,208,768]{2,1,0:T(8,128)(2,1)}, bf16[8,80,768]{2,1,0:T(8,128)(2,1)}, f32[8,80,768]{2,1,0:T(8,128)}, f32[8,208,512]{2,1,0:T(8,128)}) custom-call(s32[8,208,1]{2,1,0:T(8,128)} %copy.54.shuffle_ref, bf16[8,196,768]{2,1,0:T(8,128)(2,1)} %copy.55.pixels_ref, bf16[2,196,768]{2,1,0:T(8,128)(2,1)} %constant.84.clone.sin_d_ref, ...), custom_call_target="tpu_custom_call" | custom-call | tf_op jit(solution)/shard_map/order_patches/pallas_call | solution.py:406
  26.7 114.1 %all-gather.2.cloned.1.call-done.wg_ref = bf16[49280,256]{1,0:T(8,128)(2,1)} async-done(((bf16[6160,256]{1,0:T(8,128)(2,1)}), bf16[49280,256]{1,0:T(8,128)(2,1)}) %all-gather.2.cloned.1.call-update) | async-done | bytes 25231376 | tf_op jit(solution)/shard_map/all_gather | solution.py:1133
  142.5 38.0 %encoder_forward.1 = (f32[640,768]{1,0:T(8,128)}, bf16[640,768]{1,0:T(8,128)(2,1)}, bf16[640,2304]{1,0:T(8,128)(2,1)}, f32[8,3,4,80]{3,2,1,0:T(4,128)}, f32[8,3,...) custom-call(s32[177]{0:T(256)} %fusion.19.row_ref, ...), custom_call_target="tpu_custom_call" | custom-call | flops 1000 | bytes 1000 | tf_op jit(solution)/shard_map/encoder_forward/pallas_call | solution.py:435
  180.5 117.5 %decoder.1 = (bf16[1664,512]{1,0:T(8,128)(2,1)}, bf16[1664,1536]{1,0:T(8,128)(2,1)}, bf16[1664,512]{1,0:T(8,128)(2,1)}, bf16[1664,512]{1,0:T(8,128)(2,1)}, bf16[...) custom-call(s32[177]{0:T(256)} %fusion.19.row_ref, ...), custom_call_target="tpu_custom_call" | custom-call | flops 1000 | bytes 1000 | tf_op jit(solution)/shard_map/decoder/pallas_call | solution.py:435
  298.0 8.4 %weight_grad.11 = (bf16[4,60,32,256]{3,2,1,0:T(8,128)(2,1)}, bf16[4,60,32,256]{3,2,1,0:T(8,128)(2,1)}) custom-call(s32[1]{0:T(128)} %bitcast.9.index_ref, bf16[1664,512]{1,0:T(8,128)(2,1)} %get-tuple-element.131.x_ref, bf16[1664,2048]{1,0:T(8,128)(2,1)} %get-tuple-element.132.g_ref), custom_call_target="tpu_custom_call" | custom-call | flops 1000 | bytes 1000 | tf_op jit(solution)/shard_map/weight_grad/pallas_call | solution.py:898
  306.4 7.9 %weight_grad.12 = (bf16[4,60,32,256]{3,2,1,0:T(8,128)(2,1)}, bf16[4,60,32,256]{3,2,1,0:T(8,128)(2,1)}) custom-call(s32[1]{0:T(128)} %bitcast.9.index_ref, bf16[1664,2048]{1,0:T(8,128)(2,1)} %get-tuple-element.129.x_ref, bf16[1664,512]{1,0:T(8,128)(2,1)} %get-tuple-element.130.g_ref, ...), custom_call_target="tpu_custom_call", output_to_operand_aliasing={{0}: (3, {}), {1}: (4, {})} | custom-call | flops 1000 | bytes 1000 | tf_op jit(solution)/shard_map/weight_grad/pallas_call | solution.py:898
  314.3 3.9 weight_grad.13
  318.2 7.0 %weight_grad.14 = (bf16[4,60,32,256]{3,2,1,0:T(8,128)(2,1)}, bf16[4,60,32,256]{3,2,1,0:T(8,128)(2,1)}) custom-call(s32[1]{0:T(128)} %bitcast.9.index_ref, bf16[1664,512]{1,0:T(8,128)(2,1)} %get-tuple-element.125.x_ref, bf16[1664,1536]{1,0:T(8,128)(2,1)} %get-tuple-element.126.g_ref, ...), custom_call_target="tpu_custom_call", output_to_operand_aliasing={{0}: (3, {}), {1}: (4, {})} | custom-call | flops 1000 | bytes 1000 | tf_op jit(solution)/shard_map/weight_grad/pallas_call | solution.py:898
  325.2 4.8 weight_grad.15
  330.0 3.2 weight_grad.16
  333.5 18.1 %encoder_mlp_back.1 = (bf16[640,768]{1,0:T(8,128)(2,1)}, bf16[640,3072]{1,0:T(8,128)(2,1)}, f32[640,768]{1,0:T(8,128)}, bf16[640,768]{1,0:T(8,128)(2,1)}, f32[8,8192]{1,0:T(8,128)}) custom-call(s32[177]{0:T(256)} %fusion.19.row_ref, bf16[49280,256]{1,0:T(8,128)(2,1)} %all-gather.2.cloned.1.call-done.wg_ref, f32[1,21760]{1,0:T(1,128)} %reshape.118.vec_ref, ...), custom_call_target="tpu_custom_call" | custom-call | flops 1000 | bytes 1000 | tf_op jit(solution)/shard_map/encoder_mlp_back/pallas_call | solution.py:435
  351.6 4.2 add_convert_fusion.1
  360.5 8.0 %weight_grad.17 = (bf16[4,81,32,256]{3,2,1,0:T(8,128)(2,1)}, bf16[4,81,32,256]{3,2,1,0:T(8,128)(2,1)}) custom-call(s32[1]{0:T(128)} %bitcast.9.index_ref, bf16[640,768]{1,0:T(8,128)(2,1)} %get-tuple-element.158.x_ref, bf16[640,3072]{1,0:T(8,128)(2,1)} %get-tuple-element.159.g_ref), custom_call_target="tpu_custom_call" | custom-call | flops 1000 | bytes 1000 | tf_op jit(solution)/shard_map/weight_grad/pallas_call | solution.py:898
  368.6 7.9 %weight_grad.18 = (bf16[4,81,32,256]{3,2,1,0:T(8,128)(2,1)}, bf16[4,81,32,256]{3,2,1,0:T(8,128)(2,1)}) custom-call(s32[1]{0:T(128)} %bitcast.9.index_ref, bf16[640,3072]{1,0:T(8,128)(2,1)} %get-tuple-element.156.x_ref, bf16[640,768]{1,0:T(8,128)(2,1)} %get-tuple-element.157.g_ref, ...), custom_call_target="tpu_custom_call", output_to_operand_aliasing={{0}: (3, {}), {1}: (4, {})} | custom-call | flops 1000 | bytes 1000 | tf_op jit(solution)/shard_map/weight_grad/pallas_call | solution.py:898
  376.4 3.7 weight_grad.19
  387.8 17.6 %encoder_attention_back.2 = (bf16[640,2304]{1,0:T(8,128)(2,1)}, bf16[640,768]{1,0:T(8,128)(2,1)}, f32[8,4608]{1,0:T(8,128)}) custom-call(s32[177]{0:T(256)} %fusion.19.row_ref, s32[8]{0:T(128)} %len_ref.7, bf16[49280,256]{1,0:T(8,128)(2,1)} %all-gather.2.cloned.1.call-done.wg_ref, f32[1,21760]{1,0:T(1,128)} %reshape.118.vec_ref, ...), custom_call_target="tpu_custom_call" | custom-call | flops 1000 | bytes 1000 | tf_op jit(solution)/shard_map/encoder_attention_back/pallas_call | solution.py:435
  405.8 6.8 add_convert_fusion
  417.5 17.0 %encoder_attention_back.3 = (bf16[640,2304]{1,0:T(8,128)(2,1)}, bf16[640,768]{1,0:T(8,128)(2,1)}, f32[8,4608]{1,0:T(8,128)}) custom-call(s32[177]{0:T(256)} %fusion.19.row_ref, s32[8]{0:T(128)} %len_ref.7, bf16[49280,256]{1,0:T(8,128)(2,1)} %all-gather.2.cloned.1.call-done.wg_ref, ...), custom_call_target="tpu_custom_call", output_to_operand_aliasing={{0}: (10, {}), {1}: (11, {})} | custom-call | flops 1000 | bytes 1000 | tf_op jit(solution)/shard_map/encoder_attention_back/pallas_call | solution.py:435
  434.5 10.9 %collective-permute-done.6 = bf16[2,40,32,256]{3,2,1,0:T(8,128)(2,1)} collective-permute-done((bf16[2,40,32,256]{3,2,1,0:T(8,128)(2,1)}, bf16[2,40,32,256]{3,2,1,0:T(8,128)(2,1)}, u32[]{:S(2)}, u32[]{:S(2)}) %collective-permute-start.6) | collective-permute-done | bytes 1310752 | tf_op jit(solution)/shard_map/ppermute | solution.py:965
  445.5 2.2 fusion.1
  447.7 2.3 fusion
  450.1 3.4 collective-permute-start.9
  458.0 2.1 seed_buffers.1
  460.0 7.0 %weight_grad.20 = (bf16[4,38,32,256]{3,2,1,0:T(8,128)(2,1)}, bf16[4,38,32,256]{3,2,1,0:T(8,128)(2,1)}) custom-call(s32[1]{0:T(128)} %bitcast.9.index_ref, bf16[640,768]{1,0:T(8,128)(2,1)} %get-tuple-element.191.x_ref, bf16[640,2304]{1,0:T(8,128)(2,1)} %get-tuple-element.192.g_ref, ...), custom_call_target="tpu_custom_call", output_to_operand_aliasing={{0}: (3, {}), {1}: (4, {})} | custom-call | flops 1000 | bytes 1000 | tf_op jit(solution)/shard_map/weight_grad/pallas_call | solution.py:898
  467.1 3.7 weight_grad.21
  475.7 2.3 fusion.4
  485.2 2.8 add_convert_fusion.2
  489.7 21.2 %collective-permute-done.13 = bf16[30,32,256]{2,1,0:T(8,128)(2,1)S(1)} collective-permute-done((bf16[30,32,256]{2,1,0:T(8,128)(2,1)S(1)}, bf16[30,32,256]{2,1,0:T(8,128)(2,1)S(1)}, u32[]{:S(2)}, u32[]{:S(2)}) %collective-permute-start.13) | collective-permute-done | bytes 491552 | tf_op jit(solution)/shard_map/ppermute | solution.py:1002
  511.7 8.7 %collective-permute-done.15 = bf16[30,32,256]{2,1,0:T(8,128)(2,1)S(1)} collective-permute-done((bf16[30,32,256]{2,1,0:T(8,128)(2,1)S(1)}, bf16[30,32,256]{2,1,0:T(8,128)(2,1)S(1)}, u32[]{:S(2)}, u32[]{:S(2)}) %collective-permute-start.15) | collective-permute-done | bytes 491552 | tf_op jit(solution)/shard_map/ppermute | solution.py:1002
  526.4 10.8 %collective-permute-done.17 = bf16[40,32,256]{2,1,0:T(8,128)(2,1)S(1)} collective-permute-done((bf16[40,32,256]{2,1,0:T(8,128)(2,1)S(1)}, bf16[40,32,256]{2,1,0:T(8,128)(2,1)S(1)}, u32[]{:S(2)}, u32[]{:S(2)}) %collective-permute-start.17) | collective-permute-done | bytes 655392 | tf_op jit(solution)/shard_map/ppermute | solution.py:996
  538.3 7.1 %collective-permute-start.30 = (bf16[19,32,256]{2,1,0:T(8,128)(2,1)S(1)}, bf16[19,32,256]{2,1,0:T(8,128)(2,1)S(1)}, u32[]{:S(2)}, u32[]{:S(2)}) collective-permute-start(bf16[19,32,256]{2,1,0:T(8,128)(2,1)S(1)} %fusion.10), channel_id=1, source_target_pairs={{0,1},{3,2},{4,5},{7,6},{8,9},{11,10},{12,13},{15,14},{16,17},{19,... | collective-permute-start | bytes 933896 | tf_op jit(solution)/shard_map/ppermute | solution.py:996
  546.8 4.8 collective-permute-done.20
  552.6 5.7 collective-permute-done.30
  559.1 4.1 collective-permute-done.25
  570.0 16.4 %collective-permute-done.19 = bf16[40,32,256]{2,1,0:T(8,128)(2,1)S(1)} collective-permute-done((bf16[40,32,256]{2,1,0:T(8,128)(2,1)S(1)}, bf16[40,32,256]{2,1,0:T(8,128)(2,1)S(1)}, u32[]{:S(2)}, u32[]{:S(2)}) %collective-permute-start.19) | collective-permute-done | bytes 655392 | tf_op jit(solution)/shard_map/ppermute | solution.py:1002
  586.7 14.1 %collective-permute-done.22 = bf16[41,32,256]{2,1,0:T(8,128)(2,1)S(1)} collective-permute-done((bf16[41,32,256]{2,1,0:T(8,128)(2,1)S(1)}, bf16[41,32,256]{2,1,0:T(8,128)(2,1)S(1)}, u32[]{:S(2)}, u32[]{:S(2)}) %collective-permute-start.22) | collective-permute-done | bytes 671776 | tf_op jit(solution)/shard_map/ppermute | solution.py:1002
  601.1 10.4 %collective-permute-done.27 = bf16[19,32,256]{2,1,0:T(8,128)(2,1)S(1)} collective-permute-done((bf16[19,32,256]{2,1,0:T(8,128)(2,1)S(1)}, bf16[19,32,256]{2,1,0:T(8,128)(2,1)S(1)}, u32[]{:S(2)}, u32[]{:S(2)}) %collective-permute-start.27) | collective-permute-done | bytes 311328 | tf_op jit(solution)/shard_map/ppermute | solution.py:1002
  612.4 2.7 gather_fusion.1
  615.1 4.0 all-to-all-start
  629.2 2.1 multiply_reduce_fusion.1
  632.0 2.1 multiply_reduce_fusion
  636.9 3.5 collective-permute-done.33
  640.5 4.4 collective-permute-done.34
  646.1 2.0 collective-permute-start.36
  648.1 7.9 %collective-permute-done.36 = f32[3]{0:T(128)S(1)} collective-permute-done((f32[3]{0:T(128)S(1)}, f32[3]{0:T(128)S(1)}, u32[]{:S(2)}, u32[]{:S(2)}) %collective-permute-start.36) | collective-permute-done | bytes 44 | tf_op jit(solution)/shard_map/ppermute | solution.py:965
  657.4 2.1 collective-permute-done.37
  665.1 22.1 %tile_update.1 = (f32[24,256,256]{2,1,0:T(8,128)}, f32[24,256,256]{2,1,0:T(8,128)}, f32[24,256,256]{2,1,0:T(8,128)}, f32[24,256,256]{2,1,0:T(8,128)}) custom-call(f32[1]{0:T(128)} %bitcast.41.scale_ref, bf16[8,24,32,256]{3,2,1,0:T(8,128)(2,1)} %bitcast.97, f32[24,256,256]{2,1,0:T(8,128)} %w_ref.1, f32[24,256,256]{2,1,0:T(8,128)} %left_stat_ref.1, ...), custom_call_target="tpu_custom_call" | custom-call | tf_op jit(solution)/shard_map/tile_update/pallas_call | solution.py:1059
  (208 shorter events, 77.7 us)
Async XLA Ops:
  7.2 133.7 %all-gather.2.cloned.1.call-start = ((), (), s32[]{:S(2)}) async-start(), calls=%async_computation.1 | async-start | bytes 28385280 | tf_op jit(solution)/shard_map/all_gather | solution.py:1133
  333.2 18.4 %collective-permute-start = (bf16[4,60,32,256]{3,2,1,0:T(8,128)(2,1)}, bf16[4,60,32,256]{3,2,1,0:T(8,128)(2,1)}, u32[]{:S(2)}, u32[]{:S(2)}) collective-permute-start(bf16[4,60,32,256]{3,2,1,0:T(8,128)(2,1)} %get-tuple-element.153), channel_id=1, source_target_pairs={{0,4},{4,0},{8,12},{12,8},{16,20},{20,16},{24,28},{28,24},{1,5},{5... | collective-permute-start | bytes 11796488 | tf_op jit(solution)/shard_map/ppermute | solution.py:965
  357.5 24.2 %collective-permute-start.2 = (bf16[2,30,32,256]{3,2,1,0:T(8,128)(2,1)}, bf16[2,30,32,256]{3,2,1,0:T(8,128)(2,1)}, u32[]{:S(2)}, u32[]{:S(2)}) collective-permute-start(bf16[2,30,32,256]{3,2,1,0:T(8,128)(2,1)} %slice_bitcast_fusion.3), channel_id=1, source_target_pairs={{0,16},{4,20},{8,24},{12,28},{16,0},{20,4},{24,8},{28,12},{1,17},{... | collective-permute-start | bytes 2949128 | tf_op jit(solution)/shard_map/ppermute | solution.py:965
  358.9 24.4 %collective-permute-start.1 = (bf16[2,30,32,256]{3,2,1,0:T(8,128)(2,1)}, bf16[2,30,32,256]{3,2,1,0:T(8,128)(2,1)}, u32[]{:S(2)}, u32[]{:S(2)}) collective-permute-start(bf16[2,30,32,256]{3,2,1,0:T(8,128)(2,1)} %slice_bitcast_fusion.4), channel_id=1, source_target_pairs={{0,8},{4,12},{8,0},{12,4},{16,24},{20,28},{24,16},{28,20},{1,9},{5... | collective-permute-start | bytes 2949128 | tf_op jit(solution)/shard_map/ppermute | solution.py:965
  385.3 20.5 %collective-permute-start.5 = (bf16[4,81,32,256]{3,2,1,0:T(8,128)(2,1)}, bf16[4,81,32,256]{3,2,1,0:T(8,128)(2,1)}, u32[]{:S(2)}, u32[]{:S(2)}) collective-permute-start(bf16[4,81,32,256]{3,2,1,0:T(8,128)(2,1)} %get-tuple-element.179), channel_id=1, source_target_pairs={{0,4},{4,0},{8,12},{12,8},{16,20},{20,16},{24,28},{28,24},{1,5},{5... | collective-permute-start | bytes 15925256 | tf_op jit(solution)/shard_map/ppermute | solution.py:965
  385.4 20.0 %collective-permute-start.4 = (bf16[30,32,256]{2,1,0:T(8,128)(2,1)S(1)}, bf16[30,32,256]{2,1,0:T(8,128)(2,1)S(1)}, u32[]{:S(2)}, u32[]{:S(2)}) collective-permute-start(bf16[30,32,256]{2,1,0:T(8,128)(2,1)S(1)} %slice_bitcast_fusion.10), channel_id=1, source_target_pairs={{0,8},{4,12},{8,0},{12,4},{16,24},{20,28},{24,16},{28,20},{1,9},{5... | collective-permute-start | bytes 1474568 | tf_op jit(solution)/shard_map/ppermute | solution.py:965
  387.0 18.6 %collective-permute-start.3 = (bf16[30,32,256]{2,1,0:T(8,128)(2,1)S(1)}, bf16[30,32,256]{2,1,0:T(8,128)(2,1)S(1)}, u32[]{:S(2)}, u32[]{:S(2)}) collective-permute-start(bf16[30,32,256]{2,1,0:T(8,128)(2,1)S(1)} %slice_bitcast_fusion.11), channel_id=1, source_target_pairs={{0,16},{4,20},{8,24},{12,28},{16,0},{20,4},{24,8},{28,12},{1,17},{... | collective-permute-start | bytes 1474568 | tf_op jit(solution)/shard_map/ppermute | solution.py:965
  414.5 30.9 %collective-permute-start.6 = (bf16[2,40,32,256]{3,2,1,0:T(8,128)(2,1)}, bf16[2,40,32,256]{3,2,1,0:T(8,128)(2,1)}, u32[]{:S(2)}, u32[]{:S(2)}) collective-permute-start(bf16[2,40,32,256]{3,2,1,0:T(8,128)(2,1)} %slice_bitcast_fusion.1), channel_id=1, source_target_pairs={{0,8},{4,12},{8,0},{12,4},{16,24},{20,28},{24,16},{28,20},{1,9},{5... | collective-permute-start | bytes 3932168 | tf_op jit(solution)/shard_map/ppermute | solution.py:965
  416.3 31.4 %collective-permute-start.7 = (bf16[2,41,32,256]{3,2,1,0:T(8,128)(2,1)}, bf16[2,41,32,256]{3,2,1,0:T(8,128)(2,1)}, u32[]{:S(2)}, u32[]{:S(2)}) collective-permute-start(bf16[2,41,32,256]{3,2,1,0:T(8,128)(2,1)} %slice_bitcast_fusion), channel_id=1, source_target_pairs={{0,16},{4,20},{8,24},{12,28},{16,0},{20,4},{24,8},{28,12},{1,17},{... | collective-permute-start | bytes 4030472 | tf_op jit(solution)/shard_map/ppermute | solution.py:965
  450.1 20.8 %collective-permute-start.9 = (bf16[30,32,256]{2,1,0:T(8,128)(2,1)S(1)}, bf16[30,32,256]{2,1,0:T(8,128)(2,1)S(1)}, u32[]{:S(2)}, u32[]{:S(2)}) collective-permute-start(bf16[30,32,256]{2,1,0:T(8,128)(2,1)S(1)} %fusion.8), channel_id=1, source_target_pairs={{0,1},{3,2},{4,5},{7,6},{8,9},{11,10},{12,13},{15,14},{16,17},{19,... | collective-permute-start | bytes 1474568 | tf_op jit(solution)/shard_map/ppermute | solution.py:996
  453.6 21.1 %collective-permute-start.10 = (bf16[40,32,256]{2,1,0:T(8,128)(2,1)S(1)}, bf16[40,32,256]{2,1,0:T(8,128)(2,1)S(1)}, u32[]{:S(2)}, u32[]{:S(2)}) collective-permute-start(bf16[40,32,256]{2,1,0:T(8,128)(2,1)S(1)} %slice_bitcast_fusion.6), channel_id=1, source_target_pairs={{0,16},{4,20},{8,24},{12,28},{16,0},{20,4},{24,8},{28,12},{1,17},{... | collective-permute-start | bytes 1966088 | tf_op jit(solution)/shard_map/ppermute | solution.py:965
  454.8 18.8 %collective-permute-start.8 = (bf16[30,32,256]{2,1,0:T(8,128)(2,1)S(1)}, bf16[30,32,256]{2,1,0:T(8,128)(2,1)S(1)}, u32[]{:S(2)}, u32[]{:S(2)}) collective-permute-start(bf16[30,32,256]{2,1,0:T(8,128)(2,1)S(1)} %fusion.9), channel_id=1, source_target_pairs={{0,1},{3,2},{4,5},{7,6},{8,9},{11,10},{12,13},{15,14},{16,17},{19,... | collective-permute-start | bytes 1474568 | tf_op jit(solution)/shard_map/ppermute | solution.py:996
  457.1 18.7 %collective-permute-start.11 = (bf16[41,32,256]{2,1,0:T(8,128)(2,1)}, bf16[41,32,256]{2,1,0:T(8,128)(2,1)}, u32[]{:S(2)}, u32[]{:S(2)}) collective-permute-start(bf16[41,32,256]{2,1,0:T(8,128)(2,1)} %slice_bitcast_fusion.5), channel_id=1, source_target_pairs={{0,8},{4,12},{8,0},{12,4},{16,24},{20,28},{24,16},{28,20},{1,9},{5... | collective-permute-start | bytes 2015240 | tf_op jit(solution)/shard_map/ppermute | solution.py:965
  478.1 7.1 %collective-permute-start.16 = (bf16[4,38,32,256]{3,2,1,0:T(8,128)(2,1)}, bf16[4,38,32,256]{3,2,1,0:T(8,128)(2,1)}, u32[]{:S(2)}, u32[]{:S(2)}) collective-permute-start(bf16[4,38,32,256]{3,2,1,0:T(8,128)(2,1)} %get-tuple-element.211), channel_id=1, source_target_pairs={{0,4},{4,0},{8,12},{12,8},{16,20},{20,16},{24,28},{28,24},{1,5},{5... | collective-permute-start | bytes 7471112 | tf_op jit(solution)/shard_map/ppermute | solution.py:965
  478.1 3.1 collective-permute-start.12
  480.4 3.3 collective-permute-start.14
  482.4 28.5 %copy-start.11 = (bf16[30,32,256]{2,1,0:T(8,128)(2,1)}, bf16[30,32,256]{2,1,0:T(8,128)(2,1)S(1)}, u32[]{:S(2)}) copy-start(bf16[30,32,256]{2,1,0:T(8,128)(2,1)S(1)} %add_convert_fusion.8) | copy-start | bytes 1474564
  482.4 28.5 %collective-permute-start.13 = (bf16[30,32,256]{2,1,0:T(8,128)(2,1)S(1)}, bf16[30,32,256]{2,1,0:T(8,128)(2,1)S(1)}, u32[]{:S(2)}, u32[]{:S(2)}) collective-permute-start(bf16[30,32,256]{2,1,0:T(8,128)(2,1)S(1)} %add_convert_fusion.8), channel_id=1, source_target_pairs={{1,0},{2,3},{5,4},{6,7},{9,8},{10,11},{13,12},{14,15},{17,16},{18,... | collective-permute-start | bytes 1474568 | tf_op jit(solution)/shard_map/ppermute | solution.py:1002
  483.9 36.5 %copy-start.12 = (bf16[30,32,256]{2,1,0:T(8,128)(2,1)}, bf16[30,32,256]{2,1,0:T(8,128)(2,1)S(1)}, u32[]{:S(2)}) copy-start(bf16[30,32,256]{2,1,0:T(8,128)(2,1)S(1)} %add_convert_fusion.7) | copy-start | bytes 1474564
  483.9 36.5 %collective-permute-start.15 = (bf16[30,32,256]{2,1,0:T(8,128)(2,1)S(1)}, bf16[30,32,256]{2,1,0:T(8,128)(2,1)S(1)}, u32[]{:S(2)}, u32[]{:S(2)}) collective-permute-start(bf16[30,32,256]{2,1,0:T(8,128)(2,1)S(1)} %add_convert_fusion.7), channel_id=1, source_target_pairs={{1,0},{2,3},{5,4},{6,7},{9,8},{10,11},{13,12},{14,15},{17,16},{18,... | collective-permute-start | bytes 1474568 | tf_op jit(solution)/shard_map/ppermute | solution.py:1002
  488.3 32.3 %copy-start.18 = (bf16[40,32,256]{2,1,0:T(8,128)(2,1)S(1)}, bf16[40,32,256]{2,1,0:T(8,128)(2,1)}, u32[]{:S(2)}) copy-start(bf16[40,32,256]{2,1,0:T(8,128)(2,1)} %fusion.5) | copy-start | bytes 1966084
  488.3 33.8 %copy-start.16 = (bf16[41,32,256]{2,1,0:T(8,128)(2,1)S(1)}, bf16[41,32,256]{2,1,0:T(8,128)(2,1)}, u32[]{:S(2)}) copy-start(bf16[41,32,256]{2,1,0:T(8,128)(2,1)} %fusion.4) | copy-start | bytes 2015236
  488.4 35.1 %collective-permute-start.28 = (bf16[2,19,32,256]{3,2,1,0:T(8,128)(2,1)S(1)}, bf16[2,19,32,256]{3,2,1,0:T(8,128)(2,1)S(1)}, u32[]{:S(2)}, u32[]{:S(2)}) collective-permute-start(bf16[2,19,32,256]{3,2,1,0:T(8,128)(2,1)S(1)} %slice_bitcast_fusion.8), channel_id=1, source_target_pairs={{0,16},{4,20},{8,24},{12,28},{16,0},{20,4},{24,8},{28,12},{1,17},{... | collective-permute-start | bytes 1867784 | tf_op jit(solution)/shard_map/ppermute | solution.py:965
  511.1 13.8 %collective-permute-start.23 = (bf16[2,19,32,256]{3,2,1,0:T(8,128)(2,1)S(1)}, bf16[2,19,32,256]{3,2,1,0:T(8,128)(2,1)S(1)}, u32[]{:S(2)}, u32[]{:S(2)}) collective-permute-start(bf16[2,19,32,256]{3,2,1,0:T(8,128)(2,1)S(1)} %slice_bitcast_fusion.9), channel_id=1, source_target_pairs={{0,8},{4,12},{8,0},{12,4},{16,24},{20,28},{24,16},{28,20},{1,9},{5... | collective-permute-start | bytes 1867784 | tf_op jit(solution)/shard_map/ppermute | solution.py:965
  520.6 16.6 %collective-permute-start.17 = (bf16[40,32,256]{2,1,0:T(8,128)(2,1)S(1)}, bf16[40,32,256]{2,1,0:T(8,128)(2,1)S(1)}, u32[]{:S(2)}, u32[]{:S(2)}) collective-permute-start(bf16[40,32,256]{2,1,0:T(8,128)(2,1)S(1)} %copy-done.18), channel_id=1, source_target_pairs={{0,1},{3,2},{4,5},{7,6},{8,9},{11,10},{12,13},{15,14},{16,17},{19,... | collective-permute-start | bytes 1966088 | tf_op jit(solution)/shard_map/ppermute | solution.py:996
  522.1 29.5 %collective-permute-start.20 = (bf16[41,32,256]{2,1,0:T(8,128)(2,1)S(1)}, bf16[41,32,256]{2,1,0:T(8,128)(2,1)S(1)}, u32[]{:S(2)}, u32[]{:S(2)}) collective-permute-start(bf16[41,32,256]{2,1,0:T(8,128)(2,1)S(1)} %copy-done.16), channel_id=1, source_target_pairs={{0,1},{3,2},{4,5},{7,6},{8,9},{11,10},{12,13},{15,14},{16,17},{19,... | collective-permute-start | bytes 2015240 | tf_op jit(solution)/shard_map/ppermute | solution.py:996
  523.8 14.4 %collective-permute-start.29 = (bf16[19,32,256]{2,1,0:T(8,128)(2,1)S(1)}, bf16[19,32,256]{2,1,0:T(8,128)(2,1)S(1)}, u32[]{:S(2)}, u32[]{:S(2)}) collective-permute-start(bf16[19,32,256]{2,1,0:T(8,128)(2,1)S(1)} %slice_bitcast_fusion.12), channel_id=1, source_target_pairs={{0,8},{4,12},{8,0},{12,4},{16,24},{20,28},{24,16},{28,20},{1,9},{5... | collective-permute-start | bytes 933896 | tf_op jit(solution)/shard_map/ppermute | solution.py:965
  525.1 20.3 %collective-permute-start.24 = (bf16[19,32,256]{2,1,0:T(8,128)(2,1)S(1)}, bf16[19,32,256]{2,1,0:T(8,128)(2,1)S(1)}, u32[]{:S(2)}, u32[]{:S(2)}) collective-permute-start(bf16[19,32,256]{2,1,0:T(8,128)(2,1)S(1)} %slice_bitcast_fusion.14), channel_id=1, source_target_pairs={{0,16},{4,20},{8,24},{12,28},{16,0},{20,4},{24,8},{28,12},{1,17},{... | collective-permute-start | bytes 933896 | tf_op jit(solution)/shard_map/ppermute | solution.py:965
  537.5 26.5 %collective-permute-start.18 = (bf16[40,32,256]{2,1,0:T(8,128)(2,1)S(1)}, bf16[40,32,256]{2,1,0:T(8,128)(2,1)S(1)}, u32[]{:S(2)}, u32[]{:S(2)}) collective-permute-start(bf16[40,32,256]{2,1,0:T(8,128)(2,1)S(1)} %add_convert_fusion.6), channel_id=1, source_target_pairs={{1,2},{2,1},{5,6},{6,5},{9,10},{10,9},{13,14},{14,13},{17,18},{18,... | collective-permute-start | bytes 1966088 | tf_op jit(solution)/shard_map/ppermute | solution.py:999
  538.3 20.0 %collective-permute-start.30 = (bf16[19,32,256]{2,1,0:T(8,128)(2,1)S(1)}, bf16[19,32,256]{2,1,0:T(8,128)(2,1)S(1)}, u32[]{:S(2)}, u32[]{:S(2)}) collective-permute-start(bf16[19,32,256]{2,1,0:T(8,128)(2,1)S(1)} %fusion.10), channel_id=1, source_target_pairs={{0,1},{3,2},{4,5},{7,6},{8,9},{11,10},{12,13},{15,14},{16,17},{19,... | collective-permute-start | bytes 933896 | tf_op jit(solution)/shard_map/ppermute | solution.py:996
  545.5 17.7 %collective-permute-start.25 = (bf16[19,32,256]{2,1,0:T(8,128)(2,1)S(1)}, bf16[19,32,256]{2,1,0:T(8,128)(2,1)S(1)}, u32[]{:S(2)}, u32[]{:S(2)}) collective-permute-start(bf16[19,32,256]{2,1,0:T(8,128)(2,1)S(1)} %fusion.11), channel_id=1, source_target_pairs={{0,1},{3,2},{4,5},{7,6},{8,9},{11,10},{12,13},{15,14},{16,17},{19,... | collective-permute-start | bytes 933896 | tf_op jit(solution)/shard_map/ppermute | solution.py:996
  551.9 13.7 %collective-permute-start.21 = (bf16[41,32,256]{2,1,0:T(8,128)(2,1)S(1)}, bf16[41,32,256]{2,1,0:T(8,128)(2,1)S(1)}, u32[]{:S(2)}, u32[]{:S(2)}) collective-permute-start(bf16[41,32,256]{2,1,0:T(8,128)(2,1)S(1)} %add_convert_fusion.4), channel_id=1, source_target_pairs={{1,2},{2,1},{5,6},{6,5},{9,10},{10,9},{13,14},{14,13},{17,18},{18,... | collective-permute-start | bytes 2015240 | tf_op jit(solution)/shard_map/ppermute | solution.py:999
  558.4 8.7 %collective-permute-start.31 = (bf16[19,32,256]{2,1,0:T(8,128)(2,1)S(1)}, bf16[19,32,256]{2,1,0:T(8,128)(2,1)S(1)}, u32[]{:S(2)}, u32[]{:S(2)}) collective-permute-start(bf16[19,32,256]{2,1,0:T(8,128)(2,1)S(1)} %add_convert_fusion.12), channel_id=1, source_target_pairs={{1,2},{2,1},{5,6},{6,5},{9,10},{10,9},{13,14},{14,13},{17,18},{18,... | collective-permute-start | bytes 933896 | tf_op jit(solution)/shard_map/ppermute | solution.py:999
  563.3 5.2 collective-permute-start.26
  564.3 22.1 %collective-permute-start.19 = (bf16[40,32,256]{2,1,0:T(8,128)(2,1)S(1)}, bf16[40,32,256]{2,1,0:T(8,128)(2,1)S(1)}, u32[]{:S(2)}, u32[]{:S(2)}) collective-permute-start(bf16[40,32,256]{2,1,0:T(8,128)(2,1)S(1)} %add_convert_fusion.5), channel_id=1, source_target_pairs={{1,0},{2,3},{5,4},{6,7},{9,8},{10,11},{13,12},{14,15},{17,16},{18,... | collective-permute-start | bytes 1966088 | tf_op jit(solution)/shard_map/ppermute | solution.py:1002
  565.8 35.2 %copy-start.5 = (bf16[41,32,256]{2,1,0:T(8,128)(2,1)}, bf16[41,32,256]{2,1,0:T(8,128)(2,1)S(1)}, u32[]{:S(2)}) copy-start(bf16[41,32,256]{2,1,0:T(8,128)(2,1)S(1)} %add_convert_fusion.3) | copy-start | bytes 2015236
  565.8 34.9 %collective-permute-start.22 = (bf16[41,32,256]{2,1,0:T(8,128)(2,1)S(1)}, bf16[41,32,256]{2,1,0:T(8,128)(2,1)S(1)}, u32[]{:S(2)}, u32[]{:S(2)}) collective-permute-start(bf16[41,32,256]{2,1,0:T(8,128)(2,1)S(1)} %add_convert_fusion.3), channel_id=1, source_target_pairs={{1,0},{2,3},{5,4},{6,7},{9,8},{10,11},{13,12},{14,15},{17,16},{18,... | collective-permute-start | bytes 2015240 | tf_op jit(solution)/shard_map/ppermute | solution.py:1002
  567.3 44.3 %collective-permute-start.32 = (bf16[19,32,256]{2,1,0:T(8,128)(2,1)S(1)}, bf16[19,32,256]{2,1,0:T(8,128)(2,1)S(1)}, u32[]{:S(2)}, u32[]{:S(2)}) collective-permute-start(bf16[19,32,256]{2,1,0:T(8,128)(2,1)S(1)} %add_convert_fusion.11), channel_id=1, source_target_pairs={{1,0},{2,3},{5,4},{6,7},{9,8},{10,11},{13,12},{14,15},{17,16},{18,... | collective-permute-start | bytes 933896 | tf_op jit(solution)/shard_map/ppermute | solution.py:1002
  568.7 42.8 %collective-permute-start.27 = (bf16[19,32,256]{2,1,0:T(8,128)(2,1)S(1)}, bf16[19,32,256]{2,1,0:T(8,128)(2,1)S(1)}, u32[]{:S(2)}, u32[]{:S(2)}) collective-permute-start(bf16[19,32,256]{2,1,0:T(8,128)(2,1)S(1)} %add_convert_fusion.13), channel_id=1, source_target_pairs={{1,0},{2,3},{5,4},{6,7},{9,8},{10,11},{13,12},{14,15},{17,16},{18,... | collective-permute-start | bytes 933896 | tf_op jit(solution)/shard_map/ppermute | solution.py:1002
  586.4 26.0 %copy-start.17 = (bf16[40,32,256]{2,1,0:T(8,128)(2,1)}, bf16[40,32,256]{2,1,0:T(8,128)(2,1)S(1)}, u32[]{:S(2)}) copy-start(bf16[40,32,256]{2,1,0:T(8,128)(2,1)S(1)} %collective-permute-done.19) | copy-start | bytes 1966084
  615.1 48.4 %all-to-all-start = ((bf16[192,32,256]{2,1,0:T(8,128)(2,1)}), bf16[192,32,256]{2,1,0:T(8,128)(2,1)S(1)}, u32[]{:S(2)}, u32[]{:S(2)}) async-start(bf16[192,32,256]{2,1,0:T(8,128)(2,1)} %gather_fusion.1), calls=%async_computation | async-start | bytes 6291456 | tf_op jit(solution)/shard_map/all_to_all | solution.py:1249
  622.4 40.5 %copy-start.26 = (f32[2560]{0:T(1024)S(1)}, f32[2560]{0:T(1024)}, u32[]{:S(2)}) copy-start(f32[2560]{0:T(1024)} %param.22) | copy-start | bytes 30724
  622.4 40.5 %copy-start.27 = (f32[2560]{0:T(1024)S(1)}, f32[2560]{0:T(1024)}, u32[]{:S(2)}) copy-start(f32[2560]{0:T(1024)} %param.21) | copy-start | bytes 30724
  636.9 3.5 collective-permute-start.33
  640.5 4.4 collective-permute-start.34
  645.0 1.1 collective-permute-start.35
  646.1 9.8 %collective-permute-start.36 = (f32[3]{0:T(128)S(1)}, f32[3]{0:T(128)S(1)}, u32[]{:S(2)}, u32[]{:S(2)}) collective-permute-start(f32[3]{0:T(128)S(1)} %add.190), channel_id=1, source_target_pairs={{0,8},{4,12},{8,0},{12,4},{16,24},{20,28},{24,16},{28,20},{1,9},{5... | collective-permute-start | bytes 44 | tf_op jit(solution)/shard_map/ppermute | solution.py:965
  655.9 3.5 collective-permute-start.37
  (23 other events, 166.5 us)
Sparse Core Ops, SparseCore 0:
  12.5 128.2 all-gather.1

commit v7 on v6

--- a/solution.py
+++ b/solution.py
@@ -1157,40 +1157,44 @@
 
     rows_cut = BS // parts
 
-    def gradients(chunk, pairs, *vector):
+    def gradients(chunk, pairs, vector=(), first=0, buffers=None):
         used = sum(r * c for _, r, c, _ in CHUNKS[chunk])
-        at, buffers = 0, None
-        if sizes[chunk] > used:
+        if sizes[chunk] > used and buffers is None:
             buffers = seed_buffers(index, parts, sizes[chunk], used, *vector)
-        for (x, g), (_, row_tiles, col_tiles, block) in zip(pairs, CHUNKS[chunk]):
+        at = sum(r * c for _, r, c, _ in CHUNKS[chunk][:first])
+        for (x, g), (_, row_tiles, col_tiles, block) in zip(pairs, CHUNKS[chunk][first:]):
             buffers = weight_grad(index, parts, sizes[chunk], at, x, g, block, buffers)
             at += row_tiles * col_tiles
         return buffers
-
-    after = lax.optimization_barrier
-    buf0 = gradients(
-        0, [(d_h2, d_du), (d_act, d_gdown), (d_att, d_gproj), (d_h1, d_dqkv), (d_hn, d_gpred), (hn, glat)]
-    )
-    glat, buf0 = after((glat, buf0))
-    gdown, du, grad_mid, gproj, m_sums = encoder_mlp_back(tile_rows, gathered, vector, glat, x1, mid, slope, 2)
-    half0, left0 = reduce_core(buf0, parts)
-    gdown, du, gproj, half0 = after((gdown, du, gproj, half0))
-    buf1 = gradients(1, [(h2, du), (act, gdown), (att, gproj)])
-    half0, left0 = reduce_chips((half0, left0), parts, 1)
-    gproj, buf1, half0 = after((gproj, buf1, half0))
 
     def attention_back(gproj, k, given):
         return encoder_attention_back(
             tile_rows, vis_len, gathered, vector, gproj, grad_mid, qkv, lse, out_t, x0, 2, (k, 2), given
         )
 
+    def core(buffers):
+        return reduce_core(buffers, parts)
+
+    def chips(state, steps):
+        return reduce_chips(state, parts, steps)
+
+    after = lax.optimization_barrier
+    steps = patch_steps(groups)
+    gdown, du, grad_mid, gproj, m_sums = encoder_mlp_back(tile_rows, gathered, vector, glat, x1, mid, slope, 2)
+    buf1 = gradients(1, [(h2, du), (act, gdown), (att, gproj)])
+    d_h2, d_act, buf1 = after((d_h2, d_act, buf1))
+    buf0 = gradients(0, [(d_h2, d_du), (d_act, d_gdown)])
+    half1, left1 = core(buf1)
+    d_att, d_h1, d_hn, hn, buf0, half1 = after((d_att, d_h1, d_hn, hn, buf0, half1))
+    half1, left1 = chips((half1, left1), 1)
+    buf0 = gradients(0, [(d_att, d_gproj), (d_h1, d_dqkv), (d_hn, d_gpred), (hn, glat)], (), 2, buf0)
+    gproj, buf0 = after((gproj, buf0))
     dqkv, gembed, a_sums = attention_back(gproj, 0, ())
-    half0, left0 = reduce_chips((half0, left0), parts, 99)
-    half1, left1 = reduce_core(buf1, parts)
-    gproj, dqkv, gembed, half0, half1 = after((gproj, dqkv, gembed, half0, half1))
+    gproj, dqkv, gembed, buf0, half1 = after((gproj, dqkv, gembed, buf0, half1))
     dqkv, gembed, b_sums = attention_back(gproj, 1, (dqkv, gembed))
-    half1, left1 = reduce_chips((half1, left1), parts, 1)
-    dqkv, gembed, b_sums, half0, half1 = after((dqkv, gembed, b_sums, half0, half1))
+    (one, two), _ = chips((half1, left1), 99)
+    half0, left0 = core(buf0)
+    dqkv, gembed, b_sums, half0, one, two = after((dqkv, gembed, b_sums, half0, one, two))
 
     late, early, dec = (0, 1), (2,), (3,)
     parcels = [
@@ -1215,15 +1219,27 @@
         (dec, DS_NORM, 2 * E),
         (dec, DS_HEAD, PIX),
     ]
-    buf2 = gradients(2, [(h1, dqkv), (visible_pix.reshape(-1, PIX), gembed)], (a_sums, b_sums, m_sums, d_sums), parcels, own)
-    half1, _ = reduce_chips((half1, left1), parts, 99)
-    steps = patch_steps(groups)
+    sums = (a_sums, b_sums, m_sums, d_sums)
+    buf2 = gradients(2, [(h1, dqkv), (visible_pix.reshape(-1, PIX), gembed)], (sums, parcels, own))
+    half0, left0 = chips((half0, left0), 1)
+    one = sum_patch(one, steps[:1])
+    two = sum_patch(two, steps[:1])
+    buf2, half0, one = after((buf2, half0, one))
+    half2, left2 = core(buf2)
+    half0, _ = chips((half0, left0), 99)
+    one = sum_patch(one, steps[1:2])
+    half2, half0, one, two = after((half2, half0, one, two))
+    half2, left2 = chips((half2, left2), 1)
+    one = sum_patch(one, steps[2:])
+    two = sum_patch(two, steps[1:2])
     half0 = [sum_patch(x, steps[:1]) for x in half0]
-    buf2, half0, half1 = after((buf2, half0, half1))
-    half2, left2 = reduce_core(buf2, parts)
-    half1, half2 = after((half1, half2))
-    half2, _ = reduce_chips((half2, left2), parts, 99)
-    pieces = [sum_patch(x, steps[1:]) for x in half0] + [sum_patch(x, steps) for x in half1 + half2]
+    half2, two = after((half2, two))
+    half2, _ = chips((half2, left2), 99)
+    two = sum_patch(two, steps[2:])
+    half2, half0 = after((half2, half0))
+    half2 = [sum_patch(x, steps) for x in half2]
+    half0 = [sum_patch(x, steps[1:]) for x in half0]
+    pieces = half0 + [one, two] + half2
     mine = jnp.where(lax.axis_index("patch") == 0, 1.0, 0.0)
 
     def squares(x):

time: 704 us -> 693 us (0.984)
  waiting for transfers between devices: 244 us -> 212 us
  other arithmetic: 51.7 us -> 64.5 us
    ppermute x6, waiting for transfers between devices: 70.8 us -> 43.4 us  [outwards(): lax.ppermute(x, 'patch', [(k + 1, k), (groups - 2 - k, groups - 1 - k)])]
    convert_element_type x27, other arithmetic: 30.9 us -> 40.7 us  [low_sum(): return (a.astype(F32) + b.astype(F32)).astype(BF)]
    ppermute x6, waiting for transfers between devices: 27.4 us -> 19.2 us  [inwards(): lax.ppermute(x, 'patch', [(k, k + 1), (groups - 1 - k, groups - 2 - k)])]
  transfers between devices with their start and end apart: 40 -> 40, of which waited for: 19 -> 19; matrix products, arithmetic and copies ran while one was open for 5% -> 8% of each run, Pallas kernels for 14% -> 13%
where the time goes in v7:
time: 693 us; the launch traced here: 684 us
  Pallas kernels  306 us (44%)
  waiting for transfers between devices  212 us (31%)
  other arithmetic  64.5 us (9%)
  starting transfers between devices  52.4 us (8%)
  local copies, waits for them, and re-layouts  25 us (4%)
  between operations  24.3 us (4%)
    pallas_call x5, Pallas kernels, group_call(): pl.pallas_call(functools.partial(kernel, start, len(given)), grid_spec=pl...  207 us
    all_gather x1, waiting for transfers between devices, shards(): gathered = lax.all_gather(mine, 'dp', axis=0, tiled=True)  114 us
    pallas_call x11, Pallas kernels, weight_grad(): pl.pallas_call(functools.partial(weight_grad_kernel, parts, cut, len(give...  66 us
    ppermute x6, waiting for transfers between devices, outwards(): lax.ppermute(x, 'patch', [(k + 1, k), (groups - 2 - k, groups - 1 - k)])  43.4 us
    convert_element_type x27, other arithmetic, low_sum(): return (a.astype(F32) + b.astype(F32)).astype(BF)  40.7 us
    ppermute x18, waiting for transfers between devices, swap_bit(): return lax.ppermute(x, 'dp', [(i, i ^ 1 << bit) for i in range(size)])  27.8 us
    pallas_call x1, Pallas kernels, tile_update(): pl.pallas_call(tile_kernel, grid_spec=pltpu.PrefetchScalarGridSpec(num_sc...  22.1 us
    ppermute x6, waiting for transfers between devices, inwards(): lax.ppermute(x, 'patch', [(k, k + 1), (groups - 1 - k, groups - 2 - k)])  19.2 us
  transfers between devices with their start and end apart: 40, of which 19 were waited for; matrix products, arithmetic and copies ran while one was open for 8% of the time, Pallas kernels for 13%

profile of v7, /device:TPU:0, one launch (start us, length us, event | category | flops | bytes accessed | tf_op | source)
XLA Modules:
  0.0 683.9 jit_solution(6778627945536267562)
XLA Ops:
  7.2 3.2 convert_element_type.318
  17.2 8.8 %order_patches.1 = (bf16[8,208,768]{2,1,0:T(8,128)(2,1)}, bf16[8,80,768]{2,1,0:T(8,128)(2,1)}, f32[8,80,768]{2,1,0:T(8,128)}, f32[8,208,512]{2,1,0:T(8,128)}) custom-call(s32[8,208,1]{2,1,0:T(8,128)} %copy.54.shuffle_ref, bf16[8,196,768]{2,1,0:T(8,128)(2,1)} %copy.55.pixels_ref, bf16[2,196,768]{2,1,0:T(8,128)(2,1)} %constant.84.clone.sin_d_ref, ...), custom_call_target="tpu_custom_call" | custom-call | tf_op jit(solution)/shard_map/order_patches/pallas_call | solution.py:406
  26.7 114.1 %all-gather.2.cloned.1.call-done.wg_ref = bf16[49280,256]{1,0:T(8,128)(2,1)} async-done(((bf16[6160,256]{1,0:T(8,128)(2,1)}), bf16[49280,256]{1,0:T(8,128)(2,1)}) %all-gather.2.cloned.1.call-update) | async-done | bytes 25231376 | tf_op jit(solution)/shard_map/all_gather | solution.py:1133
  142.5 38.0 %encoder_forward.1 = (f32[640,768]{1,0:T(8,128)}, bf16[640,768]{1,0:T(8,128)(2,1)}, bf16[640,2304]{1,0:T(8,128)(2,1)}, f32[8,3,4,80]{3,2,1,0:T(4,128)}, f32[8,3,...) custom-call(s32[177]{0:T(256)} %fusion.19.row_ref, ...), custom_call_target="tpu_custom_call" | custom-call | flops 1000 | bytes 1000 | tf_op jit(solution)/shard_map/encoder_forward/pallas_call | solution.py:435
  180.5 117.5 %decoder.1 = (bf16[1664,512]{1,0:T(8,128)(2,1)}, bf16[1664,1536]{1,0:T(8,128)(2,1)}, bf16[1664,512]{1,0:T(8,128)(2,1)}, bf16[1664,512]{1,0:T(8,128)(2,1)}, bf16[...) custom-call(s32[177]{0:T(256)} %fusion.19.row_ref, ...), custom_call_target="tpu_custom_call" | custom-call | flops 1000 | bytes 1000 | tf_op jit(solution)/shard_map/decoder/pallas_call | solution.py:435
  298.0 17.4 %encoder_mlp_back.1 = (bf16[640,768]{1,0:T(8,128)(2,1)}, bf16[640,3072]{1,0:T(8,128)(2,1)}, f32[640,768]{1,0:T(8,128)}, bf16[640,768]{1,0:T(8,128)(2,1)}, f32[8,8192]{1,0:T(8,128)}) custom-call(s32[177]{0:T(256)} %fusion.19.row_ref, bf16[49280,256]{1,0:T(8,128)(2,1)} %all-gather.2.cloned.1.call-done.wg_ref, f32[1,21760]{1,0:T(1,128)} %reshape.118.vec_ref, ...), custom_call_target="tpu_custom_call" | custom-call | flops 1000 | bytes 1000 | tf_op jit(solution)/shard_map/encoder_mlp_back/pallas_call | solution.py:435
  315.4 8.1 %weight_grad.11 = (bf16[4,81,32,256]{3,2,1,0:T(8,128)(2,1)}, bf16[4,81,32,256]{3,2,1,0:T(8,128)(2,1)}) custom-call(s32[1]{0:T(128)} %bitcast.9.index_ref, bf16[640,768]{1,0:T(8,128)(2,1)} %get-tuple-element.145.x_ref, bf16[640,3072]{1,0:T(8,128)(2,1)} %get-tuple-element.146.g_ref), custom_call_target="tpu_custom_call" | custom-call | flops 1000 | bytes 1000 | tf_op jit(solution)/shard_map/weight_grad/pallas_call | solution.py:898
  323.4 7.9 %weight_grad.12 = (bf16[4,81,32,256]{3,2,1,0:T(8,128)(2,1)}, bf16[4,81,32,256]{3,2,1,0:T(8,128)(2,1)}) custom-call(s32[1]{0:T(128)} %bitcast.9.index_ref, bf16[640,3072]{1,0:T(8,128)(2,1)} %get-tuple-element.143.x_ref, bf16[640,768]{1,0:T(8,128)(2,1)} %get-tuple-element.144.g_ref, ...), custom_call_target="tpu_custom_call", output_to_operand_aliasing={{0}: (3, {}), {1}: (4, {})} | custom-call | flops 1000 | bytes 1000 | tf_op jit(solution)/shard_map/weight_grad/pallas_call | solution.py:898
  331.3 3.7 weight_grad.13
  335.3 8.3 %weight_grad.14 = (bf16[4,60,32,256]{3,2,1,0:T(8,128)(2,1)}, bf16[4,60,32,256]{3,2,1,0:T(8,128)(2,1)}) custom-call(s32[1]{0:T(128)} %bitcast.9.index_ref, bf16[1664,512]{1,0:T(8,128)(2,1)} %get-tuple-element.155.x_ref, bf16[1664,2048]{1,0:T(8,128)(2,1)} %get-tuple-element.156.g_ref), custom_call_target="tpu_custom_call" | custom-call | flops 1000 | bytes 1000 | tf_op jit(solution)/shard_map/weight_grad/pallas_call | solution.py:898
  343.6 8.1 %weight_grad.15 = (bf16[4,60,32,256]{3,2,1,0:T(8,128)(2,1)}, bf16[4,60,32,256]{3,2,1,0:T(8,128)(2,1)}) custom-call(s32[1]{0:T(128)} %bitcast.9.index_ref, bf16[1664,2048]{1,0:T(8,128)(2,1)} %get-tuple-element.153.x_ref, bf16[1664,512]{1,0:T(8,128)(2,1)} %get-tuple-element.154.g_ref, ...), custom_call_target="tpu_custom_call", output_to_operand_aliasing={{0}: (3, {}), {1}: (4, {})} | custom-call | flops 1000 | bytes 1000 | tf_op jit(solution)/shard_map/weight_grad/pallas_call | solution.py:898
  351.7 6.8 add_convert_fusion
  362.6 4.0 weight_grad.16
  366.6 7.0 %weight_grad.17 = (bf16[4,60,32,256]{3,2,1,0:T(8,128)(2,1)}, bf16[4,60,32,256]{3,2,1,0:T(8,128)(2,1)}) custom-call(s32[1]{0:T(128)} %bitcast.9.index_ref, bf16[1664,512]{1,0:T(8,128)(2,1)} %get-tuple-element.166.x_ref, bf16[1664,1536]{1,0:T(8,128)(2,1)} %get-tuple-element.167.g_ref, ...), custom_call_target="tpu_custom_call", output_to_operand_aliasing={{0}: (3, {}), {1}: (4, {})} | custom-call | flops 1000 | bytes 1000 | tf_op jit(solution)/shard_map/weight_grad/pallas_call | solution.py:898
  373.6 4.8 weight_grad.18
  378.4 3.1 weight_grad.19
  381.5 17.3 %encoder_attention_back.2 = (bf16[640,2304]{1,0:T(8,128)(2,1)}, bf16[640,768]{1,0:T(8,128)(2,1)}, f32[8,4608]{1,0:T(8,128)}) custom-call(s32[177]{0:T(256)} %fusion.19.row_ref, s32[8]{0:T(128)} %len_ref.7, bf16[49280,256]{1,0:T(8,128)(2,1)} %all-gather.2.cloned.1.call-done.wg_ref, f32[1,21760]{1,0:T(1,128)} %reshape.118.vec_ref, ...), custom_call_target="tpu_custom_call" | custom-call | flops 1000 | bytes 1000 | tf_op jit(solution)/shard_map/encoder_attention_back/pallas_call | solution.py:435
  401.0 2.4 fusion
  408.2 17.0 %encoder_attention_back.3 = (bf16[640,2304]{1,0:T(8,128)(2,1)}, bf16[640,768]{1,0:T(8,128)(2,1)}, f32[8,4608]{1,0:T(8,128)}) custom-call(s32[177]{0:T(256)} %fusion.19.row_ref, s32[8]{0:T(128)} %len_ref.7, bf16[49280,256]{1,0:T(8,128)(2,1)} %all-gather.2.cloned.1.call-done.wg_ref, ...), custom_call_target="tpu_custom_call", output_to_operand_aliasing={{0}: (10, {}), {1}: (11, {})} | custom-call | flops 1000 | bytes 1000 | tf_op jit(solution)/shard_map/encoder_attention_back/pallas_call | solution.py:435
  425.3 2.5 fusion.5
  427.8 2.4 fusion.4
  430.2 4.0 add_convert_fusion.1
  436.5 3.4 collective-permute-start.8
  444.0 7.3 %weight_grad.20 = (bf16[4,38,32,256]{3,2,1,0:T(8,128)(2,1)}, bf16[4,38,32,256]{3,2,1,0:T(8,128)(2,1)}) custom-call(s32[1]{0:T(128)} %bitcast.9.index_ref, bf16[640,768]{1,0:T(8,128)(2,1)} %get-tuple-element.203.x_ref, bf16[640,2304]{1,0:T(8,128)(2,1)} %get-tuple-element.204.g_ref, ...), custom_call_target="tpu_custom_call", output_to_operand_aliasing={{0}: (3, {}), {1}: (4, {})} | custom-call | flops 1000 | bytes 1000 | tf_op jit(solution)/shard_map/weight_grad/pallas_call | solution.py:898
  451.2 3.7 weight_grad.21
  455.0 2.3 add_convert_fusion.6
  457.3 2.4 collective-permute-done.7
  461.5 2.8 collective-permute-done.6
  464.3 2.5 fusion.3
  473.0 10.8 %collective-permute-done.13 = bf16[41,32,256]{2,1,0:T(8,128)(2,1)S(1)} collective-permute-done((bf16[41,32,256]{2,1,0:T(8,128)(2,1)}, bf16[41,32,256]{2,1,0:T(8,128)(2,1)S(1)}, u32[]{:S(2)}, u32[]{:S(2)}) %collective-permute-start.13) | collective-permute-done | bytes 671776 | tf_op jit(solution)/shard_map/ppermute | solution.py:996
  488.1 3.1 add_convert_fusion.2
  491.5 5.2 collective-permute-start.20
  504.6 3.3 collective-permute-done.20
  509.2 4.1 collective-permute-done.15
  520.2 4.4 collective-permute-done.18
  525.5 5.9 collective-permute-start.30
  536.0 2.5 collective-permute-done.30
  539.3 2.5 collective-permute-done.27
  547.8 30.2 %collective-permute-done.22 = bf16[30,32,256]{2,1,0:T(8,128)(2,1)S(1)} collective-permute-done((bf16[30,32,256]{2,1,0:T(8,128)(2,1)S(1)}, bf16[30,32,256]{2,1,0:T(8,128)(2,1)S(1)}, u32[]{:S(2)}, u32[]{:S(2)}) %collective-permute-start.22) | collective-permute-done | bytes 491552 | tf_op jit(solution)/shard_map/ppermute | solution.py:1002
  580.4 8.1 %collective-permute-done.24 = bf16[30,32,256]{2,1,0:T(8,128)(2,1)S(1)} collective-permute-done((bf16[30,32,256]{2,1,0:T(8,128)(2,1)S(1)}, bf16[30,32,256]{2,1,0:T(8,128)(2,1)S(1)}, u32[]{:S(2)}, u32[]{:S(2)}) %collective-permute-start.24) | collective-permute-done | bytes 491552 | tf_op jit(solution)/shard_map/ppermute | solution.py:1002
  591.7 5.1 collective-permute-done.29
  598.6 4.5 gather_fusion.1
  603.1 3.8 all-to-all-start
  610.3 2.2 multiply_reduce_fusion.1
  622.8 3.5 collective-permute-done.33
  627.3 3.5 collective-permute-done.34
  634.0 9.8 %collective-permute-done.36 = f32[3]{0:T(128)S(1)} collective-permute-done((f32[3]{0:T(128)S(1)}, f32[3]{0:T(128)S(1)}, u32[]{:S(2)}, u32[]{:S(2)}) %collective-permute-start.36) | collective-permute-done | bytes 44 | tf_op jit(solution)/shard_map/ppermute | solution.py:965
  653.6 22.1 %tile_update.1 = (f32[24,256,256]{2,1,0:T(8,128)}, f32[24,256,256]{2,1,0:T(8,128)}, f32[24,256,256]{2,1,0:T(8,128)}, f32[24,256,256]{2,1,0:T(8,128)}) custom-call(f32[1]{0:T(128)} %bitcast.41.scale_ref, bf16[8,24,32,256]{3,2,1,0:T(8,128)(2,1)} %bitcast.91, f32[24,256,256]{2,1,0:T(8,128)} %w_ref.1, f32[24,256,256]{2,1,0:T(8,128)} %left_stat_ref.1, ...), custom_call_target="tpu_custom_call" | custom-call | tf_op jit(solution)/shard_map/tile_update/pallas_call | solution.py:1059
  (223 shorter events, 94.2 us)
Async XLA Ops:
  7.2 133.7 %all-gather.2.cloned.1.call-start = ((), (), s32[]{:S(2)}) async-start(), calls=%async_computation.1 | async-start | bytes 28385280 | tf_op jit(solution)/shard_map/all_gather | solution.py:1133
  335.0 16.6 %collective-permute-start = (bf16[4,81,32,256]{3,2,1,0:T(8,128)(2,1)}, bf16[4,81,32,256]{3,2,1,0:T(8,128)(2,1)}, u32[]{:S(2)}, u32[]{:S(2)}) collective-permute-start(bf16[4,81,32,256]{3,2,1,0:T(8,128)(2,1)} %get-tuple-element.162), channel_id=1, source_target_pairs={{0,4},{4,0},{8,12},{12,8},{16,20},{20,16},{24,28},{28,24},{1,5},{5... | collective-permute-start | bytes 15925256 | tf_op jit(solution)/shard_map/ppermute | solution.py:965
  359.3 39.5 %collective-permute-start.1 = (bf16[2,40,32,256]{3,2,1,0:T(8,128)(2,1)S(1)}, bf16[2,40,32,256]{3,2,1,0:T(8,128)(2,1)}, u32[]{:S(2)}, u32[]{:S(2)}) collective-permute-start(bf16[2,40,32,256]{3,2,1,0:T(8,128)(2,1)S(1)} %slice_bitcast_fusion.1), channel_id=1, source_target_pairs={{0,8},{4,12},{8,0},{12,4},{16,24},{20,28},{24,16},{28,20},{1,9},{5... | collective-permute-start | bytes 3932168 | tf_op jit(solution)/shard_map/ppermute | solution.py:965
  362.1 38.8 %collective-permute-start.2 = (bf16[2,41,32,256]{3,2,1,0:T(8,128)(2,1)}, bf16[2,41,32,256]{3,2,1,0:T(8,128)(2,1)}, u32[]{:S(2)}, u32[]{:S(2)}) collective-permute-start(bf16[2,41,32,256]{3,2,1,0:T(8,128)(2,1)} %slice_bitcast_fusion), channel_id=1, source_target_pairs={{0,16},{4,20},{8,24},{12,28},{16,0},{20,4},{24,8},{28,12},{1,17},{... | collective-permute-start | bytes 4030472 | tf_op jit(solution)/shard_map/ppermute | solution.py:965
  403.9 26.3 %collective-permute-start.3 = (bf16[4,60,32,256]{3,2,1,0:T(8,128)(2,1)S(1)}, bf16[4,60,32,256]{3,2,1,0:T(8,128)(2,1)}, u32[]{:S(2)}, u32[]{:S(2)}) collective-permute-start(bf16[4,60,32,256]{3,2,1,0:T(8,128)(2,1)S(1)} %copy-done.2), channel_id=1, source_target_pairs={{0,4},{4,0},{8,12},{12,8},{16,20},{20,16},{24,28},{28,24},{1,5},{5... | collective-permute-start | bytes 11796488 | tf_op jit(solution)/shard_map/ppermute | solution.py:965
  404.8 20.5 %collective-permute-start.4 = (bf16[40,32,256]{2,1,0:T(8,128)(2,1)}, bf16[40,32,256]{2,1,0:T(8,128)(2,1)}, u32[]{:S(2)}, u32[]{:S(2)}) collective-permute-start(bf16[40,32,256]{2,1,0:T(8,128)(2,1)} %slice_bitcast_fusion.5), channel_id=1, source_target_pairs={{0,16},{4,20},{8,24},{12,28},{16,0},{20,4},{24,8},{28,12},{1,17},{... | collective-permute-start | bytes 1966088 | tf_op jit(solution)/shard_map/ppermute | solution.py:965
  407.1 20.7 %collective-permute-start.5 = (bf16[41,32,256]{2,1,0:T(8,128)(2,1)}, bf16[41,32,256]{2,1,0:T(8,128)(2,1)}, u32[]{:S(2)}, u32[]{:S(2)}) collective-permute-start(bf16[41,32,256]{2,1,0:T(8,128)(2,1)} %slice_bitcast_fusion.4), channel_id=1, source_target_pairs={{0,8},{4,12},{8,0},{12,4},{16,24},{20,28},{24,16},{28,20},{1,9},{5... | collective-permute-start | bytes 2015240 | tf_op jit(solution)/shard_map/ppermute | solution.py:965
  435.9 23.7 %collective-permute-start.7 = (bf16[2,30,32,256]{3,2,1,0:T(8,128)(2,1)S(1)}, bf16[2,30,32,256]{3,2,1,0:T(8,128)(2,1)}, u32[]{:S(2)}, u32[]{:S(2)}) collective-permute-start(bf16[2,30,32,256]{3,2,1,0:T(8,128)(2,1)S(1)} %slice_bitcast_fusion.2), channel_id=1, source_target_pairs={{0,16},{4,20},{8,24},{12,28},{16,0},{20,4},{24,8},{28,12},{1,17},{... | collective-permute-start | bytes 2949128 | tf_op jit(solution)/shard_map/ppermute | solution.py:965
  436.5 18.5 %collective-permute-start.8 = (bf16[40,32,256]{2,1,0:T(8,128)(2,1)}, bf16[40,32,256]{2,1,0:T(8,128)(2,1)S(1)}, u32[]{:S(2)}, u32[]{:S(2)}) collective-permute-start(bf16[40,32,256]{2,1,0:T(8,128)(2,1)} %fusion.5), channel_id=1, source_target_pairs={{0,1},{3,2},{4,5},{7,6},{8,9},{11,10},{12,13},{15,14},{16,17},{19,... | collective-permute-start | bytes 1966088 | tf_op jit(solution)/shard_map/ppermute | solution.py:996
  440.9 23.4 %collective-permute-start.6 = (bf16[2,30,32,256]{3,2,1,0:T(8,128)(2,1)}, bf16[2,30,32,256]{3,2,1,0:T(8,128)(2,1)}, u32[]{:S(2)}, u32[]{:S(2)}) collective-permute-start(bf16[2,30,32,256]{3,2,1,0:T(8,128)(2,1)} %slice_bitcast_fusion.3), channel_id=1, source_target_pairs={{0,8},{4,12},{8,0},{12,4},{16,24},{20,28},{24,16},{28,20},{1,9},{5... | collective-permute-start | bytes 2949128 | tf_op jit(solution)/shard_map/ppermute | solution.py:965
  466.8 21.2 %collective-permute-start.9 = (bf16[4,38,32,256]{3,2,1,0:T(8,128)(2,1)S(1)}, bf16[4,38,32,256]{3,2,1,0:T(8,128)(2,1)}, u32[]{:S(2)}, u32[]{:S(2)}) collective-permute-start(bf16[4,38,32,256]{3,2,1,0:T(8,128)(2,1)S(1)} %copy-done.7), channel_id=1, source_target_pairs={{0,4},{4,0},{8,12},{12,8},{16,20},{20,16},{24,28},{28,24},{1,5},{5... | collective-permute-start | bytes 7471112 | tf_op jit(solution)/shard_map/ppermute | solution.py:965
  466.9 16.9 %collective-permute-start.13 = (bf16[41,32,256]{2,1,0:T(8,128)(2,1)}, bf16[41,32,256]{2,1,0:T(8,128)(2,1)S(1)}, u32[]{:S(2)}, u32[]{:S(2)}) collective-permute-start(bf16[41,32,256]{2,1,0:T(8,128)(2,1)} %fusion.4), channel_id=1, source_target_pairs={{0,1},{3,2},{4,5},{7,6},{8,9},{11,10},{12,13},{15,14},{16,17},{19,... | collective-permute-start | bytes 2015240 | tf_op jit(solution)/shard_map/ppermute | solution.py:996
  468.4 18.4 %copy-start.20 = (bf16[2,30,32,256]{3,2,1,0:T(8,128)(2,1)S(1)}, bf16[2,30,32,256]{3,2,1,0:T(8,128)(2,1)}, u32[]{:S(2)}) copy-start(bf16[2,30,32,256]{3,2,1,0:T(8,128)(2,1)} %fusion.3) | copy-start | bytes 2949124
  468.4 19.4 %collective-permute-start.12 = (bf16[40,32,256]{2,1,0:T(8,128)(2,1)}, bf16[40,32,256]{2,1,0:T(8,128)(2,1)S(1)}, u32[]{:S(2)}, u32[]{:S(2)}) collective-permute-start(bf16[40,32,256]{2,1,0:T(8,128)(2,1)} %add_convert_fusion.6), channel_id=1, source_target_pairs={{1,2},{2,1},{5,6},{6,5},{9,10},{10,9},{13,14},{14,13},{17,18},{18,... | collective-permute-start | bytes 1966088 | tf_op jit(solution)/shard_map/ppermute | solution.py:999
  469.3 16.6 %collective-permute-start.11 = (bf16[30,32,256]{2,1,0:T(8,128)(2,1)S(1)}, bf16[30,32,256]{2,1,0:T(8,128)(2,1)S(1)}, u32[]{:S(2)}, u32[]{:S(2)}) collective-permute-start(bf16[30,32,256]{2,1,0:T(8,128)(2,1)S(1)} %slice_bitcast_fusion.9), channel_id=1, source_target_pairs={{0,8},{4,12},{8,0},{12,4},{16,24},{20,28},{24,16},{28,20},{1,9},{5... | collective-permute-start | bytes 1474568 | tf_op jit(solution)/shard_map/ppermute | solution.py:965
  471.4 16.4 %copy-start.24 = (bf16[40,32,256]{2,1,0:T(8,128)(2,1)S(1)}, bf16[40,32,256]{2,1,0:T(8,128)(2,1)}, u32[]{:S(2)}) copy-start(bf16[40,32,256]{2,1,0:T(8,128)(2,1)} %add_convert_fusion.6) | copy-start | bytes 1966084
  471.4 15.5 %collective-permute-start.10 = (bf16[30,32,256]{2,1,0:T(8,128)(2,1)S(1)}, bf16[30,32,256]{2,1,0:T(8,128)(2,1)S(1)}, u32[]{:S(2)}, u32[]{:S(2)}) collective-permute-start(bf16[30,32,256]{2,1,0:T(8,128)(2,1)S(1)} %slice_bitcast_fusion.10), channel_id=1, source_target_pairs={{0,16},{4,20},{8,24},{12,28},{16,0},{20,4},{24,8},{28,12},{1,17},{... | collective-permute-start | bytes 1474568 | tf_op jit(solution)/shard_map/ppermute | solution.py:965
  488.1 101.4 %copy-start.12 = (bf16[40,32,256]{2,1,0:T(8,128)(2,1)}, bf16[40,32,256]{2,1,0:T(8,128)(2,1)S(1)}, u32[]{:S(2)}) copy-start(bf16[40,32,256]{2,1,0:T(8,128)(2,1)S(1)} %add_convert_fusion.5) | copy-start | bytes 1966084
  491.5 16.4 %collective-permute-start.20 = (bf16[30,32,256]{2,1,0:T(8,128)(2,1)}, bf16[30,32,256]{2,1,0:T(8,128)(2,1)}, u32[]{:S(2)}, u32[]{:S(2)}) collective-permute-start(bf16[30,32,256]{2,1,0:T(8,128)(2,1)} %fusion.8), channel_id=1, source_target_pairs={{0,1},{3,2},{4,5},{7,6},{8,9},{11,10},{12,13},{15,14},{16,17},{19,... | collective-permute-start | bytes 1474568 | tf_op jit(solution)/shard_map/ppermute | solution.py:996
  497.6 15.7 %collective-permute-start.15 = (bf16[2,19,32,256]{3,2,1,0:T(8,128)(2,1)}, bf16[2,19,32,256]{3,2,1,0:T(8,128)(2,1)}, u32[]{:S(2)}, u32[]{:S(2)}) collective-permute-start(bf16[2,19,32,256]{3,2,1,0:T(8,128)(2,1)} %slice_bitcast_fusion.7), channel_id=1, source_target_pairs={{0,16},{4,20},{8,24},{12,28},{16,0},{20,4},{24,8},{28,12},{1,17},{... | collective-permute-start | bytes 1867784 | tf_op jit(solution)/shard_map/ppermute | solution.py:965
  499.9 15.5 %collective-permute-start.14 = (bf16[2,19,32,256]{3,2,1,0:T(8,128)(2,1)}, bf16[2,19,32,256]{3,2,1,0:T(8,128)(2,1)}, u32[]{:S(2)}, u32[]{:S(2)}) collective-permute-start(bf16[2,19,32,256]{3,2,1,0:T(8,128)(2,1)} %slice_bitcast_fusion.8), channel_id=1, source_target_pairs={{0,8},{4,12},{8,0},{12,4},{16,24},{20,28},{24,16},{28,20},{1,9},{5... | collective-permute-start | bytes 1867784 | tf_op jit(solution)/shard_map/ppermute | solution.py:965
  502.5 16.5 %collective-permute-start.19 = (bf16[30,32,256]{2,1,0:T(8,128)(2,1)}, bf16[30,32,256]{2,1,0:T(8,128)(2,1)S(1)}, u32[]{:S(2)}, u32[]{:S(2)}) collective-permute-start(bf16[30,32,256]{2,1,0:T(8,128)(2,1)} %fusion.9), channel_id=1, source_target_pairs={{0,1},{3,2},{4,5},{7,6},{8,9},{11,10},{12,13},{15,14},{16,17},{19,... | collective-permute-start | bytes 1474568 | tf_op jit(solution)/shard_map/ppermute | solution.py:996
  503.8 12.9 %collective-permute-start.16 = (bf16[41,32,256]{2,1,0:T(8,128)(2,1)S(1)}, bf16[41,32,256]{2,1,0:T(8,128)(2,1)S(1)}, u32[]{:S(2)}, u32[]{:S(2)}) collective-permute-start(bf16[41,32,256]{2,1,0:T(8,128)(2,1)S(1)} %copy-done.22), channel_id=1, source_target_pairs={{1,2},{2,1},{5,6},{6,5},{9,10},{10,9},{13,14},{14,13},{17,18},{18,... | collective-permute-start | bytes 2015240 | tf_op jit(solution)/shard_map/ppermute | solution.py:999
  517.0 73.7 %copy-start.11 = (bf16[41,32,256]{2,1,0:T(8,128)(2,1)}, bf16[41,32,256]{2,1,0:T(8,128)(2,1)S(1)}, u32[]{:S(2)}) copy-start(bf16[41,32,256]{2,1,0:T(8,128)(2,1)S(1)} %add_convert_fusion.3) | copy-start | bytes 2015236
  517.0 7.6 %collective-permute-start.18 = (bf16[19,32,256]{2,1,0:T(8,128)(2,1)S(1)}, bf16[19,32,256]{2,1,0:T(8,128)(2,1)S(1)}, u32[]{:S(2)}, u32[]{:S(2)}) collective-permute-start(bf16[19,32,256]{2,1,0:T(8,128)(2,1)S(1)} %slice_bitcast_fusion.11), channel_id=1, source_target_pairs={{0,8},{4,12},{8,0},{12,4},{16,24},{20,28},{24,16},{28,20},{1,9},{5... | collective-permute-start | bytes 933896 | tf_op jit(solution)/shard_map/ppermute | solution.py:965
  518.0 7.3 %collective-permute-start.17 = (bf16[19,32,256]{2,1,0:T(8,128)(2,1)S(1)}, bf16[19,32,256]{2,1,0:T(8,128)(2,1)S(1)}, u32[]{:S(2)}, u32[]{:S(2)}) collective-permute-start(bf16[19,32,256]{2,1,0:T(8,128)(2,1)S(1)} %slice_bitcast_fusion.12), channel_id=1, source_target_pairs={{0,16},{4,20},{8,24},{12,28},{16,0},{20,4},{24,8},{28,12},{1,17},{... | collective-permute-start | bytes 933896 | tf_op jit(solution)/shard_map/ppermute | solution.py:965
  525.5 13.0 %collective-permute-start.30 = (bf16[19,32,256]{2,1,0:T(8,128)(2,1)S(1)}, bf16[19,32,256]{2,1,0:T(8,128)(2,1)S(1)}, u32[]{:S(2)}, u32[]{:S(2)}) collective-permute-start(bf16[19,32,256]{2,1,0:T(8,128)(2,1)S(1)} %fusion.10), channel_id=1, source_target_pairs={{0,1},{3,2},{4,5},{7,6},{8,9},{11,10},{12,13},{15,14},{16,17},{19,... | collective-permute-start | bytes 933896 | tf_op jit(solution)/shard_map/ppermute | solution.py:996
  531.4 10.5 %collective-permute-start.27 = (bf16[19,32,256]{2,1,0:T(8,128)(2,1)S(1)}, bf16[19,32,256]{2,1,0:T(8,128)(2,1)S(1)}, u32[]{:S(2)}, u32[]{:S(2)}) collective-permute-start(bf16[19,32,256]{2,1,0:T(8,128)(2,1)S(1)} %fusion.11), channel_id=1, source_target_pairs={{0,1},{3,2},{4,5},{7,6},{8,9},{11,10},{12,13},{15,14},{16,17},{19,... | collective-permute-start | bytes 933896 | tf_op jit(solution)/shard_map/ppermute | solution.py:996
  532.7 56.8 %collective-permute-start.25 = (bf16[40,32,256]{2,1,0:T(8,128)(2,1)S(1)}, bf16[40,32,256]{2,1,0:T(8,128)(2,1)S(1)}, u32[]{:S(2)}, u32[]{:S(2)}) collective-permute-start(bf16[40,32,256]{2,1,0:T(8,128)(2,1)S(1)} %add_convert_fusion.5), channel_id=1, source_target_pairs={{1,0},{2,3},{5,4},{6,7},{9,8},{10,11},{13,12},{14,15},{17,16},{18,... | collective-permute-start | bytes 1966088 | tf_op jit(solution)/shard_map/ppermute | solution.py:1002
  534.0 56.6 %collective-permute-start.26 = (bf16[41,32,256]{2,1,0:T(8,128)(2,1)S(1)}, bf16[41,32,256]{2,1,0:T(8,128)(2,1)S(1)}, u32[]{:S(2)}, u32[]{:S(2)}) collective-permute-start(bf16[41,32,256]{2,1,0:T(8,128)(2,1)S(1)} %add_convert_fusion.3), channel_id=1, source_target_pairs={{1,0},{2,3},{5,4},{6,7},{9,8},{10,11},{13,12},{14,15},{17,16},{18,... | collective-permute-start | bytes 2015240 | tf_op jit(solution)/shard_map/ppermute | solution.py:1002
  535.3 7.3 %collective-permute-start.21 = (bf16[30,32,256]{2,1,0:T(8,128)(2,1)S(1)}, bf16[30,32,256]{2,1,0:T(8,128)(2,1)S(1)}, u32[]{:S(2)}, u32[]{:S(2)}) collective-permute-start(bf16[30,32,256]{2,1,0:T(8,128)(2,1)S(1)} %add_convert_fusion.10), channel_id=1, source_target_pairs={{1,2},{2,1},{5,6},{6,5},{9,10},{10,9},{13,14},{14,13},{17,18},{18,... | collective-permute-start | bytes 1474568 | tf_op jit(solution)/shard_map/ppermute | solution.py:999
  538.5 5.0 collective-permute-start.23
  541.9 3.1 collective-permute-start.31
  542.6 3.8 collective-permute-start.28
  543.5 46.0 %copy-start.16 = (bf16[30,32,256]{2,1,0:T(8,128)(2,1)}, bf16[30,32,256]{2,1,0:T(8,128)(2,1)S(1)}, u32[]{:S(2)}) copy-start(bf16[30,32,256]{2,1,0:T(8,128)(2,1)S(1)} %add_convert_fusion.8) | copy-start | bytes 1474564
  543.5 34.5 %collective-permute-start.22 = (bf16[30,32,256]{2,1,0:T(8,128)(2,1)S(1)}, bf16[30,32,256]{2,1,0:T(8,128)(2,1)S(1)}, u32[]{:S(2)}, u32[]{:S(2)}) collective-permute-start(bf16[30,32,256]{2,1,0:T(8,128)(2,1)S(1)} %add_convert_fusion.8), channel_id=1, source_target_pairs={{1,0},{2,3},{5,4},{6,7},{9,8},{10,11},{13,12},{14,15},{17,16},{18,... | collective-permute-start | bytes 1474568 | tf_op jit(solution)/shard_map/ppermute | solution.py:1002
  545.0 43.5 %copy-start.18 = (bf16[30,32,256]{2,1,0:T(8,128)(2,1)}, bf16[30,32,256]{2,1,0:T(8,128)(2,1)S(1)}, u32[]{:S(2)}) copy-start(bf16[30,32,256]{2,1,0:T(8,128)(2,1)S(1)} %add_convert_fusion.7) | copy-start | bytes 1474564
  545.0 43.5 %collective-permute-start.24 = (bf16[30,32,256]{2,1,0:T(8,128)(2,1)S(1)}, bf16[30,32,256]{2,1,0:T(8,128)(2,1)S(1)}, u32[]{:S(2)}, u32[]{:S(2)}) collective-permute-start(bf16[30,32,256]{2,1,0:T(8,128)(2,1)S(1)} %add_convert_fusion.7), channel_id=1, source_target_pairs={{1,0},{2,3},{5,4},{6,7},{9,8},{10,11},{13,12},{14,15},{17,16},{18,... | collective-permute-start | bytes 1474568 | tf_op jit(solution)/shard_map/ppermute | solution.py:1002
  546.4 51.2 %collective-permute-start.32 = (bf16[19,32,256]{2,1,0:T(8,128)(2,1)S(1)}, bf16[19,32,256]{2,1,0:T(8,128)(2,1)S(1)}, u32[]{:S(2)}, u32[]{:S(2)}) collective-permute-start(bf16[19,32,256]{2,1,0:T(8,128)(2,1)S(1)} %add_convert_fusion.11), channel_id=1, source_target_pairs={{1,0},{2,3},{5,4},{6,7},{9,8},{10,11},{13,12},{14,15},{17,16},{18,... | collective-permute-start | bytes 933896 | tf_op jit(solution)/shard_map/ppermute | solution.py:1002
  578.0 18.8 %collective-permute-start.29 = (bf16[19,32,256]{2,1,0:T(8,128)(2,1)S(1)}, bf16[19,32,256]{2,1,0:T(8,128)(2,1)S(1)}, u32[]{:S(2)}, u32[]{:S(2)}) collective-permute-start(bf16[19,32,256]{2,1,0:T(8,128)(2,1)S(1)} %add_convert_fusion.13), channel_id=1, source_target_pairs={{1,0},{2,3},{5,4},{6,7},{9,8},{10,11},{13,12},{14,15},{17,16},{18,... | collective-permute-start | bytes 933896 | tf_op jit(solution)/shard_map/ppermute | solution.py:1002
  603.1 48.9 %all-to-all-start = ((bf16[192,32,256]{2,1,0:T(8,128)(2,1)}), bf16[192,32,256]{2,1,0:T(8,128)(2,1)S(1)}, u32[]{:S(2)}, u32[]{:S(2)}) async-start(bf16[192,32,256]{2,1,0:T(8,128)(2,1)} %gather_fusion.1), calls=%async_computation | async-start | bytes 6291456 | tf_op jit(solution)/shard_map/all_to_all | solution.py:1265
  610.2 41.1 %copy-start.33 = (f32[2560]{0:T(1024)S(1)}, f32[2560]{0:T(1024)}, u32[]{:S(2)}) copy-start(f32[2560]{0:T(1024)} %param.22) | copy-start | bytes 30724
  610.3 41.1 %copy-start.34 = (f32[2560]{0:T(1024)S(1)}, f32[2560]{0:T(1024)}, u32[]{:S(2)}) copy-start(f32[2560]{0:T(1024)} %param.21) | copy-start | bytes 30724
  622.8 3.5 collective-permute-start.33
  626.4 4.4 collective-permute-start.34
  630.9 1.1 collective-permute-start.35
  632.0 11.7 %collective-permute-start.36 = (f32[3]{0:T(128)S(1)}, f32[3]{0:T(128)S(1)}, u32[]{:S(2)}, u32[]{:S(2)}) collective-permute-start(f32[3]{0:T(128)S(1)} %add.190), channel_id=1, source_target_pairs={{0,8},{4,12},{8,0},{12,4},{16,24},{20,28},{24,16},{28,20},{1,9},{5... | collective-permute-start | bytes 44 | tf_op jit(solution)/shard_map/ppermute | solution.py:965
  643.8 3.5 collective-permute-start.37
  (30 other events, 154.7 us)
Sparse Core Ops, SparseCore 0:
  12.5 128.2 all-gather.1

commit v8 on v7

--- a/solution.py
+++ b/solution.py
@@ -148,7 +148,7 @@
         body(j, pl.ds(pl.multiple_of(j * BS, BS), BS))
         return c
 
-    loop(0, count, one, 0, 4)
+    loop(0, count, one, 0, 12)
 
 
 def vec_at(vec_ref, start, j):
@@ -161,8 +161,8 @@
     return jnp.where(inside, 1.0, 0.0).astype(BF)
 
 
-def masked_scores(k_masked, q, head_size, count):
-    scores = mm(k_masked, q) * (head_size**-0.5 * LOG2E)
+def masked_scores(raw, head_size, count):
+    scores = raw * (head_size**-0.5 * LOG2E)
     if isinstance(count, int):
         whole = count // 8 * 8
         tail = scores[whole:]
@@ -191,6 +191,7 @@
 def attention_forward(qkv_ref, att_ref, out_t_ref, lse_ref, image, seq, width, head_size, count, bounded):
     rows = pl.ds(pl.multiple_of(image * seq, 16), seq)
     per = BS // head_size
+    most = min(8, per)
 
     def group(g, c):
         def part(which):
@@ -202,7 +203,10 @@
         ones = jnp.ones((16, seq), BF)
         outs, logs = [], []
         for h in range(per):
-            scores = masked_scores(k * head_mask(h, head_size), q, head_size, count)
+            if h % most == 0:
+                stacked = jnp.concatenate([k * head_mask(i, head_size) for i in range(h, h + most)], axis=0)
+                many = mm(stacked, q)
+            scores = masked_scores(many[h % most * seq : (h % most + 1) * seq], head_size, count)
             top = 0.0
             if not bounded:
                 top = jnp.max(scores, axis=0, keepdims=True)
@@ -232,7 +236,7 @@
             )
             return c
 
-        lax.fori_loop(0, images, one, 0)
+        loop(0, images, one, 0)
 
     @pl.when(safe)
     def _():
@@ -247,6 +251,7 @@
     rows = pl.ds(pl.multiple_of(image * seq, 16), seq)
     per = BS // head_size
     scale = head_size**-0.5
+    most = min(8, per)
 
     def group(g, c):
         def cols(which):
@@ -257,16 +262,29 @@
         lse = lse_ref[image, g]
         q_t, k_t, d_out_t = q.T, k.T, d_out.T
         along = d_out_t.astype(F32) * out_t_ref[image, g]
-        d_q, d_k, d_v = [], jnp.zeros((seq, BS), F32), jnp.zeros((seq, BS), F32)
-        for h in range(per):
-            mask = head_mask(h, head_size)
-            part = slice(h * head_size, (h + 1) * head_size)
-            delta = jnp.sum(along[part, :], axis=0, keepdims=True)
-            probs = jnp.exp2(masked_scores(k * mask, q_t, head_size, count) - lse[h : h + 1, :])
-            d_scores = (probs * (mm(v * mask, d_out_t) - delta)).astype(BF)
-            d_v = d_v + mm(probs.astype(BF), d_out * mask)
-            d_k = d_k + mm(d_scores, q * mask)
-            d_q.append(mm(k_t[part, :], d_scores))
+        lane = lax.broadcasted_iota(jnp.int32, (seq, BS), 1)
+        d_q, d_k, d_v = [], None, None
+        for start in range(0, per, most):
+            heads = range(start, start + most)
+            many = mm(jnp.concatenate([k * head_mask(h, head_size) for h in heads], axis=0), q_t)
+            more = mm(jnp.concatenate([v * head_mask(h, head_size) for h in heads], axis=0), d_out_t)
+            probs_all, scores_all = [], []
+            for h in heads:
+                part = slice(h * head_size, (h + 1) * head_size)
+                at = slice((h - start) * seq, (h - start + 1) * seq)
+                delta = jnp.sum(along[part, :], axis=0, keepdims=True)
+                probs = jnp.exp2(masked_scores(many[at], head_size, count) - lse[h : h + 1, :])
+                d_scores = (probs * (more[at] - delta)).astype(BF)
+                d_q.append(mm(k_t[part, :], d_scores))
+                probs_all.append(probs.astype(BF))
+                scores_all.append(d_scores)
+            for_v = mm(jnp.concatenate(probs_all, axis=0), d_out)
+            for_k = mm(jnp.concatenate(scores_all, axis=0), q)
+            for h in heads:
+                at = slice((h - start) * seq, (h - start + 1) * seq)
+                inside = (lane >= h * head_size) & (lane < (h + 1) * head_size)
+                d_v = for_v[at] if d_v is None else jnp.where(inside, for_v[at], d_v)
+                d_k = for_k[at] if d_k is None else jnp.where(inside, for_k[at], d_k)
         dqkv_ref[rows, cols(0)] = (jnp.concatenate(d_q, axis=0).T * scale).astype(BF)
         dqkv_ref[rows, cols(1)] = (d_k * scale).astype(BF)
         dqkv_ref[rows, cols(2)] = d_v.astype(BF)
@@ -593,7 +611,7 @@
         loop(VMAX // chunk, SD // chunk, tail_rows, 0)
         return c
 
-    lax.fori_loop(0, images, place, 0)
+    loop(0, images, place, 0)
     norm_forward(x0, vec(DEC["g1"]), vec(DEC["s1"]), h1_ref)
     ready(0)
     qkv_forward(h1_ref, w_qkv, vec_ref, DEC["bqkv"], qkv)
@@ -628,7 +646,7 @@
         return loop(0, SD // chunk, one, c)
 
     zero = jnp.zeros((8, PIX), F32)
-    loss, bias = lax.fori_loop(0, images, errors, (zero, zero))
+    loss, bias = loop(0, images, errors, (zero, zero))
     add_sum(sum_ref, DS_LOSS, loss)
     add_sum(sum_ref, DS_HEAD, bias)
 
@@ -653,7 +671,7 @@
         attention_backward(qkv, datt, out_t, lse, dqkv_ref, image, SD, E, E // HD, POS)
         return c
 
-    lax.fori_loop(0, images, attend_back, 0)
+    loop(0, images, attend_back, 0)
     sum_rows(dqkv_ref, sum_ref, DS["bqkv"])
     back_linear(dqkv_ref, w_qkv, dy)
     d_gain, d_shift = norm_backward(x0, dy, vec(DEC["g1"]), grad, True)
@@ -675,7 +693,7 @@
         c = loop(0, VMAX // chunk, head_rows, c)
         return loop(VMAX // chunk, SD // chunk, tail_rows, c)
 
-    add_sum(sum_ref, DS_MASK, lax.fori_loop(0, images, unplace, jnp.zeros((8, E), F32)))
+    add_sum(sum_ref, DS_MASK, loop(0, images, unplace, jnp.zeros((8, E), F32)))
 
 
 def decoder(tile_rows, vis_len, gathered, vector, latent, pos_e, ordered, steps):
@@ -824,7 +842,7 @@
         attention_backward(qkv_ref, datt, out_t_ref, lse_ref, dqkv_ref, image, VMAX, D, D // HE, count)
         return c
 
-    lax.fori_loop(0, images, attend_back, 0)
+    loop(0, images, attend_back, 0)
     sum_rows(dqkv_ref, sum_ref, EA_QKV)
     ready(1)
     back_linear(dqkv_ref, w_qkv, dy)
@@ -1233,10 +1251,10 @@
     one = sum_patch(one, steps[2:])
     two = sum_patch(two, steps[1:2])
     half0 = [sum_patch(x, steps[:1]) for x in half0]
-    half2, two = after((half2, two))
+    half2, one, two = after((half2, one, two))
     half2, _ = chips((half2, left2), 99)
     two = sum_patch(two, steps[2:])
-    half2, half0 = after((half2, half0))
+    half2, half0, two = after((half2, half0, two))
     half2 = [sum_patch(x, steps) for x in half2]
     half0 = [sum_patch(x, steps[1:]) for x in half0]
     pieces = half0 + [one, two] + half2

time: 693 us -> 641 us (0.925)
  Pallas kernels: 306 us -> 258 us
    pallas_call x5, Pallas kernels: 207 us -> 159 us  [group_call(): pl.pallas_call(functools.partial(kernel, start, len(given)), grid_spec=pl...]
  transfers between devices with their start and end apart: 40 -> 40, of which waited for: 19 -> 21; matrix products, arithmetic and copies ran while one was open for 8% -> 8% of each run, Pallas kernels for 13% -> 13%
where the time goes in v8:
time: 641 us; the launch traced here: 629 us
  Pallas kernels  258 us (40%)
  waiting for transfers between devices  210 us (33%)
  other arithmetic  61.2 us (10%)
  starting transfers between devices  51.1 us (8%)
  between operations  24.6 us (4%)
  local copies, waits for them, and re-layouts  23.3 us (4%)
    pallas_call x5, Pallas kernels, group_call(): pl.pallas_call(functools.partial(kernel, start, len(given)), grid_spec=pl...  159 us
    all_gather x1, waiting for transfers between devices, shards(): gathered = lax.all_gather(mine, 'dp', axis=0, tiled=True)  114 us
    pallas_call x11, Pallas kernels, weight_grad(): pl.pallas_call(functools.partial(weight_grad_kernel, parts, cut, len(give...  65.9 us
    ppermute x6, waiting for transfers between devices, outwards(): lax.ppermute(x, 'patch', [(k + 1, k), (groups - 2 - k, groups - 1 - k)])  43.3 us
    convert_element_type x27, other arithmetic, low_sum(): return (a.astype(F32) + b.astype(F32)).astype(BF)  40 us
    ppermute x18, waiting for transfers between devices, swap_bit(): return lax.ppermute(x, 'dp', [(i, i ^ 1 << bit) for i in range(size)])  24.2 us
    pallas_call x1, Pallas kernels, tile_update(): pl.pallas_call(tile_kernel, grid_spec=pltpu.PrefetchScalarGridSpec(num_sc...  22.2 us
    ppermute x6, waiting for transfers between devices, inwards(): lax.ppermute(x, 'patch', [(k, k + 1), (groups - 1 - k, groups - 2 - k)])  21.2 us
  transfers between devices with their start and end apart: 40, of which 21 were waited for; matrix products, arithmetic and copies ran while one was open for 8% of the time, Pallas kernels for 13%

profile of v8, /device:TPU:0, one launch (start us, length us, event | category | flops | bytes accessed | tf_op | source)
XLA Modules:
  0.0 628.9 jit_solution(5090877982352937231)
XLA Ops:
  7.2 3.2 convert_element_type.318
  17.2 8.8 %order_patches.1 = (bf16[8,208,768]{2,1,0:T(8,128)(2,1)}, bf16[8,80,768]{2,1,0:T(8,128)(2,1)}, f32[8,80,768]{2,1,0:T(8,128)}, f32[8,208,512]{2,1,0:T(8,128)}) custom-call(s32[8,208,1]{2,1,0:T(8,128)} %copy.54.shuffle_ref, bf16[8,196,768]{2,1,0:T(8,128)(2,1)} %copy.55.pixels_ref, bf16[2,196,768]{2,1,0:T(8,128)(2,1)} %constant.84.clone.sin_d_ref, ...), custom_call_target="tpu_custom_call" | custom-call | tf_op jit(solution)/shard_map/order_patches/pallas_call | solution.py:424
  26.7 114.1 %all-gather.2.cloned.1.call-done.wg_ref = bf16[49280,256]{1,0:T(8,128)(2,1)} async-done(((bf16[6160,256]{1,0:T(8,128)(2,1)}), bf16[49280,256]{1,0:T(8,128)(2,1)}) %all-gather.2.cloned.1.call-update) | async-done | bytes 25231376 | tf_op jit(solution)/shard_map/all_gather | solution.py:1151
  142.5 34.0 %encoder_forward.1 = (f32[640,768]{1,0:T(8,128)}, bf16[640,768]{1,0:T(8,128)(2,1)}, bf16[640,2304]{1,0:T(8,128)(2,1)}, f32[8,3,4,80]{3,2,1,0:T(4,128)}, f32[8,3,...) custom-call(s32[177]{0:T(256)} %fusion.17.row_ref, ...), custom_call_target="tpu_custom_call" | custom-call | flops 1000 | bytes 1000 | tf_op jit(solution)/shard_map/encoder_forward/pallas_call | solution.py:453
  176.6 83.5 %decoder.1 = (bf16[1664,512]{1,0:T(8,128)(2,1)}, bf16[1664,1536]{1,0:T(8,128)(2,1)}, bf16[1664,512]{1,0:T(8,128)(2,1)}, bf16[1664,512]{1,0:T(8,128)(2,1)}, bf16[...) custom-call(s32[177]{0:T(256)} %fusion.17.row_ref, ...), custom_call_target="tpu_custom_call" | custom-call | flops 1000 | bytes 1000 | tf_op jit(solution)/shard_map/decoder/pallas_call | solution.py:453
  260.1 17.6 %encoder_mlp_back.1 = (bf16[640,768]{1,0:T(8,128)(2,1)}, bf16[640,3072]{1,0:T(8,128)(2,1)}, f32[640,768]{1,0:T(8,128)}, bf16[640,768]{1,0:T(8,128)(2,1)}, f32[8,8192]{1,0:T(8,128)}) custom-call(s32[177]{0:T(256)} %fusion.17.row_ref, bf16[49280,256]{1,0:T(8,128)(2,1)} %all-gather.2.cloned.1.call-done.wg_ref, f32[1,21760]{1,0:T(1,128)} %reshape.118.vec_ref, ...), custom_call_target="tpu_custom_call" | custom-call | flops 1000 | bytes 1000 | tf_op jit(solution)/shard_map/encoder_mlp_back/pallas_call | solution.py:453
  277.7 8.1 %weight_grad.11 = (bf16[4,81,32,256]{3,2,1,0:T(8,128)(2,1)}, bf16[4,81,32,256]{3,2,1,0:T(8,128)(2,1)}) custom-call(s32[1]{0:T(128)} %bitcast.9.index_ref, bf16[640,768]{1,0:T(8,128)(2,1)} %get-tuple-element.147.x_ref, bf16[640,3072]{1,0:T(8,128)(2,1)} %get-tuple-element.148.g_ref), custom_call_target="tpu_custom_call" | custom-call | flops 1000 | bytes 1000 | tf_op jit(solution)/shard_map/weight_grad/pallas_call | solution.py:916
  285.7 7.9 %weight_grad.12 = (bf16[4,81,32,256]{3,2,1,0:T(8,128)(2,1)}, bf16[4,81,32,256]{3,2,1,0:T(8,128)(2,1)}) custom-call(s32[1]{0:T(128)} %bitcast.9.index_ref, bf16[640,3072]{1,0:T(8,128)(2,1)} %get-tuple-element.145.x_ref, bf16[640,768]{1,0:T(8,128)(2,1)} %get-tuple-element.146.g_ref, ...), custom_call_target="tpu_custom_call", output_to_operand_aliasing={{0}: (3, {}), {1}: (4, {})} | custom-call | flops 1000 | bytes 1000 | tf_op jit(solution)/shard_map/weight_grad/pallas_call | solution.py:916
  293.6 3.7 weight_grad.13
  297.6 8.3 %weight_grad.14 = (bf16[4,60,32,256]{3,2,1,0:T(8,128)(2,1)}, bf16[4,60,32,256]{3,2,1,0:T(8,128)(2,1)}) custom-call(s32[1]{0:T(128)} %bitcast.9.index_ref, bf16[1664,512]{1,0:T(8,128)(2,1)} %get-tuple-element.157.x_ref, bf16[1664,2048]{1,0:T(8,128)(2,1)} %get-tuple-element.158.g_ref), custom_call_target="tpu_custom_call" | custom-call | flops 1000 | bytes 1000 | tf_op jit(solution)/shard_map/weight_grad/pallas_call | solution.py:916
  305.9 8.3 %weight_grad.15 = (bf16[4,60,32,256]{3,2,1,0:T(8,128)(2,1)}, bf16[4,60,32,256]{3,2,1,0:T(8,128)(2,1)}) custom-call(s32[1]{0:T(128)} %bitcast.9.index_ref, bf16[1664,2048]{1,0:T(8,128)(2,1)} %get-tuple-element.155.x_ref, bf16[1664,512]{1,0:T(8,128)(2,1)} %get-tuple-element.156.g_ref, ...), custom_call_target="tpu_custom_call", output_to_operand_aliasing={{0}: (3, {}), {1}: (4, {})} | custom-call | flops 1000 | bytes 1000 | tf_op jit(solution)/shard_map/weight_grad/pallas_call | solution.py:916
  314.3 6.8 %add_convert_fusion = bf16[4,81,32,256]{3,2,1,0:T(8,128)(2,1)S(1)} fusion(bf16[4,81,32,256]{3,2,1,0:T(8,128)(2,1)} %collective-permute-done, bf16[4,81,32,256]{3,2,1,0:T(8,128)(2,1)} %get-tuple-element.163), kind=kLoop, calls=%fused_computation.2 | loop fusion | flops 10616832 | bytes 15925248 | tf_op jit(solution)/shard_map/convert_element_type | solution.py:979
  325.2 4.0 weight_grad.16
  329.2 7.0 %weight_grad.17 = (bf16[4,60,32,256]{3,2,1,0:T(8,128)(2,1)}, bf16[4,60,32,256]{3,2,1,0:T(8,128)(2,1)}) custom-call(s32[1]{0:T(128)} %bitcast.9.index_ref, bf16[1664,512]{1,0:T(8,128)(2,1)} %get-tuple-element.168.x_ref, bf16[1664,1536]{1,0:T(8,128)(2,1)} %get-tuple-element.169.g_ref, ...), custom_call_target="tpu_custom_call", output_to_operand_aliasing={{0}: (3, {}), {1}: (4, {})} | custom-call | flops 1000 | bytes 1000 | tf_op jit(solution)/shard_map/weight_grad/pallas_call | solution.py:916
  336.2 4.8 weight_grad.18
  341.0 3.2 weight_grad.19
  344.2 12.1 %encoder_attention_back.2 = (bf16[640,2304]{1,0:T(8,128)(2,1)}, bf16[640,768]{1,0:T(8,128)(2,1)}, f32[8,4608]{1,0:T(8,128)}) custom-call(s32[177]{0:T(256)} %fusion.17.row_ref, s32[8]{0:T(128)} %len_ref.7, bf16[49280,256]{1,0:T(8,128)(2,1)} %all-gather.2.cloned.1.call-done.wg_ref, f32[1,21760]{1,0:T(1,128)} %reshape.118.vec_ref, ...), custom_call_target="tpu_custom_call" | custom-call | flops 1000 | bytes 1000 | tf_op jit(solution)/shard_map/encoder_attention_back/pallas_call | solution.py:453
  358.4 2.4 fusion
  365.6 12.2 %encoder_attention_back.3 = (bf16[640,2304]{1,0:T(8,128)(2,1)}, bf16[640,768]{1,0:T(8,128)(2,1)}, f32[8,4608]{1,0:T(8,128)}) custom-call(s32[177]{0:T(256)} %fusion.17.row_ref, s32[8]{0:T(128)} %len_ref.7, bf16[49280,256]{1,0:T(8,128)(2,1)} %all-gather.2.cloned.1.call-done.wg_ref, ...), custom_call_target="tpu_custom_call", output_to_operand_aliasing={{0}: (10, {}), {1}: (11, {})} | custom-call | flops 1000 | bytes 1000 | tf_op jit(solution)/shard_map/encoder_attention_back/pallas_call | solution.py:453
  379.6 2.4 fusion.5
  382.0 2.4 fusion.4
  384.4 4.0 add_convert_fusion.1
  391.7 3.4 collective-permute-start.8
  399.3 6.9 %weight_grad.20 = (bf16[4,38,32,256]{3,2,1,0:T(8,128)(2,1)}, bf16[4,38,32,256]{3,2,1,0:T(8,128)(2,1)}) custom-call(s32[1]{0:T(128)} %bitcast.9.index_ref, bf16[640,768]{1,0:T(8,128)(2,1)} %get-tuple-element.205.x_ref, bf16[640,2304]{1,0:T(8,128)(2,1)} %get-tuple-element.206.g_ref, ...), custom_call_target="tpu_custom_call", output_to_operand_aliasing={{0}: (3, {}), {1}: (4, {})} | custom-call | flops 1000 | bytes 1000 | tf_op jit(solution)/shard_map/weight_grad/pallas_call | solution.py:916
  406.2 3.8 weight_grad.21
  409.9 2.3 add_convert_fusion.6
  415.6 3.7 collective-permute-done.6
  419.3 2.5 fusion.3
  427.4 11.3 %collective-permute-done.13 = bf16[41,32,256]{2,1,0:T(8,128)(2,1)S(1)} collective-permute-done((bf16[41,32,256]{2,1,0:T(8,128)(2,1)}, bf16[41,32,256]{2,1,0:T(8,128)(2,1)S(1)}, u32[]{:S(2)}, u32[]{:S(2)}) %collective-permute-start.13) | collective-permute-done | bytes 671776 | tf_op jit(solution)/shard_map/ppermute | solution.py:1014
  438.7 2.2 add_convert_fusion.4
  443.9 2.9 add_convert_fusion.2
  447.1 5.2 collective-permute-start.21
  459.4 2.8 collective-permute-done.21
  462.2 4.4 collective-permute-start.20
  471.5 4.3 collective-permute-done.16
  480.2 4.6 collective-permute-done.19
  485.7 7.4 %collective-permute-done.22 = bf16[41,32,256]{2,1,0:T(8,128)(2,1)S(1)} collective-permute-done((bf16[41,32,256]{2,1,0:T(8,128)(2,1)S(1)}, bf16[41,32,256]{2,1,0:T(8,128)(2,1)S(1)}, u32[]{:S(2)}, u32[]{:S(2)}) %collective-permute-start.22) | collective-permute-done | bytes 671776 | tf_op jit(solution)/shard_map/ppermute | solution.py:1020
  497.4 4.5 collective-permute-done.30
  502.7 2.5 collective-permute-done.27
  511.8 11.8 %collective-permute-done.24 = bf16[30,32,256]{2,1,0:T(8,128)(2,1)S(1)} collective-permute-done((bf16[30,32,256]{2,1,0:T(8,128)(2,1)S(1)}, bf16[30,32,256]{2,1,0:T(8,128)(2,1)S(1)}, u32[]{:S(2)}, u32[]{:S(2)}) %collective-permute-start.24) | collective-permute-done | bytes 491552 | tf_op jit(solution)/shard_map/ppermute | solution.py:1020
  523.8 11.6 %collective-permute-done.26 = bf16[30,32,256]{2,1,0:T(8,128)(2,1)S(1)} collective-permute-done((bf16[30,32,256]{2,1,0:T(8,128)(2,1)S(1)}, bf16[30,32,256]{2,1,0:T(8,128)(2,1)S(1)}, u32[]{:S(2)}, u32[]{:S(2)}) %collective-permute-start.26) | collective-permute-done | bytes 491552 | tf_op jit(solution)/shard_map/ppermute | solution.py:1020
  535.8 8.1 %collective-permute-done.29 = bf16[19,32,256]{2,1,0:T(8,128)(2,1)S(1)} collective-permute-done((bf16[19,32,256]{2,1,0:T(8,128)(2,1)S(1)}, bf16[19,32,256]{2,1,0:T(8,128)(2,1)S(1)}, u32[]{:S(2)}, u32[]{:S(2)}) %collective-permute-start.29) | collective-permute-done | bytes 311328 | tf_op jit(solution)/shard_map/ppermute | solution.py:1020
  544.9 2.7 gather_fusion.1
  547.6 4.0 all-to-all-start
  569.4 3.5 collective-permute-done.33
  573.5 4.0 collective-permute-done.34
  580.6 7.9 %collective-permute-done.36 = f32[3]{0:T(128)S(1)} collective-permute-done((f32[3]{0:T(128)S(1)}, f32[3]{0:T(128)S(1)}, u32[]{:S(2)}, u32[]{:S(2)}) %collective-permute-start.36) | collective-permute-done | bytes 44 | tf_op jit(solution)/shard_map/ppermute | solution.py:983
  598.3 22.2 %tile_update.1 = (f32[24,256,256]{2,1,0:T(8,128)}, f32[24,256,256]{2,1,0:T(8,128)}, f32[24,256,256]{2,1,0:T(8,128)}, f32[24,256,256]{2,1,0:T(8,128)}) custom-call(f32[1]{0:T(128)} %bitcast.41.scale_ref, bf16[8,24,32,256]{3,2,1,0:T(8,128)(2,1)} %bitcast.91, f32[24,256,256]{2,1,0:T(8,128)} %w_ref.1, f32[24,256,256]{2,1,0:T(8,128)} %left_stat_ref.1, ...), custom_call_target="tpu_custom_call" | custom-call | tf_op jit(solution)/shard_map/tile_update/pallas_call | solution.py:1077
  (217 shorter events, 94.9 us)
Async XLA Ops:
  7.2 133.7 %all-gather.2.cloned.1.call-start = ((), (), s32[]{:S(2)}) async-start(), calls=%async_computation.1 | async-start | bytes 28385280 | tf_op jit(solution)/shard_map/all_gather | solution.py:1151
  297.3 16.9 %collective-permute-start = (bf16[4,81,32,256]{3,2,1,0:T(8,128)(2,1)}, bf16[4,81,32,256]{3,2,1,0:T(8,128)(2,1)}, u32[]{:S(2)}, u32[]{:S(2)}) collective-permute-start(bf16[4,81,32,256]{3,2,1,0:T(8,128)(2,1)} %get-tuple-element.164), channel_id=1, source_target_pairs={{0,4},{4,0},{8,12},{12,8},{16,20},{20,16},{24,28},{28,24},{1,5},{5... | collective-permute-start | bytes 15925256 | tf_op jit(solution)/shard_map/ppermute | solution.py:983
  321.9 34.3 %collective-permute-start.1 = (bf16[2,40,32,256]{3,2,1,0:T(8,128)(2,1)S(1)}, bf16[2,40,32,256]{3,2,1,0:T(8,128)(2,1)}, u32[]{:S(2)}, u32[]{:S(2)}) collective-permute-start(bf16[2,40,32,256]{3,2,1,0:T(8,128)(2,1)S(1)} %slice_bitcast_fusion.1), channel_id=1, source_target_pairs={{0,8},{4,12},{8,0},{12,4},{16,24},{20,28},{24,16},{28,20},{1,9},{5... | collective-permute-start | bytes 3932168 | tf_op jit(solution)/shard_map/ppermute | solution.py:983
  324.6 33.6 %collective-permute-start.2 = (bf16[2,41,32,256]{3,2,1,0:T(8,128)(2,1)}, bf16[2,41,32,256]{3,2,1,0:T(8,128)(2,1)}, u32[]{:S(2)}, u32[]{:S(2)}) collective-permute-start(bf16[2,41,32,256]{3,2,1,0:T(8,128)(2,1)} %slice_bitcast_fusion), channel_id=1, source_target_pairs={{0,16},{4,20},{8,24},{12,28},{16,0},{20,4},{24,8},{28,12},{1,17},{... | collective-permute-start | bytes 4030472 | tf_op jit(solution)/shard_map/ppermute | solution.py:983
  361.3 23.2 %collective-permute-start.3 = (bf16[4,60,32,256]{3,2,1,0:T(8,128)(2,1)S(1)}, bf16[4,60,32,256]{3,2,1,0:T(8,128)(2,1)}, u32[]{:S(2)}, u32[]{:S(2)}) collective-permute-start(bf16[4,60,32,256]{3,2,1,0:T(8,128)(2,1)S(1)} %copy-done.2), channel_id=1, source_target_pairs={{0,4},{4,0},{8,12},{12,8},{16,20},{20,16},{24,28},{28,24},{1,5},{5... | collective-permute-start | bytes 11796488 | tf_op jit(solution)/shard_map/ppermute | solution.py:983
  362.2 17.5 %collective-permute-start.4 = (bf16[40,32,256]{2,1,0:T(8,128)(2,1)}, bf16[40,32,256]{2,1,0:T(8,128)(2,1)}, u32[]{:S(2)}, u32[]{:S(2)}) collective-permute-start(bf16[40,32,256]{2,1,0:T(8,128)(2,1)} %slice_bitcast_fusion.5), channel_id=1, source_target_pairs={{0,16},{4,20},{8,24},{12,28},{16,0},{20,4},{24,8},{28,12},{1,17},{... | collective-permute-start | bytes 1966088 | tf_op jit(solution)/shard_map/ppermute | solution.py:983
  364.5 17.5 %collective-permute-start.5 = (bf16[41,32,256]{2,1,0:T(8,128)(2,1)}, bf16[41,32,256]{2,1,0:T(8,128)(2,1)}, u32[]{:S(2)}, u32[]{:S(2)}) collective-permute-start(bf16[41,32,256]{2,1,0:T(8,128)(2,1)} %slice_bitcast_fusion.4), channel_id=1, source_target_pairs={{0,8},{4,12},{8,0},{12,4},{16,24},{20,28},{24,16},{28,20},{1,9},{5... | collective-permute-start | bytes 2015240 | tf_op jit(solution)/shard_map/ppermute | solution.py:983
  390.2 23.4 %collective-permute-start.7 = (bf16[2,30,32,256]{3,2,1,0:T(8,128)(2,1)S(1)}, bf16[2,30,32,256]{3,2,1,0:T(8,128)(2,1)}, u32[]{:S(2)}, u32[]{:S(2)}) collective-permute-start(bf16[2,30,32,256]{3,2,1,0:T(8,128)(2,1)S(1)} %slice_bitcast_fusion.2), channel_id=1, source_target_pairs={{0,16},{4,20},{8,24},{12,28},{16,0},{20,4},{24,8},{28,12},{1,17},{... | collective-permute-start | bytes 2949128 | tf_op jit(solution)/shard_map/ppermute | solution.py:983
  391.7 18.3 %collective-permute-start.8 = (bf16[40,32,256]{2,1,0:T(8,128)(2,1)}, bf16[40,32,256]{2,1,0:T(8,128)(2,1)S(1)}, u32[]{:S(2)}, u32[]{:S(2)}) collective-permute-start(bf16[40,32,256]{2,1,0:T(8,128)(2,1)} %fusion.5), channel_id=1, source_target_pairs={{0,1},{3,2},{4,5},{7,6},{8,9},{11,10},{12,13},{15,14},{16,17},{19,... | collective-permute-start | bytes 1966088 | tf_op jit(solution)/shard_map/ppermute | solution.py:1014
  396.1 23.1 %collective-permute-start.6 = (bf16[2,30,32,256]{3,2,1,0:T(8,128)(2,1)}, bf16[2,30,32,256]{3,2,1,0:T(8,128)(2,1)}, u32[]{:S(2)}, u32[]{:S(2)}) collective-permute-start(bf16[2,30,32,256]{3,2,1,0:T(8,128)(2,1)} %slice_bitcast_fusion.3), channel_id=1, source_target_pairs={{0,8},{4,12},{8,0},{12,4},{16,24},{20,28},{24,16},{28,20},{1,9},{5... | collective-permute-start | bytes 2949128 | tf_op jit(solution)/shard_map/ppermute | solution.py:983
  421.8 22.1 %collective-permute-start.9 = (bf16[4,38,32,256]{3,2,1,0:T(8,128)(2,1)S(1)}, bf16[4,38,32,256]{3,2,1,0:T(8,128)(2,1)}, u32[]{:S(2)}, u32[]{:S(2)}) collective-permute-start(bf16[4,38,32,256]{3,2,1,0:T(8,128)(2,1)S(1)} %copy-done.7), channel_id=1, source_target_pairs={{0,4},{4,0},{8,12},{12,8},{16,20},{20,16},{24,28},{28,24},{1,5},{5... | collective-permute-start | bytes 7471112 | tf_op jit(solution)/shard_map/ppermute | solution.py:983
  421.8 16.9 %collective-permute-start.13 = (bf16[41,32,256]{2,1,0:T(8,128)(2,1)}, bf16[41,32,256]{2,1,0:T(8,128)(2,1)S(1)}, u32[]{:S(2)}, u32[]{:S(2)}) collective-permute-start(bf16[41,32,256]{2,1,0:T(8,128)(2,1)} %fusion.4), channel_id=1, source_target_pairs={{0,1},{3,2},{4,5},{7,6},{8,9},{11,10},{12,13},{15,14},{16,17},{19,... | collective-permute-start | bytes 2015240 | tf_op jit(solution)/shard_map/ppermute | solution.py:1014
  423.4 18.4 %copy-start.18 = (bf16[2,30,32,256]{3,2,1,0:T(8,128)(2,1)S(1)}, bf16[2,30,32,256]{3,2,1,0:T(8,128)(2,1)}, u32[]{:S(2)}) copy-start(bf16[2,30,32,256]{3,2,1,0:T(8,128)(2,1)} %fusion.3) | copy-start | bytes 2949124
  423.4 19.4 %collective-permute-start.12 = (bf16[40,32,256]{2,1,0:T(8,128)(2,1)}, bf16[40,32,256]{2,1,0:T(8,128)(2,1)S(1)}, u32[]{:S(2)}, u32[]{:S(2)}) collective-permute-start(bf16[40,32,256]{2,1,0:T(8,128)(2,1)} %add_convert_fusion.6), channel_id=1, source_target_pairs={{1,2},{2,1},{5,6},{6,5},{9,10},{10,9},{13,14},{14,13},{17,18},{18,... | collective-permute-start | bytes 1966088 | tf_op jit(solution)/shard_map/ppermute | solution.py:1017
  424.5 16.4 %collective-permute-start.11 = (bf16[30,32,256]{2,1,0:T(8,128)(2,1)S(1)}, bf16[30,32,256]{2,1,0:T(8,128)(2,1)S(1)}, u32[]{:S(2)}, u32[]{:S(2)}) collective-permute-start(bf16[30,32,256]{2,1,0:T(8,128)(2,1)S(1)} %slice_bitcast_fusion.9), channel_id=1, source_target_pairs={{0,8},{4,12},{8,0},{12,4},{16,24},{20,28},{24,16},{28,20},{1,9},{5... | collective-permute-start | bytes 1474568 | tf_op jit(solution)/shard_map/ppermute | solution.py:983
  426.7 15.1 %collective-permute-start.10 = (bf16[30,32,256]{2,1,0:T(8,128)(2,1)S(1)}, bf16[30,32,256]{2,1,0:T(8,128)(2,1)S(1)}, u32[]{:S(2)}, u32[]{:S(2)}) collective-permute-start(bf16[30,32,256]{2,1,0:T(8,128)(2,1)S(1)} %slice_bitcast_fusion.10), channel_id=1, source_target_pairs={{0,16},{4,20},{8,24},{12,28},{16,0},{20,4},{24,8},{28,12},{1,17},{... | collective-permute-start | bytes 1474568 | tf_op jit(solution)/shard_map/ppermute | solution.py:983
  447.1 15.1 %collective-permute-start.21 = (bf16[30,32,256]{2,1,0:T(8,128)(2,1)}, bf16[30,32,256]{2,1,0:T(8,128)(2,1)}, u32[]{:S(2)}, u32[]{:S(2)}) collective-permute-start(bf16[30,32,256]{2,1,0:T(8,128)(2,1)} %fusion.8), channel_id=1, source_target_pairs={{0,1},{3,2},{4,5},{7,6},{8,9},{11,10},{12,13},{15,14},{16,17},{19,... | collective-permute-start | bytes 1474568 | tf_op jit(solution)/shard_map/ppermute | solution.py:1014
  453.1 15.7 %collective-permute-start.15 = (bf16[2,19,32,256]{3,2,1,0:T(8,128)(2,1)}, bf16[2,19,32,256]{3,2,1,0:T(8,128)(2,1)}, u32[]{:S(2)}, u32[]{:S(2)}) collective-permute-start(bf16[2,19,32,256]{3,2,1,0:T(8,128)(2,1)} %slice_bitcast_fusion.7), channel_id=1, source_target_pairs={{0,16},{4,20},{8,24},{12,28},{16,0},{20,4},{24,8},{28,12},{1,17},{... | collective-permute-start | bytes 1867784 | tf_op jit(solution)/shard_map/ppermute | solution.py:983
  454.6 15.6 %collective-permute-start.14 = (bf16[2,19,32,256]{3,2,1,0:T(8,128)(2,1)}, bf16[2,19,32,256]{3,2,1,0:T(8,128)(2,1)}, u32[]{:S(2)}, u32[]{:S(2)}) collective-permute-start(bf16[2,19,32,256]{3,2,1,0:T(8,128)(2,1)} %slice_bitcast_fusion.8), channel_id=1, source_target_pairs={{0,8},{4,12},{8,0},{12,4},{16,24},{20,28},{24,16},{28,20},{1,9},{5... | collective-permute-start | bytes 1867784 | tf_op jit(solution)/shard_map/ppermute | solution.py:983
  457.3 18.5 %copy-start.20 = (bf16[40,32,256]{2,1,0:T(8,128)(2,1)S(1)}, bf16[40,32,256]{2,1,0:T(8,128)(2,1)}, u32[]{:S(2)}) copy-start(bf16[40,32,256]{2,1,0:T(8,128)(2,1)} %add_convert_fusion.5) | copy-start | bytes 1966084
  457.3 18.6 %collective-permute-start.17 = (bf16[41,32,256]{2,1,0:T(8,128)(2,1)S(1)}, bf16[41,32,256]{2,1,0:T(8,128)(2,1)S(1)}, u32[]{:S(2)}, u32[]{:S(2)}) collective-permute-start(bf16[41,32,256]{2,1,0:T(8,128)(2,1)S(1)} %copy-done.19), channel_id=1, source_target_pairs={{1,2},{2,1},{5,6},{6,5},{9,10},{10,9},{13,14},{14,13},{17,18},{18,... | collective-permute-start | bytes 2015240 | tf_op jit(solution)/shard_map/ppermute | solution.py:1017
  458.1 17.7 %collective-permute-start.16 = (bf16[40,32,256]{2,1,0:T(8,128)(2,1)}, bf16[40,32,256]{2,1,0:T(8,128)(2,1)S(1)}, u32[]{:S(2)}, u32[]{:S(2)}) collective-permute-start(bf16[40,32,256]{2,1,0:T(8,128)(2,1)} %add_convert_fusion.5), channel_id=1, source_target_pairs={{1,0},{2,3},{5,4},{6,7},{9,8},{10,11},{13,12},{14,15},{17,16},{18,... | collective-permute-start | bytes 1966088 | tf_op jit(solution)/shard_map/ppermute | solution.py:1020
  462.2 17.9 %collective-permute-start.20 = (bf16[30,32,256]{2,1,0:T(8,128)(2,1)}, bf16[30,32,256]{2,1,0:T(8,128)(2,1)S(1)}, u32[]{:S(2)}, u32[]{:S(2)}) collective-permute-start(bf16[30,32,256]{2,1,0:T(8,128)(2,1)} %fusion.9), channel_id=1, source_target_pairs={{0,1},{3,2},{4,5},{7,6},{8,9},{11,10},{12,13},{15,14},{16,17},{19,... | collective-permute-start | bytes 1474568 | tf_op jit(solution)/shard_map/ppermute | solution.py:1014
  475.9 59.8 %copy-start.12 = (bf16[40,32,256]{2,1,0:T(8,128)(2,1)}, bf16[40,32,256]{2,1,0:T(8,128)(2,1)S(1)}, u32[]{:S(2)}) copy-start(bf16[40,32,256]{2,1,0:T(8,128)(2,1)S(1)} %broadcast_select_fusion.1) | copy-start | bytes 1966084
  476.2 16.9 %collective-permute-start.22 = (bf16[41,32,256]{2,1,0:T(8,128)(2,1)S(1)}, bf16[41,32,256]{2,1,0:T(8,128)(2,1)S(1)}, u32[]{:S(2)}, u32[]{:S(2)}) collective-permute-start(bf16[41,32,256]{2,1,0:T(8,128)(2,1)S(1)} %add_convert_fusion.3), channel_id=1, source_target_pairs={{1,0},{2,3},{5,4},{6,7},{9,8},{10,11},{13,12},{14,15},{17,16},{18,... | collective-permute-start | bytes 2015240 | tf_op jit(solution)/shard_map/ppermute | solution.py:1020
  477.5 7.3 %collective-permute-start.19 = (bf16[19,32,256]{2,1,0:T(8,128)(2,1)S(1)}, bf16[19,32,256]{2,1,0:T(8,128)(2,1)S(1)}, u32[]{:S(2)}, u32[]{:S(2)}) collective-permute-start(bf16[19,32,256]{2,1,0:T(8,128)(2,1)S(1)} %slice_bitcast_fusion.11), channel_id=1, source_target_pairs={{0,8},{4,12},{8,0},{12,4},{16,24},{20,28},{24,16},{28,20},{1,9},{5... | collective-permute-start | bytes 933896 | tf_op jit(solution)/shard_map/ppermute | solution.py:983
  478.5 7.1 %collective-permute-start.18 = (bf16[19,32,256]{2,1,0:T(8,128)(2,1)S(1)}, bf16[19,32,256]{2,1,0:T(8,128)(2,1)S(1)}, u32[]{:S(2)}, u32[]{:S(2)}) collective-permute-start(bf16[19,32,256]{2,1,0:T(8,128)(2,1)S(1)} %slice_bitcast_fusion.12), channel_id=1, source_target_pairs={{0,16},{4,20},{8,24},{12,28},{16,0},{20,4},{24,8},{28,12},{1,17},{... | collective-permute-start | bytes 933896 | tf_op jit(solution)/shard_map/ppermute | solution.py:983
  493.1 42.6 %copy-start.11 = (bf16[41,32,256]{2,1,0:T(8,128)(2,1)}, bf16[41,32,256]{2,1,0:T(8,128)(2,1)S(1)}, u32[]{:S(2)}) copy-start(bf16[41,32,256]{2,1,0:T(8,128)(2,1)S(1)} %broadcast_select_fusion) | copy-start | bytes 2015236
  493.1 8.8 %collective-permute-start.30 = (bf16[19,32,256]{2,1,0:T(8,128)(2,1)S(1)}, bf16[19,32,256]{2,1,0:T(8,128)(2,1)S(1)}, u32[]{:S(2)}, u32[]{:S(2)}) collective-permute-start(bf16[19,32,256]{2,1,0:T(8,128)(2,1)S(1)} %fusion.10), channel_id=1, source_target_pairs={{0,1},{3,2},{4,5},{7,6},{8,9},{11,10},{12,13},{15,14},{16,17},{19,... | collective-permute-start | bytes 933896 | tf_op jit(solution)/shard_map/ppermute | solution.py:1014
  494.6 10.6 %collective-permute-start.27 = (bf16[19,32,256]{2,1,0:T(8,128)(2,1)S(1)}, bf16[19,32,256]{2,1,0:T(8,128)(2,1)S(1)}, u32[]{:S(2)}, u32[]{:S(2)}) collective-permute-start(bf16[19,32,256]{2,1,0:T(8,128)(2,1)S(1)} %fusion.11), channel_id=1, source_target_pairs={{0,1},{3,2},{4,5},{7,6},{8,9},{11,10},{12,13},{15,14},{16,17},{19,... | collective-permute-start | bytes 933896 | tf_op jit(solution)/shard_map/ppermute | solution.py:1014
  496.0 10.1 %collective-permute-start.23 = (bf16[30,32,256]{2,1,0:T(8,128)(2,1)S(1)}, bf16[30,32,256]{2,1,0:T(8,128)(2,1)S(1)}, u32[]{:S(2)}, u32[]{:S(2)}) collective-permute-start(bf16[30,32,256]{2,1,0:T(8,128)(2,1)S(1)} %add_convert_fusion.10), channel_id=1, source_target_pairs={{1,2},{2,1},{5,6},{6,5},{9,10},{10,9},{13,14},{14,13},{17,18},{18,... | collective-permute-start | bytes 1474568 | tf_op jit(solution)/shard_map/ppermute | solution.py:1017
  496.7 10.9 %collective-permute-start.25 = (bf16[30,32,256]{2,1,0:T(8,128)(2,1)S(1)}, bf16[30,32,256]{2,1,0:T(8,128)(2,1)S(1)}, u32[]{:S(2)}, u32[]{:S(2)}) collective-permute-start(bf16[30,32,256]{2,1,0:T(8,128)(2,1)S(1)} %add_convert_fusion.9), channel_id=1, source_target_pairs={{1,2},{2,1},{5,6},{6,5},{9,10},{10,9},{13,14},{14,13},{17,18},{18,... | collective-permute-start | bytes 1474568 | tf_op jit(solution)/shard_map/ppermute | solution.py:1017
  502.0 7.0 %collective-permute-start.31 = (bf16[19,32,256]{2,1,0:T(8,128)(2,1)S(1)}, bf16[19,32,256]{2,1,0:T(8,128)(2,1)S(1)}, u32[]{:S(2)}, u32[]{:S(2)}) collective-permute-start(bf16[19,32,256]{2,1,0:T(8,128)(2,1)S(1)} %add_convert_fusion.12), channel_id=1, source_target_pairs={{1,2},{2,1},{5,6},{6,5},{9,10},{10,9},{13,14},{14,13},{17,18},{18,... | collective-permute-start | bytes 933896 | tf_op jit(solution)/shard_map/ppermute | solution.py:1017
  505.3 5.1 collective-permute-start.28
  506.2 29.5 %copy-start.15 = (bf16[30,32,256]{2,1,0:T(8,128)(2,1)}, bf16[30,32,256]{2,1,0:T(8,128)(2,1)S(1)}, u32[]{:S(2)}) copy-start(bf16[30,32,256]{2,1,0:T(8,128)(2,1)S(1)} %add_convert_fusion.8) | copy-start | bytes 1474564
  506.2 17.4 %collective-permute-start.24 = (bf16[30,32,256]{2,1,0:T(8,128)(2,1)S(1)}, bf16[30,32,256]{2,1,0:T(8,128)(2,1)S(1)}, u32[]{:S(2)}, u32[]{:S(2)}) collective-permute-start(bf16[30,32,256]{2,1,0:T(8,128)(2,1)S(1)} %add_convert_fusion.8), channel_id=1, source_target_pairs={{1,0},{2,3},{5,4},{6,7},{9,8},{10,11},{13,12},{14,15},{17,16},{18,... | collective-permute-start | bytes 1474568 | tf_op jit(solution)/shard_map/ppermute | solution.py:1020
  507.7 28.1 %copy-start.17 = (bf16[30,32,256]{2,1,0:T(8,128)(2,1)}, bf16[30,32,256]{2,1,0:T(8,128)(2,1)S(1)}, u32[]{:S(2)}) copy-start(bf16[30,32,256]{2,1,0:T(8,128)(2,1)S(1)} %add_convert_fusion.7) | copy-start | bytes 1474564
  507.7 27.8 %collective-permute-start.26 = (bf16[30,32,256]{2,1,0:T(8,128)(2,1)S(1)}, bf16[30,32,256]{2,1,0:T(8,128)(2,1)S(1)}, u32[]{:S(2)}, u32[]{:S(2)}) collective-permute-start(bf16[30,32,256]{2,1,0:T(8,128)(2,1)S(1)} %add_convert_fusion.7), channel_id=1, source_target_pairs={{1,0},{2,3},{5,4},{6,7},{9,8},{10,11},{13,12},{14,15},{17,16},{18,... | collective-permute-start | bytes 1474568 | tf_op jit(solution)/shard_map/ppermute | solution.py:1020
  509.1 34.9 %collective-permute-start.32 = (bf16[19,32,256]{2,1,0:T(8,128)(2,1)S(1)}, bf16[19,32,256]{2,1,0:T(8,128)(2,1)S(1)}, u32[]{:S(2)}, u32[]{:S(2)}) collective-permute-start(bf16[19,32,256]{2,1,0:T(8,128)(2,1)S(1)} %add_convert_fusion.11), channel_id=1, source_target_pairs={{1,0},{2,3},{5,4},{6,7},{9,8},{10,11},{13,12},{14,15},{17,16},{18,... | collective-permute-start | bytes 933896 | tf_op jit(solution)/shard_map/ppermute | solution.py:1020
  510.5 33.4 %collective-permute-start.29 = (bf16[19,32,256]{2,1,0:T(8,128)(2,1)S(1)}, bf16[19,32,256]{2,1,0:T(8,128)(2,1)S(1)}, u32[]{:S(2)}, u32[]{:S(2)}) collective-permute-start(bf16[19,32,256]{2,1,0:T(8,128)(2,1)S(1)} %add_convert_fusion.13), channel_id=1, source_target_pairs={{1,0},{2,3},{5,4},{6,7},{9,8},{10,11},{13,12},{14,15},{17,16},{18,... | collective-permute-start | bytes 933896 | tf_op jit(solution)/shard_map/ppermute | solution.py:1020
  547.6 49.1 %all-to-all-start = ((bf16[192,32,256]{2,1,0:T(8,128)(2,1)}), bf16[192,32,256]{2,1,0:T(8,128)(2,1)S(1)}, u32[]{:S(2)}, u32[]{:S(2)}) async-start(bf16[192,32,256]{2,1,0:T(8,128)(2,1)} %gather_fusion.1), calls=%async_computation | async-start | bytes 6291456 | tf_op jit(solution)/shard_map/all_to_all | solution.py:1283
  551.6 44.5 %copy-start.29 = (f32[2560]{0:T(1024)S(1)}, f32[2560]{0:T(1024)}, u32[]{:S(2)}) copy-start(f32[2560]{0:T(1024)} %param.22) | copy-start | bytes 30724
  551.6 44.5 %copy-start.30 = (f32[2560]{0:T(1024)S(1)}, f32[2560]{0:T(1024)}, u32[]{:S(2)}) copy-start(f32[2560]{0:T(1024)} %param.21) | copy-start | bytes 30724
  569.4 3.5 collective-permute-start.33
  573.0 4.4 collective-permute-start.34
  577.5 1.1 collective-permute-start.35
  578.6 9.9 %collective-permute-start.36 = (f32[3]{0:T(128)S(1)}, f32[3]{0:T(128)S(1)}, u32[]{:S(2)}, u32[]{:S(2)}) collective-permute-start(f32[3]{0:T(128)S(1)} %add.190), channel_id=1, source_target_pairs={{0,8},{4,12},{8,0},{12,4},{16,24},{20,28},{24,16},{28,20},{1,9},{5... | collective-permute-start | bytes 44 | tf_op jit(solution)/shard_map/ppermute | solution.py:983
  588.5 3.5 collective-permute-start.37
  (26 other events, 155.8 us)
Sparse Core Ops, SparseCore 0:
  12.5 128.2 all-gather.1
